TPU v7x, 128 devices: a whole 4x4x4 slice. The times are simulated.
128 devices in a mesh: branch: 2 (over core), seq: 16 (over y, z), fsdp: 4 (over x).
Axes of the slice: x: 4, y: 4, z: 4, core: 2. Of those that a mesh axis runs over, the one named last changes fastest.
Arguments:
- tokens: bfloat16 [4, 2048, 1600], P('fsdp', 'seq'), may hold values from -6 to 6
- seq_lengths: int32 [4, 3], P('fsdp'), may hold values from 1 to 2046, as said below
- norm_gain: float32 [1600], P(('seq', 'fsdp')), may hold values from 0.25 to 1.75
- meta_tokens: float32 [128, 1600], P(None, ('seq', 'fsdp')), may hold values from -6 to 6
- w_query: float32 [1600, 1600], P(('seq', 'fsdp')), may hold values from -0.15625 to 0.15625
- w_key_value: float32 [1600, 640], P(('seq', 'fsdp')), may hold values from -0.15625 to 0.15625
- w_attn_out: float32 [1600, 1600], P(('seq', 'fsdp')), may hold values from -0.15625 to 0.15625
- attn_gain: float32 [1600], P(('seq', 'fsdp')), may hold values from 0.25 to 1.75
- w_mamba_in: float32 [1600, 6400], P(('seq', 'fsdp')), may hold values from -0.15625 to 0.15625
- conv_weight: float32 [4, 3200], P(None, ('seq', 'fsdp')), may hold values from -3 to 3
- conv_bias: float32 [3200], P(('seq', 'fsdp')), may hold values from -3 to 3
- w_ssm_x: float32 [3200, 132], P(('seq', 'fsdp')), may hold values from -0.109375 to 0.109375
- w_dt: float32 [100, 3200], P(None, ('seq', 'fsdp')), may hold values from -0.625 to 0.625
- dt_bias: float32 [3200], P(('seq', 'fsdp')), may hold values from -2 to 1
- a_log: float32 [16, 3200], P(None, ('seq', 'fsdp')), may hold values from -10 to -3
- skip_d: float32 [3200], P(('seq', 'fsdp')), may hold values from 0.5 to 1.5
- w_mamba_out: float32 [3200, 1600], P(('seq', 'fsdp')), may hold values from -0.109375 to 0.109375
- mamba_gain: float32 [1600], P(('seq', 'fsdp')), may hold values from 0.25 to 1.75
- ffn_gain: float32 [1600], P(('seq', 'fsdp')), may hold values from 0.25 to 1.75
- w_gate_up: float32 [1600, 11008], P(('seq', 'fsdp')), may hold values from -0.15625 to 0.15625
- w_down: float32 [5504, 1600], P(('seq', 'fsdp')), may hold values from -0.078125 to 0.078125
- cotangent: bfloat16 [4, 2048, 1600], P('fsdp', 'seq'), may hold values from -6 to 6
Outputs:
- mixed: bfloat16 [4, 2048, 1600], P('fsdp', 'seq')
- input_grad: float32 [4, 2048, 1600], P('fsdp', 'seq')
- grad_norm_gain: float32 [1600], P(('seq', 'fsdp'))
- grad_meta_tokens: float32 [128, 1600], P(None, ('seq', 'fsdp'))
- grad_w_query: float32 [1600, 1600], P(('seq', 'fsdp'))
- grad_w_key_value: float32 [1600, 640], P(('seq', 'fsdp'))
- grad_w_attn_out: float32 [1600, 1600], P(('seq', 'fsdp'))
- grad_attn_gain: float32 [1600], P(('seq', 'fsdp'))
- grad_w_mamba_in: float32 [1600, 6400], P(('seq', 'fsdp'))
- grad_conv_weight: float32 [4, 3200], P(None, ('seq', 'fsdp'))
- grad_conv_bias: float32 [3200], P(('seq', 'fsdp'))
- grad_w_ssm_x: float32 [3200, 132], P(('seq', 'fsdp'))
- grad_w_dt: float32 [100, 3200], P(None, ('seq', 'fsdp'))
- grad_dt_bias: float32 [3200], P(('seq', 'fsdp'))
- grad_a_log: float32 [16, 3200], P(None, ('seq', 'fsdp'))
- grad_skip_d: float32 [3200], P(('seq', 'fsdp'))
- grad_w_mamba_out: float32 [3200, 1600], P(('seq', 'fsdp'))
- grad_mamba_gain: float32 [1600], P(('seq', 'fsdp'))
- grad_ffn_gain: float32 [1600], P(('seq', 'fsdp'))
- grad_w_gate_up: float32 [1600, 11008], P(('seq', 'fsdp'))
- grad_w_down: float32 [5504, 1600], P(('seq', 'fsdp'))
Inputs may be any that keep to these rules, and one draw needn't show every extreme that they name: `seq_lengths`: each row lists the lengths of 3 sequences packed in order into the 2048 rows of one batch; they sum to 2048, and exactly one of them is longer than 1920, at a place drawn from the seed.
All inputs are finite; a program needn't handle non-finite values.
Results may differ from a plain program's by a relative error of at most 0.015.
The roundings to bfloat16 on the way count: a program that leaves them out, or rounds other values in their place, can miss the bound.
Values may be sent and summed in bfloat16 or wider, within the bound.
A program may use at most 768 MiB of HBM per device.

v0:
```python
import math

import jax
import jax.numpy as jnp
from jax import lax
from jax.sharding import PartitionSpec as P

HEAD = 64
CONV = 4


epsilon = 1e-05
negative_fill = -1e30
score_scale = 0.125
highest = lax.Precision.HIGHEST


def partner(value, axis, stride):
    mask = 2**stride
    pairs = [(source, source ^ mask) for source in range(lax.axis_size(axis))]
    return lax.ppermute(value, axis, pairs)


def from_behind(block, axis, distance):
    devices = range(lax.axis_size(axis))
    route = [(i - distance, i) for i in devices if i - distance in devices]
    return lax.ppermute(block, axis, route)


def prefix(value, axis, join, neutral, backward):
    count, mine = (lax.axis_size(axis), lax.axis_index(axis))
    pieces = jax.tree.map(lambda part: lax.all_gather(part, axis), value)
    if backward:
        pieces = jax.tree.map(lambda part: part[::-1], pieces)
        mine = count - 1 - mine
    subtotal = jax.tree.map(
        lambda part, zero: jnp.full_like(part, 0) + jnp.asarray(zero, part.dtype), value, neutral
    )

    def turn(position, subtotal):
        longer = join(subtotal, jax.tree.map(lambda part: part[position], pieces))
        return jax.tree.map(lambda new, old: jnp.where(position < mine, new, old), longer, subtotal)

    return lax.fori_loop(0, count - 1, turn, subtotal)


def rms_norm(values, gain):
    return values * lax.rsqrt(jnp.mean(values * values, axis=-1, keepdims=True) + epsilon) * gain


def matmul(left, right):
    return jnp.dot(left, right, preferred_element_type=jnp.float32)


def matmul_tn(left, right):
    return lax.dot_general(
        left, right, (((0,), (0,)), ((), ())), preferred_element_type=jnp.float32
    )


def matmul_nt(left, right):
    return lax.dot_general(
        left, right, (((1,), (1,)), ((), ())), preferred_element_type=jnp.float32
    )


def exact_tn(left, right):
    return lax.dot_general(left, right, (((0,), (0,)), ((), ())), precision=highest)


def exact_nt(left, right):
    return lax.dot_general(left, right, (((1,), (1,)), ((), ())), precision=highest)


def segment_of(row_ids, end_rows):
    return jnp.sum((row_ids[:, None] >= end_rows[None, :]).astype(jnp.int32), axis=1)


def branch_partner(values):
    return partner(values, "branch", 0)


def pack_grads(members, pieces, width):
    flattened = jnp.concatenate(
        [(member.T if across else member).reshape(pieces, -1) for member, across in members], axis=1
    )
    return jnp.pad(flattened, ((0, 0), (0, width - flattened.shape[1])))


def layout_width(layout):
    return sum((math.prod(shard_shape) for shard_shape, across in layout))


def unpack_grads(packed_row, layout):
    results = []
    position = 0
    for shard_shape, across in layout:
        entry_count = math.prod(shard_shape)
        portion = packed_row[position : position + entry_count]
        if across:
            results.append(portion.reshape(shard_shape[1], shard_shape[0]).T)
        else:
            results.append(portion.reshape(shard_shape))
        position = position + entry_count
    return results


def conv_silu(conv_in, rim_rows, taps, offset, valid_rows):
    conv_width = taps.shape[0]
    row_count = conv_in.shape[0]
    extended = jnp.concatenate([rim_rows, conv_in], axis=0)
    summed = taps[conv_width - 1] * conv_in + offset
    for shift_by in range(1, conv_width):
        begin_row = conv_width - 1 - shift_by
        summed = (
            summed
            + taps[conv_width - 1 - shift_by]
            * extended[begin_row : begin_row + row_count]
            * valid_rows[shift_by - 1][:, None]
        )
    return jax.nn.silu(summed)


def ssm_scan(inputs_m, steps, b_rows, c_rows, log_decay, keep_rows, state_in):
    row_count = inputs_m.shape[0]
    block_len = math.gcd(row_count, 16)
    decay_rate = -jnp.exp(log_decay)

    def block_step(state_now, pieces):
        input_blk, step_blk, b_blk, c_blk, keep_blk = pieces
        outputs = []
        for position in range(block_len):
            state_now = (
                keep_blk[position] * jnp.exp(step_blk[position][None, :] * decay_rate) * state_now
                + (step_blk[position] * input_blk[position])[None, :] * b_blk[position][:, None]
            )
            outputs.append(jnp.sum(c_blk[position][:, None] * state_now, axis=0))
        return (state_now, jnp.stack(outputs))

    pieces = tuple(
        (
            member.reshape((row_count // block_len, block_len) + member.shape[1:])
            for member in (inputs_m, steps, b_rows, c_rows, keep_rows)
        )
    )
    last_state, outputs = lax.scan(jax.checkpoint(block_step), state_in, pieces)
    return (outputs.reshape(row_count, -1), last_state)


def gate_mix(ssm_out, skip_gain, inputs_m, gate_z):
    return (ssm_out + skip_gain * inputs_m) * jax.nn.silu(gate_z)


def swiglu(gate_up):
    half_width = gate_up.shape[1] // 2
    return jax.nn.silu(gate_up[:, :half_width]) * gate_up[:, half_width:]


def combine_maps(earlier, later):
    return (later[0] * earlier[0], later[1] + later[0] * earlier[1])


def shards(
    tokens,
    seq_lengths,
    norm_gain,
    meta_tokens,
    w_query,
    w_key_value,
    w_attn_out,
    attn_gain,
    w_mamba_in,
    conv_weight,
    conv_bias,
    w_ssm_x,
    w_dt,
    dt_bias,
    a_log,
    skip_d,
    w_mamba_out,
    mamba_gain,
    ffn_gain,
    w_gate_up,
    w_down,
    cotangent,
):
    inputs_f = tokens[0].astype(jnp.float32)
    rows_dev = inputs_f.shape[0]
    model_width = inputs_f.shape[1]
    seq_count = lax.axis_size("seq")
    pieces = lax.axis_size("seq") * lax.axis_size("fsdp")
    group_rows = rows_dev * seq_count
    branch_id = lax.axis_index("branch")
    on_attention = branch_id == 0
    lengths = seq_lengths[0]
    end_rows = jnp.cumsum(lengths)
    start_rows = end_rows - lengths
    all_rows = jnp.arange(group_rows, dtype=jnp.int32)
    all_segments = segment_of(all_rows, end_rows)
    my_rows = lax.axis_index("seq") * rows_dev + jnp.arange(rows_dev, dtype=jnp.int32)
    my_segments = segment_of(my_rows, end_rows)
    keep_rows = 1.0 - jnp.any(my_rows[:, None] == start_rows[None, :], axis=1).astype(jnp.float32)
    valid_rows = jnp.stack(
        [
            (
                (my_rows - shift_by >= 0)
                & (segment_of(my_rows - shift_by, end_rows) == my_segments)
            ).astype(jnp.float32)
            for shift_by in range(1, CONV)
        ]
    )
    shards_block = max(
        [1]
        + [
            count_in
            for count_in in range(1, seq_count + 1)
            if seq_count % count_in == 0 and count_in * rows_dev <= 1024
        ]
    )
    block_rows = shards_block * rows_dev
    needed = my_rows[rows_dev - 1] // block_rows + 1
    masters_b = (
        norm_gain.astype(jnp.bfloat16),
        meta_tokens.astype(jnp.bfloat16),
        w_query.astype(jnp.bfloat16),
        w_key_value.astype(jnp.bfloat16),
        w_attn_out.astype(jnp.bfloat16),
        attn_gain.astype(jnp.bfloat16),
        w_mamba_in.astype(jnp.bfloat16),
        conv_weight.astype(jnp.bfloat16),
        conv_bias.astype(jnp.bfloat16),
        w_ssm_x.astype(jnp.bfloat16),
        w_dt.astype(jnp.bfloat16),
        dt_bias.astype(jnp.bfloat16),
        a_log.astype(jnp.bfloat16),
        skip_d.astype(jnp.bfloat16),
        w_mamba_out.astype(jnp.bfloat16),
        mamba_gain.astype(jnp.bfloat16),
        ffn_gain.astype(jnp.bfloat16),
        w_gate_up.astype(jnp.bfloat16),
        w_down.astype(jnp.bfloat16),
    )
    gathered = (
        lax.all_gather(masters_b[0], ("seq", "fsdp"), axis=0, tiled=True),
        lax.all_gather(masters_b[1], ("seq", "fsdp"), axis=1, tiled=True),
        lax.all_gather(masters_b[2], ("seq", "fsdp"), axis=0, tiled=True),
        lax.all_gather(masters_b[3], ("seq", "fsdp"), axis=0, tiled=True),
        lax.all_gather(masters_b[4], ("seq", "fsdp"), axis=0, tiled=True),
        lax.all_gather(masters_b[5], ("seq", "fsdp"), axis=0, tiled=True),
        lax.all_gather(masters_b[6], ("seq", "fsdp"), axis=0, tiled=True),
        lax.all_gather(masters_b[7], ("seq", "fsdp"), axis=1, tiled=True),
        lax.all_gather(masters_b[8], ("seq", "fsdp"), axis=0, tiled=True),
        lax.all_gather(masters_b[9], ("seq", "fsdp"), axis=0, tiled=True),
        lax.all_gather(masters_b[10], ("seq", "fsdp"), axis=1, tiled=True),
        lax.all_gather(masters_b[11], ("seq", "fsdp"), axis=0, tiled=True),
        lax.all_gather(masters_b[12], ("seq", "fsdp"), axis=1, tiled=True),
        lax.all_gather(masters_b[13], ("seq", "fsdp"), axis=0, tiled=True),
        lax.all_gather(masters_b[14], ("seq", "fsdp"), axis=0, tiled=True),
        lax.all_gather(masters_b[15], ("seq", "fsdp"), axis=0, tiled=True),
        lax.all_gather(masters_b[16], ("seq", "fsdp"), axis=0, tiled=True),
        lax.all_gather(masters_b[17], ("seq", "fsdp"), axis=0, tiled=True),
        lax.all_gather(masters_b[18], ("seq", "fsdp"), axis=0, tiled=True),
    )
    (
        gain_norm,
        meta_rows,
        weight_query,
        weight_keys,
        weight_attn,
        gain_attn,
        weight_mamba,
        conv_taps,
        conv_offset,
        weight_ssm,
        weight_step,
        step_bias,
        log_decay,
        skip_gain,
        weight_back,
        gain_mamba,
        gain_feed,
        weight_gate,
        weight_down,
    ) = gathered
    query_width = weight_query.shape[1]
    keyval_half = weight_keys.shape[1] // 2
    inner_width = weight_mamba.shape[1] // 2
    state_len = log_decay.shape[0]
    step_rank = weight_step.shape[0]
    meta_count = meta_rows.shape[0]
    group_count = keyval_half // HEAD
    per_group = query_width // HEAD // group_count
    head_shape = (rows_dev, group_count, per_group)
    gain_norm_f = gain_norm.astype(jnp.float32)
    meta_f = meta_rows.astype(jnp.float32)
    meta_normed_b = rms_norm(meta_f, gain_norm_f).astype(jnp.bfloat16)
    meta_kv_b = matmul(meta_normed_b, weight_keys).astype(jnp.bfloat16)
    meta_keys = meta_kv_b[:, :keyval_half].reshape(meta_count, group_count, HEAD)
    meta_values = meta_kv_b[:, keyval_half:].reshape(meta_count, group_count, HEAD)
    normed = rms_norm(inputs_f, gain_norm_f)
    normed_b = normed.astype(jnp.bfloat16)

    def attention_first():
        return (
            matmul(normed_b, weight_query).astype(jnp.bfloat16),
            matmul(normed_b, weight_keys).astype(jnp.bfloat16),
            jnp.zeros((rows_dev, inner_width), jnp.bfloat16),
            jnp.zeros((rows_dev, inner_width), jnp.float32),
        )

    def mamba_first():
        mamba_in = matmul(normed_b, weight_mamba)
        return (
            jnp.zeros((rows_dev, query_width), jnp.bfloat16),
            jnp.zeros((rows_dev, 2 * keyval_half), jnp.bfloat16),
            mamba_in[:, :inner_width].astype(jnp.bfloat16),
            mamba_in[:, inner_width:],
        )

    query_b, keyval_b, conv_input, gate_z = lax.cond(on_attention, attention_first, mamba_first)
    keyval_all = lax.all_gather(keyval_b, "seq", axis=0, tiled=True)
    rim_in = from_behind(conv_input[rows_dev - (CONV - 1) :], "seq", 1)
    query_heads = query_b.reshape(rows_dev, group_count, per_group, HEAD)

    def meta_scores():
        return (
            jnp.einsum("qgjd,kgd->qgjk", query_heads, meta_keys, preferred_element_type=jnp.float32)
            * score_scale
        )

    def masked_scores(start_row):
        key_piece = lax.dynamic_slice_in_dim(keyval_all, start_row, block_rows, 0)
        key_rows = key_piece[:, :keyval_half].reshape(block_rows, group_count, HEAD)
        value_rows = key_piece[:, keyval_half:].reshape(block_rows, group_count, HEAD)
        rows_block = lax.dynamic_slice_in_dim(all_rows, start_row, block_rows, 0)
        segments_block = lax.dynamic_slice_in_dim(all_segments, start_row, block_rows, 0)
        scores = (
            jnp.einsum("qgjd,kgd->qgjk", query_heads, key_rows, preferred_element_type=jnp.float32)
            * score_scale
        )
        allowed = (my_segments[:, None] == segments_block[None, :]) & (
            rows_block[None, :] <= my_rows[:, None]
        )
        return (jnp.where(allowed[:, None, None, :], scores, negative_fill), key_rows, value_rows)

    def attention_core():
        meta_first = meta_scores()
        start_max = jnp.max(meta_first, axis=-1)
        start_sum = jnp.sum(jnp.exp(meta_first - start_max[..., None]), axis=-1)

        def max_step(block_id, running):
            running_max, running_sum = running
            scores, key_rows, value_rows = masked_scores(block_id * block_rows)
            new_max = jnp.maximum(running_max, jnp.max(scores, axis=-1))
            running_sum = running_sum * jnp.exp(running_max - new_max) + jnp.sum(
                jnp.exp(scores - new_max[..., None]), axis=-1
            )
            return (new_max, running_sum)

        running_max, running_sum = lax.fori_loop(0, needed, max_step, (start_max, start_sum))
        log_mass = running_max + jnp.log(running_sum)
        meta_probs = jnp.exp(meta_first - log_mass[..., None]).astype(jnp.bfloat16)
        start_out = jnp.einsum(
            "qgjk,kgd->qgjd", meta_probs, meta_values, preferred_element_type=jnp.float32
        )

        def out_step(block_id, summed):
            scores, key_rows, value_rows = masked_scores(block_id * block_rows)
            probs_block = jnp.exp(scores - log_mass[..., None])
            return summed + jnp.einsum(
                "qgjk,kgd->qgjd",
                probs_block.astype(jnp.bfloat16),
                value_rows,
                preferred_element_type=jnp.float32,
            )

        attended = lax.fori_loop(0, needed, out_step, start_out).reshape(rows_dev, query_width)
        pre_norm = matmul(attended.astype(jnp.bfloat16), weight_attn)
        sent_own = rms_norm(pre_norm, gain_attn.astype(jnp.float32)).astype(jnp.bfloat16)
        return (
            attended,
            log_mass,
            pre_norm,
            sent_own,
            jnp.zeros((rows_dev, inner_width), jnp.bfloat16),
            jnp.zeros((rows_dev, step_rank), jnp.bfloat16),
            jnp.zeros((rows_dev, inner_width), jnp.float32),
            jnp.zeros((rows_dev, inner_width), jnp.float32),
            jnp.zeros((rows_dev, state_len), jnp.float32),
            jnp.zeros((rows_dev, state_len), jnp.float32),
            jnp.zeros((state_len, inner_width), jnp.float32),
            jnp.zeros((state_len, inner_width), jnp.float32),
        )

    def mamba_pre():
        inputs_m = conv_silu(
            conv_input.astype(jnp.float32),
            rim_in.astype(jnp.float32),
            conv_taps.astype(jnp.float32),
            conv_offset.astype(jnp.float32),
            valid_rows,
        )
        inputs_b = inputs_m.astype(jnp.bfloat16)
        projected = matmul(inputs_b, weight_ssm)
        step_low = projected[:, :step_rank].astype(jnp.bfloat16)
        b_rows = projected[:, step_rank : step_rank + state_len]
        c_rows = projected[:, step_rank + state_len :]
        step_pre = matmul(step_low, weight_step) + step_bias.astype(jnp.float32)
        steps = jax.nn.softplus(step_pre)
        decay_f = log_decay.astype(jnp.float32)
        _, end_state = ssm_scan(
            inputs_b.astype(jnp.float32),
            steps,
            b_rows,
            c_rows,
            decay_f,
            keep_rows,
            jnp.zeros((state_len, inner_width), jnp.float32),
        )
        decay_all = jnp.prod(keep_rows) * jnp.exp(
            -jnp.exp(decay_f) * jnp.sum(steps, axis=0)[None, :]
        )
        return (
            jnp.zeros((rows_dev, query_width), jnp.float32),
            jnp.zeros(head_shape, jnp.float32),
            jnp.zeros((rows_dev, model_width), jnp.float32),
            jnp.zeros((rows_dev, model_width), jnp.bfloat16),
            inputs_b,
            step_low,
            step_pre,
            steps,
            b_rows,
            c_rows,
            decay_all,
            end_state,
        )

    (
        attended,
        log_mass,
        pre_norm,
        sent_own,
        inputs_b,
        step_low,
        step_pre,
        steps,
        b_rows,
        c_rows,
        decay_all,
        end_state,
    ) = lax.cond(on_attention, attention_core, mamba_pre)
    carried = prefix(
        (decay_all, end_state),
        "seq",
        combine_maps,
        (jnp.ones_like(decay_all), jnp.zeros_like(end_state)),
        False,
    )
    start_state = carried[1]

    def attention_keep():
        return (
            sent_own,
            pre_norm,
            jnp.zeros((rows_dev, inner_width), jnp.float32),
            jnp.zeros((rows_dev, inner_width), jnp.bfloat16),
        )

    def mamba_post():
        ssm_out, _ = ssm_scan(
            inputs_b.astype(jnp.float32),
            steps,
            b_rows,
            c_rows,
            log_decay.astype(jnp.float32),
            keep_rows,
            start_state,
        )
        mixed_y = gate_mix(
            ssm_out, skip_gain.astype(jnp.float32), inputs_b.astype(jnp.float32), gate_z
        ).astype(jnp.bfloat16)
        mamba_out = matmul(mixed_y, weight_back)
        return (
            rms_norm(mamba_out, gain_mamba.astype(jnp.float32)).astype(jnp.bfloat16),
            mamba_out,
            ssm_out,
            mixed_y,
        )

    sent_own, pre_norm, ssm_out, mixed_y = lax.cond(on_attention, attention_keep, mamba_post)
    other_sent = partner(sent_own, "branch", 0)
    hidden = inputs_f + 0.5 * (sent_own.astype(jnp.float32) + other_sent.astype(jnp.float32))
    gain_feed_f = gain_feed.astype(jnp.float32)
    half_rows = rows_dev // 2
    row_start = branch_id * half_rows
    hidden_part = lax.dynamic_slice_in_dim(hidden, row_start, half_rows, 0)
    feed_b = rms_norm(hidden_part, gain_feed_f).astype(jnp.bfloat16)
    gate_up = matmul(feed_b, weight_gate)
    active_b = swiglu(gate_up).astype(jnp.bfloat16)
    out_part = hidden_part + matmul(active_b, weight_down)
    out_other = branch_partner(out_part)
    mixed = jnp.where(
        on_attention,
        jnp.concatenate([out_part, out_other], axis=0),
        jnp.concatenate([out_other, out_part], axis=0),
    ).astype(jnp.bfloat16)
    gathered = (
        lax.all_gather(masters_b[0], ("seq", "fsdp"), axis=0, tiled=True),
        lax.all_gather(masters_b[1], ("seq", "fsdp"), axis=1, tiled=True),
        lax.all_gather(masters_b[2], ("seq", "fsdp"), axis=0, tiled=True),
        lax.all_gather(masters_b[3], ("seq", "fsdp"), axis=0, tiled=True),
        lax.all_gather(masters_b[4], ("seq", "fsdp"), axis=0, tiled=True),
        lax.all_gather(masters_b[5], ("seq", "fsdp"), axis=0, tiled=True),
        lax.all_gather(masters_b[6], ("seq", "fsdp"), axis=0, tiled=True),
        lax.all_gather(masters_b[7], ("seq", "fsdp"), axis=1, tiled=True),
        lax.all_gather(masters_b[8], ("seq", "fsdp"), axis=0, tiled=True),
        lax.all_gather(masters_b[9], ("seq", "fsdp"), axis=0, tiled=True),
        lax.all_gather(masters_b[10], ("seq", "fsdp"), axis=1, tiled=True),
        lax.all_gather(masters_b[11], ("seq", "fsdp"), axis=0, tiled=True),
        lax.all_gather(masters_b[12], ("seq", "fsdp"), axis=1, tiled=True),
        lax.all_gather(masters_b[13], ("seq", "fsdp"), axis=0, tiled=True),
        lax.all_gather(masters_b[14], ("seq", "fsdp"), axis=0, tiled=True),
        lax.all_gather(masters_b[15], ("seq", "fsdp"), axis=0, tiled=True),
        lax.all_gather(masters_b[16], ("seq", "fsdp"), axis=0, tiled=True),
        lax.all_gather(masters_b[17], ("seq", "fsdp"), axis=0, tiled=True),
        lax.all_gather(masters_b[18], ("seq", "fsdp"), axis=0, tiled=True),
    )
    (
        gain_norm,
        meta_rows,
        weight_query,
        weight_keys,
        weight_attn,
        gain_attn,
        weight_mamba,
        conv_taps,
        conv_offset,
        weight_ssm,
        weight_step,
        step_bias,
        log_decay,
        skip_gain,
        weight_back,
        gain_mamba,
        gain_feed,
        weight_gate,
        weight_down,
    ) = gathered
    grad_out = cotangent[0].astype(jnp.float32)
    grad_part = lax.dynamic_slice_in_dim(grad_out, row_start, half_rows, 0)
    grad_part_b = grad_part.astype(jnp.bfloat16)
    grad_down = matmul_tn(active_b, grad_part_b)
    grad_active = matmul_nt(grad_part_b, weight_down)
    _, pull_glu = jax.vjp(swiglu, gate_up)
    (grad_gate_up,) = pull_glu(grad_active)
    grad_gate_up_b = grad_gate_up.astype(jnp.bfloat16)
    grad_gate = matmul_tn(feed_b, grad_gate_up_b)
    grad_feed = matmul_nt(grad_gate_up_b, weight_gate)
    _, pull_feed = jax.vjp(rms_norm, hidden_part, gain_feed_f)
    grad_hidden_norm, grad_gain_feed = pull_feed(grad_feed)
    grad_hidden_part = grad_part + grad_hidden_norm
    grad_hidden_other = branch_partner(grad_hidden_part)
    grad_hidden = jnp.where(
        on_attention,
        jnp.concatenate([grad_hidden_part, grad_hidden_other], axis=0),
        jnp.concatenate([grad_hidden_other, grad_hidden_part], axis=0),
    )
    feed_shards = (
        lax.psum_scatter(grad_gain_feed, ("seq", "fsdp"), scatter_dimension=0, tiled=True),
        lax.psum_scatter(grad_gate, ("seq", "fsdp"), scatter_dimension=0, tiled=True),
        lax.psum_scatter(grad_down, ("seq", "fsdp"), scatter_dimension=0, tiled=True),
    )
    grad_sent = 0.5 * grad_hidden

    def attention_back_one():
        _, pull_norm = jax.vjp(rms_norm, pre_norm, gain_attn.astype(jnp.float32))
        grad_pre, grad_gain_attn = pull_norm(grad_sent)
        grad_pre_b = grad_pre.astype(jnp.bfloat16)
        grad_weight_attn = matmul_tn(attended.astype(jnp.bfloat16), grad_pre_b)
        grad_attended_b = matmul_nt(grad_pre_b, weight_attn).astype(jnp.bfloat16)
        grad_heads = grad_attended_b.reshape(rows_dev, group_count, per_group, HEAD)
        balance = jnp.sum(
            grad_heads.astype(jnp.float32)
            * attended.reshape(rows_dev, group_count, per_group, HEAD),
            axis=-1,
        )
        meta_first = meta_scores()
        meta_probs = jnp.exp(meta_first - log_mass[..., None])
        meta_grad_probs = jnp.einsum(
            "qgjd,kgd->qgjk", grad_heads, meta_values, preferred_element_type=jnp.float32
        )
        meta_grad_scores = (meta_probs * (meta_grad_probs - balance[..., None])).astype(
            jnp.bfloat16
        )
        start_query = (
            jnp.einsum(
                "qgjk,kgd->qgjd", meta_grad_scores, meta_keys, preferred_element_type=jnp.float32
            )
            * score_scale
        )
        grad_meta_keys = (
            jnp.einsum(
                "qgjk,qgjd->kgd", meta_grad_scores, query_heads, preferred_element_type=jnp.float32
            )
            * score_scale
        )
        grad_meta_values = jnp.einsum(
            "qgjk,qgjd->kgd",
            meta_probs.astype(jnp.bfloat16),
            grad_heads,
            preferred_element_type=jnp.float32,
        )
        grad_meta_kv = jnp.concatenate(
            [
                grad_meta_keys.reshape(meta_count, keyval_half),
                grad_meta_values.reshape(meta_count, keyval_half),
            ],
            axis=1,
        )

        def back_step(block_id, running):
            grad_query, grad_keyval = running
            start_row = block_id * block_rows
            scores, key_rows, value_rows = masked_scores(start_row)
            probs_block = jnp.exp(scores - log_mass[..., None])
            grad_probs = jnp.einsum(
                "qgjd,kgd->qgjk", grad_heads, value_rows, preferred_element_type=jnp.float32
            )
            grad_scores = (probs_block * (grad_probs - balance[..., None])).astype(jnp.bfloat16)
            grad_query = (
                grad_query
                + jnp.einsum(
                    "qgjk,kgd->qgjd", grad_scores, key_rows, preferred_element_type=jnp.float32
                )
                * score_scale
            )
            grad_keys = (
                jnp.einsum(
                    "qgjk,qgjd->kgd", grad_scores, query_heads, preferred_element_type=jnp.float32
                )
                * score_scale
            )
            grad_values = jnp.einsum(
                "qgjk,qgjd->kgd",
                probs_block.astype(jnp.bfloat16),
                grad_heads,
                preferred_element_type=jnp.float32,
            )
            key_piece = jnp.concatenate(
                [
                    grad_keys.reshape(block_rows, keyval_half),
                    grad_values.reshape(block_rows, keyval_half),
                ],
                axis=1,
            )
            return (
                grad_query,
                lax.dynamic_update_slice_in_dim(grad_keyval, key_piece, start_row, 0),
            )

        grad_query, grad_keyval = lax.fori_loop(
            0,
            needed,
            back_step,
            (start_query, jnp.zeros((group_rows, 2 * keyval_half), jnp.float32)),
        )
        return (
            grad_query.reshape(rows_dev, query_width).astype(jnp.bfloat16),
            grad_keyval,
            grad_meta_kv,
            grad_weight_attn,
            grad_gain_attn,
            jnp.zeros((inner_width, model_width), jnp.float32),
            jnp.zeros((model_width,), jnp.float32),
            jnp.zeros((rows_dev, inner_width), jnp.float32),
            jnp.zeros((inner_width,), jnp.float32),
            jnp.zeros((rows_dev, inner_width), jnp.float32),
            jnp.zeros((rows_dev, inner_width), jnp.float32),
            jnp.zeros((state_len, inner_width), jnp.float32),
        )

    def mamba_back_one():
        _, pull_norm = jax.vjp(rms_norm, pre_norm, gain_mamba.astype(jnp.float32))
        grad_pre, grad_gain_mamba = pull_norm(grad_sent)
        grad_pre_b = grad_pre.astype(jnp.bfloat16)
        grad_weight_back = matmul_tn(mixed_y, grad_pre_b)
        grad_mixed = matmul_nt(grad_pre_b, weight_back)
        inputs_full = inputs_b.astype(jnp.float32)
        _, pull_gate = jax.vjp(
            gate_mix, ssm_out, skip_gain.astype(jnp.float32), inputs_full, gate_z
        )
        grad_ssm, grad_skip, grad_inputs_gate, grad_gate_z = pull_gate(grad_mixed)
        decay_f = log_decay.astype(jnp.float32)

        def outputs_of_state(state_in):
            return ssm_scan(inputs_full, steps, b_rows, c_rows, decay_f, keep_rows, state_in)[0]

        _, pull_state = jax.vjp(outputs_of_state, start_state)
        (own_state_grad,) = pull_state(grad_ssm)
        return (
            jnp.zeros((rows_dev, query_width), jnp.bfloat16),
            jnp.zeros((group_rows, 2 * keyval_half), jnp.float32),
            jnp.zeros((meta_count, 2 * keyval_half), jnp.float32),
            jnp.zeros((query_width, model_width), jnp.float32),
            jnp.zeros((model_width,), jnp.float32),
            grad_weight_back,
            grad_gain_mamba,
            grad_ssm,
            grad_skip,
            grad_inputs_gate,
            grad_gate_z,
            own_state_grad,
        )

    (
        grad_query_b,
        grad_keyval,
        grad_meta_kv,
        grad_weight_attn,
        grad_gain_attn,
        grad_weight_back,
        grad_gain_mamba,
        grad_ssm,
        grad_skip,
        grad_inputs_gate,
        grad_gate_z,
        own_state_grad,
    ) = lax.cond(on_attention, attention_back_one, mamba_back_one)
    keyval_sum = lax.psum_scatter(
        grad_keyval.astype(jnp.bfloat16), "seq", scatter_dimension=0, tiled=True
    )
    returned = prefix(
        (decay_all, own_state_grad),
        "seq",
        combine_maps,
        (jnp.ones_like(decay_all), jnp.zeros_like(own_state_grad)),
        True,
    )
    end_grad = returned[1]

    def attention_back_two():
        grad_weight_query = matmul_tn(normed_b, grad_query_b)
        grad_weight_keys = matmul_tn(normed_b, keyval_sum) + exact_tn(
            meta_normed_b.astype(jnp.float32), grad_meta_kv
        )
        grad_normed = matmul_nt(grad_query_b, weight_query) + matmul_nt(keyval_sum, weight_keys)
        grad_meta_normed = exact_nt(grad_meta_kv, weight_keys.astype(jnp.float32))
        _, pull_meta = jax.vjp(rms_norm, meta_f, gain_norm_f)
        grad_meta_rows, grad_gain_meta = pull_meta(grad_meta_normed)
        return (
            grad_weight_query,
            grad_weight_keys,
            grad_normed,
            grad_meta_rows,
            grad_gain_meta,
            jnp.zeros((rows_dev, inner_width), jnp.float32),
            jnp.zeros((CONV - 1, inner_width), jnp.float32),
            jnp.zeros((CONV, inner_width), jnp.float32),
            jnp.zeros((inner_width,), jnp.float32),
            jnp.zeros((inner_width, step_rank + 2 * state_len), jnp.float32),
            jnp.zeros((step_rank, inner_width), jnp.float32),
            jnp.zeros((inner_width,), jnp.float32),
            jnp.zeros((state_len, inner_width), jnp.float32),
        )

    def mamba_back_two():
        inputs_full = inputs_b.astype(jnp.float32)

        def scan_outputs(inputs_arg, steps_arg, b_arg, c_arg, decay_arg):
            return ssm_scan(inputs_arg, steps_arg, b_arg, c_arg, decay_arg, keep_rows, start_state)

        _, pull_scan = jax.vjp(
            scan_outputs, inputs_full, steps, b_rows, c_rows, log_decay.astype(jnp.float32)
        )
        grad_in_scan, grad_steps, grad_b_rows, grad_c_rows, grad_log_decay = pull_scan(
            (grad_ssm, end_grad)
        )
        _, pull_step = jax.vjp(jax.nn.softplus, step_pre)
        (grad_step_pre,) = pull_step(grad_steps)
        grad_step_bias = jnp.sum(grad_step_pre, axis=0)
        grad_step_b = grad_step_pre.astype(jnp.bfloat16)
        grad_weight_step = matmul_tn(step_low, grad_step_b)
        grad_step_low = matmul_nt(grad_step_b, weight_step)
        grad_proj_b = jnp.concatenate([grad_step_low, grad_b_rows, grad_c_rows], axis=1).astype(
            jnp.bfloat16
        )
        grad_weight_ssm = matmul_tn(inputs_b, grad_proj_b)
        grad_inputs = grad_inputs_gate + grad_in_scan + matmul_nt(grad_proj_b, weight_ssm)

        def conv_only(conv_arg, rim_arg, taps_arg, offset_arg):
            return conv_silu(conv_arg, rim_arg, taps_arg, offset_arg, valid_rows)

        _, pull_conv = jax.vjp(
            conv_only,
            conv_input.astype(jnp.float32),
            rim_in.astype(jnp.float32),
            conv_taps.astype(jnp.float32),
            conv_offset.astype(jnp.float32),
        )
        grad_conv_local, grad_rim, grad_taps, grad_offset = pull_conv(grad_inputs)
        return (
            jnp.zeros((model_width, query_width), jnp.float32),
            jnp.zeros((model_width, 2 * keyval_half), jnp.float32),
            jnp.zeros((rows_dev, model_width), jnp.float32),
            jnp.zeros((meta_count, model_width), jnp.float32),
            jnp.zeros((model_width,), jnp.float32),
            grad_conv_local,
            grad_rim,
            grad_taps,
            grad_offset,
            grad_weight_ssm,
            grad_weight_step,
            grad_step_bias,
            grad_log_decay,
        )

    (
        grad_weight_query,
        grad_weight_keys,
        grad_normed,
        grad_meta_rows,
        grad_gain_meta,
        grad_conv_local,
        grad_rim,
        grad_taps,
        grad_offset,
        grad_weight_ssm,
        grad_weight_step,
        grad_step_bias,
        grad_log_decay,
    ) = lax.cond(on_attention, attention_back_two, mamba_back_two)
    rim_back = from_behind(grad_rim.astype(jnp.bfloat16), "seq", -1).astype(grad_rim.dtype)

    def attention_back_three():
        return (jnp.zeros((model_width, 2 * inner_width), jnp.float32), grad_normed)

    def mamba_back_three():
        grad_conv = grad_conv_local + jnp.concatenate(
            [jnp.zeros((rows_dev - (CONV - 1), inner_width), jnp.float32), rim_back], axis=0
        )
        grad_mamba_b = jnp.concatenate([grad_conv, grad_gate_z], axis=1).astype(jnp.bfloat16)
        return (matmul_tn(normed_b, grad_mamba_b), matmul_nt(grad_mamba_b, weight_mamba))

    grad_weight_mamba, grad_normed = lax.cond(on_attention, attention_back_three, mamba_back_three)
    _, pull_input = jax.vjp(rms_norm, inputs_f, gain_norm_f)
    grad_input_part, grad_gain_input = pull_input(grad_normed)
    grad_gain_norm = grad_gain_input + grad_gain_meta
    width_dev = model_width // pieces
    inner_dev = inner_width // pieces
    attn_layout = [
        ((width_dev,), False),
        ((width_dev, query_width), False),
        ((width_dev, 2 * keyval_half), False),
        ((query_width // pieces, model_width), False),
        ((width_dev,), False),
        ((meta_count, width_dev), True),
    ]
    mamba_layout = [
        ((width_dev,), False),
        ((width_dev, 2 * inner_width), False),
        ((CONV, inner_dev), True),
        ((inner_dev,), False),
        ((inner_dev, step_rank + 2 * state_len), False),
        ((step_rank, inner_dev), True),
        ((inner_dev,), False),
        ((state_len, inner_dev), True),
        ((inner_dev,), False),
        ((inner_dev, model_width), False),
        ((width_dev,), False),
    ]
    pack_width = max(layout_width(attn_layout), layout_width(mamba_layout))

    def attention_pack():
        return pack_grads(
            [
                (grad_gain_norm, False),
                (grad_weight_query, False),
                (grad_weight_keys, False),
                (grad_weight_attn, False),
                (grad_gain_attn, False),
                (grad_meta_rows, True),
            ],
            pieces,
            pack_width,
        )

    def mamba_pack():
        return pack_grads(
            [
                (grad_gain_norm, False),
                (grad_weight_mamba, False),
                (grad_taps, True),
                (grad_offset, False),
                (grad_weight_ssm, False),
                (grad_weight_step, True),
                (grad_step_bias, False),
                (grad_log_decay, True),
                (grad_skip, False),
                (grad_weight_back, False),
                (grad_gain_mamba, False),
            ],
            pieces,
            pack_width,
        )

    packed = lax.cond(on_attention, attention_pack, mamba_pack)
    own_row = lax.psum_scatter(packed, ("seq", "fsdp"), scatter_dimension=0, tiled=True)[0]
    other_row, other_gain_feed, other_gate, other_down, other_input = branch_partner(
        (own_row, feed_shards[0], feed_shards[1], feed_shards[2], grad_input_part)
    )
    attn_parts = unpack_grads(jnp.where(on_attention, own_row, other_row), attn_layout)
    mamba_parts = unpack_grads(jnp.where(on_attention, other_row, own_row), mamba_layout)
    total_gain_norm = attn_parts[0] + mamba_parts[0]
    total_gain_feed = feed_shards[0] + other_gain_feed
    total_gate = feed_shards[1] + other_gate
    total_down = feed_shards[2] + other_down
    input_grad = grad_hidden + (grad_input_part + other_input)
    return (
        mixed[None],
        input_grad[None],
        total_gain_norm,
        attn_parts[5],
        attn_parts[1],
        attn_parts[2],
        attn_parts[3],
        attn_parts[4],
        mamba_parts[1],
        mamba_parts[2],
        mamba_parts[3],
        mamba_parts[4],
        mamba_parts[5],
        mamba_parts[6],
        mamba_parts[7],
        mamba_parts[8],
        mamba_parts[9],
        mamba_parts[10],
        total_gain_feed,
        total_gate,
        total_down,
    )


def solution(mesh):
    placed = (
        P("fsdp", "seq", None),
        P("fsdp", None),
        P(("seq", "fsdp")),
        P(None, ("seq", "fsdp")),
        P(("seq", "fsdp"), None),
        P(("seq", "fsdp"), None),
        P(("seq", "fsdp"), None),
        P(("seq", "fsdp")),
        P(("seq", "fsdp"), None),
        P(None, ("seq", "fsdp")),
        P(("seq", "fsdp")),
        P(("seq", "fsdp"), None),
        P(None, ("seq", "fsdp")),
        P(("seq", "fsdp")),
        P(None, ("seq", "fsdp")),
        P(("seq", "fsdp")),
        P(("seq", "fsdp"), None),
        P(("seq", "fsdp")),
        P(("seq", "fsdp")),
        P(("seq", "fsdp"), None),
        P(("seq", "fsdp"), None),
        P("fsdp", "seq", None),
    )
    return jax.shard_map(
        shards,
        mesh=mesh,
        in_specs=placed,
        out_specs=(
            P("fsdp", "seq", None),
            P("fsdp", "seq", None),
            P(("seq", "fsdp")),
            P(None, ("seq", "fsdp")),
            P(("seq", "fsdp"), None),
            P(("seq", "fsdp"), None),
            P(("seq", "fsdp"), None),
            P(("seq", "fsdp")),
            P(("seq", "fsdp"), None),
            P(None, ("seq", "fsdp")),
            P(("seq", "fsdp")),
            P(("seq", "fsdp"), None),
            P(None, ("seq", "fsdp")),
            P(("seq", "fsdp")),
            P(None, ("seq", "fsdp")),
            P(("seq", "fsdp")),
            P(("seq", "fsdp"), None),
            P(("seq", "fsdp")),
            P(("seq", "fsdp")),
            P(("seq", "fsdp"), None),
            P(("seq", "fsdp"), None),
        ),
        check_vma=False,
    )
```

profile of v0, /device:TPU:1, one launch (start us, length us, event | category | flops | bytes accessed | tf_op | source)
XLA Modules:
  0.0 5811.8 jit_solution(16845965213899253862)
XLA Ops:
  13.4 154.4 %all-gather.10 = bf16[64,25,128]{2,1,0:T(8,128)(2,1)S(1)} all-gather(bf16[1,25,128]{2,1,0:T(8,128)(2,1)S(1)} %convert_bitcast_fusion.9), channel_id=1, replica_groups=mesh['branch'=2,'seq'=16,'fsdp'=4] {'seq','fsdp'}, dimensions={0}, use_global_device_ids=true | all-gather | bytes 416000 | tf_op jit(solution)/shard_map/all_gather | solution.py:245
  172.2 288.8 %all-reduce.104 = (bf16[1600]{0:T(1024)(128)(2,1)S(1)}, bf16[3200]{0:T(1024)(128)(2,1)S(1)}, bf16[3200]{0:T(1024)(128)(2,1)S(1)}, bf16[1600]{0:T(1024)(128)(2,1)...) all-reduce(bf16[1600]{0:T(1024)(128)(2,1)S(1)} %dynamic-update-slic, ...), channel_id=1, replica_groups=mesh['branch'=2,'seq'=16,'fsdp'=4] {'seq','fsdp'}, use_global_device_ids=true, to_apply=%add.91 | all-reduce | flops 16000 | bytes 64000
  475.2 19.5 reshape.2106
  509.2 141.6 %all-gather.3 = bf16[64,50,4]{1,2,0:T(4,128)(2,1)S(1)} all-gather(bf16[1,50,4]{1,2,0:T(4,128)(2,1)S(1)} %convert_bitcast_fusion.11), channel_id=1, replica_groups=mesh['branch'=2,'seq'=16,'fsdp'=4] {'seq','fsdp'}, dimensions={0}, use_global_device_ids=true | all-gather | bytes 26000 | tf_op jit(solution)/shard_map/all_gather | solution.py:251
  651.1 168.0 %all-gather.7 = bf16[64,50,132]{2,1,0:T(8,128)(2,1)} all-gather(bf16[1,50,132]{2,1,0:T(8,128)(2,1)S(1)} %convert_bitcast_fusion.7), channel_id=1, replica_groups=mesh['branch'=2,'seq'=16,'fsdp'=4] {'seq','fsdp'}, dimensions={0}, use_global_device_ids=true | all-gather | bytes 858000 | tf_op jit(solution)/shard_map/all_gather | solution.py:253
  825.5 156.8 %all-gather.8 = bf16[64,50,100]{2,1,0:T(8,128)(2,1)} all-gather(bf16[1,50,100]{2,1,0:T(8,128)(2,1)S(1)} %convert_bitcast_fusion.8), channel_id=1, replica_groups=mesh['branch'=2,'seq'=16,'fsdp'=4] {'seq','fsdp'}, dimensions={0}, use_global_device_ids=true | all-gather | bytes 650000 | tf_op jit(solution)/shard_map/all_gather | solution.py:254
  984.5 145.0 %all-gather.9 = bf16[64,50,16]{1,2,0:T(8,128)(2,1)S(1)} all-gather(bf16[1,50,16]{1,2,0:T(8,128)(2,1)S(1)} %convert_bitcast_fusion.10), channel_id=1, replica_groups=mesh['branch'=2,'seq'=16,'fsdp'=4] {'seq','fsdp'}, dimensions={0}, use_global_device_ids=true | all-gather | bytes 104000 | tf_op jit(solution)/shard_map/all_gather | solution.py:256
  1145.3 174.2 %conditional.8 = (f32[128,1600]{1,0:T(8,128)}, f32[128,5,5]{2,1,0:T(8,128)}, f32[128,1600]{1,0:T(8,128)}, bf16[128,1600]{1,0:T(8,128)(2,1)}, bf16[128,3200]{1,0:...) conditional(s32[]{:T(128)} %convert_element_type.301, ...), branch_computations={%region_11.16_spmd, %region_16.26_spmd} | conditional | flops 2059236096 | bytes 72040400 | solution.py:451
  1154.6 152.2 %while.129 = (s32[]{:T(128)}, f32[16,3200]{1,0:T(8,128)}, f32[8,16]{1,0:T(8,128)}, f32[8,16,3200]{2,1,0:T(8,128)}, f32[16,3200]{1,0:T(8,128)}, /*index=5*/f32[8,...) while((s32[]{:T(128)}, f32[16,3200]{1,0:T(8,128)}, ...), condition=%wide.region_15.15_spmd.clone, body=%wide.region_14.14_spmd.clone.sunk | while | flops 4198418 | bytes 2461535 | solution.py:146
  1339.7 80.6 %all-gather.29.cloned.1.call-done = f32[256,3200]{1,0:T(8,128)} async-done(((f32[16,3200]{1,0:T(8,128)}), f32[256,3200]{1,0:T(8,128)}) %all-gather.29.cloned.1.call-update) | async-done | bytes 3276816 | tf_op jit(solution)/shard_map/all_gather | solution.py:32
  1420.3 50.0 all-gather.31.cloned.1.call-done
  1470.3 27.8 while.137
  1498.1 219.9 %conditional.9 = (f32[128,1600]{0,1:T(8,128)S(1)}, f32[128,3200]{1,0:T(8,128)}, bf16[128,3200]{1,0:T(8,128)(2,1)S(1)}, f32[128,1600]{1,0:T(8,128)}, bf16[128,1600]{1,0:T(8,128)(2,1)}) conditional(s32[]{:T(128)} %convert_element_type.301, (bf16[128,3200]{1,0:T(8,128)(2,1)S(1)}, f32[128,3200]{1,0:T(8,128)}, f32[128,16]{0,1:T(8,128)S(1)}, ...), branch_computations={%region_28.48_spmd, %region_48.49_spmd} | conditional | flops 1323729664 | bytes 32206912 | solution.py:490
  1503.2 198.6 %while.130 = (s32[]{:T(128)}, f32[16,3200]{1,0:T(8,128)S(1)}, f32[8,16,3200]{2,1,0:T(8,128)}, f32[8,16]{1,0:T(8,128)}, f32[8,16,3200]{2,1,0:T(8,128)}, /*index=5...) while((s32[]{:T(128)}, f32[16,3200]{1,0:T(8,128)S(1)}, ...), condition=%wide.region_46.46_spmd, body=%wide.region_29.45_spmd.sunk | while | flops 7782417 | bytes 8813961 | solution.py:146
  1720.4 21.7 reshape.2126
  1743.6 42.6 all-gather.45.cloned.1.call-done
  1786.2 50.9 reshape.2124
  1867.0 18.2 multiply_reduce_fusion.113
  1889.4 166.5 %conditional.10 = (bf16[128,1600]{0,1:T(8,128)(2,1)}, bf16[2048,640]{0,1:T(8,128)(2,1)}, f32[128,640]{0,1:T(8,128)}, f32[1600,1600]{0,1:T(8,128)}, f32[1600]{0:T...) conditional(s32[]{:T(128)} %convert_element_type.301, ...), branch_computations={%region_51.58_spmd, %region_58.65_spmd} | conditional | flops 3713742336 | bytes 172747552 | solution.py:728
  1901.5 24.2 copy.262
  1937.6 110.0 %while.131 = (s32[]{:T(128)}, f32[16,3200]{1,0:T(8,128)S(1)}, f32[8,16,3200]{2,1,0:T(8,128)}, f32[8,16,16]{2,1,0:T(8,128)S(1)}, f32[8,16]{1,0:T(8,128)S(1)}, /*i...) while((s32[]{:T(128)}, f32[16,3200]{1,0:T(8,128)S(1)}, ...), condition=%wide.region_57.57_spmd.clone, body=%wide.region_56.56_spmd.clone.sunk | while | flops 4147204 | bytes 3077583 | solution.py:146
  2090.4 450.7 %fusion.1 = f32[96,1600]{1,0:T(8,128)} fusion(f32[5504,1600]{1,0:T(8,128)} %fusion.249), kind=kCustom, calls=%all-reduce-scatter.1 | all-reduce-scatter fusion | flops 9830401 | bytes 35840512
  2541.1 28.0 reduce-scatter.6.cloned.1.call-done
  2569.1 51.6 all-gather.33.cloned.1.call-done
  2624.7 18.4 while.138
  2643.1 770.2 %conditional.11 = (f32[1600,1600]{1,0:T(8,128)}, f32[1600,640]{1,0:T(8,128)S(1)}, f32[128,1600]{1,0:T(8,128)}, f32[1600]{0:T(1024)S(1)}, f32[128,3200]{1,0:T(8,1...) conditional(s32[]{:T(128)} %convert_element_type.301, ...), branch_computations={%region_68.143_spmd, %region_143.147_spmd} | conditional | flops 4984626176 | bytes 106677592 | solution.py:831
  2651.2 165.7 %while.133 = (s32[]{:T(128)}, f32[16,3200]{1,0:T(8,128)}, f32[8,16,3200]{2,1,0:T(8,128)}, f32[8,16]{1,0:T(8,128)}, f32[8,16,3200]{2,1,0:T(8,128)}, /*index=5*/f3...) while((s32[]{:T(128)}, f32[16,3200]{1,0:T(8,128)}, ...), condition=%wide.region_70.70_spmd, body=%wide.region_69.69_spmd.sunk | while | flops 4147217 | bytes 2871137 | solution.py:146
  2821.5 565.8 %while.134 = (s32[]{:T(128)}, f32[16,3200]{1,0:T(8,128)}, f32[16,3200]{1,0:T(8,128)S(1)}, f32[8,16,3200]{2,1,0:T(8,128)}, f32[8,16,3200]{2,1,0:T(8,128)}, /*inde...) while((s32[]{:T(128)}, f32[16,3200]{1,0:T(8,128)}, ...), condition=%wide.region_136.136_spmd.clone, body=%wide.region_71.135_spmd.clone.sunk | while | flops 36973572 | bytes 24586256 | solution.py:146
  3420.5 27.1 fusion.220
  3461.4 147.2 %all-reduce.99 = f32[1600]{0:T(1024)S(1)} all-reduce(f32[1600]{0:T(1024)S(1)} %copy-done.117), channel_id=7, replica_groups=mesh['branch'=2,'seq'=16,'fsdp'=4] {'seq','fsdp'}, use_global_device_ids=true, to_apply=%region_155.156.clone | all-reduce | flops 1600 | bytes 12800
  3609.4 29.0 conditional.12
  3611.0 16.0 convolution_bitcast_fusion.4
  3641.1 273.8 %conditional.13 = (f32[64,252800]{1,0:T(8,128)}) conditional(s32[]{:T(128)} %convert_element_type.301, (f32[1600]{0:T(1024)S(1)}, f32[1600,6400]{1,0:T(8,128)}, f32[4,3200]{1,0:T(4,128)}, f32[3200]{0:T(1024)}, f32[3200,132]{0,1:T(8,128)}, /*index=5*/f32[100,3200]{1,0:T(8,128)}, f32[3200]{0:T(1024)S(1)}, f32[16,3200]{1,0:T(8,128)S(1)}, ...), branch_computations={%region_151.152_spmd, %region_152.153_spmd} | conditional | bytes 270720128 | solution.py:906
  3642.8 50.8 reshape.2030
  3693.7 112.1 %dynamic-update-slice.8 = f32[64,252800]{1,0:T(8,128)} dynamic-update-slice(f32[64,252800]{1,0:T(8,128)} %dynamic-update-slice.7, f32[64,160000]{1,0:T(8,128)} %reshape.2030, s32[]{} %constant.883, s32[]{} %constant.884) | dynamic-update-slice | bytes 81920000 | tf_op jit(solution)/shard_map/cond
  3836.3 20.1 reshape.2038
  3856.4 56.5 dynamic-update-slice.16
  3919.3 1138.4 %fusion = f32[32,11008]{1,0:T(8,128)S(1)} fusion(f32[1600,11008]{1,0:T(8,128)} %fusion.220), kind=kCustom, calls=%all-reduce-scatter | all-reduce-scatter fusion | flops 22544384 | bytes 71860736
  5077.3 28.8 collective-permute-start.25
  5106.2 25.0 collective-permute-start.23
  5142.5 32.4 collective-permute-done.24
  5185.7 21.2 collective-permute-start.18
  5213.7 24.6 collective-permute-start.16
  5251.6 70.1 %collective-permute-start.14 = (f32[32,11008]{1,0:T(8,128)S(1)}, f32[32,11008]{1,0:T(8,128)}, u32[]{:S(2)}, u32[]{:S(2)}) collective-permute-start(f32[32,11008]{1,0:T(8,128)S(1)} %fusion), channel_id=1, source_target_pairs={{0,5},{1,6},{2,7},{3,8},{4,9},{5,10},{6,11},{7,12},{8,13},{9,14},{... | collective-permute-start | bytes 4227080
  5337.3 22.4 collective-permute-start.10
  5364.7 25.2 concatenate.66
  5391.8 112.9 %concatenate.65 = f32[473,11008]{1,0:T(8,128)} concatenate(f32[25,11008]{1,0:T(8,128)} %copy-done.64, f32[32,11008]{1,0:T(8,128)S(1)} %collective-permute-done.22, f32[32,11008]{1,0:T(8,128)} %copy-done.62, f32[32,11008]{1,0:T(8,128)} %copy-done.63, f32[32,11008]{1,0:T(8,128)} %copy-done.65, f32[32,11008]{1,0:T(8,128)} %copy-done.66, f32[32,11008]{1,0:T(8,128)} %copy-done.67, ...), dimensions={0} | concatenate | bytes 41654272
  5513.3 250.7 %all-reduce.107.cloned.1.call-done = f32[64,252800]{1,0:T(8,128)} async-done(((f32[64,252800]{1,0:T(8,128)}), f32[64,252800]{1,0:T(8,128)}) %all-reduce.107.cloned.1.call-update) | async-done | bytes 64716816
  (1955 shorter events, 1706.5 us)
Async XLA Ops:
  7.2 454.8 %all-gather.37.cloned.1.call-start = ((), (), s32[]{:S(2)}) async-start(), calls=%async_computation.7 | async-start | bytes 2662400 | tf_op jit(solution)/shard_map/all_gather | solution.py:247
  8.8 457.7 %all-gather.39.cloned.1.call-start = ((), (), s32[]{:S(2)}) async-start(), calls=%async_computation.8 | async-start | bytes 6922240 | tf_op jit(solution)/shard_map/all_gather | solution.py:246
  10.5 464.7 %all-gather.35.cloned.1.call-start = ((), (), s32[]{:S(2)}) async-start(), calls=%async_computation.6 | async-start | bytes 26624000 | tf_op jit(solution)/shard_map/all_gather | solution.py:250
  12.5 1124.1 %all-gather.41.cloned.1.call-start = ((), (), s32[]{:S(2)}) async-start(), calls=%async_computation.9 | async-start | bytes 6922240 | tf_op jit(solution)/shard_map/all_gather | solution.py:248
  13.3 1131.9 %all-gather.27.cloned.1.call-start = ((), (), s32[]{:S(2)}) async-start(), calls=%async_computation.1 | async-start | bytes 2785280 | tf_op jit(solution)/shard_map/all_gather | solution.py:321
  461.0 684.2 %copy-start.118 = (bf16[3200]{0:T(1024)(128)(2,1)}, bf16[3200]{0:T(1024)(128)(2,1)S(1)}, u32[]{:S(2)}) copy-start(bf16[3200]{0:T(1024)(128)(2,1)S(1)} %get-tuple-element.2772) | copy-start | bytes 19204
  462.0 669.0 %copy-start.46 = (bf16[128,1600]{1,0:T(8,128)(2,1)}, bf16[128,1600]{1,0:T(8,128)(2,1)S(1)}, u32[]{:S(2)}) copy-start(bf16[128,1600]{1,0:T(8,128)(2,1)S(1)} %get-tuple-element.3145) | copy-start | bytes 1228804
  504.8 640.4 %copy-start.24 = (bf16[128,3200]{1,0:T(8,128)(2,1)}, bf16[128,3200]{1,0:T(8,128)(2,1)S(1)}, u32[]{:S(2)}) copy-start(bf16[128,3200]{1,0:T(8,128)(2,1)S(1)} %get-tuple-element.1384) | copy-start | bytes 2457604
  505.8 818.7 %all-gather.43.cloned.1.call-start = ((), (), s32[]{:S(2)}) async-start(), calls=%async_computation.10 | async-start | bytes 12113920 | tf_op jit(solution)/shard_map/all_gather | solution.py:258
  506.5 913.8 %all-gather.29.cloned.1.call-start = ((), (), s32[]{:S(2)}) async-start(), calls=%async_computation.3 | async-start | bytes 3481600 | tf_op jit(solution)/shard_map/all_gather | solution.py:32
  506.6 638.6 %copy-start.96 = (s32[128]{0:T(128)}, s32[128]{0:T(128)S(1)}, u32[]{:S(2)}) copy-start(s32[128]{0:T(128)S(1)} %iota_add_fusion) | copy-start | bytes 1540
  1133.1 12.1 collective-permute-start
  1319.5 150.8 %all-gather.31.cloned.1.call-start = ((), (), s32[]{:S(2)}) async-start(), calls=%async_computation.4 | async-start | bytes 3481600 | tf_op jit(solution)/shard_map/all_gather | solution.py:32
  1320.3 400.1 %all-gather.47.cloned.1.call-start = ((), (), s32[]{:S(2)}) async-start(), calls=%async_computation.12 | async-start | bytes 19036160 | tf_op jit(solution)/shard_map/all_gather | solution.py:262
  1322.2 464.0 %all-gather.45.cloned.1.call-start = ((), (), s32[]{:S(2)}) async-start(), calls=%async_computation.11 | async-start | bytes 45793280 | tf_op jit(solution)/shard_map/all_gather | solution.py:261
  1323.2 1245.9 %reduce-scatter.6.cloned.1.call-start = ((), (), s32[]{:S(2)}) async-start(), calls=%async_computation.2 | async-start | bytes 2785280 | tf_op jit(solution)/shard_map/reduce_scatter | solution.py:729
  1718.0 24.1 collective-permute-start.1
  1886.5 2.2 collective-permute-start.3
  2060.5 560.3 %all-gather.33.cloned.1.call-start = ((), (), s32[]{:S(2)}) async-start(), calls=%async_computation.5 | async-start | bytes 3481600 | tf_op jit(solution)/shard_map/all_gather | solution.py:32
  2075.5 1841.7 %collective-permute-start.2 = (bf16[64,1600]{1,0:T(8,128)(2,1)}, bf16[64,1600]{1,0:T(8,128)(2,1)}, u32[]{:S(2)}, u32[]{:S(2)}) collective-permute-start(bf16[64,1600]{1,0:T(8,128)(2,1)} %convolution_add_fusion.4), channel_id=1, source_target_pairs={{0,64},{64,0},{1,65},{65,1},{2,66},{66,2},{3,67},{67,3},{4,68},{68... | collective-permute-start | bytes 614408 | tf_op jit(solution)/shard_map/ppermute | solution.py:21
  2090.3 3673.7 %all-reduce.107.cloned.1.call-start = ((), (), s32[]{:S(2)}) async-start(), calls=%async_computation.13 | async-start | bytes 129433600
  3417.5 191.8 %collective-permute-start.4 = (bf16[3,3200]{1,0:T(4,128)(2,1)S(1)}, bf16[3,3200]{1,0:T(4,128)(2,1)S(1)}, u32[]{:S(2)}, u32[]{:S(2)}) collective-permute-start(bf16[3,3200]{1,0:T(4,128)(2,1)S(1)} %get-tuple-element.1413), channel_id=1, source_target_pairs={{4,0},{8,4},{12,8},{16,12},{20,16},{24,20},{28,24},{32,28},{36,32}... | collective-permute-start | bytes 57608 | tf_op jit(solution)/shard_map/ppermute | solution.py:27
  3449.3 1619.1 %collective-permute-start.29 = (f32[96,1600]{1,0:T(8,128)}, f32[96,1600]{1,0:T(8,128)}, u32[]{:S(2)}, u32[]{:S(2)}) collective-permute-start(f32[96,1600]{1,0:T(8,128)} %fusion.1), channel_id=1, source_target_pairs={{0,6},{1,7},{2,8},{3,9},{4,10},{5,11},{6,12},{7,13},{8,14},{9,15},... | collective-permute-start | bytes 1843208
  3455.2 1614.7 %collective-permute-start.28 = (f32[96,1600]{1,0:T(8,128)}, f32[96,1600]{1,0:T(8,128)}, u32[]{:S(2)}, u32[]{:S(2)}) collective-permute-start(f32[96,1600]{1,0:T(8,128)} %fusion.1), channel_id=1, source_target_pairs={{0,5},{1,6},{2,7},{3,8},{4,9},{5,10},{6,11},{7,12},{8,13},{9,14},{... | collective-permute-start | bytes 1843208
  3458.9 1618.4 %collective-permute-start.27 = (f32[96,1600]{1,0:T(8,128)}, f32[96,1600]{1,0:T(8,128)}, u32[]{:S(2)}, u32[]{:S(2)}) collective-permute-start(f32[96,1600]{1,0:T(8,128)} %fusion.1), channel_id=1, source_target_pairs={{0,4},{1,5},{2,6},{3,7},{4,8},{5,9},{6,10},{7,11},{8,12},{9,13},{1... | collective-permute-start | bytes 1843208
  3609.3 305.7 %collective-permute-start.7 = (f32[25]{0:T(128)}, f32[25]{0:T(128)}, u32[]{:S(2)}, u32[]{:S(2)}) collective-permute-start(f32[25]{0:T(128)} %dynamic-slice.11), channel_id=1, source_target_pairs={{0,64},{64,0},{1,65},{65,1},{2,66},{66,2},{3,67},{67,3},{4,68},{68... | collective-permute-start | bytes 308 | tf_op jit(solution)/shard_map/ppermute | solution.py:21
  3915.0 1191.3 %collective-permute-start.26 = (f32[96,1600]{1,0:T(8,128)}, f32[96,1600]{1,0:T(8,128)}, u32[]{:S(2)}, u32[]{:S(2)}) collective-permute-start(f32[96,1600]{1,0:T(8,128)} %fusion.1), channel_id=1, source_target_pairs={{0,3},{1,4},{2,5},{3,6},{4,7},{5,8},{6,9},{7,10},{8,11},{9,12},{10... | collective-permute-start | bytes 1843208
  3917.2 1140.4 %collective-permute-start.30 = (f32[54,1600]{1,0:T(8,128)S(1)}, f32[54,1600]{1,0:T(8,128)}, u32[]{:S(2)}, u32[]{:S(2)}) collective-permute-start(f32[54,1600]{1,0:T(8,128)S(1)} %copy-done.84), channel_id=1, source_target_pairs={{0,7},{1,8},{2,9},{3,10},{4,11},{5,12},{6,13},{7,14},{8,15},{9,16}... | collective-permute-start | bytes 1036808
  5057.7 149.3 %collective-permute-start.22 = (f32[32,11008]{1,0:T(8,128)S(1)}, f32[32,11008]{1,0:T(8,128)S(1)}, u32[]{:S(2)}, u32[]{:S(2)}) collective-permute-start(f32[32,11008]{1,0:T(8,128)S(1)} %fusion), channel_id=1, source_target_pairs={{0,13},{1,14},{2,15},{3,16},{4,17},{5,18},{6,19},{7,20},{8,21},{9,... | collective-permute-start | bytes 4227080
  5068.5 145.2 %collective-permute-start.21 = (f32[32,11008]{1,0:T(8,128)S(1)}, f32[32,11008]{1,0:T(8,128)S(1)}, u32[]{:S(2)}, u32[]{:S(2)}) collective-permute-start(f32[32,11008]{1,0:T(8,128)S(1)} %fusion), channel_id=1, source_target_pairs={{0,12},{1,13},{2,14},{3,15},{4,16},{5,17},{6,18},{7,19},{8,20},{9,... | collective-permute-start | bytes 4227080
  5069.9 168.4 %collective-permute-start.20 = (f32[32,11008]{1,0:T(8,128)S(1)}, f32[32,11008]{1,0:T(8,128)S(1)}, u32[]{:S(2)}, u32[]{:S(2)}) collective-permute-start(f32[32,11008]{1,0:T(8,128)S(1)} %fusion), channel_id=1, source_target_pairs={{0,11},{1,12},{2,13},{3,14},{4,15},{5,16},{6,17},{7,18},{8,19},{9,... | collective-permute-start | bytes 4227080
  5077.3 53.9 collective-permute-start.25
  5106.2 79.5 %collective-permute-start.23 = (f32[25,11008]{1,0:T(8,128)S(1)}, f32[25,11008]{1,0:T(8,128)S(1)}, u32[]{:S(2)}, u32[]{:S(2)}) collective-permute-start(f32[25,11008]{1,0:T(8,128)S(1)} %slice.2450), channel_id=1, source_target_pairs={{0,14},{1,15},{2,16},{3,17},{4,18},{5,19},{6,20},{7,21},{8,22},{9,... | collective-permute-start | bytes 3302408
  5131.2 43.7 collective-permute-start.24
  5174.9 76.6 %collective-permute-start.19 = (f32[32,11008]{1,0:T(8,128)S(1)}, f32[32,11008]{1,0:T(8,128)S(1)}, u32[]{:S(2)}, u32[]{:S(2)}) collective-permute-start(f32[32,11008]{1,0:T(8,128)S(1)} %fusion), channel_id=1, source_target_pairs={{0,10},{1,11},{2,12},{3,13},{4,14},{5,15},{6,16},{7,17},{8,18},{9,... | collective-permute-start | bytes 4227080
  5185.7 135.9 %collective-permute-start.18 = (f32[32,11008]{1,0:T(8,128)S(1)}, f32[32,11008]{1,0:T(8,128)S(1)}, u32[]{:S(2)}, u32[]{:S(2)}) collective-permute-start(f32[32,11008]{1,0:T(8,128)S(1)} %fusion), channel_id=1, source_target_pairs={{0,9},{1,10},{2,11},{3,12},{4,13},{5,14},{6,15},{7,16},{8,17},{9,1... | collective-permute-start | bytes 4227080
  5207.0 117.1 %collective-permute-start.17 = (f32[32,11008]{1,0:T(8,128)S(1)}, f32[32,11008]{1,0:T(8,128)S(1)}, u32[]{:S(2)}, u32[]{:S(2)}) collective-permute-start(f32[32,11008]{1,0:T(8,128)S(1)} %fusion), channel_id=1, source_target_pairs={{0,8},{1,9},{2,10},{3,11},{4,12},{5,13},{6,14},{7,15},{8,16},{9,17... | collective-permute-start | bytes 4227080
  5213.7 114.9 %collective-permute-start.16 = (f32[32,11008]{1,0:T(8,128)S(1)}, f32[32,11008]{1,0:T(8,128)S(1)}, u32[]{:S(2)}, u32[]{:S(2)}) collective-permute-start(f32[32,11008]{1,0:T(8,128)S(1)} %fusion), channel_id=1, source_target_pairs={{0,7},{1,8},{2,9},{3,10},{4,11},{5,12},{6,13},{7,14},{8,15},{9,16}... | collective-permute-start | bytes 4227080
  5238.3 99.0 %collective-permute-start.15 = (f32[32,11008]{1,0:T(8,128)S(1)}, f32[32,11008]{1,0:T(8,128)S(1)}, u32[]{:S(2)}, u32[]{:S(2)}) collective-permute-start(f32[32,11008]{1,0:T(8,128)S(1)} %fusion), channel_id=1, source_target_pairs={{0,6},{1,7},{2,8},{3,9},{4,10},{5,11},{6,12},{7,13},{8,14},{9,15},... | collective-permute-start | bytes 4227080
  5251.6 140.2 %collective-permute-start.14 = (f32[32,11008]{1,0:T(8,128)S(1)}, f32[32,11008]{1,0:T(8,128)}, u32[]{:S(2)}, u32[]{:S(2)}) collective-permute-start(f32[32,11008]{1,0:T(8,128)S(1)} %fusion), channel_id=1, source_target_pairs={{0,5},{1,6},{2,7},{3,8},{4,9},{5,10},{6,11},{7,12},{8,13},{9,14},{... | collective-permute-start | bytes 4227080
  5321.7 70.2 %collective-permute-start.13 = (f32[32,11008]{1,0:T(8,128)S(1)}, f32[32,11008]{1,0:T(8,128)}, u32[]{:S(2)}, u32[]{:S(2)}) collective-permute-start(f32[32,11008]{1,0:T(8,128)S(1)} %fusion), channel_id=1, source_target_pairs={{0,4},{1,5},{2,6},{3,7},{4,8},{5,9},{6,10},{7,11},{8,12},{9,13},{1... | collective-permute-start | bytes 4227080
  5324.1 67.7 %collective-permute-start.12 = (f32[32,11008]{1,0:T(8,128)S(1)}, f32[32,11008]{1,0:T(8,128)}, u32[]{:S(2)}, u32[]{:S(2)}) collective-permute-start(f32[32,11008]{1,0:T(8,128)S(1)} %fusion), channel_id=1, source_target_pairs={{0,3},{1,4},{2,5},{3,6},{4,7},{5,8},{6,9},{7,10},{8,11},{9,12},{10... | collective-permute-start | bytes 4227080
  5328.6 63.3 %collective-permute-start.11 = (f32[32,11008]{1,0:T(8,128)S(1)}, f32[32,11008]{1,0:T(8,128)}, u32[]{:S(2)}, u32[]{:S(2)}) collective-permute-start(f32[32,11008]{1,0:T(8,128)S(1)} %fusion), channel_id=1, source_target_pairs={{0,2},{1,3},{2,4},{3,5},{4,6},{5,7},{6,8},{7,9},{8,10},{9,11},{10,... | collective-permute-start | bytes 4227080
  5337.3 54.5 collective-permute-start.10
  5391.8 116.6 %collective-permute-start.9 = (f32[86,1600]{1,0:T(8,128)}, f32[86,1600]{1,0:T(8,128)}, u32[]{:S(2)}, u32[]{:S(2)}) collective-permute-start(f32[86,1600]{1,0:T(8,128)} %constant_dynamic-slice_fusion.104), channel_id=1, source_target_pairs={{0,64},{64,0},{1,65},{65,1},{2,66},{66,2},{3,67},{67,3},{4,68},{68... | collective-permute-start | bytes 1651208 | tf_op jit(solution)/shard_map/ppermute | solution.py:21
  5507.7 277.2 %collective-permute-start.8 = (f32[25,11008]{1,0:T(8,128)}, f32[25,11008]{1,0:T(8,128)S(1)}, u32[]{:S(2)}, u32[]{:S(2)}) collective-permute-start(f32[25,11008]{1,0:T(8,128)} %constant_dynamic-slice_fusion.105), channel_id=1, source_target_pairs={{0,64},{64,0},{1,65},{65,1},{2,66},{66,2},{3,67},{67,3},{4,68},{68... | collective-permute-start | bytes 3302408 | tf_op jit(solution)/shard_map/ppermute | solution.py:21
  5513.3 274.4 %collective-permute-start.5 = (f32[128,1600]{0,1:T(8,128)}, f32[128,1600]{0,1:T(8,128)}, u32[]{:S(2)}, u32[]{:S(2)}) collective-permute-start(f32[128,1600]{0,1:T(8,128)} %copy.298), channel_id=1, source_target_pairs={{0,64},{64,0},{1,65},{65,1},{2,66},{66,2},{3,67},{67,3},{4,68},{68... | collective-permute-start | bytes 2457608 | tf_op jit(solution)/shard_map/ppermute | solution.py:21
  5777.2 16.6 collective-permute-start.6
  (189 other events, 6153.4 us)
Sparse Core Ops, SparseCore 0:
  11.5 68.6 all-gather.36
  83.7 72.9 all-gather.38
  160.1 136.4 all-gather.34
  299.9 73.5 all-gather.40
  505.9 123.6 all-gather.26
  632.8 91.1 all-gather.42
  1319.6 100.6 all-gather.28
  1423.1 47.1 all-gather.30
  1473.7 109.3 all-gather.46
  1585.8 200.3 all-gather.44
  2060.6 508.4 reduce-scatter.5
  2571.7 48.9 all-gather.32
  3915.1 1848.8 all-reduce.106
where the time goes:
time: 5850 us; the launch traced here: 5810 us
  blocking collectives  2790 us (48%)
  other arithmetic  1050 us (18%)
  local copies, waits for them, and re-layouts  910 us (16%)
  waiting for transfers between devices  538 us (9%)
  starting transfers between devices  301 us (5%)
  matrix products  180 us (3%)
    unnamed x4, blocking collectives  2030 us
    unnamed x235, local copies, waits for them, and re-layouts  296 us
    unnamed x22, starting transfers between devices  286 us
    unnamed x35, waiting for transfers between devices  284 us
    reduce_sum x64, other arithmetic, block_step(): step_blk[position][None, :] * decay_rate  253 us
    reduce_sum x64, other arithmetic, block_step(): outputs.append(jnp.sum(c_blk[position][:, None] * state_now, axis=0))  224 us
    add x16, other arithmetic, block_step(): keep_blk[position] * jnp.exp(step_blk[position][None, :] * decay_rate)  203 us
    cond x74, local copies, waits for them, and re-layouts  195 us
  transfers between devices with their start and end apart: 44, of which 8 were waited for; matrix products, arithmetic and copies ran while one was open for 59% of the time, Pallas kernels for 0%

commit v1 on v0

v1 whole, which is shorter than its diff:
```python
import functools
import types

import jax
import jax.numpy as jnp
from jax import lax
from jax.experimental import pallas as pl
from jax.experimental.pallas import tpu as pltpu
from jax.sharding import PartitionSpec as P

HEAD = 64
CONV = 4
SIDE = 4

epsilon = 1e-05
negative_fill = -1e30
score_scale = 0.125
log2_e = 1.4426950408889634
highest = lax.Precision.HIGHEST
MESH = pl.DeviceIdType.MESH
ANY = pl.BlockSpec(memory_space=pl.ANY)
VMEM = pl.BlockSpec(memory_space=pltpu.VMEM)
SEMS = 128
HOPS = (1, 3, 2)
X, Y, Z = range(3)


class Net:
    def __init__(self, core, coords, names, send, recv):
        self.core = core
        self.at = coords
        self.names = names
        self.send = send
        self.recv = recv
        self.begun = []

    def device(self, axis=None, hop=0, other_core=False):
        place = dict(self.at)
        if axis is not None:
            place[axis] = (place[axis] + hop) % SIDE
        core = 1 - self.core if other_core else self.core
        return (core, place[Y] * SIDE + place[Z], place[X])

    def slot(self, name):
        return self.names.setdefault(name, len(self.names))

    def copy(self, name, source, target, device):
        i = self.slot(name)
        return pltpu.make_async_remote_copy(
            source,
            target,
            self.send.at[i],
            self.recv.at[i],
            device_id=device,
            device_id_type=MESH,
        )

    def start(self, name, source, target, device):
        copy = self.copy(name, source, target, device)
        copy.start()
        self.begun.append(copy)
        return copy

    def local(self, name, source, target):
        copy = pltpu.make_async_copy(source, target, self.send.at[self.slot(name)])
        copy.start()
        return copy


def pick(axes, fixed):
    return tuple(fixed.get(axis, slice(None)) for axis in axes)


def gather(net, name, source, out, axes, order):
    at = net.at
    fixed = {axis: at[axis] for axis in axes}
    own = net.local((name, -1), source, out.at[pick(axes, fixed)])
    here = source
    for axis in order:
        place = pick(axes, fixed)
        copies = [
            net.start(
                (name, axis, hop),
                out.at[place] if here is None else here,
                out.at[place],
                net.device(axis, hop),
            )
            for hop in HOPS
        ]
        yield
        for copy in copies:
            copy.wait_recv()
        if here is not None:
            own.wait()
        here = None
        del fixed[axis]


def gather_two(net, name, source, out, order, after=None, patience=0):
    at = net.at
    first, second = order
    axes = (Y, Z)

    def place(back):
        spot = dict(at)
        spot[first] = (spot[first] - back + SIDE) % SIDE
        return (spot[Y], spot[Z])

    mine = place(0)
    own = net.local((name, -1), source, out.at[mine])
    ones = [
        net.start((name, 1, hop), source, out.at[mine], net.device(first, hop)) for hop in HOPS
    ]
    twos = []

    def forward(back):
        spot = place(back)
        for hop in HOPS:
            twos.append(
                net.start(
                    (name, 2, back, hop),
                    source if back == 0 else out.at[spot],
                    out.at[spot],
                    net.device(second, hop),
                )
            )

    forward(0)
    yield
    for copy, hop in zip(ones, HOPS):
        copy.wait_recv()
        forward(hop)
    own.wait()
    for _ in range(1 + patience):
        yield
    if after is None:
        for copy in twos:
            copy.wait_recv()
        return
    lines = [twos[3 * i : 3 * i + 3] for i in range(SIDE)]
    after(at[second])
    for h, hop in enumerate(HOPS):
        for line in lines:
            line[h].wait_recv()
        after((at[second] - hop + SIDE) % SIDE)


def scatter_sum(total, rows, own, others, out):
    chunk = 16 if rows % 16 == 0 else 8
    per = rows // chunk

    def step(i, carry):
        lead = i // per
        part = pl.ds(pl.multiple_of((i % per) * chunk, chunk), chunk)
        value = own(lead, part).astype(jnp.float32)
        for other in others:
            value = value + other(lead, part).astype(jnp.float32)
        out(lead, part, value)
        return carry

    lax.fori_loop(0, total * per, step, 0)


def reduce_two(net, name, source, pad, out, order):
    at = net.at
    first, second = order
    one, mid, two, kept = pad.one, pad.mid, pad.two, pad.own
    rows = source.shape[2]

    def part_of(line):
        return source.at[:, line] if first == Z else source.at[line]

    own = net.local((name, -4), part_of(at[first]), kept)
    ones = [
        net.start(
            (name, 1, hop),
            part_of((at[first] + hop) % SIDE),
            one.at[hop - 1],
            net.device(first, hop),
        )
        for hop in HOPS
    ]
    yield
    own.wait()
    for copy in ones:
        copy.wait_recv()

    def put_mid(lead, part, value):
        mid[lead, part, :] = value.astype(mid.dtype)

    scatter_sum(
        SIDE,
        rows,
        lambda lead, part: kept[lead, part, :],
        [lambda lead, part, k=k: one[k, lead, part, :] for k in range(3)],
        put_mid,
    )
    twos = [
        net.start(
            (name, 2, hop),
            mid.at[(at[second] + hop) % SIDE],
            two.at[hop - 1],
            net.device(second, hop),
        )
        for hop in HOPS
    ]
    yield
    for copy in twos:
        copy.wait_recv()
    spot = at[second]

    def put_out(lead, part, value):
        out[part, :] = value.astype(out.dtype)

    scatter_sum(
        1,
        rows,
        lambda lead, part: kept[spot, part, :],
        [lambda lead, part, k=k: one[k, spot, part, :] for k in range(3)]
        + [lambda lead, part, k=k: two[k, part, :] for k in range(3)],
        put_out,
    )


def swap_two(net, name, source, mid, out):
    at = net.at
    own = net.local((name, -1), source.at[:, at[Z]], mid.at[at[Z]])
    ones = [
        net.start(
            (name, 1, hop),
            source.at[:, (at[Z] + hop) % SIDE],
            mid.at[at[Z]],
            net.device(Z, hop),
        )
        for hop in HOPS
    ]
    yield
    for copy in ones:
        copy.wait_recv()
    own.wait()
    own = net.local((name, -2), mid.at[:, at[Y]], out.at[at[Y]])
    twos = [
        net.start(
            (name, 2, hop),
            mid.at[:, (at[Y] + hop) % SIDE],
            out.at[at[Y]],
            net.device(Y, hop),
        )
        for hop in HOPS
    ]
    yield
    for copy in twos:
        copy.wait_recv()
    own.wait()


def run_jobs(jobs):
    jobs = list(jobs)
    while jobs:
        jobs = [job for job in jobs if next(job, True) is None]


def flat(group):
    return [
        leaf
        for value in group.values()
        for leaf in (flat(value) if isinstance(value, dict) else [value])
    ]


def named(group, leaves):
    return types.SimpleNamespace(
        **{
            key: named(value, leaves) if isinstance(value, dict) else next(leaves)
            for key, value in group.items()
        }
    )


def exchange(name, number, program, inputs, outputs, scratch=None, vmem=None, cores=(0, 1)):
    scratch = scratch or {}
    parts = (inputs, outputs, scratch)
    counts = [len(flat(part)) for part in parts]

    def kernel(*refs):
        held = types.SimpleNamespace()
        begin = 0
        for part, count in zip(parts, counts):
            vars(held).update(vars(named(part, iter(refs[begin : begin + count]))))
            begin += count
        send, recv = refs[begin:]
        core = lax.axis_index("branch")
        seq = lax.axis_index("seq")
        coords = {X: lax.axis_index("fsdp"), Y: seq // SIDE, Z: seq % SIDE}
        names = {}
        for one_core in cores:

            @pl.when(core == one_core)
            def _():
                net = Net(one_core, coords, names, send, recv)
                barrier = pltpu.get_barrier_semaphore()
                peers = [net.device(axis, hop) for axis in (X, Y, Z) for hop in HOPS]
                if len(cores) == 2:
                    peers.append(net.device(other_core=True))
                for peer in peers:
                    pl.semaphore_signal(barrier, inc=1, device_id=peer, device_id_type=MESH)
                pl.semaphore_wait(barrier, len(peers))
                run_jobs(program(net, held))
                for copy in net.begun:
                    copy.wait_send()

        assert len(names) <= SEMS

    results = pl.pallas_call(
        kernel,
        out_shape=[jax.ShapeDtypeStruct(s, d) for s, d, _ in flat(outputs)],
        in_specs=[spec for _, spec in flat(inputs)],
        out_specs=[spec for _, _, spec in flat(outputs)],
        scratch_shapes=[pltpu.VMEM(s, d) for s, d in flat(scratch)]
        + [pltpu.SemaphoreType.DMA((SEMS,)), pltpu.SemaphoreType.DMA((SEMS,))],
        compiler_params=pltpu.CompilerParams(
            collective_id=number, has_side_effects=True, vmem_limit_bytes=vmem
        ),
        name=name,
    )(*[array for array, _ in flat(inputs)])
    return named(outputs, iter(results))


CHUNKS = 128
STEPS = 16
LINES = 8
WIDE = 40
far_away = 1e30


def to_lanes(source, target):
    for block in range(source.shape[0]):
        part = pl.ds(block * CHUNKS, CHUNKS)

        def move(l, carry):
            target[l, part, :] = source[block, pl.ds(l, CHUNKS, stride=STEPS), :].T
            return carry

        lax.fori_loop(0, STEPS, move, 0, unroll=2)


def to_rows(source, target):
    for block in range(target.shape[0]):
        part = pl.ds(block * CHUNKS, CHUNKS)

        def move(l, carry):
            target[block, pl.ds(l, CHUNKS, stride=STEPS), :] = source[l, part, :].T
            return carry

        lax.fori_loop(0, STEPS, move, 0, unroll=2)


def chunk_starts(ends, span, rates, reverse):
    lanes = lax.broadcasted_iota(jnp.int32, span.shape, 1)
    by = 1
    while by < CHUNKS:
        turn = CHUNKS - by if reverse else by
        inside = lanes < turn if reverse else lanes >= turn
        reach = jnp.where(inside, span, far_away)
        ends = [
            end + jnp.exp2(reach * rate) * pltpu.roll(end, turn, 1)
            for end, rate in zip(ends, rates)
        ]
        span = span + jnp.where(inside, pltpu.roll(span, turn, 1), 0.0)
        by *= 2
    turn = CHUNKS - 1 if reverse else 1
    inside = lanes < turn if reverse else lanes >= turn
    return [jnp.where(inside, pltpu.roll(end, turn, 1), 0.0) for end in ends]


def rate_lines(rate_ref, lines, states):
    tile = rate_ref[lines, :]
    return [jnp.broadcast_to(tile[:, s : s + 1], (lines.size, CHUNKS)) for s in range(states)]


def join_chunks(used, ends_ref, decay_t, rate_ref, reverse):
    states = rate_ref.shape[1]

    def channels(g, carry):
        lines = pl.ds(pl.multiple_of(g * WIDE, LINES), WIDE)
        span = decay_t[0, lines, :]
        for l in range(1, STEPS):
            span = span + decay_t[l, lines, :]
        starts = chunk_starts(
            [ends_ref[s, lines, :] for s in range(states)],
            span,
            rate_lines(rate_ref, lines, states),
            reverse,
        )
        for s in range(states):
            ends_ref[s, lines, :] = starts[s]
        return carry

    lax.fori_loop(0, used // WIDE, channels, 0)


def scan_forward_kernel(
    used, decay_ref, drive_ref, cols_ref, rate_ref, out_ref, start_ref, decay_t, drive_t, out_t
):
    states = rate_ref.shape[1]
    to_lanes(decay_ref, decay_t)
    to_lanes(drive_ref, drive_t)
    out_t[...] = jnp.zeros_like(out_t)

    def ends(g, carry):
        lines = pl.ds(pl.multiple_of(g * LINES, LINES), LINES)
        decays = [decay_t[l, lines, :] for l in range(STEPS)]
        drives = [drive_t[l, lines, :] for l in range(STEPS)]
        rates = rate_lines(rate_ref, lines, states)
        for s in range(states):
            state = drives[0] * cols_ref[s, 0:1, :]
            for l in range(1, STEPS):
                state = jnp.exp2(decays[l] * rates[s]) * state + drives[l] * cols_ref[s, l : l + 1, :]
            start_ref[s, lines, :] = state
        return carry

    lax.fori_loop(0, used // LINES, ends, 0)
    join_chunks(used, start_ref, decay_t, rate_ref, False)

    def channels(g, carry):
        lines = pl.ds(pl.multiple_of(g * LINES, LINES), LINES)
        decays = [decay_t[l, lines, :] for l in range(STEPS)]
        drives = [drive_t[l, lines, :] for l in range(STEPS)]
        rates = rate_lines(rate_ref, lines, states)
        outs = [jnp.zeros((LINES, CHUNKS), jnp.float32)] * STEPS
        for s in range(states):
            state = start_ref[s, lines, :]
            for l in range(STEPS):
                state = jnp.exp2(decays[l] * rates[s]) * state + drives[l] * cols_ref[s, l : l + 1, :]
                outs[l] = outs[l] + state * cols_ref[states + s, l : l + 1, :]
        for l in range(STEPS):
            out_t[l, lines, :] = outs[l]
        return carry

    lax.fori_loop(0, used // LINES, channels, 0)
    to_rows(out_t, out_ref)


def scan_forward(decay, drive, cols, rate, used):
    width = decay.shape[0] * CHUNKS
    states = rate.shape[1]
    turned = jax.ShapeDtypeStruct((STEPS, width, CHUNKS), jnp.float32)
    return pl.pallas_call(
        functools.partial(scan_forward_kernel, used),
        out_shape=[
            jax.ShapeDtypeStruct(decay.shape, jnp.float32),
            jax.ShapeDtypeStruct((states, width, CHUNKS), jnp.float32),
            turned,
            turned,
        ],
        in_specs=[VMEM] * 4,
        out_specs=[VMEM] * 4,
        scratch_shapes=[pltpu.VMEM(turned.shape, jnp.float32)],
        compiler_params=pltpu.CompilerParams(vmem_limit_bytes=32 * 2**20),
        name="scan_forward",
    )(decay, drive, cols, rate)


def scan_backward_kernel(
    used,
    decay_t,
    drive_t,
    cols_ref,
    rate_ref,
    start_ref,
    grad_ref,
    g_decay_ref,
    g_drive_ref,
    g_cols_ref,
    g_rate_ref,
    grad_t,
    g_decay_t,
    g_drive_t,
    sums_t,
    ends_t,
):
    states = rate_ref.shape[1]
    blank = jnp.zeros((LINES, CHUNKS), jnp.float32)
    to_lanes(grad_ref, grad_t)
    g_decay_t[...] = jnp.zeros_like(g_decay_t)
    g_drive_t[...] = jnp.zeros_like(g_drive_t)
    sums_t[...] = jnp.zeros_like(sums_t)
    g_rate_ref[...] = jnp.zeros_like(g_rate_ref)
    marks = lax.broadcasted_iota(jnp.int32, (LINES, states), 1)

    def ends(g, carry):
        lines = pl.ds(pl.multiple_of(g * LINES, LINES), LINES)
        rates = rate_lines(rate_ref, lines, states)
        decays = [decay_t[l, lines, :] for l in range(STEPS)]
        grads = [grad_t[l, lines, :] for l in range(STEPS)]
        for s in range(states):
            back = blank
            for l in reversed(range(STEPS)):
                back = jnp.exp2(decays[l] * rates[s]) * (
                    grads[l] * cols_ref[states + s, l : l + 1, :] + back
                )
            ends_t[s, lines, :] = back
        return carry

    lax.fori_loop(0, used // LINES, ends, 0)
    join_chunks(used, ends_t, decay_t, rate_ref, True)

    def channels(g, carry):
        lines = pl.ds(pl.multiple_of(g * LINES, LINES), LINES)
        tile = rate_ref[lines, :]

        def state_step(s, g_rate):
            rate = jnp.sum(jnp.where(marks == s, tile, 0.0), axis=1, keepdims=True)
            rate = jnp.broadcast_to(rate, (LINES, CHUNKS))
            state = start_ref[s, lines, :]
            befores, factors = [], []
            for l in range(STEPS):
                factor = jnp.exp2(decay_t[l, lines, :] * rate)
                befores.append(state)
                factors.append(factor)
                state = factor * state + drive_t[l, lines, :] * cols_ref[s, pl.ds(l, 1), :]
            back = ends_t[s, lines, :]
            total_rate = blank
            for l in reversed(range(STEPS)):
                grad = grad_t[l, lines, :]
                total = grad * cols_ref[states + s, pl.ds(l, 1), :] + back
                sums_t[s, l] += total * drive_t[l, lines, :]
                sums_t[states + s, l] += grad * state
                g_drive_t[l, lines, :] += total * cols_ref[s, pl.ds(l, 1), :]
                back = total * factors[l]
                moved = back * befores[l]
                g_decay_t[l, lines, :] += moved * rate
                total_rate = total_rate + moved * decay_t[l, lines, :]
                state = befores[l]
            total_rate = jnp.sum(total_rate, axis=1, keepdims=True)
            return jnp.where(marks == s, total_rate, g_rate)

        g_rate_ref[lines, :] = lax.fori_loop(
            0, states, state_step, jnp.zeros((LINES, states), jnp.float32), unroll=16
        )
        return carry

    lax.fori_loop(0, used // LINES, channels, 0)

    def collapse(i, carry):
        g_cols_ref[i] = jnp.sum(sums_t[i], axis=1)
        return carry

    lax.fori_loop(0, 2 * states, collapse, 0)
    to_rows(g_decay_t, g_decay_ref)
    to_rows(g_drive_t, g_drive_ref)


def scan_backward(decay_t, drive_t, cols, rate, starts, grad, used):
    states = rate.shape[1]
    turned = pltpu.VMEM(decay_t.shape, jnp.float32)
    return pl.pallas_call(
        functools.partial(scan_backward_kernel, used),
        out_shape=[
            jax.ShapeDtypeStruct(grad.shape, jnp.float32),
            jax.ShapeDtypeStruct(grad.shape, jnp.float32),
            jax.ShapeDtypeStruct(cols.shape, jnp.float32),
            jax.ShapeDtypeStruct(rate.shape, jnp.float32),
        ],
        in_specs=[VMEM] * 6,
        out_specs=[VMEM] * 4,
        scratch_shapes=[
            turned,
            turned,
            turned,
            pltpu.VMEM((2 * states, STEPS, LINES, CHUNKS), jnp.float32),
            pltpu.VMEM(starts.shape, jnp.float32),
        ],
        compiler_params=pltpu.CompilerParams(vmem_limit_bytes=48 * 2**20),
        name="scan_backward",
    )(decay_t, drive_t, cols, rate, starts, grad)


KEY_ROWS = 256
PIECE = 25
PADDED = 32
LANES = 128


def dot_on(left, right, left_dim, right_dim, **options):
    return lax.dot_general(
        left,
        right,
        (((left_dim,), (right_dim,)), ((), ())),
        preferred_element_type=jnp.float32,
        **options,
    )


def spread_matrix(low, high, wide_low, wide_high):
    shape = (high - low, wide_high - wide_low)
    column = low + lax.broadcasted_iota(jnp.int32, shape, 0)
    place = wide_low + lax.broadcasted_iota(jnp.int32, shape, 1)
    inside = place % PADDED
    match = (column == (place // PADDED) * PIECE + inside) & (inside < PIECE)
    return jnp.where(match, 1.0, 0.0).astype(jnp.bfloat16)


def spread_columns(values):
    width = values.shape[1]
    step = LANES // PADDED * PIECE
    parts = []
    for begin in range(0, width, step):
        low = begin // LANES * LANES
        high = min(low + 2 * LANES, width)
        wide = begin // PIECE * PADDED
        parts.append(dot_on(values[:, low:high], spread_matrix(low, high, wide, wide + LANES), 1, 0))
    return jnp.concatenate(parts, axis=1).astype(jnp.bfloat16)


def close_columns(values):
    width = values.shape[1] // PADDED * PIECE
    parts = []
    for begin in range(0, width, LANES):
        end = min(begin + LANES, width)
        low = begin // PIECE * PADDED // LANES * LANES
        high = -(-((end - 1) // PIECE + 1) * PADDED // LANES) * LANES
        matrix = spread_matrix(begin, end, low, high)
        value = values[:, low:high]
        most = value.astype(jnp.bfloat16)
        closed = dot_on(most, matrix, 1, 1)
        if values.dtype != jnp.bfloat16:
            rest = (value - most.astype(jnp.float32)).astype(jnp.bfloat16)
            closed = closed + dot_on(rest, matrix, 1, 1)
        parts.append(closed)
    return jnp.concatenate(parts, axis=1)


def unit_rows(values):
    return values * lax.rsqrt(jnp.mean(values * values, axis=-1, keepdims=True) + epsilon)


def whole_call(name, body, arrays, results, scratch=(), scalars=0, room=48):
    return pl.pallas_call(
        body,
        out_shape=[jax.ShapeDtypeStruct(shape, kind) for shape, kind in results],
        in_specs=[pl.BlockSpec(memory_space=pltpu.SMEM)] * scalars
        + [VMEM] * (len(arrays) - scalars),
        out_specs=[VMEM] * len(results),
        scratch_shapes=[pltpu.VMEM(shape, kind) for shape, kind in scratch],
        compiler_params=pltpu.CompilerParams(vmem_limit_bytes=room * 2**20),
        name=name,
    )(*arrays)


def attention_project_kernel(
    tokens_ref,
    meta_ref,
    gain_ref,
    first_ref,
    second_ref,
    wide_ref,
    query_ref,
    keyval_ref,
    meta_wide_ref,
    meta_kv_ref,
):
    gain = gain_ref[...]
    third = first_ref.shape[1]
    rest = query_ref.shape[1] - third
    begin = -(-rest // LANES) * LANES
    keys = pl.ds(begin, keyval_ref.shape[1])
    wide = spread_columns((unit_rows(tokens_ref[...].astype(jnp.float32)) * gain).astype(jnp.bfloat16))
    wide_ref[...] = wide
    query_ref[:, pl.ds(0, third)] = dot_on(wide, first_ref[...], 1, 0).astype(jnp.bfloat16)
    query_ref[:, pl.ds(third, rest)] = dot_on(wide, second_ref[:, pl.ds(0, rest)], 1, 0).astype(
        jnp.bfloat16
    )
    keyval_ref[...] = dot_on(wide, second_ref[:, keys], 1, 0).astype(jnp.bfloat16)
    meta_wide = spread_columns((unit_rows(meta_ref[...]) * gain).astype(jnp.bfloat16))
    meta_wide_ref[...] = meta_wide
    meta_kv_ref[...] = dot_on(meta_wide, second_ref[:, keys], 1, 0).astype(jnp.bfloat16)


def attention_project(tokens, meta, gain, first, second, query_width, keys_width):
    rows, metas, wide = tokens.shape[0], meta.shape[0], first.shape[0]
    low = jnp.bfloat16
    return whole_call(
        "attention_project",
        attention_project_kernel,
        (tokens, meta, gain, first, second),
        (
            ((rows, wide), low),
            ((rows, query_width), low),
            ((rows, keys_width), low),
            ((metas, wide), low),
            ((metas, keys_width), low),
        ),
    )


def attention_weights_kernel(
    wide_ref,
    out_wide_ref,
    g_query_ref,
    g_pre_ref,
    first_ref,
    second_ref,
    one_ref,
    two_ref,
    three_ref,
    gain_ref,
):
    third = first_ref.shape[1]
    one = dot_on(wide_ref[...], g_query_ref[...], 0, 0)
    cut = one_ref.shape[1]
    one_ref[...] = one[:, :cut].astype(jnp.bfloat16)
    gain = jnp.sum(one[:, :third] * first_ref[...].astype(jnp.float32), axis=1, keepdims=True)
    rest = one.shape[1] - third
    gain = gain + jnp.sum(
        one[:, third:] * second_ref[:, pl.ds(0, rest)].astype(jnp.float32), axis=1, keepdims=True
    )
    gain_ref[...] = gain
    two = dot_on(out_wide_ref[...], g_pre_ref[...], 0, 0)
    size = one.shape[1] - cut
    begin = -(-size // LANES) * LANES
    left = two_ref.shape[1] - begin
    two_ref[...] = jnp.zeros_like(two_ref)
    two_ref[:, pl.ds(0, size)] = one[:, cut:].astype(jnp.bfloat16)
    two_ref[:, pl.ds(begin, left)] = two[:, :left].astype(jnp.bfloat16)
    three_ref[...] = two[:, left:].astype(jnp.bfloat16)


def attention_weights(wide, out_wide, g_query, g_pre, first, second, cuts):
    rows, places = wide.shape
    size = 2 * LANES
    columns = pl.BlockSpec((rows, size), lambda i: (0, i))

    def lines(width):
        return pl.BlockSpec((size, width), lambda i: (i, 0))

    return pl.pallas_call(
        attention_weights_kernel,
        grid=(places // size,),
        out_shape=[jax.ShapeDtypeStruct((places, cut), jnp.bfloat16) for cut in cuts]
        + [jax.ShapeDtypeStruct((places, 1), jnp.float32)],
        in_specs=[columns, columns]
        + [pl.BlockSpec(part.shape, lambda i: (0, 0)) for part in (g_query, g_pre)]
        + [lines(first.shape[1]), lines(second.shape[1])],
        out_specs=[lines(cut) for cut in cuts] + [lines(1)],
        compiler_params=pltpu.CompilerParams(vmem_limit_bytes=32 * 2**20),
        name="attention_weights",
    )(wide, out_wide, g_query, g_pre, first, second)


def attention_inputs_kernel(
    keyval_ref,
    g_query_ref,
    wide_ref,
    meta_wide_ref,
    g_meta_ref,
    first_ref,
    second_ref,
    meta_ref,
    gain_ref,
    one_ref,
    two_ref,
    three_ref,
    g_normed_ref,
    part_ref,
    meta_gain_ref,
):
    third = first_ref.shape[1]
    rest = g_query_ref.shape[1] - third
    begin = -(-rest // LANES) * LANES
    keys = pl.ds(begin, keyval_ref.shape[1])
    keyval = keyval_ref[...].astype(jnp.bfloat16)
    weight = second_ref[:, keys]
    weight_f = weight.astype(jnp.float32)
    grad = dot_on(wide_ref[...], keyval, 0, 0)
    part_ref[...] = jnp.sum(grad * weight_f, axis=1, keepdims=True)
    g_meta = g_meta_ref[...]
    grad = grad + dot_on(
        meta_wide_ref[...].astype(jnp.float32), g_meta, 0, 0, precision=highest
    )
    half = one_ref.shape[1]
    one_ref[...] = grad[:, :half].astype(jnp.bfloat16)
    two_ref[...] = grad[:, half:].astype(jnp.bfloat16)
    g_normed = dot_on(g_query_ref[:, pl.ds(0, third)], first_ref[...], 1, 1)
    g_normed = g_normed + dot_on(
        g_query_ref[:, pl.ds(third, rest)], second_ref[:, pl.ds(0, rest)], 1, 1
    )
    g_normed_ref[...] = close_columns(g_normed + dot_on(keyval, weight, 1, 1))
    g_meta_normed = close_columns(dot_on(g_meta, weight_f, 1, 1, precision=highest))
    meta = meta_ref[...]
    scale = lax.rsqrt(jnp.mean(meta * meta, axis=-1, keepdims=True) + epsilon)
    unit = meta * scale
    meta_gain_ref[...] = jnp.sum(g_meta_normed * unit, axis=0, keepdims=True)
    g_unit = g_meta_normed * gain_ref[...]
    g_rows = scale * (g_unit - unit * jnp.mean(g_unit * unit, axis=-1, keepdims=True))
    three_ref[...] = spread_columns(g_rows.astype(jnp.bfloat16)).T


def attention_inputs(
    keyval_sum, g_query, wide, meta_wide, g_meta, first, second, meta, gain
):
    rows, places = wide.shape
    keys_width = keyval_sum.shape[1]
    metas, width = meta.shape
    low, full = jnp.bfloat16, jnp.float32
    return whole_call(
        "attention_inputs",
        attention_inputs_kernel,
        (keyval_sum, g_query, wide, meta_wide, g_meta, first, second, meta, gain),
        (
            ((places, keys_width // 2), low),
            ((places, keys_width // 2), low),
            ((places, metas), low),
            ((rows, width), full),
            ((places, 1), full),
            ((1, width), full),
        ),
        room=60,
    )


def stack_heads(source, target, scale, in_values):
    rows = source.shape[0]
    groups = target.shape[0]
    per = target.shape[1] // rows
    blank = jnp.zeros((rows, HEAD), target.dtype)
    for group in range(groups):
        for j in range(per):
            head = source[:, pl.ds((group * per + j) * HEAD, HEAD)].astype(jnp.float32) * scale
            head = head.astype(target.dtype)
            pair = [blank, head] if in_values else [head, blank]
            target[group, pl.ds(j * rows, rows), :] = jnp.concatenate(pair, axis=1)


def lay_keys(source, target):
    rows = source.shape[2]

    def move(place, carry):
        for half in range(2):
            begin = pl.multiple_of((place * 2 + half) * rows, rows)
            target[pl.ds(begin, rows), :] = source[half, place]
        return carry

    lax.fori_loop(0, source.shape[1], move, 0)


def key_bias(bounds_ref, begin, per):
    rows = bounds_ref.shape[0]
    keys = begin + lax.broadcasted_iota(jnp.int32, (rows, KEY_ROWS), 1)
    allowed = (keys >= bounds_ref[:, 0:1]) & (keys <= bounds_ref[:, 1:2])
    bias = jnp.where(allowed, 0.0, negative_fill)
    return jnp.concatenate([bias] * per, axis=0)


def attend_forward_kernel(
    count_ref,
    query_ref,
    keyval_ref,
    meta_ref,
    bounds_ref,
    second_ref,
    third_ref,
    out_ref,
    mass_ref,
    wide_ref,
    pre_ref,
    heads,
    keys,
    scores,
):
    rows = query_ref.shape[0]
    groups = heads.shape[0]
    per = heads.shape[1] // rows
    width = 2 * HEAD
    metas = meta_ref.shape[0]
    meta_part = pl.ds(scores.shape[1] - metas, metas)
    stack_heads(query_ref, heads, score_scale, False)
    lay_keys(keyval_ref, keys)
    count = count_ref[0]
    lanes = lax.broadcasted_iota(jnp.int32, mass_ref.shape, 1)
    for group in range(groups):
        part = pl.ds(group * width, width)
        query = heads[group]

        def score(b, top):
            begin = pl.multiple_of(b * KEY_ROWS, KEY_ROWS)
            value = dot_on(query, keys[pl.ds(begin, KEY_ROWS), part], 1, 1)
            value = value + key_bias(bounds_ref, begin, per)
            scores[:, pl.ds(begin, KEY_ROWS)] = value
            return jnp.maximum(top, jnp.max(value, axis=1, keepdims=True))

        value = dot_on(query, meta_ref[:, part], 1, 1)
        scores[:, meta_part] = value
        top = lax.fori_loop(0, count, score, jnp.max(value, axis=1, keepdims=True))

        def weigh(b, total):
            spot = pl.ds(pl.multiple_of(b * KEY_ROWS, KEY_ROWS), KEY_ROWS)
            value = jnp.exp(scores[:, spot] - top)
            scores[:, spot] = value
            return total + jnp.sum(value, axis=1, keepdims=True)

        value = jnp.exp(scores[:, meta_part] - top)
        scores[:, meta_part] = value
        total = lax.fori_loop(0, count, weigh, jnp.sum(value, axis=1, keepdims=True))
        share = 1.0 / total

        def gather_values(b, out):
            begin = pl.multiple_of(b * KEY_ROWS, KEY_ROWS)
            probs = (scores[:, pl.ds(begin, KEY_ROWS)] * share).astype(jnp.bfloat16)
            return out + dot_on(probs, keys[pl.ds(begin, KEY_ROWS), part], 1, 0)

        probs = (scores[:, meta_part] * share).astype(jnp.bfloat16)
        out = lax.fori_loop(0, count, gather_values, dot_on(probs, meta_ref[:, part], 1, 0))
        for j in range(per):
            out_ref[:, pl.ds((group * per + j) * HEAD, HEAD)] = out[
                j * rows : (j + 1) * rows, HEAD:
            ]
        mass = top + jnp.log(total)
        before = mass_ref[...] if group else jnp.zeros_like(mass_ref)
        mass_ref[...] = jnp.where(lanes == group, mass, before)
    wide = spread_columns(out_ref[...].astype(jnp.bfloat16))
    wide_ref[...] = wide
    most = third_ref.shape[1]
    part = pre_ref.shape[1] - most
    pre_ref[:, pl.ds(0, part)] = dot_on(
        wide, second_ref[:, pl.ds(second_ref.shape[1] - part, part)], 1, 0
    )
    pre_ref[:, pl.ds(part, most)] = dot_on(wide, third_ref[...], 1, 0)


def attend_forward(count, query, keyval, meta, bounds, second, third):
    rows, query_width = query.shape
    groups = meta.shape[1] // (2 * HEAD)
    stacked = query_width // HEAD // groups * rows
    key_rows = 2 * keyval.shape[1] * keyval.shape[2]
    places, low, full = second.shape[0], jnp.bfloat16, jnp.float32
    return whole_call(
        "attend_forward",
        attend_forward_kernel,
        (count, query, keyval, meta, bounds, second, third),
        (
            ((rows, query_width), full),
            ((stacked, 2 * HEAD), full),
            ((rows, places), low),
            ((rows, query_width), full),
        ),
        (
            ((groups, stacked, 2 * HEAD), low),
            ((key_rows, meta.shape[1]), low),
            ((stacked, key_rows + meta.shape[0]), full),
        ),
        scalars=1,
    )


def attend_backward_kernel(
    count_ref,
    query_ref,
    keyval_ref,
    meta_ref,
    bounds_ref,
    out_ref,
    mass_ref,
    g_pre_ref,
    second_ref,
    third_ref,
    g_query_ref,
    g_keyval_ref,
    g_meta_ref,
    heads,
    grads,
    keys,
    grad_ref,
):
    rows = query_ref.shape[0]
    groups = heads.shape[0]
    per = heads.shape[1] // rows
    width = 2 * HEAD
    most = third_ref.shape[1]
    left = g_pre_ref.shape[1] - most
    grad_wide = dot_on(
        g_pre_ref[:, pl.ds(0, left)],
        second_ref[:, pl.ds(second_ref.shape[1] - left, left)],
        1,
        1,
    )
    grad_wide = grad_wide + dot_on(g_pre_ref[:, pl.ds(left, most)], third_ref[...], 1, 1)
    grad_ref[...] = close_columns(grad_wide.astype(jnp.bfloat16)).astype(jnp.bfloat16)
    stack_heads(query_ref, heads, score_scale, False)
    stack_heads(grad_ref, grads, 1.0, True)
    lay_keys(keyval_ref, keys)
    g_keyval_ref[...] = jnp.zeros_like(g_keyval_ref)
    count = count_ref[0]
    lanes = lax.broadcasted_iota(jnp.int32, mass_ref.shape, 1)
    for group in range(groups):
        part = pl.ds(group * width, width)
        query, grad = heads[group], grads[group]
        mass = jnp.sum(jnp.where(lanes == group, mass_ref[...], 0.0), axis=1, keepdims=True)
        balance = []
        for j in range(per):
            head = pl.ds((group * per + j) * HEAD, HEAD)
            balance.append(
                jnp.sum(grad_ref[:, head].astype(jnp.float32) * out_ref[:, head], axis=1, keepdims=True)
            )
        balance = jnp.concatenate(balance, axis=0)

        def pieces(block, bias):
            value = dot_on(query, block, 1, 1)
            if bias is not None:
                value = value + bias
            probs = jnp.exp(value - mass)
            g_scores = (probs * (dot_on(grad, block, 1, 1) - balance)).astype(jnp.bfloat16)
            g_block = dot_on(g_scores, query, 0, 0) + dot_on(probs.astype(jnp.bfloat16), grad, 0, 0)
            return dot_on(g_scores, block, 1, 0), g_block

        g_query, g_meta = pieces(meta_ref[:, part], None)
        g_meta_ref[:, part] = g_meta

        def step(b, g_query):
            begin = pl.multiple_of(b * KEY_ROWS, KEY_ROWS)
            more, g_block = pieces(
                keys[pl.ds(begin, KEY_ROWS), part], key_bias(bounds_ref, begin, per)
            )
            g_keyval_ref[pl.ds(begin, KEY_ROWS), part] = g_block.astype(jnp.bfloat16)
            return g_query + more

        g_query = lax.fori_loop(0, count, step, g_query) * score_scale
        for j in range(per):
            g_query_ref[:, pl.ds((group * per + j) * HEAD, HEAD)] = g_query[
                j * rows : (j + 1) * rows, :HEAD
            ].astype(jnp.bfloat16)


def attend_backward(count, query, keyval, meta, bounds, out, mass, g_pre, second, third):
    rows, query_width = query.shape
    groups = meta.shape[1] // (2 * HEAD)
    stacked = mass.shape[0]
    key_rows = 2 * keyval.shape[1] * keyval.shape[2]
    low = jnp.bfloat16
    return whole_call(
        "attend_backward",
        attend_backward_kernel,
        (count, query, keyval, meta, bounds, out, mass, g_pre, second, third),
        (
            ((rows, query_width), low),
            ((key_rows, meta.shape[1]), low),
            (meta.shape, jnp.float32),
        ),
        (
            ((groups, stacked, 2 * HEAD), low),
            ((groups, stacked, 2 * HEAD), low),
            ((key_rows, meta.shape[1]), low),
            ((rows, query_width), low),
        ),
        scalars=1,
        room=56,
    )


def rms_norm(values, gain):
    return values * lax.rsqrt(jnp.mean(values * values, axis=-1, keepdims=True) + epsilon) * gain


def rms_unit(values):
    return values * lax.rsqrt(jnp.mean(values * values, axis=-1, keepdims=True) + epsilon)


def contract(left, right, left_dim, right_dim, **options):
    return lax.dot_general(
        left,
        right,
        (((left_dim,), (right_dim,)), ((), ())),
        **(options or {"preferred_element_type": jnp.float32}),
    )


def matmul(left, right):
    return contract(left, right, 1, 0)


def matmul_tn(left, right):
    return contract(left, right, 0, 0)


def matmul_nt(left, right):
    return contract(left, right, 1, 1)


def segment_of(row_ids, end_rows):
    return jnp.sum((row_ids[:, None] >= end_rows[None, :]).astype(jnp.int32), axis=1)


def conv_silu(conv_in, taps, offset, valid_rows):
    row_count = conv_in.shape[0]
    summed = taps[CONV - 1] * conv_in + offset
    for back in range(1, CONV):
        earlier = jnp.pad(conv_in, ((back, 0), (0, 0)))[:row_count]
        summed = summed + taps[CONV - 1 - back] * earlier * valid_rows[back - 1][:, None]
    return jax.nn.silu(summed)


def gate_mix(ssm_out, skip_gain, inputs_m, gate_z):
    return (ssm_out + skip_gain * inputs_m) * jax.nn.silu(gate_z)


def swiglu(gate, up):
    return jax.nn.silu(gate) * up


def pad_to(array, dim, size):
    widths = [(0, 0)] * array.ndim
    widths[dim] = (0, size - array.shape[dim])
    return jnp.pad(array, widths)


def zeros(shape, kind=jnp.float32):
    return jnp.zeros(shape, kind)


def halves_first(rows_by_place):
    width = rows_by_place.shape[-1]
    return rows_by_place.reshape(16, 2, -1, width).transpose(1, 0, 2, 3).reshape(-1, width)


def places_first(rows_by_half):
    width = rows_by_half.shape[-1]
    return rows_by_half.reshape(2, 16, -1, width).transpose(1, 0, 2, 3).reshape(-1, width)


def blank(shapes):
    leaves, nest = jax.tree.flatten(shapes)
    outs = pl.pallas_call(
        lambda *refs: None,
        out_shape=[jax.ShapeDtypeStruct(leaf.shape, leaf.dtype) for leaf in leaves],
        out_specs=[ANY] * len(leaves),
        name="blank",
    )()
    return jax.tree.unflatten(nest, outs)


def order_of(net):
    return (Z, Y) if net.core == 0 else (Y, Z)


def gather_halves(net, name, source, out, patience=0):
    if net.core == 0:
        count = []

        def after(line):
            net.start(
                (name, -3, len(count)),
                out.at[0, line],
                out.at[0, line],
                net.device(other_core=True),
            )
            count.append(line)

        yield from gather_two(net, name, source, out.at[0], (Z, Y), after, patience)
    else:
        yield from gather_two(net, name, source, out.at[1], (Y, Z), None, patience)
        for i in range(SIDE):
            net.copy(
                (name, -3, i), out.at[0, i], out.at[0, i], net.device(other_core=True)
            ).wait_recv()


def reduce_halves(net, name, source, pad, out):
    if net.core == 1:
        for y in range(SIDE):
            net.start(
                (name, -3, y), source.at[0, y], pad.half.at[y], net.device(other_core=True)
            )
        own = net.local((name, -1), source.at[1], pad.half)
        yield
        own.wait()
    else:
        yield
        for y in range(SIDE):
            net.copy(
                (name, -3, y), source.at[0, y], pad.half.at[y], net.device(other_core=True)
            ).wait_recv()
    yield from reduce_two(net, name, pad.half, pad, out, order_of(net))


def share_x(net, name, source, view):
    x = net.at[X]
    core, other = net.core, 1 - net.core
    own = net.local((name, -1), source, view(core, x))
    copies = [
        net.start((name, -2, hop), source, view(core, x), net.device(X, hop)) for hop in HOPS
    ]
    net.start((name, core, 0), source, view(core, x), net.device(other_core=True))
    yield
    for copy, hop in zip(copies, HOPS):
        copy.wait_recv()
        spot = (x - hop + SIDE) % SIDE
        net.start(
            (name, core, hop), view(core, spot), view(core, spot), net.device(other_core=True)
        )
    yield
    for i in (0,) + HOPS:
        net.copy(
            (name, other, i), source, view(other, x), net.device(other_core=True)
        ).wait_recv()
    own.wait()


def swap_cores(net, name, source, out):
    net.start((name, net.core), source, out.at[net.core], net.device(other_core=True))
    own = net.local((name, -1), source, out.at[net.core])
    yield
    net.copy(
        (name, 1 - net.core), source, out.at[1 - net.core], net.device(other_core=True)
    ).wait_recv()
    own.wait()


def hand(net, name, giver, source, target):
    if net.core == giver:
        net.start(name, source, target, net.device(other_core=True))
    else:
        net.copy(name, source, target, net.device(other_core=True)).wait_recv()


def keep_and_hand(net, name, giver, source, target):
    if net.core == giver:
        own = net.local((name, -1), source, target)
    hand(net, (name, 0), giver, source, target)
    yield
    if net.core == giver:
        own.wait()


def reduce_x(net, name, source, pad, out):
    x = net.at[X]
    recv, kept = pad.recv, pad.own
    own = net.local((name, -4), source.at[x], kept)
    copies = [
        net.start(
            (name, 5, hop), source.at[(x + hop) % SIDE], recv.at[hop - 1], net.device(X, hop)
        )
        for hop in HOPS
    ]
    yield
    own.wait()
    for copy in copies:
        copy.wait_recv()

    def put(lead, part, value):
        index = (lead,) if len(out.shape) == 3 else (lead // SIDE, lead % SIDE)
        out[index + (part, slice(None))] = value.astype(out.dtype)

    scatter_sum(
        source.shape[1],
        source.shape[2],
        lambda lead, part: kept[lead, part, :],
        [lambda lead, part, k=k: recv[k, lead, part, :] for k in range(3)],
        put,
    )


def reduce_three(net, name, source, pad, out, order):
    left = [Y, Z, X]
    held = source
    stages = ((pad.recv0, pad.mid0), (pad.recv1, pad.mid1), (pad.recv2, out))
    for stage, axis in enumerate(order):
        recv, mid = stages[stage]
        spot = left.index(axis)
        size = len(left)

        def part_of(place, held=held, spot=spot):
            return held.at[(slice(None),) * spot + (place,)]

        if stage == 0:
            fetch = net.local((name, -4), part_of(net.at[axis]), pad.own)
        copies = [
            net.start(
                (name, stage, hop),
                part_of((net.at[axis] + hop) % SIDE),
                recv.at[hop - 1],
                net.device(axis, hop),
            )
            for hop in HOPS
        ]
        yield
        if stage == 0:
            fetch.wait()
        for copy in copies:
            copy.wait_recv()

        def split(lead, size=size):
            return tuple((lead // SIDE**i) % SIDE for i in reversed(range(size - 1)))

        def own(lead, part, held=held, spot=spot, split=split, axis=axis):
            index = split(lead)
            if len(index) == 2:
                return pad.own[index + (part, slice(None))]
            index = index[:spot] + (net.at[axis],) + index[spot:]
            return held[index + (part, slice(None))]

        def put(lead, part, value, mid=mid, split=split):
            mid[split(lead) + (part, slice(None))] = value.astype(mid.dtype)

        scatter_sum(
            SIDE ** (size - 1),
            source.shape[3],
            own,
            [
                lambda lead, part, k=k, recv=recv, split=split: recv[
                    (k,) + split(lead) + (part, slice(None))
                ]
                for k in range(3)
            ],
            put,
        )
        held = mid
        del left[spot]


def three_pad(rows, width, kind=jnp.bfloat16):
    block = (rows, width)
    return dict(
        own=((SIDE, SIDE) + block, kind),
        recv0=((3, SIDE, SIDE) + block, kind),
        mid0=((SIDE, SIDE) + block, kind),
        recv1=((3, SIDE) + block, kind),
        mid1=((SIDE,) + block, kind),
        recv2=((3,) + block, kind),
    )


def two_pad(rows, width, kind=jnp.bfloat16):
    return dict(
        one=((3, SIDE, rows, width), kind),
        mid=((SIDE, rows, width), kind),
        two=((3, rows, width), kind),
        own=((SIDE, rows, width), kind),
    )


def half_pad(rows, width, kind=jnp.bfloat16):
    return dict(two_pad(rows, width, kind), half=((SIDE, SIDE, rows, width), kind))


def shrink_pad(lead, rows, width, kind=jnp.bfloat16):
    return dict(
        mine=((SIDE, lead, rows, width), kind),
        other=((SIDE, lead, rows, width), kind),
        mid=((SIDE, lead, rows, width), kind),
        **x_pad(lead, rows, width, kind),
    )


def x_pad(lead, rows, width, kind=jnp.bfloat16):
    return dict(recv=((3, lead, rows, width), kind), own=((lead, rows, width), kind))


def program_start(net, held):
    core = net.core
    rows = held.tokens.shape[0] // 2
    axes = (Y, Z, X)
    jobs = []
    if core == 1:

        def mamba():
            target = held.mamba_all.at[net.at[X]]
            yield from swap_two(net, 2, held.mamba, held.mamba_mid, target)
            copies = [
                net.start((2, 3, hop), target, target, net.device(X, hop)) for hop in HOPS
            ]
            yield
            for copy in copies:
                copy.wait_recv()

        jobs = [
            mamba(),
            gather(net, 3, held.back, held.back_all, (X,), (X,)),
            gather(net, 4, held.channel, held.channel_all, (X,), (X,)),
        ]
    return jobs + [
        gather(net, 1, held.small, held.small_all, axes, order_of(net) + (X,)),
        gather_halves(
            net, 0, held.tokens.at[pl.ds(core * rows, rows)], held.tokens_all, patience=2
        ),
    ]


def program_weights(net, held):
    axes = (Y, Z, X)
    jobs, begin = [], 0
    for i, (target, order) in enumerate(
        ((held.first, (X, Z, Y)), (held.second, (Z, Y, X)), (held.third, (Y, X, Z)))
    ):
        size = target.shape[-1]
        jobs.append(gather(net, i, held.whole.at[:, pl.ds(begin, size)], target, axes, order))
        begin += size
    return jobs


def program_keyval(net, held):
    rows = held.keyval.shape[0] // 2
    return [
        gather_two(
            net,
            i,
            held.keyval.at[pl.ds(i * rows, rows)],
            held.keyval_all.at[i],
            ((Z, Y), (Y, Z))[i],
        )
        for i in range(2)
    ] + [swap_two(net, 2, held.gate.at[0], held.gate_mid, held.gate_own)]


def program_project(net, held):
    jobs = []
    for i, order in enumerate(((Z, Y), (Y, Z))):
        source = (held.first, held.second)[i]
        pad = (held.first_pad, held.second_pad)[i]
        target = (held.first_all, held.second_all)[i]

        def job(source=source, pad=pad, target=target, order=order, i=i):
            yield from reduce_two(net, 2 * i, source, pad, pad.sum, order)
            yield from gather_two(net, 2 * i + 1, pad.sum, target, order)

        jobs.append(job())
    return jobs + [swap_two(net, 4, held.gate, held.gate_mid, held.gate_own)]


def program_mixers(net, held):
    core = net.core
    half = held.down.shape[0] // 2
    rows = held.attn_pre.shape[0] // 2

    def attn():
        if core == 0:
            own = net.local((1, -1), held.attn_pre.at[pl.ds(0, rows)], held.attn_half)
        hand(net, (1, 0), 0, held.attn_pre.at[pl.ds(rows, rows)], held.attn_half)
        yield
        if core == 0:
            own.wait()

    return [
        attn(),
        share_x(
            net,
            2,
            held.gate_first if core == 0 else held.gate_second,
            lambda b, x: held.gate_all.at[b, x],
        ),
        share_x(
            net,
            3,
            held.down.at[pl.ds(core * half, half)],
            lambda b, x: held.down_all.at[x, pl.ds(b * half, half)],
        ),
        reduce_halves(net, 0, held.partial, held.pad, held.mamba_pre),
    ]


def program_feed(net, held):
    return [gather_two(net, 0, held.feed, held.feed_all, order_of(net))]


def program_ffn(net, held):
    return [
        reduce_two(net, 0, held.out, held.out_pad, held.out_sum, order_of(net)),
        reduce_two(net, 1, held.grad, held.grad_pad, held.grad_sum, order_of(net)),
    ]


def shrink(net, name, source, pad, out):
    core = net.core
    lead, rows = source.shape[2:4]
    mine = net.local((name, -5), source.at[core], pad.mine)
    net.start((name, 6, core), source.at[1 - core], pad.other, net.device(other_core=True))
    yield
    net.copy(
        (name, 6, 1 - core), source.at[1 - core], pad.other, net.device(other_core=True)
    ).wait_recv()

    mine.wait()

    def put(i, part, value):
        pad.mid[i // lead, i % lead, part, :] = value.astype(pad.mid.dtype)

    scatter_sum(
        SIDE * lead,
        rows,
        lambda i, part: pad.mine[i // lead, i % lead, part, :],
        [lambda i, part: pad.other[i // lead, i % lead, part, :]],
        put,
    )
    yield from reduce_x(net, name, pad.mid, pad, out)


def program_back(net, held):
    core = net.core

    def attn():
        if core == 0:
            own = net.local((5, -1), held.g_attn, held.g_attn_both.at[0])
        hand(net, (5, 0), 1, held.g_attn, held.g_attn_both.at[1])
        yield
        if core == 0:
            own.wait()

    return [
        swap_cores(net, 3, held.mixed, held.mixed_both),
        swap_cores(net, 4, held.g_hidden, held.g_hidden_both),
        attn(),
        shrink(net, 1, held.g_gate, held.gate_pad, held.g_gate_sum),
        shrink(net, 2, held.g_down, held.down_pad, held.g_down_sum),
        gather_halves(net, 0, held.g_mamba, held.g_mamba_all, patience=1),
    ]


def three_sums(net, held):
    return [
        reduce_three(net, 10, held.one, held.one_pad, held.one_sum, (Y, Z, X)),
        reduce_three(net, 11, held.two, held.two_pad, held.two_sum, (X, Y, Z)),
        reduce_three(net, 12, held.three, held.three_pad, held.three_sum, (Z, X, Y)),
    ]


def program_attention(net, held):
    def last():
        for _ in range(4):
            yield
        begin = 0
        for part in (held.one_sum, held.two_sum, held.three_sum):
            held.sums[:, pl.ds(begin, part.shape[1])] = part[...]
            begin += part.shape[1]

    return [
        reduce_two(net, 0, held.keyval, held.keyval_pad, held.keyval_sum, (Z, Y)),
        *three_sums(net, held),
        swap_two(net, 3, held.gate, held.gate_mid, held.gate_own),
        last(),
    ]


def program_keys(net, held):
    return three_sums(net, held)


def program_end(net, held):
    core = net.core

    def normed():
        yield from reduce_halves(net, 0, held.partial, held.normed_pad, held.normed_sum)
        yield from swap_cores(net, 1, held.normed_sum, held.normed_both)

    def gains():
        yield from reduce_three(
            net, 2, held.gains, held.gains_pad, held.gains_sum, order_of(net) + (X,)
        )
        yield from swap_cores(net, 3, held.gains_sum, held.gains_both)

    def mamba():
        if core == 1:
            yield from reduce_x(net, 4, held.mamba, held.mamba_pad, held.mamba_part)
            yield from swap_two(net, 5, held.mamba_part, held.mamba_mid, held.mamba_sum)
        else:
            for _ in range(4):
                yield
        hand(net, (6, 0), 1, held.mamba_sum, held.mamba_sum)

    def channel(name, source, pad, total):
        if core == 1:
            yield from reduce_x(net, name, source, pad, total)
        else:
            for _ in range(2):
                yield
        hand(net, (name, 0), 1, total, total)

    return [
        normed(),
        mamba(),
        channel(7, held.back, held.back_pad, held.back_sum),
        channel(8, held.channel, held.channel_pad, held.channel_sum),
        gains(),
        keep_and_hand(net, 9, 0, held.g_attn, held.g_attn_both),
        keep_and_hand(net, 10, 0, held.sums_in, held.sums),
        keep_and_hand(net, 12, 0, held.keys, held.keys_sum),
        swap_cores(net, 13, held.gate, held.gate_both),
        swap_cores(net, 14, held.down, held.down_both),
    ]


def blocks_of(weight, splits):
    rows, columns = weight.shape
    cut = weight.reshape(rows, splits, 16, columns // splits // 16).transpose(1, 2, 0, 3)
    return pad_to(cut, 2, 32)


def rows_of(blocks, rows):
    width = blocks.shape[-1]
    return blocks.reshape(-1, blocks.shape[-2], width)[:, :rows].reshape(-1, width)


def padded_blocks(rows, count, size, kind=jnp.bfloat16):
    width = rows.shape[-1]
    return pad_to(rows.reshape(count, -1, width), 1, size).astype(kind)


def shards(
    tokens,
    seq_lengths,
    norm_gain,
    meta_tokens,
    w_query,
    w_key_value,
    w_attn_out,
    attn_gain,
    w_mamba_in,
    conv_weight,
    conv_bias,
    w_ssm_x,
    w_dt,
    dt_bias,
    a_log,
    skip_d,
    w_mamba_out,
    mamba_gain,
    ffn_gain,
    w_gate_up,
    w_down,
    cotangent,
):
    low = jnp.bfloat16
    full = jnp.float32
    core = lax.axis_index("branch")
    on_attention = core == 0
    tokens_b, cotangent_b = tokens[0], cotangent[0]
    rows, width = tokens_b.shape
    half = rows // 2
    group = rows * 16
    piece = w_query.shape[0]
    query_width = w_query.shape[1]
    keys_width = w_key_value.shape[1]
    inner_piece = w_mamba_out.shape[0]
    inner = inner_piece * SIDE
    rank = w_dt.shape[0]
    states = a_log.shape[0]
    proj = rank + 2 * states
    proj_pad = 136
    proj_cut = 72
    metas = meta_tokens.shape[0]
    down_piece = w_down.shape[0]
    units = down_piece * SIDE
    row_start = core * half

    lengths = seq_lengths[0]
    end_rows = jnp.cumsum(lengths)
    start_rows = end_rows - lengths
    all_rows = jnp.arange(group, dtype=jnp.int32)
    all_segments = segment_of(all_rows, end_rows)
    my_rows = lax.axis_index("seq") * rows + jnp.arange(rows, dtype=jnp.int32)
    keep_rows = jnp.logical_not(jnp.any(all_rows[:, None] == start_rows[None, :], axis=1))
    valid_rows = jnp.stack(
        [
            (
                (all_rows - back >= 0)
                & (segment_of(all_rows - back, end_rows) == all_segments)
            ).astype(jnp.float32)
            for back in range(1, CONV)
        ]
    )

    gains_in = jnp.stack([norm_gain, attn_gain, mamba_gain, ffn_gain], axis=1)
    small_in = jnp.concatenate([gains_in, meta_tokens.T], axis=1)
    small_in = pad_to(pad_to(small_in, 1, 256), 0, 32).astype(low)
    keys_in = w_key_value.reshape(piece, 2, -1, HEAD).transpose(0, 2, 1, 3).reshape(piece, -1)
    query_most = -(-query_width // LANES) * LANES
    attention_in = jnp.concatenate(
        [pad_to(w_query, 1, query_most).astype(low), keys_in.astype(low), w_attn_out.astype(low)], axis=1
    )
    attention_in = pad_to(attention_in, 0, 32)
    third = 10 * LANES
    last_third = attention_in.shape[1] - 2 * third
    mamba_in = blocks_of(w_mamba_in.astype(low), 2)
    mamba_in = jnp.concatenate([mamba_in[0], mamba_in[1]], axis=-1).reshape(SIDE, SIDE, 32, -1)
    back_in = pad_to(w_mamba_out, 0, 64).astype(low)
    channel_in = jnp.concatenate(
        [
            w_ssm_x,
            conv_weight.T,
            jnp.stack([conv_bias, dt_bias, skip_d], axis=1),
            a_log.T,
            w_dt.T,
        ],
        axis=1,
    )
    channel_in = pad_to(pad_to(channel_in, 0, 64), 1, 256).astype(low)
    gate_in = blocks_of(w_gate_up.astype(low), 2).reshape(2, SIDE, SIDE, 32, units)
    down_in = pad_to(w_down, 0, 96).astype(low)
    cube = (SIDE, SIDE, SIDE)

    begun = exchange(
        "exchange_start",
        0,
        program_start,
        dict(
            tokens=(tokens_b, ANY),
            small=(small_in, ANY),
            mamba=(mamba_in, ANY),
            back=(back_in, ANY),
            channel=(channel_in, ANY),
        ),
        dict(
            tokens_all=((2, SIDE, SIDE, half, width), low, ANY),
            small_all=(cube + small_in.shape, low, ANY),
            mamba_all=(cube + mamba_in.shape[2:], low, ANY),
            back_all=((SIDE,) + back_in.shape, low, ANY),
            channel_all=((SIDE,) + channel_in.shape, low, ANY),
        ),
        dict(mamba_mid=(mamba_in.shape, low)),
    )
    weights = exchange(
        "exchange_weights",
        1,
        program_weights,
        dict(whole=(attention_in, ANY)),
        dict(
            first=(cube + (32, third), low, ANY),
            second=(cube + (32, third), low, ANY),
            third=(cube + (32, last_third), low, ANY),
        ),
        cores=(0,),
    )
    weight_one, weight_two, weight_three = (
        part.reshape(64 * 32, -1) for part in (weights.first, weights.second, weights.third)
    )
    cotangent_part = lax.dynamic_slice_in_dim(cotangent_b, row_start, half, 0)
    cotangent_all = lax.all_gather(cotangent_part, "seq", axis=0, tiled=True)

    small = rows_of(begun.small_all, piece).astype(jnp.float32)
    gain_norm, gain_attn, gain_mamba, gain_feed = (small[:, i] for i in range(4))
    meta_f = small[:, 4 : 4 + metas].T
    channel = rows_of(begun.channel_all, inner_piece)
    weight_ssm = channel[:, :proj]
    conv_taps = channel[:, proj : proj + CONV].T.astype(jnp.float32)
    conv_offset, step_bias, skip_gain = (
        channel[:, proj + CONV + i].astype(jnp.float32) for i in range(3)
    )
    first_log = proj + CONV + 3
    log_decay = channel[:, first_log : first_log + states].T.astype(jnp.float32)
    weight_step = channel[:, first_log + states : first_log + states + rank]

    def on_core(which, work):
        shapes = jax.eval_shape(work)
        return lax.cond(core == which, work, lambda: blank(shapes))

    inputs_f = tokens_b.astype(jnp.float32)

    gain_row = gain_norm[None, :]
    normed_wide, query_b, keyval_b, meta_wide, meta_kv = on_core(
        0,
        lambda: attention_project(
            tokens_b, meta_f, gain_row, weight_one, weight_two, query_width, keys_width
        ),
    )
    keyval = exchange(
        "exchange_keyval",
        2,
        program_keyval,
        dict(keyval=(keyval_b, ANY), gate=(gate_in, ANY)),
        dict(
            keyval_all=((2, SIDE, SIDE, half, keys_width), low, ANY),
            gate_own=((SIDE, SIDE, 32, units), low, ANY),
        ),
        dict(gate_mid=((SIDE, SIDE, 32, units), low)),
        cores=(0,),
    )

    def mamba_first():
        normed_b = rms_norm(
            begun.tokens_all.reshape(group, width).astype(jnp.float32), gain_norm
        ).astype(low)
        weight_mamba = rows_of(begun.mamba_all.transpose(1, 2, 0, 3, 4), piece)
        mixed_in = places_first(matmul(normed_b, weight_mamba))
        conv_in = mixed_in[:, :inner].astype(low)
        inputs_b = conv_silu(
            conv_in.astype(jnp.float32), conv_taps, conv_offset, valid_rows
        ).astype(low)
        projected = contract(pad_to(weight_ssm, 1, proj_pad), inputs_b, 0, 1)
        projected = projected.reshape(proj_pad, SIDE, SIDE, rows).transpose(1, 2, 0, 3)
        return (
            normed_b,
            weight_mamba,
            conv_in,
            mixed_in[:, inner:],
            inputs_b,
            projected[:, :, :proj_cut],
            projected[:, :, proj_cut:],
        )

    normed_all, weight_mamba, conv_in, gate_z, inputs_b, proj_first, proj_second = on_core(
        1, mamba_first
    )

    def proj_pads(size):
        return dict(
            two_pad(size, rows, jnp.float32), sum=((size, rows), jnp.float32)
        )

    def spread_projection(name, number, first, second, gate):
        cuts = (proj_cut, proj_pad - proj_cut)
        results = exchange(
            name,
            number,
            program_project,
            dict(first=(first, ANY), second=(second, ANY), gate=(gate, ANY)),
            dict(
                first_all=((SIDE, SIDE, cuts[0], rows), jnp.float32, ANY),
                second_all=((SIDE, SIDE, cuts[1], rows), jnp.float32, ANY),
                gate_own=((SIDE, SIDE, 32, units), low, ANY),
            ),
            dict(
                first_pad=proj_pads(cuts[0]),
                second_pad=proj_pads(cuts[1]),
                gate_mid=((SIDE, SIDE, 32, units), low),
            ),
            vmem=32 * 2**20,
            cores=(1,),
        )
        return results

    def whole_projection(results):
        joined = jnp.concatenate([results.first_all, results.second_all], axis=2)
        return joined.transpose(2, 0, 1, 3).reshape(proj_pad, group)

    middle = spread_projection("exchange_project", 3, proj_first, proj_second, gate_in[1])
    keyval_all = keyval.keyval_all.reshape(2, 16, half, keys_width)

    my_starts = jnp.max(
        jnp.where(my_rows[:, None] >= start_rows[None, :], start_rows[None, :], 0), axis=1
    )
    bounds = jnp.stack([my_starts, my_rows], axis=1).astype(jnp.int32)
    key_blocks = (my_rows[-1:] // KEY_ROWS + 1).astype(jnp.int32)

    decay_rate = -jnp.exp(log_decay)
    scan_rate = pad_to(decay_rate * log2_e, 1, 2 * CHUNKS).T

    def blocked(lines):
        return jnp.stack([lines[:, :CHUNKS], pad_to(lines[:, CHUNKS:], 1, CHUNKS)])

    def unblocked(blocks):
        return jnp.concatenate([blocks[0], blocks[1][:, : inner - CHUNKS]], axis=1)

    attended, mass, attended_wide, attn_pre = on_core(
        0,
        lambda: attend_forward(
            key_blocks, query_b, keyval_all, meta_kv, bounds, weight_two, weight_three
        ),
    )

    def mamba_core():
        projected = whole_projection(middle)
        step_low = projected[:rank].astype(low)
        step_pre = contract(step_low, weight_step, 0, 1) + step_bias
        steps = jax.nn.softplus(step_pre)
        inputs_full = inputs_b.astype(jnp.float32)
        cols = projected[rank:proj].reshape(2 * states, CHUNKS, STEPS).transpose(0, 2, 1)
        scanned, starts, decay_t, drive_t = scan_forward(
            blocked(jnp.where(keep_rows[:, None], steps, far_away)),
            blocked(steps * inputs_full),
            cols,
            scan_rate,
            inner,
        )
        ssm_out = unblocked(scanned)
        mixed_y = halves_first(gate_mix(ssm_out, skip_gain, inputs_full, gate_z).astype(low))
        weight_back = rows_of(begun.back_all, inner_piece)
        return (
            matmul(mixed_y, weight_back).astype(low),
            step_low,
            step_pre,
            ssm_out,
            mixed_y,
            cols,
            starts,
            decay_t,
            drive_t,
        )

    partial, step_low, step_pre, ssm_out, mixed_y, cols, starts, decay_t, drive_t = on_core(
        1, mamba_core
    )

    mixers = exchange(
        "exchange_mixers",
        4,
        program_mixers,
        dict(
            partial=(partial.reshape(2, SIDE, SIDE, half, width), ANY),
            attn_pre=(attn_pre, ANY),
            gate_first=(keyval.gate_own, ANY),
            gate_second=(middle.gate_own, ANY),
            down=(down_in, ANY),
        ),
        dict(
            mamba_pre=((half, width), jnp.float32, VMEM),
            attn_half=((half, width), jnp.float32, ANY),
            gate_all=((2,) + cube + (32, units), low, ANY),
            down_all=((SIDE,) + down_in.shape, low, ANY),
        ),
        dict(pad=half_pad(half, width)),
        vmem=32 * 2**20,
    )
    weight_gate = mixers.gate_all.transpose(0, 2, 3, 1, 4, 5).reshape(2, 64, 32, units)
    weight_gate = weight_gate[:, :, :piece].reshape(2, width, units)
    weight_down = rows_of(mixers.down_all, down_piece)

    tokens_part = lax.dynamic_slice_in_dim(inputs_f, row_start, half, 0)
    sent = rms_norm(mixers.attn_half, gain_attn).astype(low).astype(jnp.float32)
    sent = sent + rms_norm(mixers.mamba_pre, gain_mamba).astype(low).astype(jnp.float32)
    hidden = tokens_part + 0.5 * sent
    feed = exchange(
        "exchange_feed",
        5,
        program_feed,
        dict(feed=(rms_norm(hidden, gain_feed).astype(low), ANY)),
        dict(feed_all=((SIDE, SIDE, half, width), low, ANY)),
    ).feed_all.reshape(16 * half, width)
    gate = matmul(feed, weight_gate[0])
    up = matmul(feed, weight_gate[1])
    active, pull_glu = jax.vjp(swiglu, gate, up)
    active_b = active.astype(low)
    out_partial = matmul(active_b, weight_down).astype(low)
    grad_gate, grad_up = pull_glu(matmul_nt(cotangent_all, weight_down))
    grad_gate, grad_up = grad_gate.astype(low), grad_up.astype(low)
    feed_partial = (matmul_nt(grad_gate, weight_gate[0]) + matmul_nt(grad_up, weight_gate[1])).astype(
        low
    )
    grad_down = matmul_tn(active_b, cotangent_all)
    grad_weight_gate = (matmul_tn(feed, grad_gate), matmul_tn(feed, grad_up))
    ffn = exchange(
        "exchange_ffn",
        6,
        program_ffn,
        dict(
            out=(out_partial.reshape(SIDE, SIDE, half, width), ANY),
            grad=(feed_partial.reshape(SIDE, SIDE, half, width), ANY),
        ),
        dict(
            out_sum=((half, width), jnp.float32, VMEM),
            grad_sum=((half, width), jnp.float32, VMEM),
        ),
        dict(out_pad=two_pad(half, width), grad_pad=two_pad(half, width)),
        vmem=48 * 2**20,
    )
    mixed_part = (hidden + ffn.out_sum).astype(low)
    cotangent_f = cotangent_part.astype(jnp.float32)
    _, pull_feed = jax.vjp(rms_norm, hidden, gain_feed)
    grad_hidden_norm, grad_gain_feed = pull_feed(ffn.grad_sum)
    grad_hidden = cotangent_f + grad_hidden_norm
    grad_sent = 0.5 * grad_hidden
    _, pull_attn = jax.vjp(rms_norm, mixers.attn_half, gain_attn)
    grad_attn_pre, grad_gain_attn = pull_attn(grad_sent)
    _, pull_mamba = jax.vjp(rms_norm, mixers.mamba_pre, gain_mamba)
    grad_mamba_pre, grad_gain_mamba = pull_mamba(grad_sent)

    g_gate = jnp.stack(grad_weight_gate).reshape(2, 16, SIDE, piece, units)
    g_gate = pad_to(g_gate.transpose(0, 2, 1, 3, 4), 3, 32).astype(low)
    g_down = pad_to(grad_down.reshape(SIDE, down_piece, width), 1, 96)
    g_down = g_down.reshape(SIDE, 2, 1, 48, width).transpose(1, 0, 2, 3, 4).astype(low)
    back = exchange(
        "exchange_back",
        7,
        program_back,
        dict(
            g_mamba=(grad_mamba_pre.astype(low), ANY),
            g_attn=(grad_attn_pre.astype(low), ANY),
            mixed=(mixed_part, ANY),
            g_hidden=(grad_hidden, ANY),
            g_gate=(g_gate, ANY),
            g_down=(g_down, ANY),
        ),
        dict(
            g_mamba_all=((2, SIDE, SIDE, half, width), low, ANY),
            g_attn_both=((2, half, width), low, ANY),
            mixed_both=((2, half, width), low, ANY),
            g_hidden_both=((2, half, width), jnp.float32, ANY),
            g_gate_sum=((16, 32, units), low, VMEM),
            g_down_sum=((1, 48, width), jnp.float32, VMEM),
        ),
        dict(gate_pad=shrink_pad(16, 32, units), down_pad=shrink_pad(1, 48, width)),
        vmem=32 * 2**20,
    )
    mixed = back.mixed_both.reshape(rows, width)
    grad_hidden_all = back.g_hidden_both.reshape(rows, width)
    g_gate_own = back.g_gate_sum.reshape(SIDE, SIDE, 32, units)

    cuts = (8 * LANES, 9 * LANES, query_most + width - 17 * LANES)

    def attention_back_one():
        g_pre = back.g_attn_both.reshape(rows, width)
        g_query, g_keyval, g_meta = attend_backward(
            key_blocks,
            query_b,
            keyval_all,
            meta_kv,
            bounds,
            attended,
            mass,
            g_pre,
            weight_two,
            weight_three,
        )
        pieces = attention_weights(
            normed_wide, attended_wide, g_query, g_pre, weight_one, weight_two, cuts
        )
        return [g_query, g_keyval, g_meta] + list(pieces)

    grad_query_b, grad_keyval, grad_meta_kv, sum_one, sum_two, sum_three, gain_query = on_core(
        0, attention_back_one
    )

    def cubed(blocks):
        return blocks.reshape(cube + (32, blocks.shape[-1]))

    attention = exchange(
        "exchange_attention",
        8,
        program_attention,
        dict(
            keyval=(grad_keyval.reshape(SIDE, SIDE, rows, keys_width), ANY),
            one=(cubed(sum_one), ANY),
            two=(cubed(sum_two), ANY),
            three=(cubed(sum_three), ANY),
            gate=(g_gate_own, ANY),
        ),
        dict(
            keyval_sum=((rows, keys_width), full, VMEM),
            sums=((32, query_most + width), full, VMEM),
            gate_own=((SIDE, SIDE, 32, units), low, ANY),
        ),
        dict(
            keyval_pad=two_pad(rows, keys_width),
            one_pad=three_pad(32, cuts[0]),
            two_pad=three_pad(32, cuts[1]),
            three_pad=three_pad(32, cuts[2]),
            one_sum=((32, cuts[0]), full),
            two_sum=((32, cuts[1]), full),
            three_sum=((32, cuts[2]), full),
            gate_mid=((SIDE, SIDE, 32, units), low),
        ),
        vmem=60 * 2**20,
        cores=(0,),
    )

    keys_one, keys_two, meta_out, grad_normed_attn, gain_keys, gain_meta = on_core(
        0,
        lambda: attention_inputs(
            attention.keyval_sum,
            grad_query_b,
            normed_wide,
            meta_wide,
            grad_meta_kv,
            weight_one,
            weight_two,
            meta_f,
            gain_row,
        ),
    )
    gain_attention = (gain_query + gain_keys).reshape(64, 32)[:, :piece].reshape(width)
    gain_attention = gain_attention / gain_norm + gain_meta[0]
    keys = exchange(
        "exchange_keys",
        9,
        program_keys,
        dict(
            one=(cubed(keys_one), ANY),
            two=(cubed(keys_two), ANY),
            three=(cubed(meta_out), ANY),
        ),
        dict(
            one_sum=((32, keys_width // 2), full, VMEM),
            two_sum=((32, keys_width // 2), full, VMEM),
            three_sum=((32, metas), full, VMEM),
        ),
        dict(
            one_pad=three_pad(32, keys_width // 2),
            two_pad=three_pad(32, keys_width // 2),
            three_pad=three_pad(32, metas),
        ),
        vmem=32 * 2**20,
        cores=(0,),
    )

    def mamba_back_one():
        grad_pre_b = back.g_mamba_all.reshape(group, width)
        grad_weight_back = matmul_tn(mixed_y, grad_pre_b)
        weight_back = rows_of(begun.back_all, inner_piece)
        grad_mixed = places_first(matmul_nt(grad_pre_b, weight_back))
        inputs_full = inputs_b.astype(jnp.float32)
        _, pull_gate = jax.vjp(gate_mix, ssm_out, skip_gain, inputs_full, gate_z)
        grad_ssm, grad_skip, grad_inputs, grad_gate_z = pull_gate(grad_mixed)
        steps = jax.nn.softplus(step_pre)
        grad_decay, grad_drive, grad_cols, grad_rate = scan_backward(
            decay_t, drive_t, cols, scan_rate, starts, blocked(grad_ssm), inner
        )
        grad_drive = unblocked(grad_drive)
        grad_steps = unblocked(grad_decay) * (1.0 / log2_e) + grad_drive * inputs_full
        grad_inputs = grad_inputs + grad_drive * steps
        grad_step_pre = grad_steps * jax.nn.sigmoid(step_pre)
        grad_step_b = grad_step_pre.astype(low)
        grad_step_low = contract(weight_step, grad_step_b, 0, 1)
        grad_cols = grad_cols.transpose(0, 2, 1).reshape(2 * states, group)
        grad_proj = pad_to(jnp.concatenate([grad_step_low, grad_cols], axis=0), 0, proj_pad)
        grad_proj = grad_proj.reshape(proj_pad, SIDE, SIDE, rows).transpose(1, 2, 0, 3)
        return (
            grad_proj[:, :, :proj_cut],
            grad_proj[:, :, proj_cut:],
            padded_blocks(grad_weight_back, SIDE, 64)[:, None],
            grad_inputs,
            grad_gate_z.astype(low),
            grad_skip,
            jnp.sum(grad_step_pre, axis=0),
            grad_rate[:inner] * decay_rate.T,
            contract(grad_step_b, step_low, 0, 1),
        )

    (
        proj_first,
        proj_second,
        back_out,
        grad_inputs,
        grad_gate_z,
        grad_skip,
        grad_step_bias,
        grad_log_decay,
        grad_weight_step,
    ) = on_core(1, mamba_back_one)
    last = spread_projection("exchange_last", 10, proj_first, proj_second, g_gate_own)

    def mamba_back_two():
        grad_proj_b = whole_projection(last)[:proj].astype(low)
        grad_weight_ssm = contract(inputs_b, grad_proj_b, 0, 1)
        grad_inputs_all = grad_inputs + contract(grad_proj_b, weight_ssm, 0, 1)

        def conv_only(conv_arg, taps_arg, offset_arg):
            return conv_silu(conv_arg, taps_arg, offset_arg, valid_rows)

        _, pull_conv = jax.vjp(conv_only, conv_in.astype(full), conv_taps, conv_offset)
        grad_conv, grad_taps, grad_offset = pull_conv(grad_inputs_all)
        grad_mixed_in = halves_first(jnp.concatenate([grad_conv.astype(low), grad_gate_z], axis=1))
        grad_weight_mamba = matmul_tn(normed_all, grad_mixed_in)
        grad_normed = matmul_nt(grad_mixed_in, weight_mamba).astype(low)
        channel_out = jnp.concatenate(
            [
                grad_weight_ssm,
                grad_taps.T,
                jnp.stack([grad_offset, grad_step_bias, grad_skip], axis=1),
                grad_log_decay,
                grad_weight_step,
            ],
            axis=1,
        )
        mamba_out = grad_weight_mamba.reshape(16, SIDE, piece, 2 * inner).transpose(1, 0, 2, 3)
        return (
            grad_normed,
            pad_to(mamba_out, 2, 32).astype(low),
            pad_to(padded_blocks(channel_out, SIDE, 64, full), 2, 256)[:, None],
            jnp.sum(grad_weight_mamba * weight_mamba.astype(full), axis=1) / gain_norm,
        )

    grad_normed_partial, mamba_out, channel_out, gain_mixer = on_core(1, mamba_back_two)
    grad_gain_norm = jnp.where(on_attention, gain_attention, gain_mixer)
    gains_out = jnp.stack([grad_gain_norm, grad_gain_attn, grad_gain_mamba, grad_gain_feed], axis=1)
    gains_out = padded_blocks(pad_to(gains_out, 1, 128), 64, 32)
    ended = exchange(
        "exchange_end",
        11,
        program_end,
        dict(
            partial=(grad_normed_partial.reshape(2, SIDE, SIDE, half, width), ANY),
            g_attn=(grad_normed_attn, ANY),
            sums_in=(attention.sums, ANY),
            keys=(jnp.concatenate([keys.one_sum, keys.two_sum, keys.three_sum], axis=1), ANY),
            gate=(jnp.where(on_attention, attention.gate_own, last.gate_own), ANY),
            down=(back.g_down_sum.reshape(48, width), ANY),
            mamba=(mamba_out, ANY),
            back=(back_out, ANY),
            channel=(channel_out, ANY),
            gains=(gains_out.reshape(cube + (32, 128)), ANY),
        ),
        dict(
            normed_both=((2, half, width), full, ANY),
            g_attn_both=((rows, width), full, ANY),
            sums=((32, query_most + width), full, ANY),
            keys_sum=((32, keys_width + metas), full, ANY),
            gate_both=((2, SIDE, SIDE, 32, units), low, ANY),
            down_both=((2, 48, width), full, ANY),
            mamba_sum=((SIDE, SIDE, 32, 2 * inner), low, ANY),
            back_sum=((1, 64, width), full, VMEM),
            channel_sum=((1, 64, 256), full, VMEM),
            gains_both=((2, 32, 128), full, ANY),
        ),
        dict(
            normed_pad=half_pad(half, width),
            normed_sum=((half, width), full),
            gains_pad=three_pad(32, 128),
            gains_sum=((32, 128), full),
            mamba_pad=x_pad(16, 32, 2 * inner),
            mamba_part=((SIDE, SIDE, 32, 2 * inner), low),
            mamba_mid=((SIDE, SIDE, 32, 2 * inner), low),
            back_pad=x_pad(1, 64, width),
            channel_pad=x_pad(1, 64, 256, full),
        ),
        vmem=48 * 2**20,
    )
    grad_normed = ended.normed_both.reshape(rows, width) + ended.g_attn_both
    _, pull_input = jax.vjp(lambda rows_in: rms_norm(rows_in, gain_norm), inputs_f)
    input_grad = grad_hidden_all + pull_input(grad_normed)[0]
    gains_sum = (ended.gains_both[0] + ended.gains_both[1])[:piece]
    keys_sum = ended.keys_sum[:piece]
    grad_keys = keys_sum[:, :keys_width].reshape(piece, -1, 2, HEAD).transpose(0, 2, 1, 3)
    grad_keys = grad_keys.reshape(piece, keys_width)
    grad_mamba_in = ended.mamba_sum.reshape(16, 32, 2, inner)[:, :piece]
    grad_mamba_in = grad_mamba_in.transpose(1, 2, 0, 3).reshape(piece, 2 * 16 * inner)
    grad_gate_up = ended.gate_both.reshape(2, 16, 32, units)[:, :, :piece]
    grad_gate_up = grad_gate_up.transpose(2, 0, 1, 3).reshape(piece, 2 * 16 * units)
    channel_sum = ended.channel_sum[0, :inner_piece]
    return (
        mixed[None],
        input_grad[None],
        gains_sum[:, 0],
        keys_sum[:, keys_width:].T,
        ended.sums[:piece, :query_width],
        grad_keys,
        ended.sums[:piece, query_most:],
        gains_sum[:, 1],
        grad_mamba_in.astype(full),
        channel_sum[:, proj : proj + CONV].T,
        channel_sum[:, proj + CONV],
        channel_sum[:, :proj],
        channel_sum[:, first_log + states : first_log + states + rank].T,
        channel_sum[:, proj + CONV + 1],
        channel_sum[:, first_log : first_log + states].T,
        channel_sum[:, proj + CONV + 2],
        ended.back_sum[0, :inner_piece],
        gains_sum[:, 2],
        gains_sum[:, 3],
        grad_gate_up.astype(full),
        ended.down_both.reshape(96, width)[:down_piece],
    )


def solution(mesh):
    spread = ("seq", "fsdp")
    rows = P("fsdp", "seq", None)
    flat, first, second = P(spread), P(spread, None), P(None, spread)
    weights = (
        flat,
        second,
        first,
        first,
        first,
        flat,
        first,
        second,
        flat,
        first,
        second,
        flat,
        second,
        flat,
        first,
        flat,
        flat,
        first,
        first,
    )
    return jax.shard_map(
        shards,
        mesh=mesh,
        in_specs=(rows, P("fsdp", None)) + weights + (rows,),
        out_specs=(rows, rows) + weights,
        check_vma=False,
    )
```

time: 5850 us -> 819 us (0.14)
  blocking collectives: 2790 us -> 0 us
  other arithmetic: 1050 us -> 62.9 us
  local copies, waits for them, and re-layouts: 910 us -> 179 us
  waiting for transfers between devices: 538 us -> 0.02 us
  Pallas kernels: 0 us -> 456 us
  starting transfers between devices: 301 us -> 0.04 us
  matrix products: 180 us -> 83.8 us
    unnamed x4 -> x0, blocking collectives: 2030 us -> none
    all_gather x5 -> x0, blocking collectives: 766 us -> none  [the longest x1 168 us: shards(): lax.all_gather(masters_b[9], ('seq', 'fsdp'), axis=0, tiled=True)]
    reduce_sum x169 -> x1, other arithmetic: 525 us -> 4.34 us  [mamba_back_one(): jnp.sum(grad_step_pre, axis=0)]
    pallas_call x0 -> x18, Pallas kernels: none -> 456 us  [the longest x12 379 us: exchange(): pl.pallas_call(kernel, out_shape=[jax.ShapeDtypeStruct(s, d) for s, d, _...]
    unnamed x22 -> x0, starting transfers between devices: 286 us -> none
    unnamed x35 -> x1, waiting for transfers between devices: 284 us -> 0.02 us
    unnamed x235 -> x204, local copies, waits for them, and re-layouts: 296 us -> 23.2 us
    all_gather x11 -> x1, waiting for transfers between devices: 225 us -> 0.01 us  [shards(): cotangent_all = lax.all_gather(cotangent_part, 'seq', axis=0, tiled=True)]
  transfers between devices with their start and end apart: 44 -> 1, of which waited for: 8 -> 0; matrix products, arithmetic and copies ran while one was open for 59% -> 15% of each run, Pallas kernels for 0% -> 27%
where the time goes in v1:
time: 819 us; the launch traced here: 809 us
  Pallas kernels  456 us (56%)
  local copies, waits for them, and re-layouts  179 us (22%)
  matrix products  83.8 us (10%)
  other arithmetic  62.9 us (8%)
  between operations  18.5 us (2%)
  loops' own time  8.34 us (1%)
    pallas_call x12, Pallas kernels, exchange(): pl.pallas_call(kernel, out_shape=[jax.ShapeDtypeStruct(s, d) for s, d, _...  379 us
    dot_general x21, matrix products, contract(): lax.dot_general(left, right, (((left_dim,), (right_dim,)), ((), ())), **o...  83.8 us
    pallas_call x1, Pallas kernels, scan_backward(): pl.pallas_call(functools.partial(scan_backward_kernel, used), out_shape=[...  49.5 us
    pallas_call x1, Pallas kernels, scan_forward(): pl.pallas_call(functools.partial(scan_forward_kernel, used), out_shape=[j...  27.2 us
    another operation x21, local copies, waits for them, and re-layouts  24.3 us
    cond x49, local copies, waits for them, and re-layouts  24 us
    unnamed x204, local copies, waits for them, and re-layouts  23.2 us
  transfers between devices with their start and end apart: 1, of which 0 were waited for; matrix products, arithmetic and copies ran while one was open for 15% of the time, Pallas kernels for 27%

profile of v1, /device:TPU:1, one launch (start us, length us, event | category | flops | bytes accessed | tf_op | source)
XLA Modules:
  0.0 808.5 jit_solution(361530616652988481)
XLA Ops:
  16.7 55.0 %exchange_start.1 = (bf16[2,4,4,64,1600]{4,3,2,1,0:T(8,128)(2,1)}, bf16[4,4,4,32,256]{4,3,2,1,0:T(8,128)(2,1)}, bf16[4,4,4,32,400]{4,3,2,1,0:T(8,128)(2,1)}, bf1...) custom-call(bf16[128,1600]{1,0:T(8,128)(2,1)S(1)} %bitcast.327, bf16[32,256]{1,0:T(8,128)(2,1)} %pad.223.refs_1_, ...), custom_call_target="tpu_custom_call" | custom-call | tf_op jit(solution)/shard_map/exchange_start/pallas_call | solution.py:314
  93.1 37.1 %conditional.8 = ((bf16[2048,1600]{1,0:T(8,128)(2,1)}, bf16[1600,400]{1,0:T(8,128)(2,1)}, bf16[2048,200]{1,0:T(8,128)(2,1)}, f32[2048,200]{1,0:T(8,128)}, bf16[2...) conditional(s32[]{:T(128)} %convert_element_type.304, () %tuple.104, ...), branch_computations={%region_5.6_spmd, %region_6.8_spmd} | conditional | flops 2775861248 | bytes 80628800 | solution.py:1752
  93.5 4.4 multiply_reduce_fusion.5
  98.0 7.6 fusion.25
  107.6 4.6 multiply_convert_fusion
  112.2 5.4 convolution_bitcast_fusion.4
  122.5 3.7 multiply_convert_fusion.1
  131.2 26.2 %exchange_project.1 = (f32[4,4,72,128]{3,2,1,0:T(8,128)}, f32[4,4,64,128]{3,2,1,0:T(8,128)S(1)}, bf16[4,4,32,344]{3,2,1,0:T(8,128)(2,1)S(1)}) custom-call(f32[4,4,72,128]{3,2,1,0:T(8,128)} %get-tuple-element.1575.refs_0_, f32[4,4,64,128]{3,2,1,0:T(8,128)S(1)} %get-tuple-element.1576.refs_1_, bf16[4,4,32,344]{3,2,1,0:T(8,128)(2,1)S(1)} %bitcast.308), custom_call_target="tpu_custom_call" | custom-call | tf_op jit(solution)/shard_map/exchange_project/pallas_call | solution.py:314
  158.2 64.2 %conditional.9 = (bf16[100,2048]{0,1:T(8,128)(2,1)S(1)}, f32[2048,200]{1,0:T(8,128)}, f32[2048,200]{1,0:T(8,128)}, bf16[2048,200]{1,0:T(8,128)(2,1)}, f32[32,16,...) conditional(s32[]{:T(128)} %convert_element_type.304, ...), branch_computations={%region_8.9_spmd, %region_9.11_spmd} | conditional | flops 1405448448 | bytes 91970632 | solution.py:1752
  162.3 3.8 convert_multiply_fusion.1
  173.8 27.2 %scan_forward.2 = (f32[2,2048,128]{2,1,0:T(8,128)S(1)}, f32[16,256,128]{2,1,0:T(8,128)}, f32[16,256,128]{2,1,0:T(8,128)}, f32[16,256,128]{2,1,0:T(8,128)}) custom-call(f32[2,2048,128]{2,1,0:T(8,128)S(1)} %pad_maximum_fusion.decay_ref, f32[2,2048,128]{2,1,0:T(8,128)S(1)} %copy-done.2, f32[32,16,128]{2,1,0:T(8,128)S(1)} %bitcast.372, f32[256,16]{1,0:T(8,128)S(1)} %copy.575.rate_ref), custom_call_target="tpu_custom_call" | custom-call | tf_op jit(solution)/shard_map/cond/branch_1_fun/scan_forward/pallas_call | solution.py:448
  201.1 3.9 fusion.2
  206.9 5.8 convolution_convert_fusion
  212.8 9.7 %copy.631 = bf16[2048,1600]{1,0:T(8,128)(2,1)} copy(bf16[2048,1600]{0,1:T(8,128)(2,1)} %convolution_convert_fusion) | data formatting | bytes 13107200 | tf_op jit(solution)/shard_map/cond
  230.2 72.0 %exchange_mixers.1 = (f32[64,1600]{1,0:T(8,128)S(1)}, f32[64,1600]{1,0:T(8,128)S(1)}, bf16[2,4,4,4,32,344]{5,4,3,2,1,0:T(8,128)(2,1)S(1)}, bf16[4,96,1600]{2,1,0:T(8,128)(2,1)S(1)}) custom-call(bf16[2,4,4,64,1600]{4,3,2,1,0:T(8,128)(2,1)} %bitcast.342, f32[128,1600]{1,0:T(8,128)} %get-tuple-element.526.refs_1_, bf16[4,4,32,344]{3,2,1,0:T(8,128)(2,1)S(1)} %copy-done.25, ...), custom_call_target="tpu_custom_call" | custom-call | tf_op jit(solution)/shard_map/exchange_mixers/pallas_call | solution.py:314
  304.9 29.9 %exchange_feed.1 = bf16[4,4,64,1600]{3,2,1,0:T(8,128)(2,1)} custom-call(bf16[64,1600]{1,0:T(8,128)(2,1)} %multiply_convert_fusion.4.refs_0_), custom_call_target="tpu_custom_call" | custom-call | tf_op jit(solution)/shard_map/exchange_feed/pallas_call | solution.py:314
  336.9 3.4 squeeze.83
  343.5 5.5 copy.583
  349.0 5.1 reshape.506
  354.1 4.0 fusion.91
  360.6 6.2 multiply_convert_fusion.2
  367.7 3.6 convolution_convert_fusion.3
  371.3 4.8 copy.581
  376.1 3.5 fusion.93
  379.7 3.6 fusion.59
  383.2 3.6 fusion.56
  386.8 3.8 add_convert_fusion
  390.6 5.4 copy.582
  396.0 56.2 %exchange_ffn.1 = (f32[64,1600]{1,0:T(8,128)S(1)}, f32[64,1600]{1,0:T(8,128)S(1)}) custom-call(bf16[4,4,64,1600]{3,2,1,0:T(8,128)(2,1)S(1)} %bitcast.304, bf16[4,4,64,1600]{3,2,1,0:T(8,128)(2,1)} %bitcast.332), custom_call_target="tpu_custom_call" | custom-call | tf_op jit(solution)/shard_map/exchange_ffn/pallas_call | solution.py:314
  465.7 45.1 %exchange_back.1 = (bf16[2,4,4,64,1600]{4,3,2,1,0:T(8,128)(2,1)}, bf16[2,64,1600]{2,1,0:T(8,128)(2,1)}, bf16[2,64,1600]{2,1,0:T(8,128)(2,1)S(1)}, f32[2,64,1600]...) custom-call(bf16[64,1600]{1,0:T(8,128)(2,1)S(1)} %get-tuple-element.1674.refs_0_, ...), custom_call_target="tpu_custom_call" | custom-call | tf_op jit(solution)/shard_map/exchange_back/pallas_call | solution.py:314
  514.3 3.1 exchange_attention.1
  517.5 4.9 conditional.15
  524.7 89.2 %conditional.12 = (bf16[4,1,64,1600]{3,2,0,1:T(8,128)(2,1)}, f32[2048,200]{1,0:T(8,128)}, bf16[2048,200]{1,0:T(8,128)(2,1)}, f32[200]{0:T(256)S(1)}, f32[200]{0:...) conditional(s32[]{:T(128)} %convert_element_type.304, ...), branch_computations={%region_22.23_spmd, %region_23.26_spmd} | conditional | flops 2803215360 | bytes 105838584 | solution.py:1752
  527.4 5.1 convolution_convert_fusion.1
  535.0 5.0 convolution_bitcast_fusion.1
  541.6 4.3 fusion.8
  549.1 49.5 %scan_backward.1 = (f32[2,2048,128]{2,1,0:T(8,128)S(1)}, f32[2,2048,128]{2,1,0:T(8,128)S(1)}, f32[32,16,128]{2,1,0:T(8,128)S(1)}, f32[256,16]{1,0:T(8,128)S(1)}) custom-call(f32[16,256,128]{2,1,0:T(8,128)S(1)} %copy-done.60, f32[16,256,128]{2,1,0:T(8,128)} %get-tuple-element.313.drive_t, f32[32,16,128]{2,1,0:T(8,128)S(1)} %get-tuple-element.314.cols_ref, ...), custom_call_target="tpu_custom_call" | custom-call | tf_op jit(solution)/shard_map/cond/branch_1_fun/scan_backward/pallas_call | solution.py:557
  600.3 4.3 fusion.82
  614.7 30.7 %exchange_last.1 = (f32[4,4,72,128]{3,2,1,0:T(8,128)}, f32[4,4,64,128]{3,2,1,0:T(8,128)}, bf16[4,4,32,344]{3,2,1,0:T(8,128)(2,1)S(1)}) custom-call(f32[4,4,72,128]{3,2,1,0:T(8,128)} %get-tuple-element.1578.refs_0_, f32[4,4,64,128]{3,2,1,0:T(8,128)} %copy-done.75, bf16[4,4,32,344]{3,2,1,0:T(8,128)(2,1)S(1)} %bitcast.310), custom_call_target="tpu_custom_call" | custom-call | tf_op jit(solution)/shard_map/exchange_last/pallas_call | solution.py:314
  645.5 67.9 %conditional.13 = (f32[1600]{0:T(1024)S(1)}, bf16[2048,1600]{1,0:T(8,128)(2,1)}, bf16[4,16,32,400]{3,2,1,0:T(8,128)(2,1)S(1)}, f32[4,1,64,256]{3,2,1,0:T(8,128)}) conditional(s32[]{:T(128)} %convert_element_type.304, () %tuple.111, (f32[4,200]{0,1:T(8,128)}, f32[4,4,72,128]{3,2,1,0:T(8,128)}, f32[4,4,64,128]{3,2,1,0:T(8,128)}, ...), branch_computations={%region_26.27_spmd, %region_27.34_spmd} | conditional | flops 5486155264 | bytes 104915736 | solution.py:1752
  645.6 3.5 copy.600
  654.4 2.9 copy.596
  661.7 8.2 %multiply_reduce_fusion.4 = (f32[200]{0:T(256)S(1)}, f32[200]{0:T(256)S(1)}, f32[200]{0:T(256)S(1)}, f32[200]{0:T(256)S(1)}, f32[200]{0:T(256)S(1)}, /*index=5*/...) fusion(f32[2048,200]{0,1:T(8,128)} %convert_element_type.250, ...), kind=kOutput, calls=%fused_computation.80 | convolution fusion | flops 123288600 | bytes 11275648 | tf_op jit(solution)/shard_map/cond/branch_1_fun/dot_general | solution.py:1069
  676.8 6.2 fusion.86
  683.0 7.0 convolution_convert_fusion.2
  689.9 9.6 %copy.637 = bf16[2048,1600]{1,0:T(8,128)(2,1)} copy(bf16[2048,1600]{0,1:T(8,128)(2,1)} %convolution_convert_fusion.2) | data formatting | bytes 13107200 | tf_op jit(solution)/shard_map/cond | solution.py:1752
  701.8 3.1 reshape.445
  719.5 53.6 %exchange_end.1 = (f32[2,64,1600]{2,1,0:T(8,128)S(1)}, f32[128,1600]{1,0:T(8,128)}, f32[32,3264]{1,0:T(8,128)S(1)}, f32[32,768]{1,0:T(8,128)S(1)}, bf16[2,4,4,32...) custom-call(bf16[2,4,4,64,1600]{4,3,2,1,0:T(8,128)(2,1)} %bitcast.34, ...), custom_call_target="tpu_custom_call" | custom-call | tf_op jit(solution)/shard_map/exchange_end/pallas_call | solution.py:314
  (505 shorter events, 173.8 us)
Async XLA Ops:
  7.2 3.6 copy-start.113
  7.2 3.7 copy-start.114
  7.2 3.8 copy-start.100
  7.3 3.8 copy-start.72
  7.3 353.4 %all-gather.3.cloned.1.call-start = ((), (), s32[]{:S(2)}) async-start(), calls=%async_computation | async-start | bytes 3620864 | tf_op jit(solution)/shard_map/all_gather | solution.py:1735
  10.6 214.7 %copy-start.32 = (bf16[1,128,1600]{2,1,0:T(8,128)(2,1)}, bf16[1,128,1600]{2,1,0:T(8,128)(2,1)S(1)}, u32[]{:S(2)}) copy-start(bf16[1,128,1600]{2,1,0:T(8,128)(2,1)S(1)} %copy.554) | copy-start | bytes 1228804
  11.2 3.6 copy-start.103
  11.2 3.7 copy-start.96
  78.1 7.4 copy-start.81
  78.7 79.5 %copy-start.50 = (bf16[200,256]{1,0:T(8,128)(2,1)}, bf16[200,256]{1,0:T(8,128)(2,1)S(1)}, u32[]{:S(2)}) copy-start(bf16[200,256]{1,0:T(8,128)(2,1)S(1)} %reshape.492) | copy-start | bytes 307204
  78.8 79.4 %copy-start.76 = (bf16[200,100]{1,0:T(8,128)(2,1)}, bf16[200,100]{1,0:T(8,128)(2,1)S(1)}, u32[]{:S(2)}) copy-start(bf16[200,100]{1,0:T(8,128)(2,1)S(1)} %slice.371) | copy-start | bytes 120004
  84.1 8.9 %copy-start.36 = (bf16[25,2,16,344]{3,0,2,1:T(8,128)(2,1)}, bf16[25,2,16,344]{3,0,2,1:T(8,128)(2,1)S(1)}, u32[]{:S(2)}) copy-start(bf16[25,2,16,344]{3,0,2,1:T(8,128)(2,1)S(1)} %copy.667) | copy-start | bytes 1651204
  85.6 139.7 %copy-start.93 = (f32[1,1600]{1,0:T(1,128)}, f32[1,1600]{1,0:T(1,128)S(1)}, u32[]{:S(2)}) copy-start(f32[1,1600]{1,0:T(1,128)S(1)} %broadcast_in_dim_squeeze.3) | copy-start | bytes 19204
  85.6 7.4 copy-start.49
  91.7 66.5 %copy-start.101 = (f32[200]{0:T(256)}, f32[200]{0:T(256)S(1)}, u32[]{:S(2)}) copy-start(f32[200]{0:T(256)S(1)} %get-tuple-element.1609) | copy-start | bytes 2404
  98.0 7.6 copy-start.56
  162.0 4.0 copy-start.43
  172.1 28.9 %copy-start.69 = (f32[32,128,16]{1,2,0:T(8,128)}, f32[32,128,16]{1,2,0:T(8,128)S(1)}, u32[]{:S(2)}) copy-start(f32[32,128,16]{1,2,0:T(8,128)S(1)} %copy.531) | copy-start | bytes 786436 | tf_op jit(solution)/shard_map/cond
  212.8 9.7 %copy-start.44 = (bf16[100,4,4,128]{0,3,2,1:T(8,128)(2,1)S(1)}, bf16[100,4,4,128]{0,3,2,1:T(8,128)(2,1)}, u32[]{:S(2)}) copy-start(bf16[100,4,4,128]{0,3,2,1:T(8,128)(2,1)} %copy-done.43) | copy-start | bytes 1228804 | tf_op jit(solution)/shard_map/cond
  230.2 72.3 %copy-start.33 = (bf16[1,128,1600]{2,1,0:T(8,128)(2,1)S(1)}, bf16[1,128,1600]{2,1,0:T(8,128)(2,1)}, u32[]{:S(2)}) copy-start(bf16[1,128,1600]{2,1,0:T(8,128)(2,1)} %copy-done.32) | copy-start | bytes 1228804
  349.0 5.1 copy-start.35
  354.1 4.0 copy-start.41
  360.6 7.1 copy-start.68
  396.0 56.2 %copy-start.38 = (f32[64,1600]{1,0:T(8,128)S(1)}, f32[64,1600]{1,0:T(8,128)}, u32[]{:S(2)}) copy-start(f32[64,1600]{1,0:T(8,128)} %copy-done.37) | copy-start | bytes 1228804
  396.0 56.4 %copy-start.4 = (f32[64,1600]{1,0:T(8,128)S(1)}, f32[64,1600]{1,0:T(8,128)}, u32[]{:S(2)}) copy-start(f32[64,1600]{1,0:T(8,128)} %copy-done.3) | copy-start | bytes 1228804
  396.0 56.4 %copy-start.7 = (f32[64,1600]{1,0:T(8,128)S(1)}, f32[64,1600]{1,0:T(8,128)}, u32[]{:S(2)}) copy-start(f32[64,1600]{1,0:T(8,128)} %copy-done.6) | copy-start | bytes 1228804
  396.0 56.4 %copy-start.63 = (bf16[1,64,1600]{2,1,0:T(8,128)(2,1)S(1)}, bf16[1,64,1600]{2,1,0:T(8,128)(2,1)}, u32[]{:S(2)}) copy-start(bf16[1,64,1600]{2,1,0:T(8,128)(2,1)} %copy.643) | copy-start | bytes 614404
  524.7 90.0 %copy-start.11 = (bf16[16,32,344]{2,1,0:T(8,128)(2,1)S(1)}, bf16[16,32,344]{2,1,0:T(8,128)(2,1)}, u32[]{:S(2)}) copy-start(bf16[16,32,344]{2,1,0:T(8,128)(2,1)} %copy-done.10) | copy-start | bytes 1056772
  524.7 120.8 %copy-start.51 = (bf16[200,256]{1,0:T(8,128)(2,1)S(1)}, bf16[200,256]{1,0:T(8,128)(2,1)}, u32[]{:S(2)}) copy-start(bf16[200,256]{1,0:T(8,128)(2,1)} %copy-done.50) | copy-start | bytes 307204
  524.7 120.8 %copy-start.82 = (f32[1600]{0:T(1024)S(1)}, f32[1600]{0:T(1024)}, u32[]{:S(2)}) copy-start(f32[1600]{0:T(1024)} %copy-done.81) | copy-start | bytes 19204
  613.9 31.5 %copy-start.106 = (f32[200]{0:T(256)}, f32[200]{0:T(256)S(1)}, u32[]{:S(2)}) copy-start(f32[200]{0:T(256)S(1)} %get-tuple-element.556) | copy-start | bytes 2404
  645.5 68.0 %copy-start.104 = (f32[1,1600]{1,0:T(1,128)S(1)}, f32[1,1600]{1,0:T(1,128)}, u32[]{:S(2)}) copy-start(f32[1,1600]{1,0:T(1,128)} %get-tuple-element.1587) | copy-start | bytes 19204
  645.5 68.0 %copy-start.97 = (bf16[1600,1]{0,1:T(2,128)(2,1)S(1)}, bf16[1600,1]{0,1:T(2,128)(2,1)}, u32[]{:S(2)}) copy-start(bf16[1600,1]{0,1:T(2,128)(2,1)} %stack.107) | copy-start | bytes 9604
  645.5 68.0 %copy-start.98 = (bf16[1600,1]{0,1:T(2,128)(2,1)S(1)}, bf16[1600,1]{0,1:T(2,128)(2,1)}, u32[]{:S(2)}) copy-start(bf16[1600,1]{0,1:T(2,128)(2,1)} %stack.106) | copy-start | bytes 9604
  645.5 68.0 %copy-start.99 = (bf16[1600,1]{0,1:T(2,128)(2,1)S(1)}, bf16[1600,1]{0,1:T(2,128)(2,1)}, u32[]{:S(2)}) copy-start(bf16[1600,1]{0,1:T(2,128)(2,1)} %stack.105) | copy-start | bytes 9604
  645.5 5.0 copy-start.88
  645.6 5.0 copy-start.90
  645.6 5.0 copy-start.108
  654.4 4.3 copy-start.74
  661.7 8.2 %copy-start.53 = (bf16[132,2048]{1,0:T(8,128)(2,1)}, bf16[132,2048]{1,0:T(8,128)(2,1)S(1)}, u32[]{:S(2)}) copy-start(bf16[132,2048]{1,0:T(8,128)(2,1)S(1)} %convert_element_type.249) | copy-start | bytes 1622020 | tf_op jit(solution)/shard_map/cond
  719.5 60.6 %copy-start.19 = (bf16[2,64,1600]{2,1,0:T(8,128)(2,1)S(1)}, bf16[2,64,1600]{2,1,0:T(8,128)(2,1)}, u32[]{:S(2)}) copy-start(bf16[2,64,1600]{2,1,0:T(8,128)(2,1)} %copy-done.18) | copy-start | bytes 1228804
  776.0 6.7 copy-start.15
  782.8 5.1 copy-start.21
  784.0 4.7 copy-start.80
  784.0 5.6 copy-start.17
  790.7 5.0 copy-start.87
  790.7 5.7 copy-start.86
  790.7 6.3 copy-start.27
  (73 other events, 152.8 us)
Sparse Core Ops, SparseCore 0:
  10.9 60.0 all-gather.2

commit v2 on v1

--- a/solution.py
+++ b/solution.py
@@ -71,12 +71,15 @@
     return tuple(fixed.get(axis, slice(None)) for axis in axes)
 
 
-def gather(net, name, source, out, axes, order):
+def gather(net, name, source, out, axes, order, hold=0):
     at = net.at
     fixed = {axis: at[axis] for axis in axes}
     own = net.local((name, -1), source, out.at[pick(axes, fixed)])
     here = source
     for axis in order:
+        if axis == order[-1]:
+            for _ in range(hold):
+                yield
         place = pick(axes, fixed)
         copies = [
             net.start(
@@ -99,7 +102,6 @@
 def gather_two(net, name, source, out, order, after=None, patience=0):
     at = net.at
     first, second = order
-    axes = (Y, Z)
 
     def place(back):
         spot = dict(at)
@@ -145,6 +147,9 @@
         after((at[second] - hop + SIDE) % SIDE)
 
 
+NEAR = (1, 3)
+
+
 def scatter_sum(total, rows, own, others, out):
     chunk = 16 if rows % 16 == 0 else 8
     per = rows // chunk
@@ -218,6 +223,99 @@
         lambda lead, part: kept[spot, part, :],
         [lambda lead, part, k=k: one[k, spot, part, :] for k in range(3)]
         + [lambda lead, part, k=k: two[k, part, :] for k in range(3)],
+        put_out,
+    )
+
+
+def reduce_ring(net, name, source, pad, out, order):
+    at = net.at
+    rows = source.shape[2]
+    half = rows // 2
+    halves = {1: pl.ds(0, half), 3: pl.ds(half, half)}
+    stages = (
+        (order[0], pad.one, pad.via_one, pad.mix_one),
+        (order[1], pad.two, pad.via_two, pad.mix_two),
+    )
+
+    def lines(stage, place, part):
+        if stage == 1:
+            return pad.mid.at[place, part]
+        if order[0] == Z:
+            return source.at[:, place, part]
+        return source.at[place, :, part]
+
+    whole = pl.ds(0, rows)
+    own = net.local((name, -4), lines(0, at[order[0]], whole), pad.own)
+    for stage, (axis, recv, via, mix) in enumerate(stages):
+
+        def spot(hop, axis=axis):
+            return (at[axis] + hop) % SIDE
+
+        arrivals, fetched, passing = [], [], []
+        for i, hop in enumerate(NEAR):
+            device = net.device(axis, hop)
+            across = lines(stage, spot(2), halves[hop])
+            passing.append(net.start((name, stage, 0, hop), across, via.at[i], device))
+            fetched.append(
+                net.local((name, stage, 3, hop), lines(stage, spot(hop), halves[hop]), mix.at[i])
+            )
+        for i, hop in enumerate(NEAR):
+            other = halves[4 - hop]
+            target = recv.at[i, other] if stage else recv.at[i, :, other]
+            arrivals.append(
+                net.start(
+                    (name, stage, 1, hop),
+                    lines(stage, spot(hop), other),
+                    target,
+                    net.device(axis, hop),
+                )
+            )
+        yield
+        for i, hop in enumerate(NEAR):
+            fetched[i].wait()
+            passing[i].wait_recv()
+
+            def put(lead, part, value, i=i, mix=mix, stage=stage):
+                index = (i, part) if stage else (i, lead, part)
+                mix[index + (slice(None),)] = value.astype(mix.dtype)
+
+            def get(ref, i=i, stage=stage):
+                if stage:
+                    return lambda lead, part: ref[i, part, :]
+                return lambda lead, part: ref[i, lead, part, :]
+
+            scatter_sum(1 if stage else SIDE, half, get(mix), [get(via)], put)
+            target = recv.at[i, halves[hop]] if stage else recv.at[i, :, halves[hop]]
+            arrivals.append(
+                net.start((name, stage, 2, hop), mix.at[i], target, net.device(axis, hop))
+            )
+        yield
+        for copy in arrivals:
+            copy.wait_recv()
+        if stage == 0:
+            own.wait()
+
+            def put_mid(lead, part, value):
+                pad.mid[lead, part, :] = value.astype(pad.mid.dtype)
+
+            scatter_sum(
+                SIDE,
+                rows,
+                lambda lead, part: pad.own[lead, part, :],
+                [lambda lead, part, k=k: pad.one[k, lead, part, :] for k in range(2)],
+                put_mid,
+            )
+    mine = at[order[1]]
+
+    def put_out(lead, part, value):
+        out[part, :] = value.astype(out.dtype)
+
+    scatter_sum(
+        1,
+        rows,
+        lambda lead, part: pad.own[mine, part, :],
+        [lambda lead, part, k=k: pad.one[k, mine, part, :] for k in range(2)]
+        + [lambda lead, part, k=k: pad.two[k, part, :] for k in range(2)],
         put_out,
     )
 
@@ -399,7 +497,7 @@
     lax.fori_loop(0, used // WIDE, channels, 0)
 
 
-def scan_forward_kernel(
+def scan_forward_body(
     used, decay_ref, drive_ref, cols_ref, rate_ref, out_ref, start_ref, decay_t, drive_t, out_t
 ):
     states = rate_ref.shape[1]
@@ -441,27 +539,7 @@
     to_rows(out_t, out_ref)
 
 
-def scan_forward(decay, drive, cols, rate, used):
-    width = decay.shape[0] * CHUNKS
-    states = rate.shape[1]
-    turned = jax.ShapeDtypeStruct((STEPS, width, CHUNKS), jnp.float32)
-    return pl.pallas_call(
-        functools.partial(scan_forward_kernel, used),
-        out_shape=[
-            jax.ShapeDtypeStruct(decay.shape, jnp.float32),
-            jax.ShapeDtypeStruct((states, width, CHUNKS), jnp.float32),
-            turned,
-            turned,
-        ],
-        in_specs=[VMEM] * 4,
-        out_specs=[VMEM] * 4,
-        scratch_shapes=[pltpu.VMEM(turned.shape, jnp.float32)],
-        compiler_params=pltpu.CompilerParams(vmem_limit_bytes=32 * 2**20),
-        name="scan_forward",
-    )(decay, drive, cols, rate)
-
-
-def scan_backward_kernel(
+def scan_backward_body(
     used,
     decay_t,
     drive_t,
@@ -551,31 +629,6 @@
     to_rows(g_drive_t, g_drive_ref)
 
 
-def scan_backward(decay_t, drive_t, cols, rate, starts, grad, used):
-    states = rate.shape[1]
-    turned = pltpu.VMEM(decay_t.shape, jnp.float32)
-    return pl.pallas_call(
-        functools.partial(scan_backward_kernel, used),
-        out_shape=[
-            jax.ShapeDtypeStruct(grad.shape, jnp.float32),
-            jax.ShapeDtypeStruct(grad.shape, jnp.float32),
-            jax.ShapeDtypeStruct(cols.shape, jnp.float32),
-            jax.ShapeDtypeStruct(rate.shape, jnp.float32),
-        ],
-        in_specs=[VMEM] * 6,
-        out_specs=[VMEM] * 4,
-        scratch_shapes=[
-            turned,
-            turned,
-            turned,
-            pltpu.VMEM((2 * states, STEPS, LINES, CHUNKS), jnp.float32),
-            pltpu.VMEM(starts.shape, jnp.float32),
-        ],
-        compiler_params=pltpu.CompilerParams(vmem_limit_bytes=48 * 2**20),
-        name="scan_backward",
-    )(decay_t, drive_t, cols, rate, starts, grad)
-
-
 KEY_ROWS = 256
 PIECE = 25
 PADDED = 32
@@ -770,23 +823,30 @@
     begin = -(-rest // LANES) * LANES
     keys = pl.ds(begin, keyval_ref.shape[1])
     keyval = keyval_ref[...].astype(jnp.bfloat16)
-    weight = second_ref[:, keys]
-    weight_f = weight.astype(jnp.float32)
-    grad = dot_on(wide_ref[...], keyval, 0, 0)
-    part_ref[...] = jnp.sum(grad * weight_f, axis=1, keepdims=True)
     g_meta = g_meta_ref[...]
-    grad = grad + dot_on(
-        meta_wide_ref[...].astype(jnp.float32), g_meta, 0, 0, precision=highest
-    )
     half = one_ref.shape[1]
-    one_ref[...] = grad[:, :half].astype(jnp.bfloat16)
-    two_ref[...] = grad[:, half:].astype(jnp.bfloat16)
-    g_normed = dot_on(g_query_ref[:, pl.ds(0, third)], first_ref[...], 1, 1)
-    g_normed = g_normed + dot_on(
-        g_query_ref[:, pl.ds(third, rest)], second_ref[:, pl.ds(0, rest)], 1, 1
-    )
-    g_normed_ref[...] = close_columns(g_normed + dot_on(keyval, weight, 1, 1))
-    g_meta_normed = close_columns(dot_on(g_meta, weight_f, 1, 1, precision=highest))
+    places = wide_ref.shape[1]
+    size = places // 4
+    g_normed, g_meta_normed = [], []
+    for i in range(4):
+        spot = pl.ds(i * size, size)
+        weight = second_ref[spot, keys]
+        weight_f = weight.astype(jnp.float32)
+        grad = dot_on(wide_ref[:, spot], keyval, 0, 0)
+        part_ref[spot, :] = jnp.sum(grad * weight_f, axis=1, keepdims=True)
+        grad = grad + dot_on(
+            meta_wide_ref[:, spot].astype(jnp.float32), g_meta, 0, 0, precision=highest
+        )
+        one_ref[spot, :] = grad[:, :half].astype(jnp.bfloat16)
+        two_ref[spot, :] = grad[:, half:].astype(jnp.bfloat16)
+        total = dot_on(g_query_ref[:, pl.ds(0, third)], first_ref[spot, :], 1, 1)
+        total = total + dot_on(
+            g_query_ref[:, pl.ds(third, rest)], second_ref[spot, pl.ds(0, rest)], 1, 1
+        )
+        g_normed.append(total + dot_on(keyval, weight, 1, 1))
+        g_meta_normed.append(dot_on(g_meta, weight_f, 1, 1, precision=highest))
+    g_normed_ref[...] = close_columns(jnp.concatenate(g_normed, axis=1))
+    g_meta_normed = close_columns(jnp.concatenate(g_meta_normed, axis=1))
     meta = meta_ref[...]
     scale = lax.rsqrt(jnp.mean(meta * meta, axis=-1, keepdims=True) + epsilon)
     unit = meta * scale
@@ -796,27 +856,7 @@
     three_ref[...] = spread_columns(g_rows.astype(jnp.bfloat16)).T
 
 
-def attention_inputs(
-    keyval_sum, g_query, wide, meta_wide, g_meta, first, second, meta, gain
-):
-    rows, places = wide.shape
-    keys_width = keyval_sum.shape[1]
-    metas, width = meta.shape
-    low, full = jnp.bfloat16, jnp.float32
-    return whole_call(
-        "attention_inputs",
-        attention_inputs_kernel,
-        (keyval_sum, g_query, wide, meta_wide, g_meta, first, second, meta, gain),
-        (
-            ((places, keys_width // 2), low),
-            ((places, keys_width // 2), low),
-            ((places, metas), low),
-            ((rows, width), full),
-            ((places, 1), full),
-            ((1, width), full),
-        ),
-        room=60,
-    )
+INSIDE = ("g_query", "wide", "meta_wide", "g_meta", "first", "second", "meta", "gain")
 
 
 def stack_heads(source, target, scale, in_values):
@@ -850,6 +890,14 @@
     allowed = (keys >= bounds_ref[:, 0:1]) & (keys <= bounds_ref[:, 1:2])
     bias = jnp.where(allowed, 0.0, negative_fill)
     return jnp.concatenate([bias] * per, axis=0)
+
+
+def key_bias_turned(bounds_ref, begin, per):
+    rows = bounds_ref.shape[1]
+    keys = begin + lax.broadcasted_iota(jnp.int32, (KEY_ROWS, rows), 0)
+    allowed = (keys >= bounds_ref[0:1, :]) & (keys <= bounds_ref[1:2, :])
+    bias = jnp.where(allowed, 0.0, negative_fill)
+    return jnp.concatenate([bias] * per, axis=1)
 
 
 def attend_forward_kernel(
@@ -893,24 +941,22 @@
         scores[:, meta_part] = value
         top = lax.fori_loop(0, count, score, jnp.max(value, axis=1, keepdims=True))
 
-        def weigh(b, total):
-            spot = pl.ds(pl.multiple_of(b * KEY_ROWS, KEY_ROWS), KEY_ROWS)
-            value = jnp.exp(scores[:, spot] - top)
-            scores[:, spot] = value
-            return total + jnp.sum(value, axis=1, keepdims=True)
+        def weigh(b, carry):
+            total, out = carry
+            begin = pl.multiple_of(b * KEY_ROWS, KEY_ROWS)
+            value = jnp.exp(scores[:, pl.ds(begin, KEY_ROWS)] - top)
+            out = out + dot_on(
+                value.astype(jnp.bfloat16), keys[pl.ds(begin, KEY_ROWS), part], 1, 0
+            )
+            return (total + jnp.sum(value, axis=1, keepdims=True), out)
 
         value = jnp.exp(scores[:, meta_part] - top)
-        scores[:, meta_part] = value
-        total = lax.fori_loop(0, count, weigh, jnp.sum(value, axis=1, keepdims=True))
-        share = 1.0 / total
-
-        def gather_values(b, out):
-            begin = pl.multiple_of(b * KEY_ROWS, KEY_ROWS)
-            probs = (scores[:, pl.ds(begin, KEY_ROWS)] * share).astype(jnp.bfloat16)
-            return out + dot_on(probs, keys[pl.ds(begin, KEY_ROWS), part], 1, 0)
-
-        probs = (scores[:, meta_part] * share).astype(jnp.bfloat16)
-        out = lax.fori_loop(0, count, gather_values, dot_on(probs, meta_ref[:, part], 1, 0))
+        carry = (
+            jnp.sum(value, axis=1, keepdims=True),
+            dot_on(value.astype(jnp.bfloat16), meta_ref[:, part], 1, 0),
+        )
+        total, out = lax.fori_loop(0, count, weigh, carry)
+        out = out * (1.0 / total)
         for j in range(per):
             out_ref[:, pl.ds((group * per + j) * HEAD, HEAD)] = out[
                 j * rows : (j + 1) * rows, HEAD:
@@ -1004,14 +1050,16 @@
             )
         balance = jnp.concatenate(balance, axis=0)
 
+        mass_row, balance_row = mass.T, balance.T
+
         def pieces(block, bias):
-            value = dot_on(query, block, 1, 1)
+            value = dot_on(block, query, 1, 1)
             if bias is not None:
                 value = value + bias
-            probs = jnp.exp(value - mass)
-            g_scores = (probs * (dot_on(grad, block, 1, 1) - balance)).astype(jnp.bfloat16)
-            g_block = dot_on(g_scores, query, 0, 0) + dot_on(probs.astype(jnp.bfloat16), grad, 0, 0)
-            return dot_on(g_scores, block, 1, 0), g_block
+            probs = jnp.exp(value - mass_row)
+            g_scores = (probs * (dot_on(block, grad, 1, 1) - balance_row)).astype(jnp.bfloat16)
+            g_block = dot_on(g_scores, query, 1, 0) + dot_on(probs.astype(jnp.bfloat16), grad, 1, 0)
+            return dot_on(g_scores, block, 0, 0), g_block
 
         g_query, g_meta = pieces(meta_ref[:, part], None)
         g_meta_ref[:, part] = g_meta
@@ -1019,7 +1067,7 @@
         def step(b, g_query):
             begin = pl.multiple_of(b * KEY_ROWS, KEY_ROWS)
             more, g_block = pieces(
-                keys[pl.ds(begin, KEY_ROWS), part], key_bias(bounds_ref, begin, per)
+                keys[pl.ds(begin, KEY_ROWS), part], key_bias_turned(bounds_ref, begin, per)
             )
             g_keyval_ref[pl.ds(begin, KEY_ROWS), part] = g_block.astype(jnp.bfloat16)
             return g_query + more
@@ -1057,74 +1105,929 @@
     )
 
 
+def close_rows(source, target, places):
+    width = target.shape[0]
+    for begin in range(0, width, LANES):
+        end = min(begin + LANES, width)
+        low = begin // PIECE * PADDED // LANES * LANES
+        high = min(-(-((end - 1) // PIECE + 1) * PADDED // LANES) * LANES, places)
+        matrix = spread_matrix(begin, end, low, high)
+        target[pl.ds(begin, end - begin), :] = dot_on(matrix, source(low, high), 1, 0).astype(
+            target.dtype
+        )
+
+
+def spread_rows(source, put):
+    step = LANES // PADDED * PIECE
+    for n, begin in enumerate(range(0, 64 * PIECE, step)):
+        low = begin // LANES * LANES
+        high = min(low + 2 * LANES, 64 * PIECE)
+        wide = begin // PIECE * PADDED
+        matrix = spread_matrix(low, high, wide, wide + LANES)
+        put(n, dot_on(matrix, source(low, high), 0, 0).astype(jnp.bfloat16))
+
+
+def ffn_kernel(
+    feed_ref,
+    cot_ref,
+    gate_ref,
+    down_ref,
+    out_ref,
+    g_feed_ref,
+    g_gate_ref,
+    g_down_ref,
+    gate_w,
+    up_w,
+    active_s,
+    g_gate_s,
+    g_up_s,
+    sums,
+):
+    rows, size = feed_ref.shape[0], 256
+    places = gate_ref.shape[1]
+    for part, target in enumerate((gate_w, up_w)):
+        close_rows(lambda low, high: gate_ref[part, pl.ds(low, high - low), :], target, places)
+
+    def block(i, carry):
+        spot = pl.ds(pl.multiple_of(i * size, size), size)
+        feed = feed_ref[spot, :]
+        gate = dot_on(feed, gate_w[...], 1, 0)
+        up = dot_on(feed, up_w[...], 1, 0)
+        share = jax.nn.sigmoid(gate)
+        silu = gate * share
+        active = (silu * up).astype(jnp.bfloat16)
+        active_s[spot, :] = active
+        out_ref[spot, :] = dot_on(active, down_ref[...], 1, 0).astype(jnp.bfloat16)
+        g_active = dot_on(cot_ref[spot, :], down_ref[...], 1, 1)
+        g_gate = (g_active * up * (share + silu * (1.0 - share))).astype(jnp.bfloat16)
+        g_up = (g_active * silu).astype(jnp.bfloat16)
+        g_gate_s[spot, :] = g_gate
+        g_up_s[spot, :] = g_up
+        g_feed = dot_on(g_gate, gate_w[...], 1, 1) + dot_on(g_up, up_w[...], 1, 1)
+        g_feed_ref[spot, :] = g_feed.astype(jnp.bfloat16)
+        return carry
+
+    lax.fori_loop(0, rows // size, block, 0)
+    for part, grad in enumerate((g_gate_s, g_up_s)):
+        sums[...] = dot_on(feed_ref[...], grad[...], 0, 0).astype(jnp.bfloat16)
+
+        def put(n, value):
+            for x in range(SIDE):
+                g_gate_ref[part, x, n] = value[x * PADDED : (x + 1) * PADDED]
+
+        spread_rows(lambda low, high: sums[pl.ds(low, high - low), :], put)
+    g_down = dot_on(active_s[...], cot_ref[...], 0, 0).astype(jnp.bfloat16)
+    size = g_down_ref.shape[3]
+    for x in range(SIDE):
+        for part in range(2):
+            begin = (2 * x + part) * size
+            g_down_ref[part, x, 0] = g_down[begin : begin + size]
+
+
+def feed_forward(feed, cot, gate, down):
+    rows, width = feed.shape
+    units = down.shape[0]
+    low = jnp.bfloat16
+    return whole_call(
+        "feed_forward",
+        ffn_kernel,
+        (feed, cot, gate, down),
+        (
+            ((rows, width), low),
+            ((rows, width), low),
+            ((2, SIDE, 16, PADDED, units), low),
+            ((2, SIDE, 1, units // 8, width), low),
+        ),
+        (
+            ((width, units), low),
+            ((width, units), low),
+            ((rows, units), low),
+            ((rows, units), low),
+            ((rows, units), low),
+            ((width, units), low),
+        ),
+        room=60,
+    )
+
+
+STEP_ROWS = 104
+LOG_ROWS = slice(104, 120)
+TAP_ROWS = slice(120, 124)
+OFFSET_ROW = slice(124, 125)
+BIAS_ROW = slice(125, 126)
+SKIP_ROW = slice(126, 127)
+FIRST_PROJ = 128
+PROJ_CUT = 72
+
+
+def channel_matrix(size):
+    channel = lax.broadcasted_iota(jnp.int32, (size, size), 0)
+    place = lax.broadcasted_iota(jnp.int32, (size, size), 1)
+    match = (channel == (place // 64) * 50 + place % 64) & (place % 64 < 50)
+    return jnp.where(match, 1.0, 0.0).astype(jnp.bfloat16)
+
+
+def two_terms(values):
+    most = values.astype(jnp.bfloat16)
+    return most, (values - most.astype(jnp.float32)).astype(jnp.bfloat16)
+
+
+def shifted_rows(before, rows, back):
+    joined = jnp.concatenate([before, rows], axis=0)
+    return joined[8 - back : 8 - back + rows.shape[0]]
+
+
+def conv_sum(before, rows, dist, channel):
+    taps = channel[TAP_ROWS]
+    total = taps[CONV - 1 : CONV] * rows + channel[OFFSET_ROW]
+    for back in range(1, CONV):
+        earlier = shifted_rows(before, rows, back)
+        valid = jnp.where(dist >= back, 1.0, 0.0)
+        total = total + taps[CONV - 1 - back : CONV - back] * earlier * valid
+    return total
+
+
+def mixer_project_kernel(
+    tokens_ref,
+    gain_ref,
+    weight_ref,
+    channel_ref,
+    dist_ref,
+    normed_ref,
+    conv_ref,
+    gate_ref,
+    inputs_ref,
+    first_ref,
+    second_ref,
+    compact_ref,
+    rows_ref,
+    tail_ref,
+):
+    low = jnp.bfloat16
+    lanes = conv_ref.shape[1]
+
+    @pl.when(pl.program_id(0) == 0)
+    def _():
+        places = weight_ref.shape[0]
+        close_rows(lambda a, b: weight_ref[pl.ds(a, b - a), :], compact_ref, places)
+        rows_ref[...] = dot_on(channel_ref[...], channel_matrix(lanes), 0, 1)
+        tail_ref[...] = jnp.zeros_like(tail_ref)
+
+    tokens = jnp.concatenate([tokens_ref[0, 0], tokens_ref[1, 0]], axis=0).astype(jnp.float32)
+    normed = (unit_rows(tokens) * gain_ref[...]).astype(low)
+    normed_ref[...] = normed
+    mixed = dot_on(normed, compact_ref[...], 1, 0)
+    conv_in = mixed[:, :lanes].astype(low)
+    conv_ref[...] = conv_in
+    gate_ref[...] = mixed[:, lanes:]
+    rows = conv_in.astype(jnp.float32)
+    channel = rows_ref[...]
+    total = conv_sum(tail_ref[...], rows, dist_ref[...], channel)
+    tail_ref[...] = rows[-8:]
+    inputs = (total * jax.nn.sigmoid(total)).astype(low)
+    inputs_ref[...] = inputs
+    proj = dot_on(channel[FIRST_PROJ : FIRST_PROJ + 136].astype(low), inputs, 1, 1)
+    first_ref[0] = proj[:PROJ_CUT]
+    second_ref[0] = proj[PROJ_CUT:]
+
+
+def mixer_project(tokens, gain, weight, channel, dist):
+    places, rows, width = tokens.shape[1], tokens.shape[2], tokens.shape[3]
+    rows, lanes = 2 * rows, weight.shape[1] // 2
+    group = places * rows
+    low, full = jnp.bfloat16, jnp.float32
+
+    def line(size):
+        return pl.BlockSpec((rows, size), lambda i: (i, 0))
+
+    def whole(*shape):
+        return pl.BlockSpec(shape, lambda i: (0,) * len(shape))
+
+    return pl.pallas_call(
+        mixer_project_kernel,
+        grid=(places,),
+        out_shape=[
+            jax.ShapeDtypeStruct((group, width), low),
+            jax.ShapeDtypeStruct((group, lanes), low),
+            jax.ShapeDtypeStruct((group, lanes), full),
+            jax.ShapeDtypeStruct((group, lanes), low),
+            jax.ShapeDtypeStruct((places, PROJ_CUT, rows), full),
+            jax.ShapeDtypeStruct((places, 136 - PROJ_CUT, rows), full),
+            jax.ShapeDtypeStruct((width, 2 * lanes), low),
+            jax.ShapeDtypeStruct((channel.shape[1], lanes), full),
+        ],
+        in_specs=[
+            pl.BlockSpec((2, 1, rows // 2, width), lambda i: (0, i, 0, 0)),
+            whole(*gain.shape),
+            whole(*weight.shape),
+            whole(*channel.shape),
+            line(1),
+        ],
+        out_specs=[
+            line(width),
+            line(lanes),
+            line(lanes),
+            line(lanes),
+            pl.BlockSpec((1, PROJ_CUT, rows), lambda i: (i, 0, 0)),
+            pl.BlockSpec((1, 136 - PROJ_CUT, rows), lambda i: (i, 0, 0)),
+            whole(width, 2 * lanes),
+            whole(channel.shape[1], lanes),
+        ],
+        scratch_shapes=[pltpu.VMEM((8, lanes), full)],
+        compiler_params=pltpu.CompilerParams(vmem_limit_bytes=40 * 2**20),
+        name="mixer_project",
+    )(tokens, gain, weight, channel, dist)
+
+
+def step_sum(first_ref, second_ref, channel_ref, p):
+    low = jnp.bfloat16
+    one = first_ref[p].astype(low)
+    two = second_ref[p, pl.ds(0, STEP_ROWS - PROJ_CUT), :].astype(low)
+    total = dot_on(one, channel_ref[pl.ds(0, PROJ_CUT), :].astype(low), 0, 0)
+    total = total + dot_on(
+        two, channel_ref[pl.ds(PROJ_CUT, STEP_ROWS - PROJ_CUT), :].astype(low), 0, 0
+    )
+    return total + channel_ref[BIAS_ROW], one, two
+
+
+def put_blocks(target, spot, value):
+    for block in range(target.shape[0]):
+        target[block, spot, :] = value[:, block * CHUNKS : (block + 1) * CHUNKS]
+
+
+def get_blocks(source, spot):
+    return jnp.concatenate([source[block, spot, :] for block in range(source.shape[0])], axis=1)
+
+
+def softplus(values):
+    return jnp.maximum(values, 0.0) + jnp.log1p(jnp.exp(-jnp.abs(values)))
+
+
+def mixer_forward_kernel(
+    used,
+    first_ref,
+    second_ref,
+    cols_ref,
+    channel_ref,
+    inputs_ref,
+    reset_ref,
+    gate_ref,
+    back_ref,
+    partial_ref,
+    mixed_ref,
+    out_ref,
+    start_ref,
+    decay_t,
+    drive_t,
+    rate_ref,
+    decay_s,
+    drive_s,
+    out_t,
+):
+    places = first_ref.shape[0]
+    rows = first_ref.shape[2]
+    half = rows // 2
+    lanes = channel_ref.shape[1]
+    rate = -jnp.exp(channel_ref[LOG_ROWS]) * log2_e
+    channel = lax.broadcasted_iota(jnp.int32, rate.shape, 1)
+    rate_ref[...] = jnp.where(channel < used, rate, 0.0).T
+
+    def prepare(p, carry):
+        spot = pl.ds(pl.multiple_of(p * rows, rows), rows)
+        steps = softplus(step_sum(first_ref, second_ref, channel_ref, p)[0])
+        put_blocks(decay_s, spot, steps + reset_ref[spot, :])
+        put_blocks(drive_s, spot, steps * inputs_ref[spot, :].astype(jnp.float32))
+        return carry
+
+    lax.fori_loop(0, places, prepare, 0)
+    scan_forward_body(
+        used, decay_s, drive_s, cols_ref, rate_ref, out_ref, start_ref, decay_t, drive_t, out_t
+    )
+    weight = dot_on(channel_matrix(lanes), back_ref[...], 1, 0).astype(jnp.bfloat16)
+
+    def finish(p, carry):
+        spot = pl.ds(pl.multiple_of(p * rows, rows), rows)
+        gate = gate_ref[spot, :]
+        inputs = inputs_ref[spot, :].astype(jnp.float32)
+        mixed = (get_blocks(out_ref, spot) + channel_ref[SKIP_ROW] * inputs) * (
+            gate * jax.nn.sigmoid(gate)
+        )
+        mixed = mixed.astype(jnp.bfloat16)
+        mixed_ref[spot, :] = mixed
+        value = dot_on(mixed, weight, 1, 0).astype(jnp.bfloat16)
+        partial_ref[0, p] = value[:half]
+        partial_ref[1, p] = value[half:]
+        return carry
+
+    lax.fori_loop(0, places, finish, 0)
+
+
+def mixer_forward(used, first, second, cols, channel, inputs, reset, gate, back):
+    group, lanes = inputs.shape
+    places, rows = first.shape[0], first.shape[2]
+    states = cols.shape[0] // 2
+    low, full = jnp.bfloat16, jnp.float32
+    blocks = (lanes // CHUNKS, group, CHUNKS)
+    turned = (STEPS, lanes, CHUNKS)
+    return whole_call(
+        "mixer_forward",
+        functools.partial(mixer_forward_kernel, used),
+        (first, second, cols, channel, inputs, reset, gate, back),
+        (
+            ((2, places, rows // 2, back.shape[1]), low),
+            ((group, lanes), low),
+            (blocks, full),
+            ((states, lanes, CHUNKS), full),
+            (turned, full),
+            (turned, full),
+            ((lanes, states), full),
+        ),
+        ((blocks, full), (blocks, full), (turned, full)),
+    )
+
+
+def mixer_backward_kernel(
+    used,
+    first_ref,
+    second_ref,
+    cols_ref,
+    channel_ref,
+    inputs_ref,
+    gate_ref,
+    back_ref,
+    grad_ref,
+    mixed_ref,
+    out_ref,
+    start_ref,
+    decay_t,
+    drive_t,
+    rate_ref,
+    g_first_ref,
+    g_second_ref,
+    g_cols_ref,
+    g_inputs_ref,
+    g_gate_ref,
+    g_back_ref,
+    g_rows_ref,
+    g_rate_ref,
+    g_out_s,
+    g_decay_s,
+    g_drive_s,
+    g_weight,
+    grad_t,
+    g_decay_t,
+    g_drive_t,
+    sums_t,
+    ends_t,
+):
+    places = first_ref.shape[0]
+    rows = first_ref.shape[2]
+    lanes = channel_ref.shape[1]
+    low, full = jnp.bfloat16, jnp.float32
+    weight = dot_on(channel_matrix(lanes), back_ref[...], 1, 0).astype(low)
+    skip = channel_ref[SKIP_ROW]
+    g_weight[...] = jnp.zeros_like(g_weight)
+    g_rows_ref[...] = jnp.zeros_like(g_rows_ref)
+
+    def prepare(p, carry):
+        spot = pl.ds(pl.multiple_of(p * rows, rows), rows)
+        grad = jnp.concatenate([grad_ref[0, p], grad_ref[1, p]], axis=0)
+        g_weight[...] += dot_on(mixed_ref[spot, :], grad, 0, 0)
+        g_mixed = dot_on(grad, weight, 1, 1)
+        gate = gate_ref[spot, :]
+        inputs = inputs_ref[spot, :].astype(full)
+        share = jax.nn.sigmoid(gate)
+        g_out = g_mixed * (gate * share)
+        put_blocks(g_out_s, spot, g_out)
+        value = get_blocks(out_ref, spot) + skip * inputs
+        g_gate = g_mixed * value * (share + gate * share * (1.0 - share))
+        g_gate_ref[spot, :] = g_gate.astype(low)
+        g_inputs_ref[spot, :] = g_out * skip
+        g_rows_ref[SKIP_ROW] += jnp.sum(g_out * inputs, axis=0, keepdims=True)
+        return carry
+
+    lax.fori_loop(0, places, prepare, 0)
+    scan_backward_body(
+        used,
+        decay_t,
+        drive_t,
+        cols_ref,
+        rate_ref,
+        start_ref,
+        g_out_s,
+        g_decay_s,
+        g_drive_s,
+        g_cols_ref,
+        g_rate_ref,
+        grad_t,
+        g_decay_t,
+        g_drive_t,
+        sums_t,
+        ends_t,
+    )
+
+    def finish(p, carry):
+        spot = pl.ds(pl.multiple_of(p * rows, rows), rows)
+        total, one, two = step_sum(first_ref, second_ref, channel_ref, p)
+        steps = softplus(total)
+        inputs = inputs_ref[spot, :].astype(full)
+        g_drive = get_blocks(g_drive_s, spot)
+        g_steps = get_blocks(g_decay_s, spot) * (1.0 / log2_e) + g_drive * inputs
+        g_inputs_ref[spot, :] += g_drive * steps
+        g_total = g_steps * jax.nn.sigmoid(total)
+        g_rows_ref[BIAS_ROW] += jnp.sum(g_total, axis=0, keepdims=True)
+        g_total = g_total.astype(low)
+        g_rows_ref[pl.ds(0, PROJ_CUT), :] += dot_on(one, g_total, 1, 0)
+        g_rows_ref[pl.ds(PROJ_CUT, STEP_ROWS - PROJ_CUT), :] += dot_on(two, g_total, 1, 0)
+        g_low = dot_on(channel_ref[pl.ds(0, STEP_ROWS), :].astype(low), g_total, 1, 1)
+        g_first_ref[p] = g_low[:PROJ_CUT]
+        g_second_ref[p] = g_low[PROJ_CUT:]
+        return carry
+
+    lax.fori_loop(0, places, finish, 0)
+    g_back = dot_on(channel_matrix(lanes), g_weight[...].astype(low), 0, 0).astype(low)
+    size = g_back_ref.shape[2]
+    for x in range(SIDE):
+        g_back_ref[x, 0] = g_back[x * size : (x + 1) * size]
+
+
+def mixer_backward(
+    used,
+    first,
+    second,
+    cols,
+    channel,
+    inputs,
+    gate,
+    back,
+    grad,
+    mixed,
+    out,
+    starts,
+    decay_t,
+    drive_t,
+    rate,
+):
+    group, lanes = inputs.shape
+    places, rows = first.shape[0], first.shape[2]
+    low, full = jnp.bfloat16, jnp.float32
+    width = back.shape[1]
+    turned = (decay_t.shape, full)
+    states = rate.shape[1]
+    return whole_call(
+        "mixer_backward",
+        functools.partial(mixer_backward_kernel, used),
+        (
+            first,
+            second,
+            cols,
+            channel,
+            inputs,
+            gate,
+            back,
+            grad,
+            mixed,
+            out,
+            starts,
+            decay_t,
+            drive_t,
+            rate,
+        ),
+        (
+            ((places, PROJ_CUT, rows), full),
+            ((places, STEP_ROWS - PROJ_CUT, rows), full),
+            (cols.shape, full),
+            ((group, lanes), full),
+            ((group, lanes), low),
+            ((SIDE, 1, lanes // SIDE, width), low),
+            ((FIRST_PROJ, lanes), full),
+            (rate.shape, full),
+        ),
+        (
+            (out.shape, full),
+            (out.shape, full),
+            (out.shape, full),
+            ((lanes, width), full),
+            turned,
+            turned,
+            turned,
+            ((2 * states, STEPS, LINES, CHUNKS), full),
+            (starts.shape, full),
+        ),
+        room=60,
+    )
+
+
+def mixer_inputs_kernel(
+    first_ref,
+    second_ref,
+    channel_ref,
+    weight_ref,
+    normed_ref,
+    conv_ref,
+    before_ref,
+    inputs_ref,
+    g_inputs_ref,
+    g_gate_ref,
+    dist_ref,
+    later_ref,
+    g_normed_ref,
+    g_weight_ref,
+    g_rows_ref,
+    gain_ref,
+    head_ref,
+    sums,
+):
+    step = pl.program_id(0)
+    steps = pl.num_programs(0)
+    low, full = jnp.bfloat16, jnp.float32
+    lanes = conv_ref.shape[1]
+
+    @pl.when(step == 0)
+    def _():
+        head_ref[...] = jnp.zeros_like(head_ref)
+        sums[...] = jnp.zeros_like(sums)
+        g_rows_ref[...] = jnp.zeros_like(g_rows_ref)
+
+    channel = channel_ref[...]
+    proj = channel[FIRST_PROJ : FIRST_PROJ + 136].astype(low)
+    g_proj = [
+        jnp.concatenate([first_ref[i], second_ref[i]], axis=0) for i in range(first_ref.shape[0])
+    ]
+    g_proj = jnp.concatenate(g_proj, axis=1).astype(low)
+    g_inputs = g_inputs_ref[...] + dot_on(g_proj, proj, 0, 0)
+    g_rows_ref[pl.ds(FIRST_PROJ, 136), :] += dot_on(g_proj, inputs_ref[...], 1, 0)
+    rows = conv_ref[...].astype(full)
+    before = jnp.where(step == steps - 1, 0.0, 1.0) * before_ref[...].astype(full)[-8:]
+    dist = dist_ref[...]
+    total = conv_sum(before, rows, dist, channel)
+    share = jax.nn.sigmoid(total)
+    g_total = g_inputs * (share + total * share * (1.0 - share))
+    taps = channel[TAP_ROWS]
+    g_conv = taps[CONV - 1 : CONV] * g_total
+    g_taps = [jnp.sum(g_total * rows, axis=0, keepdims=True)]
+    after = jnp.concatenate([g_total, head_ref[...]], axis=0)
+    size = rows.shape[0]
+    later = later_ref[...]
+    for back in range(1, CONV):
+        earlier = shifted_rows(before, rows, back) * jnp.where(dist >= back, 1.0, 0.0)
+        g_taps.append(jnp.sum(g_total * earlier, axis=0, keepdims=True))
+        tap = taps[CONV - 1 - back : CONV - back]
+        g_conv = g_conv + tap * after[back : back + size] * jnp.where(later >= back, 1.0, 0.0)
+    head_ref[...] = g_total[:8]
+    g_rows_ref[TAP_ROWS] += jnp.concatenate(g_taps[::-1], axis=0)
+    g_rows_ref[OFFSET_ROW] += jnp.sum(g_total, axis=0, keepdims=True)
+    g_mixed = jnp.concatenate([g_conv.astype(low), g_gate_ref[...]], axis=1)
+    sums[...] += dot_on(normed_ref[...], g_mixed, 0, 0)
+    g_normed = dot_on(g_mixed, weight_ref[...], 1, 1).astype(low)
+    count, half = g_normed_ref.shape[1:3]
+    for i in range(count):
+        for part in range(2):
+            begin = (2 * i + part) * half
+            g_normed_ref[part, i] = g_normed[begin : begin + half]
+
+    @pl.when(step == steps - 1)
+    def _():
+        gain_ref[...] = jnp.sum(sums[...] * weight_ref[...].astype(full), axis=1, keepdims=True)
+
+        def put(n, value):
+            for x in range(SIDE):
+                g_weight_ref[x, n] = value[x * PADDED : (x + 1) * PADDED]
+
+        spread_rows(lambda a, b: sums[pl.ds(a, b - a), :].astype(low), put)
+
+
+def mixer_inputs(first, second, channel, weight, normed, conv, inputs, g_inputs, g_gate, dist, later):
+    places, rows = first.shape[0], first.shape[2]
+    group, lanes = conv.shape
+    width = normed.shape[1]
+    low, full = jnp.bfloat16, jnp.float32
+    count = 2
+    last = places // count - 1
+
+    def line(size):
+        return pl.BlockSpec((count * rows, size), lambda i: (last - i, 0))
+
+    def cube(size):
+        return pl.BlockSpec((count, size, rows), lambda i: (last - i, 0, 0))
+
+    def whole(*shape):
+        return pl.BlockSpec(shape, lambda i: (0,) * len(shape))
+
+    return pl.pallas_call(
+        mixer_inputs_kernel,
+        grid=(places // count,),
+        out_shape=[
+            jax.ShapeDtypeStruct((2, places, rows // 2, width), low),
+            jax.ShapeDtypeStruct((SIDE, 16, PADDED, 2 * lanes), low),
+            jax.ShapeDtypeStruct(channel.shape, full),
+            jax.ShapeDtypeStruct((width, 1), full),
+        ],
+        in_specs=[
+            cube(PROJ_CUT),
+            cube(136 - PROJ_CUT),
+            whole(*channel.shape),
+            whole(*weight.shape),
+            line(width),
+            line(lanes),
+            pl.BlockSpec((count * rows, lanes), lambda i: (jnp.maximum(last - 1 - i, 0), 0)),
+            line(lanes),
+            line(lanes),
+            line(lanes),
+            line(1),
+            line(1),
+        ],
+        out_specs=[
+            pl.BlockSpec((2, count, rows // 2, width), lambda i: (0, last - i, 0, 0)),
+            whole(SIDE, 16, PADDED, 2 * lanes),
+            whole(*channel.shape),
+            whole(width, 1),
+        ],
+        scratch_shapes=[pltpu.VMEM((8, lanes), full), pltpu.VMEM((width, 2 * lanes), full)],
+        compiler_params=pltpu.CompilerParams(vmem_limit_bytes=48 * 2**20),
+        name="mixer_inputs",
+    )(first, second, channel, weight, normed, conv, conv, inputs, g_inputs, g_gate, dist, later)
+
+
+def channel_grads_kernel(one_ref, two_ref, rate_ref, channel_ref, out_ref):
+    lanes = channel_ref.shape[1]
+    total = two_ref[...]
+    states = rate_ref.shape[1]
+    rows = lax.broadcasted_iota(jnp.int32, total.shape, 0)
+    one = one_ref[...]
+    one = jnp.concatenate([one, jnp.zeros((total.shape[0] - one.shape[0], lanes), one.dtype)], axis=0)
+    logs = rate_ref[...].T * -jnp.exp(channel_ref[LOG_ROWS])
+    blank = jnp.zeros((LOG_ROWS.start, lanes), logs.dtype)
+    rest = jnp.zeros((total.shape[0] - LOG_ROWS.start - states, lanes), logs.dtype)
+    total = total + jnp.where((rows >= LOG_ROWS.start) & (rows < LOG_ROWS.stop), 0.0, one)
+    total = total + jnp.concatenate([blank, logs, rest], axis=0)
+    matrix = channel_matrix(lanes)
+    most, left = two_terms(total)
+    wide = dot_on(matrix, most, 0, 1) + dot_on(matrix, left, 0, 1)
+    size = out_ref.shape[2]
+    for x in range(SIDE):
+        out_ref[x, 0] = wide[x * size : (x + 1) * size]
+
+
+def channel_grads(one, two, rate, channel):
+    lanes = channel.shape[1]
+    return whole_call(
+        "channel_grads",
+        channel_grads_kernel,
+        (one, two, rate, channel),
+        (((SIDE, 1, lanes // SIDE, channel.shape[0]), jnp.float32),),
+    )[0]
+
+
+def unpack_kernel(small_ref, meta_ref, gains_ref):
+    width = meta_ref.shape[1]
+    metas = meta_ref.shape[0]
+    for begin in range(0, width, LANES):
+        end = min(begin + LANES, width)
+        low = begin // PIECE * PADDED // LANES * LANES
+        high = -(-((end - 1) // PIECE + 1) * PADDED // LANES) * LANES
+        matrix = spread_matrix(begin, end, low, high)
+        value = dot_on(small_ref[pl.ds(low, high - low), :], matrix, 0, 1)
+        meta_ref[:, pl.ds(begin, end - begin)] = value[:metas]
+        gains_ref[:, pl.ds(begin, end - begin)] = value[metas : metas + gains_ref.shape[0]]
+
+
+def unpack(small, metas, width):
+    full = jnp.float32
+    return whole_call(
+        "unpack", unpack_kernel, (small,), (((metas, width), full), ((8, width), full))
+    )
+
+
+def padded_rows(value, rows):
+    blank = jnp.zeros((rows - value.shape[0], value.shape[1]), value.dtype)
+    return jnp.concatenate([value, blank], axis=0).astype(jnp.bfloat16)
+
+
+def padded_lanes(value, lanes):
+    return jnp.concatenate(
+        [value, jnp.zeros((value.shape[0], lanes - value.shape[1]), value.dtype)], axis=1
+    )
+
+
+def stacked_rows(parts, rows):
+    blank = jnp.zeros((rows - sum(part.shape[0] for part in parts), parts[0].shape[1]), jnp.float32)
+    return jnp.concatenate(parts + [blank], axis=0)
+
+
+def prepare_kernel(
+    query_ref,
+    keyval_ref,
+    attn_ref,
+    mamba_ref,
+    back_ref,
+    gate_ref,
+    down_ref,
+    meta_ref,
+    norm_gain_ref,
+    attn_gain_ref,
+    mamba_gain_ref,
+    feed_gain_ref,
+    step_ref,
+    log_ref,
+    taps_ref,
+    offset_ref,
+    bias_ref,
+    skip_ref,
+    ssm_ref,
+    attention_out,
+    mamba_out,
+    back_out,
+    gate_out,
+    down_out,
+    small_out,
+    channel_out,
+):
+    small = [meta_ref, norm_gain_ref, attn_gain_ref, mamba_gain_ref, feed_gain_ref]
+    small = stacked_rows([ref[...] for ref in small], 2 * LANES)
+    small_out[...] = padded_lanes(small, LANES).T[: small_out.shape[0]].astype(jnp.bfloat16)
+    blank = jnp.zeros((STEP_ROWS - step_ref.shape[0], step_ref.shape[1]), jnp.float32)
+    rows = [step_ref[...], blank]
+    rows += [ref[...] for ref in (log_ref, taps_ref, offset_ref, bias_ref, skip_ref)]
+    rows = padded_lanes(stacked_rows(rows, LANES), LANES).T[: channel_out.shape[0]]
+    channel_out[:, pl.ds(0, LANES)] = rows.astype(jnp.bfloat16)
+    channel_out[:, pl.ds(LANES, 2 * LANES)] = padded_rows(
+        padded_lanes(ssm_ref[...], 2 * LANES), channel_out.shape[0]
+    )
+    width = query_ref.shape[1]
+    begin = -(-width // LANES) * LANES
+    attention_out[:, pl.ds(0, begin)] = padded_rows(padded_lanes(query_ref[...], begin), PADDED)
+    half = keyval_ref.shape[1] // 2
+    for group in range(half // HEAD):
+        spot = group * HEAD
+        pair = [keyval_ref[:, pl.ds(spot, HEAD)], keyval_ref[:, pl.ds(half + spot, HEAD)]]
+        attention_out[:, pl.ds(begin + 2 * spot, 2 * HEAD)] = padded_rows(
+            jnp.concatenate(pair, axis=1), PADDED
+        )
+    attention_out[:, pl.ds(begin + 2 * half, width)] = padded_rows(attn_ref[...], PADDED)
+    places = mamba_out.shape[0]
+    lanes = mamba_out.shape[2] // 2
+    inner = mamba_ref.shape[1] // places // 2
+    for place in range(places):
+        parts = [
+            padded_lanes(mamba_ref[:, pl.ds((part * places + place) * inner, inner)], lanes)
+            for part in range(2)
+        ]
+        mamba_out[place] = padded_rows(jnp.concatenate(parts, axis=1), PADDED)
+    back_out[...] = padded_rows(back_ref[...], back_out.shape[0])
+    down_out[...] = padded_rows(down_ref[...], down_out.shape[0])
+    size = down_ref.shape[0]
+    room = gate_out.shape[3] // SIDE
+    for part in range(2):
+        for place in range(places):
+            first = (part * places + place) * SIDE * size
+            parts = [
+                padded_lanes(gate_ref[:, pl.ds(first + x * size, size)], room) for x in range(SIDE)
+            ]
+            gate_out[part, place] = padded_rows(jnp.concatenate(parts, axis=1), PADDED)
+
+
+def prepare(*arrays):
+    low = jnp.bfloat16
+    query, keyval, attn, _, back, _, down = arrays[:7]
+    most = -(-query.shape[1] // LANES) * LANES
+    return whole_call(
+        "prepare",
+        prepare_kernel,
+        arrays,
+        (
+            ((PADDED, most + keyval.shape[1] + attn.shape[1]), low),
+            ((16, PADDED, 4 * CHUNKS), low),
+            ((64, back.shape[1]), low),
+            ((2, 16, PADDED, 96 * SIDE), low),
+            ((96, down.shape[1]), low),
+            ((PADDED, 2 * LANES), low),
+            ((64, 3 * LANES), low),
+        ),
+    )
+
+
+def finish_kernel(
+    tokens_ref,
+    gain_ref,
+    g_hidden_ref,
+    normed_ref,
+    g_attn_ref,
+    sums_ref,
+    keys_ref,
+    mamba_ref,
+    back_ref,
+    channel_ref,
+    gate_ref,
+    down_ref,
+    gains_ref,
+    input_out,
+    query_out,
+    keyval_out,
+    attn_out,
+    mamba_out,
+    back_out,
+    gate_out,
+    down_out,
+    meta_out,
+    ssm_out,
+    step_out,
+    log_out,
+    taps_out,
+    rows_out,
+    gains_out,
+):
+    half = normed_ref.shape[1]
+    for i in range(2):
+        spot = pl.ds(i * half, half)
+        rows = tokens_ref[spot, :].astype(jnp.float32)
+        scale = lax.rsqrt(jnp.mean(rows * rows, axis=-1, keepdims=True) + epsilon)
+        unit = rows * scale
+        grad = (normed_ref[i] + g_attn_ref[spot, :]) * gain_ref[...]
+        grad = scale * (grad - unit * jnp.mean(grad * unit, axis=-1, keepdims=True))
+        input_out[spot, :] = g_hidden_ref[i] + grad
+    piece, width = query_out.shape
+    rows = pl.ds(0, piece)
+    begin = sums_ref.shape[1] - width
+    query_out[...] = sums_ref[rows, pl.ds(0, width)]
+    attn_out[...] = sums_ref[rows, pl.ds(begin, width)]
+    keys_half = keyval_out.shape[1] // 2
+    for group in range(keys_half // HEAD):
+        pair = keys_ref[rows, pl.ds(2 * group * HEAD, 2 * HEAD)]
+        keyval_out[:, pl.ds(group * HEAD, HEAD)] = pair[:, :HEAD]
+        keyval_out[:, pl.ds(keys_half + group * HEAD, HEAD)] = pair[:, HEAD:]
+    meta = padded_lanes(keys_ref[:, pl.ds(2 * keys_half, meta_out.shape[0])].T, LANES)
+    meta_out[...] = meta[:, :piece]
+    places = mamba_ref.shape[0]
+    lanes = mamba_ref.shape[2] // 2
+    inner = mamba_out.shape[1] // places // 2
+    for place in range(places):
+        value = mamba_ref[place].astype(jnp.float32)
+        for part in range(2):
+            mamba_out[:, pl.ds((part * places + place) * inner, inner)] = value[
+                :piece, part * lanes : part * lanes + inner
+            ]
+    back_out[...] = back_ref[0, pl.ds(0, back_out.shape[0]), :]
+    count = back_out.shape[0]
+    ssm_out[...] = channel_ref[0, pl.ds(0, count), pl.ds(FIRST_PROJ, ssm_out.shape[1])]
+    channel = channel_ref[0, :, pl.ds(0, LANES)].T
+    step_out[...] = channel[: step_out.shape[0], :count]
+    log_out[...] = channel[LOG_ROWS, :count]
+    taps_out[...] = channel[TAP_ROWS, :count]
+    rows_out[...] = channel[TAP_ROWS.start : TAP_ROWS.start + 8, :count]
+    gains = (gains_ref[0] + gains_ref[1]).T
+    gains_out[...] = gains[: gains_out.shape[0], :piece]
+    size = down_out.shape[0]
+    top = down_ref.shape[1]
+    down_out[pl.ds(0, top), :] = down_ref[0]
+    down_out[pl.ds(top, size - top), :] = down_ref[1, pl.ds(0, size - top), :]
+    room = gate_ref.shape[3] // SIDE
+    for part in range(2):
+        for place in range(places):
+            value = gate_ref[part, place].astype(jnp.float32)
+            first = (part * places + place) * SIDE * size
+            parts = [value[:piece, x * room : x * room + size] for x in range(SIDE)]
+            gate_out[:, pl.ds(first, SIDE * size)] = jnp.concatenate(parts, axis=1)
+
+
+def finish(piece, inner_piece, down_piece, inner, proj, rank, *arrays):
+    tokens = arrays[0]
+    rows, width = tokens.shape
+    full = jnp.float32
+    keys = arrays[6]
+    metas = LANES
+    return whole_call(
+        "finish",
+        finish_kernel,
+        arrays,
+        (
+            ((rows, width), full),
+            ((piece, width), full),
+            ((piece, keys.shape[1] - metas), full),
+            ((piece, width), full),
+            ((piece, 2 * 16 * inner), full),
+            ((inner_piece, width), full),
+            ((piece, 2 * 16 * SIDE * down_piece), full),
+            ((down_piece, width), full),
+            ((metas, piece), full),
+            ((inner_piece, proj), full),
+            ((rank, inner_piece), full),
+            ((LOG_ROWS.stop - LOG_ROWS.start, inner_piece), full),
+            ((CONV, inner_piece), full),
+            ((8, inner_piece), full),
+            ((8, piece), full),
+        ),
+    )
+
+
 def rms_norm(values, gain):
     return values * lax.rsqrt(jnp.mean(values * values, axis=-1, keepdims=True) + epsilon) * gain
-
-
-def rms_unit(values):
-    return values * lax.rsqrt(jnp.mean(values * values, axis=-1, keepdims=True) + epsilon)
-
-
-def contract(left, right, left_dim, right_dim, **options):
-    return lax.dot_general(
-        left,
-        right,
-        (((left_dim,), (right_dim,)), ((), ())),
-        **(options or {"preferred_element_type": jnp.float32}),
-    )
-
-
-def matmul(left, right):
-    return contract(left, right, 1, 0)
-
-
-def matmul_tn(left, right):
-    return contract(left, right, 0, 0)
-
-
-def matmul_nt(left, right):
-    return contract(left, right, 1, 1)
-
-
-def segment_of(row_ids, end_rows):
-    return jnp.sum((row_ids[:, None] >= end_rows[None, :]).astype(jnp.int32), axis=1)
-
-
-def conv_silu(conv_in, taps, offset, valid_rows):
-    row_count = conv_in.shape[0]
-    summed = taps[CONV - 1] * conv_in + offset
-    for back in range(1, CONV):
-        earlier = jnp.pad(conv_in, ((back, 0), (0, 0)))[:row_count]
-        summed = summed + taps[CONV - 1 - back] * earlier * valid_rows[back - 1][:, None]
-    return jax.nn.silu(summed)
-
-
-def gate_mix(ssm_out, skip_gain, inputs_m, gate_z):
-    return (ssm_out + skip_gain * inputs_m) * jax.nn.silu(gate_z)
-
-
-def swiglu(gate, up):
-    return jax.nn.silu(gate) * up
 
 
 def pad_to(array, dim, size):
     widths = [(0, 0)] * array.ndim
     widths[dim] = (0, size - array.shape[dim])
     return jnp.pad(array, widths)
-
-
-def zeros(shape, kind=jnp.float32):
-    return jnp.zeros(shape, kind)
-
-
-def halves_first(rows_by_place):
-    width = rows_by_place.shape[-1]
-    return rows_by_place.reshape(16, 2, -1, width).transpose(1, 0, 2, 3).reshape(-1, width)
-
-
-def places_first(rows_by_half):
-    width = rows_by_half.shape[-1]
-    return rows_by_half.reshape(2, 16, -1, width).transpose(1, 0, 2, 3).reshape(-1, width)
 
 
 def blank(shapes):
@@ -1259,7 +2162,7 @@
     )
 
 
-def reduce_three(net, name, source, pad, out, order):
+def reduce_three(net, name, source, pad, out, order, hold=0):
     left = [Y, Z, X]
     held = source
     stages = ((pad.recv0, pad.mid0), (pad.recv1, pad.mid1), (pad.recv2, out))
@@ -1284,6 +2187,8 @@
         ]
         yield
         if stage == 0:
+            for _ in range(hold):
+                yield
             fetch.wait()
         for copy in copies:
             copy.wait_recv()
@@ -1338,6 +2243,20 @@
     )
 
 
+def ring_pad(rows, width, kind=jnp.bfloat16):
+    half = rows // 2
+    return dict(
+        one=((2, SIDE, rows, width), kind),
+        via_one=((2, SIDE, half, width), kind),
+        mix_one=((2, SIDE, half, width), kind),
+        mid=((SIDE, rows, width), kind),
+        two=((2, rows, width), kind),
+        via_two=((2, half, width), kind),
+        mix_two=((2, half, width), kind),
+        own=((SIDE, rows, width), kind),
+    )
+
+
 def half_pad(rows, width, kind=jnp.bfloat16):
     return dict(two_pad(rows, width, kind), half=((SIDE, SIDE, rows, width), kind))
 
@@ -1355,6 +2274,20 @@
     return dict(recv=((3, lead, rows, width), kind), own=((lead, rows, width), kind))
 
 
+def gather_weights(net, held):
+    axes = (Y, Z, X)
+    jobs, begin = [], 0
+    for i, (target, order) in enumerate(
+        ((held.first, (X, Z, Y)), (held.second, (Z, Y, X)), (held.third, (Y, X, Z)))
+    ):
+        size = target.shape[-1]
+        jobs.append(
+            gather(net, 5 + i, held.whole.at[:, pl.ds(begin, size)], target, axes, order, hold=3)
+        )
+        begin += size
+    return jobs
+
+
 def program_start(net, held):
     core = net.core
     rows = held.tokens.shape[0] // 2
@@ -1363,7 +2296,7 @@
     if core == 1:
 
         def mamba():
-            target = held.mamba_all.at[net.at[X]]
+            target = held.mamba_all.at[:, :, net.at[X]]
             yield from swap_two(net, 2, held.mamba, held.mamba_mid, target)
             copies = [
                 net.start((2, 3, hop), target, target, net.device(X, hop)) for hop in HOPS
@@ -1377,23 +2310,12 @@
             gather(net, 3, held.back, held.back_all, (X,), (X,)),
             gather(net, 4, held.channel, held.channel_all, (X,), (X,)),
         ]
-    return jobs + [
-        gather(net, 1, held.small, held.small_all, axes, order_of(net) + (X,)),
-        gather_halves(
-            net, 0, held.tokens.at[pl.ds(core * rows, rows)], held.tokens_all, patience=2
-        ),
-    ]
-
-
-def program_weights(net, held):
-    axes = (Y, Z, X)
-    jobs, begin = [], 0
-    for i, (target, order) in enumerate(
-        ((held.first, (X, Z, Y)), (held.second, (Z, Y, X)), (held.third, (Y, X, Z)))
-    ):
-        size = target.shape[-1]
-        jobs.append(gather(net, i, held.whole.at[:, pl.ds(begin, size)], target, axes, order))
-        begin += size
+    jobs.append(gather(net, 1, held.small, held.small_all, axes, order_of(net) + (X,)))
+    jobs.append(
+        gather_halves(net, 0, held.tokens.at[pl.ds(core * rows, rows)], held.tokens_all)
+    )
+    if core == 0:
+        jobs += gather_weights(net, held)
     return jobs
 
 
@@ -1441,11 +2363,12 @@
 
     return [
         attn(),
+        reduce_halves(net, 0, held.partial, held.pad, held.mamba_pre),
         share_x(
             net,
             2,
             held.gate_first if core == 0 else held.gate_second,
-            lambda b, x: held.gate_all.at[b, x],
+            lambda b, x: held.gate_all.at[b, :, :, x],
         ),
         share_x(
             net,
@@ -1453,7 +2376,6 @@
             held.down.at[pl.ds(core * half, half)],
             lambda b, x: held.down_all.at[x, pl.ds(b * half, half)],
         ),
-        reduce_halves(net, 0, held.partial, held.pad, held.mamba_pre),
     ]
 
 
@@ -1463,8 +2385,8 @@
 
 def program_ffn(net, held):
     return [
-        reduce_two(net, 0, held.out, held.out_pad, held.out_sum, order_of(net)),
-        reduce_two(net, 1, held.grad, held.grad_pad, held.grad_sum, order_of(net)),
+        reduce_ring(net, 0, held.out, held.out_pad, held.out_sum, order_of(net)),
+        reduce_ring(net, 1, held.grad, held.grad_pad, held.grad_sum, order_of(net)),
     ]
 
 
@@ -1514,33 +2436,86 @@
     ]
 
 
-def three_sums(net, held):
-    return [
-        reduce_three(net, 10, held.one, held.one_pad, held.one_sum, (Y, Z, X)),
-        reduce_three(net, 11, held.two, held.two_pad, held.two_sum, (X, Y, Z)),
-        reduce_three(net, 12, held.three, held.three_pad, held.three_sum, (Z, X, Y)),
+SUMS = ("one", "two", "three", "four", "five", "six")
+ORDERS = ((Y, Z, X), (X, Y, Z), (Z, X, Y), (Y, Z, X), (X, Y, Z), (Z, X, Y))
+
+
+def program_attention(net, held):
+    rows = held.keyval.shape[2] // 2
+    parts = [getattr(held.parts, name) for name in SUMS]
+    taken = [
+        net.local((20, i), getattr(held.sources, name), getattr(held.inside, name))
+        for i, name in enumerate(INSIDE)
     ]
 
-
-def program_attention(net, held):
+    def weight(i, source, hold=0):
+        pad = getattr(held.pads, SUMS[i])
+        return reduce_three(net, 10 + i, source, pad, parts[i], ORDERS[i], hold)
+
+    def keyval(i):
+        pad = (held.upper_pad, held.lower_pad)[i]
+        return reduce_two(
+            net,
+            i,
+            held.keyval.at[:, :, pl.ds(i * rows, rows)],
+            pad,
+            held.keyval_sum.at[pl.ds(i * rows, rows)],
+            ((Z, Y), (Y, Z))[i],
+        )
+
+    def follow():
+        for _ in range(3):
+            yield
+        for copy in taken:
+            copy.wait()
+        inside = held.inside
+        attention_inputs_kernel(
+            held.keyval_sum,
+            inside.g_query,
+            inside.wide,
+            inside.meta_wide,
+            inside.g_meta,
+            inside.first,
+            inside.second,
+            inside.meta,
+            inside.gain,
+            held.keys.four,
+            held.keys.five,
+            held.keys.six,
+            held.g_normed,
+            held.gain_part,
+            held.meta_gain,
+        )
+        places = held.keys.four.shape[0] // SIDE**3
+
+        def cubed(ref):
+            return ref.reshape(SIDE, SIDE, SIDE, places, ref.shape[1])
+
+        later = [weight(3 + i, cubed(ref)) for i, ref in enumerate(vars(held.keys).values())]
+        while later:
+            later = [job for job in later if next(job, True) is None]
+            yield
+
     def last():
-        for _ in range(4):
+        for _ in range(9):
             yield
         begin = 0
-        for part in (held.one_sum, held.two_sum, held.three_sum):
+        for part in parts[:3]:
             held.sums[:, pl.ds(begin, part.shape[1])] = part[...]
             begin += part.shape[1]
+        begin = 0
+        for part in parts[3:]:
+            held.keys_sum[:, pl.ds(begin, part.shape[1])] = part[...]
+            begin += part.shape[1]
 
     return [
-        reduce_two(net, 0, held.keyval, held.keyval_pad, held.keyval_sum, (Z, Y)),
-        *three_sums(net, held),
+        keyval(0),
+        keyval(1),
         swap_two(net, 3, held.gate, held.gate_mid, held.gate_own),
+        follow(),
+        *(weight(i, getattr(held, SUMS[i]), 2) for i in range(3)),
         last(),
     ]
-
-
-def program_keys(net, held):
-    return three_sums(net, held)
 
 
 def program_end(net, held):
@@ -1585,17 +2560,6 @@
         swap_cores(net, 13, held.gate, held.gate_both),
         swap_cores(net, 14, held.down, held.down_both),
     ]
-
-
-def blocks_of(weight, splits):
-    rows, columns = weight.shape
-    cut = weight.reshape(rows, splits, 16, columns // splits // 16).transpose(1, 2, 0, 3)
-    return pad_to(cut, 2, 32)
-
-
-def rows_of(blocks, rows):
-    width = blocks.shape[-1]
-    return blocks.reshape(-1, blocks.shape[-2], width)[:, :rows].reshape(-1, width)
 
 
 def padded_blocks(rows, count, size, kind=jnp.bfloat16):
@@ -1644,56 +2608,47 @@
     states = a_log.shape[0]
     proj = rank + 2 * states
     proj_pad = 136
-    proj_cut = 72
     metas = meta_tokens.shape[0]
     down_piece = w_down.shape[0]
-    units = down_piece * SIDE
+    units = 96 * SIDE
     row_start = core * half
 
     lengths = seq_lengths[0]
     end_rows = jnp.cumsum(lengths)
     start_rows = end_rows - lengths
     all_rows = jnp.arange(group, dtype=jnp.int32)
-    all_segments = segment_of(all_rows, end_rows)
     my_rows = lax.axis_index("seq") * rows + jnp.arange(rows, dtype=jnp.int32)
-    keep_rows = jnp.logical_not(jnp.any(all_rows[:, None] == start_rows[None, :], axis=1))
-    valid_rows = jnp.stack(
-        [
-            (
-                (all_rows - back >= 0)
-                & (segment_of(all_rows - back, end_rows) == all_segments)
-            ).astype(jnp.float32)
-            for back in range(1, CONV)
-        ]
-    )
-
-    gains_in = jnp.stack([norm_gain, attn_gain, mamba_gain, ffn_gain], axis=1)
-    small_in = jnp.concatenate([gains_in, meta_tokens.T], axis=1)
-    small_in = pad_to(pad_to(small_in, 1, 256), 0, 32).astype(low)
-    keys_in = w_key_value.reshape(piece, 2, -1, HEAD).transpose(0, 2, 1, 3).reshape(piece, -1)
+
+    def begins(row_ids):
+        started = row_ids[:, None] >= start_rows[None, :]
+        return jnp.max(jnp.where(started, start_rows[None, :], 0), axis=1)
+
+    dist = (all_rows - begins(all_rows))[:, None]
+    left = jnp.where(all_rows[:, None] < end_rows[None, :], end_rows[None, :], group)
+    left = (jnp.min(left, axis=1) - 1 - all_rows)[:, None]
+    reset = jnp.where(dist == 0, far_away, 0.0).astype(jnp.float32)
+
+    attention_in, mamba_in, back_in, gate_in, down_in, small_in, channel_in = prepare(
+        w_query,
+        w_key_value,
+        w_attn_out,
+        w_mamba_in,
+        w_mamba_out,
+        w_gate_up,
+        w_down,
+        meta_tokens,
+        *(gain[None] for gain in (norm_gain, attn_gain, mamba_gain, ffn_gain)),
+        w_dt,
+        a_log,
+        conv_weight,
+        *(row[None] for row in (conv_bias, dt_bias, skip_d)),
+        w_ssm_x,
+    )
     query_most = -(-query_width // LANES) * LANES
-    attention_in = jnp.concatenate(
-        [pad_to(w_query, 1, query_most).astype(low), keys_in.astype(low), w_attn_out.astype(low)], axis=1
-    )
-    attention_in = pad_to(attention_in, 0, 32)
     third = 10 * LANES
     last_third = attention_in.shape[1] - 2 * third
-    mamba_in = blocks_of(w_mamba_in.astype(low), 2)
-    mamba_in = jnp.concatenate([mamba_in[0], mamba_in[1]], axis=-1).reshape(SIDE, SIDE, 32, -1)
-    back_in = pad_to(w_mamba_out, 0, 64).astype(low)
-    channel_in = jnp.concatenate(
-        [
-            w_ssm_x,
-            conv_weight.T,
-            jnp.stack([conv_bias, dt_bias, skip_d], axis=1),
-            a_log.T,
-            w_dt.T,
-        ],
-        axis=1,
-    )
-    channel_in = pad_to(pad_to(channel_in, 0, 64), 1, 256).astype(low)
-    gate_in = blocks_of(w_gate_up.astype(low), 2).reshape(2, SIDE, SIDE, 32, units)
-    down_in = pad_to(w_down, 0, 96).astype(low)
+    mamba_in = mamba_in.reshape(SIDE, SIDE, 32, -1)
+    gate_in = gate_in.reshape(2, SIDE, SIDE, 32, units)
     cube = (SIDE, SIDE, SIDE)
 
     begun = exchange(
@@ -1706,6 +2661,7 @@
             mamba=(mamba_in, ANY),
             back=(back_in, ANY),
             channel=(channel_in, ANY),
+            whole=(attention_in, ANY),
         ),
         dict(
             tokens_all=((2, SIDE, SIDE, half, width), low, ANY),
@@ -1713,47 +2669,24 @@
             mamba_all=(cube + mamba_in.shape[2:], low, ANY),
             back_all=((SIDE,) + back_in.shape, low, ANY),
             channel_all=((SIDE,) + channel_in.shape, low, ANY),
-        ),
-        dict(mamba_mid=(mamba_in.shape, low)),
-    )
-    weights = exchange(
-        "exchange_weights",
-        1,
-        program_weights,
-        dict(whole=(attention_in, ANY)),
-        dict(
             first=(cube + (32, third), low, ANY),
             second=(cube + (32, third), low, ANY),
             third=(cube + (32, last_third), low, ANY),
         ),
-        cores=(0,),
+        dict(mamba_mid=(mamba_in.shape, low)),
     )
     weight_one, weight_two, weight_three = (
-        part.reshape(64 * 32, -1) for part in (weights.first, weights.second, weights.third)
-    )
-    cotangent_part = lax.dynamic_slice_in_dim(cotangent_b, row_start, half, 0)
-    cotangent_all = lax.all_gather(cotangent_part, "seq", axis=0, tiled=True)
-
-    small = rows_of(begun.small_all, piece).astype(jnp.float32)
-    gain_norm, gain_attn, gain_mamba, gain_feed = (small[:, i] for i in range(4))
-    meta_f = small[:, 4 : 4 + metas].T
-    channel = rows_of(begun.channel_all, inner_piece)
-    weight_ssm = channel[:, :proj]
-    conv_taps = channel[:, proj : proj + CONV].T.astype(jnp.float32)
-    conv_offset, step_bias, skip_gain = (
-        channel[:, proj + CONV + i].astype(jnp.float32) for i in range(3)
-    )
-    first_log = proj + CONV + 3
-    log_decay = channel[:, first_log : first_log + states].T.astype(jnp.float32)
-    weight_step = channel[:, first_log + states : first_log + states + rank]
+        part.reshape(64 * 32, -1) for part in (begun.first, begun.second, begun.third)
+    )
+    meta_f, gains = unpack(begun.small_all.reshape(64 * 32, -1), metas, width)
+    gain_norm, gain_attn, gain_mamba, gain_feed = (gains[i] for i in range(4))
+    gain_row = gains[:1]
 
     def on_core(which, work):
         shapes = jax.eval_shape(work)
         return lax.cond(core == which, work, lambda: blank(shapes))
 
-    inputs_f = tokens_b.astype(jnp.float32)
-
-    gain_row = gain_norm[None, :]
+
     normed_wide, query_b, keyval_b, meta_wide, meta_kv = on_core(
         0,
         lambda: attention_project(
@@ -1773,30 +2706,17 @@
         cores=(0,),
     )
 
-    def mamba_first():
-        normed_b = rms_norm(
-            begun.tokens_all.reshape(group, width).astype(jnp.float32), gain_norm
-        ).astype(low)
-        weight_mamba = rows_of(begun.mamba_all.transpose(1, 2, 0, 3, 4), piece)
-        mixed_in = places_first(matmul(normed_b, weight_mamba))
-        conv_in = mixed_in[:, :inner].astype(low)
-        inputs_b = conv_silu(
-            conv_in.astype(jnp.float32), conv_taps, conv_offset, valid_rows
-        ).astype(low)
-        projected = contract(pad_to(weight_ssm, 1, proj_pad), inputs_b, 0, 1)
-        projected = projected.reshape(proj_pad, SIDE, SIDE, rows).transpose(1, 2, 0, 3)
-        return (
-            normed_b,
-            weight_mamba,
-            conv_in,
-            mixed_in[:, inner:],
-            inputs_b,
-            projected[:, :, :proj_cut],
-            projected[:, :, proj_cut:],
-        )
-
-    normed_all, weight_mamba, conv_in, gate_z, inputs_b, proj_first, proj_second = on_core(
-        1, mamba_first
+    mamba_wide = begun.mamba_all.reshape(64 * 32, -1)
+    back_wide = begun.back_all.reshape(-1, width)
+    normed_all, conv_in, gate_z, inputs_b, proj_first, proj_second, weight_mamba, channel = on_core(
+        1,
+        lambda: mixer_project(
+            begun.tokens_all.reshape(2, 16, half, width),
+            gain_row,
+            mamba_wide,
+            begun.channel_all.reshape(4 * 64, -1),
+            dist,
+        ),
     )
 
     def proj_pads(size):
@@ -1805,12 +2725,16 @@
         )
 
     def spread_projection(name, number, first, second, gate):
-        cuts = (proj_cut, proj_pad - proj_cut)
+        cuts = (PROJ_CUT, proj_pad - PROJ_CUT)
         results = exchange(
             name,
             number,
             program_project,
-            dict(first=(first, ANY), second=(second, ANY), gate=(gate, ANY)),
+            dict(
+                first=(first.reshape(SIDE, SIDE, cuts[0], rows), ANY),
+                second=(second.reshape(SIDE, SIDE, cuts[1], rows), ANY),
+                gate=(gate, ANY),
+            ),
             dict(
                 first_all=((SIDE, SIDE, cuts[0], rows), jnp.float32, ANY),
                 second_all=((SIDE, SIDE, cuts[1], rows), jnp.float32, ANY),
@@ -1824,29 +2748,21 @@
             vmem=32 * 2**20,
             cores=(1,),
         )
-        return results
-
-    def whole_projection(results):
-        joined = jnp.concatenate([results.first_all, results.second_all], axis=2)
-        return joined.transpose(2, 0, 1, 3).reshape(proj_pad, group)
-
-    middle = spread_projection("exchange_project", 3, proj_first, proj_second, gate_in[1])
+        whole = [part.reshape(16, -1, rows) for part in (results.first_all, results.second_all)]
+        return whole + [results.gate_own]
+
+    step_first, step_second, gate_second = spread_projection("exchange_project", 3, proj_first, proj_second, gate_in[1])
     keyval_all = keyval.keyval_all.reshape(2, 16, half, keys_width)
+
+    cotangent_b, step_second = lax.optimization_barrier((cotangent_b, step_second))
+    cotangent_part = lax.dynamic_slice_in_dim(cotangent_b, row_start, half, 0)
+    cotangent_all = lax.all_gather(cotangent_part, "seq", axis=0, tiled=True)
 
     my_starts = jnp.max(
         jnp.where(my_rows[:, None] >= start_rows[None, :], start_rows[None, :], 0), axis=1
     )
     bounds = jnp.stack([my_starts, my_rows], axis=1).astype(jnp.int32)
     key_blocks = (my_rows[-1:] // KEY_ROWS + 1).astype(jnp.int32)
-
-    decay_rate = -jnp.exp(log_decay)
-    scan_rate = pad_to(decay_rate * log2_e, 1, 2 * CHUNKS).T
-
-    def blocked(lines):
-        return jnp.stack([lines[:, :CHUNKS], pad_to(lines[:, CHUNKS:], 1, CHUNKS)])
-
-    def unblocked(blocks):
-        return jnp.concatenate([blocks[0], blocks[1][:, : inner - CHUNKS]], axis=1)
 
     attended, mass, attended_wide, attn_pre = on_core(
         0,
@@ -1855,38 +2771,17 @@
         ),
     )
 
+    col_rows = slice(rank - PROJ_CUT, proj - PROJ_CUT)
+
     def mamba_core():
-        projected = whole_projection(middle)
-        step_low = projected[:rank].astype(low)
-        step_pre = contract(step_low, weight_step, 0, 1) + step_bias
-        steps = jax.nn.softplus(step_pre)
-        inputs_full = inputs_b.astype(jnp.float32)
-        cols = projected[rank:proj].reshape(2 * states, CHUNKS, STEPS).transpose(0, 2, 1)
-        scanned, starts, decay_t, drive_t = scan_forward(
-            blocked(jnp.where(keep_rows[:, None], steps, far_away)),
-            blocked(steps * inputs_full),
-            cols,
-            scan_rate,
-            inner,
+        cols = step_second[:, col_rows].transpose(1, 0, 2).reshape(-1, CHUNKS, STEPS)
+        cols = cols.transpose(0, 2, 1)
+        results = mixer_forward(
+            inner, step_first, step_second, cols, channel, inputs_b, reset, gate_z, back_wide
         )
-        ssm_out = unblocked(scanned)
-        mixed_y = halves_first(gate_mix(ssm_out, skip_gain, inputs_full, gate_z).astype(low))
-        weight_back = rows_of(begun.back_all, inner_piece)
-        return (
-            matmul(mixed_y, weight_back).astype(low),
-            step_low,
-            step_pre,
-            ssm_out,
-            mixed_y,
-            cols,
-            starts,
-            decay_t,
-            drive_t,
-        )
-
-    partial, step_low, step_pre, ssm_out, mixed_y, cols, starts, decay_t, drive_t = on_core(
-        1, mamba_core
-    )
+        return [cols] + list(results)
+
+    cols, partial, mixed_y, ssm_out, starts, decay_t, drive_t, scan_rate = on_core(1, mamba_core)
 
     mixers = exchange(
         "exchange_mixers",
@@ -1896,7 +2791,7 @@
             partial=(partial.reshape(2, SIDE, SIDE, half, width), ANY),
             attn_pre=(attn_pre, ANY),
             gate_first=(keyval.gate_own, ANY),
-            gate_second=(middle.gate_own, ANY),
+            gate_second=(gate_second, ANY),
             down=(down_in, ANY),
         ),
         dict(
@@ -1908,11 +2803,7 @@
         dict(pad=half_pad(half, width)),
         vmem=32 * 2**20,
     )
-    weight_gate = mixers.gate_all.transpose(0, 2, 3, 1, 4, 5).reshape(2, 64, 32, units)
-    weight_gate = weight_gate[:, :, :piece].reshape(2, width, units)
-    weight_down = rows_of(mixers.down_all, down_piece)
-
-    tokens_part = lax.dynamic_slice_in_dim(inputs_f, row_start, half, 0)
+    tokens_part = lax.dynamic_slice_in_dim(tokens_b, row_start, half, 0).astype(full)
     sent = rms_norm(mixers.attn_half, gain_attn).astype(low).astype(jnp.float32)
     sent = sent + rms_norm(mixers.mamba_pre, gain_mamba).astype(low).astype(jnp.float32)
     hidden = tokens_part + 0.5 * sent
@@ -1923,18 +2814,12 @@
         dict(feed=(rms_norm(hidden, gain_feed).astype(low), ANY)),
         dict(feed_all=((SIDE, SIDE, half, width), low, ANY)),
     ).feed_all.reshape(16 * half, width)
-    gate = matmul(feed, weight_gate[0])
-    up = matmul(feed, weight_gate[1])
-    active, pull_glu = jax.vjp(swiglu, gate, up)
-    active_b = active.astype(low)
-    out_partial = matmul(active_b, weight_down).astype(low)
-    grad_gate, grad_up = pull_glu(matmul_nt(cotangent_all, weight_down))
-    grad_gate, grad_up = grad_gate.astype(low), grad_up.astype(low)
-    feed_partial = (matmul_nt(grad_gate, weight_gate[0]) + matmul_nt(grad_up, weight_gate[1])).astype(
-        low
-    )
-    grad_down = matmul_tn(active_b, cotangent_all)
-    grad_weight_gate = (matmul_tn(feed, grad_gate), matmul_tn(feed, grad_up))
+    out_partial, feed_partial, g_gate, g_down = feed_forward(
+        feed,
+        cotangent_all,
+        mixers.gate_all.reshape(2, 64 * 32, units),
+        mixers.down_all.reshape(units, width),
+    )
     ffn = exchange(
         "exchange_ffn",
         6,
@@ -1947,7 +2832,7 @@
             out_sum=((half, width), jnp.float32, VMEM),
             grad_sum=((half, width), jnp.float32, VMEM),
         ),
-        dict(out_pad=two_pad(half, width), grad_pad=two_pad(half, width)),
+        dict(out_pad=ring_pad(half, width), grad_pad=ring_pad(half, width)),
         vmem=48 * 2**20,
     )
     mixed_part = (hidden + ffn.out_sum).astype(low)
@@ -1961,10 +2846,6 @@
     _, pull_mamba = jax.vjp(rms_norm, mixers.mamba_pre, gain_mamba)
     grad_mamba_pre, grad_gain_mamba = pull_mamba(grad_sent)
 
-    g_gate = jnp.stack(grad_weight_gate).reshape(2, 16, SIDE, piece, units)
-    g_gate = pad_to(g_gate.transpose(0, 2, 1, 3, 4), 3, 32).astype(low)
-    g_down = pad_to(grad_down.reshape(SIDE, down_piece, width), 1, 96)
-    g_down = g_down.reshape(SIDE, 2, 1, 48, width).transpose(1, 0, 2, 3, 4).astype(low)
     back = exchange(
         "exchange_back",
         7,
@@ -1989,7 +2870,6 @@
         vmem=32 * 2**20,
     )
     mixed = back.mixed_both.reshape(rows, width)
-    grad_hidden_all = back.g_hidden_both.reshape(rows, width)
     g_gate_own = back.g_gate_sum.reshape(SIDE, SIDE, 32, units)
 
     cuts = (8 * LANES, 9 * LANES, query_most + width - 17 * LANES)
@@ -2001,7 +2881,7 @@
             query_b,
             keyval_all,
             meta_kv,
-            bounds,
+            bounds.T,
             attended,
             mass,
             g_pre,
@@ -2020,166 +2900,113 @@
     def cubed(blocks):
         return blocks.reshape(cube + (32, blocks.shape[-1]))
 
+    small_cuts = (keys_width // 2, keys_width // 2, metas)
+    sources = (
+        grad_query_b,
+        normed_wide,
+        meta_wide,
+        grad_meta_kv,
+        weight_one,
+        weight_two,
+        meta_f,
+        gain_row,
+    )
     attention = exchange(
         "exchange_attention",
         8,
         program_attention,
         dict(
             keyval=(grad_keyval.reshape(SIDE, SIDE, rows, keys_width), ANY),
+            gate=(g_gate_own, ANY),
             one=(cubed(sum_one), ANY),
             two=(cubed(sum_two), ANY),
             three=(cubed(sum_three), ANY),
-            gate=(g_gate_own, ANY),
+            sources={name: (array, ANY) for name, array in zip(INSIDE, sources)},
         ),
         dict(
-            keyval_sum=((rows, keys_width), full, VMEM),
+            gate_own=((SIDE, SIDE, 32, units), low, ANY),
             sums=((32, query_most + width), full, VMEM),
-            gate_own=((SIDE, SIDE, 32, units), low, ANY),
+            keys_sum=((32, keys_width + metas), full, VMEM),
+            g_normed=((rows, width), full, VMEM),
+            gain_part=((64 * 32, 1), full, VMEM),
+            meta_gain=((1, width), full, VMEM),
         ),
         dict(
-            keyval_pad=two_pad(rows, keys_width),
-            one_pad=three_pad(32, cuts[0]),
-            two_pad=three_pad(32, cuts[1]),
-            three_pad=three_pad(32, cuts[2]),
-            one_sum=((32, cuts[0]), full),
-            two_sum=((32, cuts[1]), full),
-            three_sum=((32, cuts[2]), full),
+            upper_pad=two_pad(half, keys_width),
+            lower_pad=two_pad(half, keys_width),
             gate_mid=((SIDE, SIDE, 32, units), low),
-        ),
-        vmem=60 * 2**20,
+            keyval_sum=((rows, keys_width), full),
+            inside={name: (array.shape, array.dtype) for name, array in zip(INSIDE, sources)},
+            keys=dict(zip(SUMS[3:], (((64 * 32, cut), low) for cut in small_cuts))),
+            pads=dict(zip(SUMS, (three_pad(32, cut) for cut in cuts + small_cuts))),
+            parts=dict(zip(SUMS, (((32, cut), full) for cut in cuts + small_cuts))),
+        ),
+        vmem=62 * 2**20,
         cores=(0,),
     )
-
-    keys_one, keys_two, meta_out, grad_normed_attn, gain_keys, gain_meta = on_core(
-        0,
-        lambda: attention_inputs(
-            attention.keyval_sum,
-            grad_query_b,
-            normed_wide,
-            meta_wide,
-            grad_meta_kv,
-            weight_one,
-            weight_two,
-            meta_f,
-            gain_row,
-        ),
-    )
-    gain_attention = (gain_query + gain_keys).reshape(64, 32)[:, :piece].reshape(width)
-    gain_attention = gain_attention / gain_norm + gain_meta[0]
-    keys = exchange(
-        "exchange_keys",
-        9,
-        program_keys,
-        dict(
-            one=(cubed(keys_one), ANY),
-            two=(cubed(keys_two), ANY),
-            three=(cubed(meta_out), ANY),
-        ),
-        dict(
-            one_sum=((32, keys_width // 2), full, VMEM),
-            two_sum=((32, keys_width // 2), full, VMEM),
-            three_sum=((32, metas), full, VMEM),
-        ),
-        dict(
-            one_pad=three_pad(32, keys_width // 2),
-            two_pad=three_pad(32, keys_width // 2),
-            three_pad=three_pad(32, metas),
-        ),
-        vmem=32 * 2**20,
-        cores=(0,),
-    )
+    gain_attention = (gain_query + attention.gain_part).reshape(64, 32)[:, :piece].reshape(width)
+    gain_attention = gain_attention / gain_norm + attention.meta_gain[0]
 
     def mamba_back_one():
-        grad_pre_b = back.g_mamba_all.reshape(group, width)
-        grad_weight_back = matmul_tn(mixed_y, grad_pre_b)
-        weight_back = rows_of(begun.back_all, inner_piece)
-        grad_mixed = places_first(matmul_nt(grad_pre_b, weight_back))
-        inputs_full = inputs_b.astype(jnp.float32)
-        _, pull_gate = jax.vjp(gate_mix, ssm_out, skip_gain, inputs_full, gate_z)
-        grad_ssm, grad_skip, grad_inputs, grad_gate_z = pull_gate(grad_mixed)
-        steps = jax.nn.softplus(step_pre)
-        grad_decay, grad_drive, grad_cols, grad_rate = scan_backward(
-            decay_t, drive_t, cols, scan_rate, starts, blocked(grad_ssm), inner
+        g_first, g_second, g_cols, *rest = mixer_backward(
+            inner,
+            step_first,
+            step_second,
+            cols,
+            channel,
+            inputs_b,
+            gate_z,
+            back_wide,
+            back.g_mamba_all.reshape(2, 16, half, width),
+            mixed_y,
+            ssm_out,
+            starts,
+            decay_t,
+            drive_t,
+            scan_rate,
         )
-        grad_drive = unblocked(grad_drive)
-        grad_steps = unblocked(grad_decay) * (1.0 / log2_e) + grad_drive * inputs_full
-        grad_inputs = grad_inputs + grad_drive * steps
-        grad_step_pre = grad_steps * jax.nn.sigmoid(step_pre)
-        grad_step_b = grad_step_pre.astype(low)
-        grad_step_low = contract(weight_step, grad_step_b, 0, 1)
-        grad_cols = grad_cols.transpose(0, 2, 1).reshape(2 * states, group)
-        grad_proj = pad_to(jnp.concatenate([grad_step_low, grad_cols], axis=0), 0, proj_pad)
-        grad_proj = grad_proj.reshape(proj_pad, SIDE, SIDE, rows).transpose(1, 2, 0, 3)
-        return (
-            grad_proj[:, :, :proj_cut],
-            grad_proj[:, :, proj_cut:],
-            padded_blocks(grad_weight_back, SIDE, 64)[:, None],
+        g_cols = g_cols.transpose(0, 2, 1).reshape(-1, 16, rows).transpose(1, 0, 2)
+        g_second = jnp.concatenate([g_second[:, : rank - PROJ_CUT], g_cols], axis=1)
+        return [g_first, pad_to(g_second, 1, proj_pad - PROJ_CUT)] + list(rest)
+
+    g_first, g_second, grad_inputs, grad_gate_z, back_out, grad_rows, grad_rate = on_core(
+        1, mamba_back_one
+    )
+    g_first, g_second, last_gate = spread_projection(
+        "exchange_last", 9, g_first, g_second, g_gate_own
+    )
+
+    def mamba_back_two():
+        g_normed, g_weight, g_rows, gain = mixer_inputs(
+            g_first,
+            g_second,
+            channel,
+            weight_mamba,
+            normed_all,
+            conv_in,
+            inputs_b,
             grad_inputs,
-            grad_gate_z.astype(low),
-            grad_skip,
-            jnp.sum(grad_step_pre, axis=0),
-            grad_rate[:inner] * decay_rate.T,
-            contract(grad_step_b, step_low, 0, 1),
+            grad_gate_z,
+            dist,
+            left,
         )
-
-    (
-        proj_first,
-        proj_second,
-        back_out,
-        grad_inputs,
-        grad_gate_z,
-        grad_skip,
-        grad_step_bias,
-        grad_log_decay,
-        grad_weight_step,
-    ) = on_core(1, mamba_back_one)
-    last = spread_projection("exchange_last", 10, proj_first, proj_second, g_gate_own)
-
-    def mamba_back_two():
-        grad_proj_b = whole_projection(last)[:proj].astype(low)
-        grad_weight_ssm = contract(inputs_b, grad_proj_b, 0, 1)
-        grad_inputs_all = grad_inputs + contract(grad_proj_b, weight_ssm, 0, 1)
-
-        def conv_only(conv_arg, taps_arg, offset_arg):
-            return conv_silu(conv_arg, taps_arg, offset_arg, valid_rows)
-
-        _, pull_conv = jax.vjp(conv_only, conv_in.astype(full), conv_taps, conv_offset)
-        grad_conv, grad_taps, grad_offset = pull_conv(grad_inputs_all)
-        grad_mixed_in = halves_first(jnp.concatenate([grad_conv.astype(low), grad_gate_z], axis=1))
-        grad_weight_mamba = matmul_tn(normed_all, grad_mixed_in)
-        grad_normed = matmul_nt(grad_mixed_in, weight_mamba).astype(low)
-        channel_out = jnp.concatenate(
-            [
-                grad_weight_ssm,
-                grad_taps.T,
-                jnp.stack([grad_offset, grad_step_bias, grad_skip], axis=1),
-                grad_log_decay,
-                grad_weight_step,
-            ],
-            axis=1,
-        )
-        mamba_out = grad_weight_mamba.reshape(16, SIDE, piece, 2 * inner).transpose(1, 0, 2, 3)
-        return (
-            grad_normed,
-            pad_to(mamba_out, 2, 32).astype(low),
-            pad_to(padded_blocks(channel_out, SIDE, 64, full), 2, 256)[:, None],
-            jnp.sum(grad_weight_mamba * weight_mamba.astype(full), axis=1) / gain_norm,
-        )
+        return g_normed, g_weight, channel_grads(grad_rows, g_rows, grad_rate, channel), gain
 
     grad_normed_partial, mamba_out, channel_out, gain_mixer = on_core(1, mamba_back_two)
+    gain_mixer = gain_mixer[:, 0] / gain_norm
     grad_gain_norm = jnp.where(on_attention, gain_attention, gain_mixer)
     gains_out = jnp.stack([grad_gain_norm, grad_gain_attn, grad_gain_mamba, grad_gain_feed], axis=1)
     gains_out = padded_blocks(pad_to(gains_out, 1, 128), 64, 32)
     ended = exchange(
         "exchange_end",
-        11,
+        1,
         program_end,
         dict(
             partial=(grad_normed_partial.reshape(2, SIDE, SIDE, half, width), ANY),
-            g_attn=(grad_normed_attn, ANY),
+            g_attn=(attention.g_normed, ANY),
             sums_in=(attention.sums, ANY),
-            keys=(jnp.concatenate([keys.one_sum, keys.two_sum, keys.three_sum], axis=1), ANY),
-            gate=(jnp.where(on_attention, attention.gate_own, last.gate_own), ANY),
+            keys=(attention.keys_sum, ANY),
+            gate=(jnp.where(on_attention, attention.gate_own, last_gate), ANY),
             down=(back.g_down_sum.reshape(48, width), ANY),
             mamba=(mamba_out, ANY),
             back=(back_out, ANY),
@@ -2193,9 +3020,9 @@
             keys_sum=((32, keys_width + metas), full, ANY),
             gate_both=((2, SIDE, SIDE, 32, units), low, ANY),
             down_both=((2, 48, width), full, ANY),
-            mamba_sum=((SIDE, SIDE, 32, 2 * inner), low, ANY),
+            mamba_sum=((SIDE, SIDE, 32, 4 * CHUNKS), low, ANY),
             back_sum=((1, 64, width), full, VMEM),
-            channel_sum=((1, 64, 256), full, VMEM),
+            channel_sum=((1, 64, 3 * LANES), full, VMEM),
             gains_both=((2, 32, 128), full, ANY),
         ),
         dict(
@@ -2203,48 +3030,73 @@
             normed_sum=((half, width), full),
             gains_pad=three_pad(32, 128),
             gains_sum=((32, 128), full),
-            mamba_pad=x_pad(16, 32, 2 * inner),
-            mamba_part=((SIDE, SIDE, 32, 2 * inner), low),
-            mamba_mid=((SIDE, SIDE, 32, 2 * inner), low),
+            mamba_pad=x_pad(16, 32, 4 * CHUNKS),
+            mamba_part=((SIDE, SIDE, 32, 4 * CHUNKS), low),
+            mamba_mid=((SIDE, SIDE, 32, 4 * CHUNKS), low),
             back_pad=x_pad(1, 64, width),
-            channel_pad=x_pad(1, 64, 256, full),
+            channel_pad=x_pad(1, 64, 3 * LANES, full),
         ),
         vmem=48 * 2**20,
     )
-    grad_normed = ended.normed_both.reshape(rows, width) + ended.g_attn_both
-    _, pull_input = jax.vjp(lambda rows_in: rms_norm(rows_in, gain_norm), inputs_f)
-    input_grad = grad_hidden_all + pull_input(grad_normed)[0]
-    gains_sum = (ended.gains_both[0] + ended.gains_both[1])[:piece]
-    keys_sum = ended.keys_sum[:piece]
-    grad_keys = keys_sum[:, :keys_width].reshape(piece, -1, 2, HEAD).transpose(0, 2, 1, 3)
-    grad_keys = grad_keys.reshape(piece, keys_width)
-    grad_mamba_in = ended.mamba_sum.reshape(16, 32, 2, inner)[:, :piece]
-    grad_mamba_in = grad_mamba_in.transpose(1, 2, 0, 3).reshape(piece, 2 * 16 * inner)
-    grad_gate_up = ended.gate_both.reshape(2, 16, 32, units)[:, :, :piece]
-    grad_gate_up = grad_gate_up.transpose(2, 0, 1, 3).reshape(piece, 2 * 16 * units)
-    channel_sum = ended.channel_sum[0, :inner_piece]
+    (
+        input_grad,
+        grad_query,
+        grad_keyval_in,
+        grad_attn,
+        grad_mamba,
+        grad_back,
+        grad_gate,
+        grad_down,
+        grad_meta,
+        grad_ssm,
+        grad_step,
+        grad_log,
+        grad_taps,
+        grad_rows,
+        grad_gains,
+    ) = finish(
+        piece,
+        inner_piece,
+        down_piece,
+        inner,
+        proj,
+        rank,
+        tokens_b,
+        gain_row,
+        back.g_hidden_both,
+        ended.normed_both,
+        ended.g_attn_both,
+        ended.sums,
+        ended.keys_sum,
+        ended.mamba_sum.reshape(16, 32, -1),
+        ended.back_sum,
+        ended.channel_sum,
+        ended.gate_both.reshape(2, 16, 32, units),
+        ended.down_both,
+        ended.gains_both,
+    )
     return (
         mixed[None],
         input_grad[None],
-        gains_sum[:, 0],
-        keys_sum[:, keys_width:].T,
-        ended.sums[:piece, :query_width],
-        grad_keys,
-        ended.sums[:piece, query_most:],
-        gains_sum[:, 1],
-        grad_mamba_in.astype(full),
-        channel_sum[:, proj : proj + CONV].T,
-        channel_sum[:, proj + CONV],
-        channel_sum[:, :proj],
-        channel_sum[:, first_log + states : first_log + states + rank].T,
-        channel_sum[:, proj + CONV + 1],
-        channel_sum[:, first_log : first_log + states].T,
-        channel_sum[:, proj + CONV + 2],
-        ended.back_sum[0, :inner_piece],
-        gains_sum[:, 2],
-        gains_sum[:, 3],
-        grad_gate_up.astype(full),
-        ended.down_both.reshape(96, width)[:down_piece],
+        grad_gains[0],
+        grad_meta,
+        grad_query,
+        grad_keyval_in,
+        grad_attn,
+        grad_gains[1],
+        grad_mamba,
+        grad_taps,
+        grad_rows[4],
+        grad_ssm,
+        grad_step,
+        grad_rows[5],
+        grad_log,
+        grad_rows[6],
+        grad_back,
+        grad_gains[2],
+        grad_gains[3],
+        grad_gate,
+        grad_down,
     )
 
 

time: 819 us -> 643 us (0.79)
  local copies, waits for them, and re-layouts: 179 us -> 58.3 us
  Pallas kernels: 456 us -> 547 us
  matrix products: 83.8 us -> 0 us
  other arithmetic: 62.9 us -> 8.11 us
    pallas_call x2 -> x9, Pallas kernels: 76.7 us -> 192 us  [the longest x7 153 us: whole_call(): pl.pallas_call(body, out_shape=[jax.ShapeDtypeStruct(shape, kind) for sha...]
    dot_general x21 -> x0, matrix products: 83.8 us -> none  [contract(): lax.dot_general(left, right, (((left_dim,), (right_dim,)), ((), ())), **o...]
    convert_element_type x19 -> x0, other arithmetic: 31.9 us -> none  [the longest x2 12.1 us: mamba_first(): normed_b = rms_norm(begun.tokens_all.reshape(group, width).astype(jnp.flo...]
    pallas_call x12 -> x10, Pallas kernels: 379 us -> 355 us  [exchange(): pl.pallas_call(kernel, out_shape=[jax.ShapeDtypeStruct(s, d) for s, d, _...]
    another operation x33 -> x3, local copies, waits for them, and re-layouts: 25.5 us -> 2.07 us
    cond x49 -> x13, local copies, waits for them, and re-layouts: 24 us -> 0.9 us
    reshape x22 -> x3, local copies, waits for them, and re-layouts: 24.1 us -> 2.61 us  [the longest x1 2.4 us: mamba_core(): step_second[:, col_rows].transpose(1, 0, 2).reshape(-1, CHUNKS, STEPS)]
    convert_element_type x12 -> x0, local copies, waits for them, and re-layouts: 20.1 us -> none  [the longest x1 5.44 us: shards(): (matmul_nt(grad_gate, weight_gate[0]) + matmul_nt(grad_up, weight_gate[1]...]
  transfers between devices with their start and end apart: 1 -> 1, of which waited for: 0 -> 0; matrix products, arithmetic and copies ran while one was open for 15% -> 1% of each run, Pallas kernels for 27% -> 20%
where the time goes in v2:
time: 643 us; the launch traced here: 632 us
  Pallas kernels  547 us (85%)
  local copies, waits for them, and re-layouts  58.3 us (9%)
  between operations  17.4 us (3%)
  other arithmetic  8.11 us (1%)
    pallas_call x10, Pallas kernels, exchange(): pl.pallas_call(kernel, out_shape=[jax.ShapeDtypeStruct(s, d) for s, d, _...  355 us
    pallas_call x7, Pallas kernels, whole_call(): pl.pallas_call(body, out_shape=[jax.ShapeDtypeStruct(shape, kind) for sha...  153 us
    unnamed x95, local copies, waits for them, and re-layouts  35.1 us
    pallas_call x1, Pallas kernels, mixer_inputs(): pl.pallas_call(mixer_inputs_kernel, grid=(places // count,), out_shape=[j...  20.5 us
    pallas_call x1, Pallas kernels, mixer_project(): pl.pallas_call(mixer_project_kernel, grid=(places,), out_shape=[jax.Shape...  18.6 us
  transfers between devices with their start and end apart: 1, of which 0 were waited for; matrix products, arithmetic and copies ran while one was open for 1% of the time, Pallas kernels for 20%

profile of v2, /device:TPU:1, one launch (start us, length us, event | category | flops | bytes accessed | tf_op | source)
XLA Modules:
  0.0 631.8 jit_solution(9352514818034941989)
XLA Ops:
  7.3 1.3 copy.108
  8.6 1.4 copy.109
  11.7 1.1 copy-done.10
  12.8 1.1 copy-done.11
  13.9 1.0 copy-done.15
  24.4 3.0 prepare.1
  31.6 61.4 %exchange_start.1 = (bf16[2,4,4,64,1600]{4,3,2,1,0:T(8,128)(2,1)}, bf16[4,4,4,32,256]{4,3,2,1,0:T(8,128)(2,1)}, bf16[4,4,4,32,512]{4,3,2,1,0:T(8,128)(2,1)}, bf1...) custom-call(bf16[128,1600]{1,0:T(8,128)(2,1)S(1)} %bitcast.141, ...), custom_call_target="tpu_custom_call" | custom-call | tf_op jit(solution)/shard_map/exchange_start/pallas_call | solution.py:412
  93.0 1.2 copy-done.9
  94.2 1.6 unpack.1
  96.2 19.0 %conditional.7 = ((bf16[2048,1600]{1,0:T(8,128)(2,1)}, bf16[2048,256]{1,0:T(8,128)(2,1)}, f32[2048,256]{1,0:T(8,128)}, bf16[2048,256]{1,0:T(8,128)(2,1)}, f32[16...) conditional(s32[]{:T(128)} %convert_element_type.51, () %tuple.107, ...), branch_computations={%region_2.3_spmd, %region_3.4_spmd} | conditional | bytes 16392 | solution.py:2687
  96.6 18.6 %mixer_project.1 = (bf16[2048,1600]{1,0:T(8,128)(2,1)}, bf16[2048,256]{1,0:T(8,128)(2,1)}, f32[2048,256]{1,0:T(8,128)}, bf16[2048,256]{1,0:T(8,128)(2,1)}, f32[1...) custom-call(bf16[2,16,64,1600]{3,2,1,0:T(8,128)(2,1)} %bitcast.146, ...), custom_call_target="tpu_custom_call" | custom-call | tf_op jit(solution)/shard_map/cond/branch_1_fun/mixer_project/pallas_call | solution.py:1306
  115.2 23.9 %exchange_project.1 = (f32[4,4,72,128]{3,2,1,0:T(8,128)}, f32[4,4,64,128]{3,2,1,0:T(8,128)}, bf16[4,4,32,384]{3,2,1,0:T(8,128)(2,1)S(1)}) custom-call(f32[4,4,72,128]{3,2,1,0:T(8,128)} %bitcast.42.refs_0_, f32[4,4,64,128]{3,2,1,0:T(8,128)} %bitcast.43.refs_1_, bf16[4,4,32,384]{3,2,1,0:T(8,128)(2,1)S(1)} %bitcast.109), custom_call_target="tpu_custom_call" | custom-call | tf_op jit(solution)/shard_map/exchange_project/pallas_call | solution.py:412
  143.1 49.6 %conditional.8 = (f32[32,16,128]{2,1,0:T(8,128)}, bf16[2048,256]{1,0:T(8,128)(2,1)}, f32[2,2048,128]{2,1,0:T(8,128)}, f32[16,256,128]{2,1,0:T(8,128)}, f32[16,25...) conditional(s32[]{:T(128)} %convert_element_type.51, () %tuple.110, ...), branch_computations={%region_4.5_spmd, %region_5.6_spmd} | conditional | flops 4096 | bytes 13271160 | solution.py:2687
  143.1 1.0 slice_bitcast_fusion
  144.1 1.3 copy.101
  145.5 2.4 copy.102
  147.8 1.3 copy.114
  149.2 1.4 compare_select_fusion.reset_ref
  150.7 42.1 %mixer_forward.2 = (bf16[2,16,64,1600]{3,2,1,0:T(8,128)(2,1)}, bf16[2048,256]{1,0:T(8,128)(2,1)}, f32[2,2048,128]{2,1,0:T(8,128)}, f32[16,256,128]{2,1,0:T(8,128...) custom-call(f32[16,72,128]{2,1,0:T(8,128)} %get-tuple-element.275.first_ref, ...), custom_call_target="tpu_custom_call" | custom-call | tf_op jit(solution)/shard_map/cond/branch_1_fun/mixer_forward/pallas_call | solution.py:692
  192.9 2.4 exchange_keyval.1
  196.5 48.9 %exchange_mixers.1 = (f32[64,1600]{1,0:T(8,128)S(1)}, f32[64,1600]{1,0:T(8,128)S(1)}, bf16[2,4,4,4,32,384]{5,4,3,2,1,0:T(8,128)(2,1)S(1)}, bf16[4,96,1600]{2,1,0:T(8,128)(2,1)S(1)}) custom-call(bf16[2,4,4,64,1600]{4,3,2,1,0:T(8,128)(2,1)} %bitcast.144, f32[128,1600]{1,0:T(8,128)} %get-tuple-element.547.refs_1_, bf16[4,4,32,384]{3,2,1,0:T(8,128)(2,1)S(1)} %copy-done.14, ...), custom_call_target="tpu_custom_call" | custom-call | tf_op jit(solution)/shard_map/exchange_mixers/pallas_call | solution.py:412
  245.4 1.7 copy-done.2
  247.1 1.0 copy-done.8
  249.4 31.3 %exchange_feed.1 = bf16[4,4,64,1600]{3,2,1,0:T(8,128)(2,1)} custom-call(bf16[64,1600]{1,0:T(8,128)(2,1)} %multiply_convert_fusion.refs_0_), custom_call_target="tpu_custom_call" | custom-call | tf_op jit(solution)/shard_map/exchange_feed/pallas_call | solution.py:412
  280.8 25.4 %feed_forward.1 = (bf16[1024,1600]{1,0:T(8,128)(2,1)}, bf16[1024,1600]{1,0:T(8,128)(2,1)}, bf16[2,4,16,32,384]{4,3,2,1,0:T(8,128)(2,1)}, bf16[2,4,1,48,1600]{4,3,2,1,0:T(8,128)(2,1)}) custom-call(bf16[1024,1600]{1,0:T(8,128)(2,1)} %bitcast.138, bf16[1024,1600]{1,0:T(8,128)(2,1)} %all-gather.2.cloned.1.call-done.cot_ref, bf16[2,2048,384]{2,1,0:T(8,128)(2,1)} %bitcast.106, ...), custom_call_target="tpu_custom_call" | custom-call | tf_op jit(solution)/shard_map/feed_forward/pallas_call | solution.py:692
  306.1 2.0 copy-done
  308.1 45.5 %exchange_ffn.1 = (f32[64,1600]{1,0:T(8,128)S(1)}, f32[64,1600]{1,0:T(8,128)S(1)}) custom-call(bf16[4,4,64,1600]{3,2,1,0:T(8,128)(2,1)S(1)} %bitcast.105, bf16[4,4,64,1600]{3,2,1,0:T(8,128)(2,1)} %bitcast.156), custom_call_target="tpu_custom_call" | custom-call | tf_op jit(solution)/shard_map/exchange_ffn/pallas_call | solution.py:412
  355.9 51.7 %exchange_back.1 = (bf16[2,4,4,64,1600]{4,3,2,1,0:T(8,128)(2,1)}, bf16[2,64,1600]{2,1,0:T(8,128)(2,1)}, bf16[2,64,1600]{2,1,0:T(8,128)(2,1)S(1)}, f32[2,64,1600]...) custom-call(bf16[64,1600]{1,0:T(8,128)(2,1)S(1)} %get-tuple-element.907.refs_0_, ...), custom_call_target="tpu_custom_call" | custom-call | tf_op jit(solution)/shard_map/exchange_back/pallas_call | solution.py:412
  408.3 0.9 copy.120
  409.7 12.1 %exchange_attention.1 = (bf16[4,4,32,384]{3,2,1,0:T(8,128)(2,1)}, f32[32,3264]{1,0:T(8,128)}, f32[32,768]{1,0:T(8,128)}, f32[128,1600]{1,0:T(8,128)}, f32[2048,1]{1,0:T(8,128)}, /*index=5*/f32[1,1600]{1,0:T(1,128)}) custom-call(bf16[4,4,128,640]{3,2,1,0:T(8,128)(2,1)} %get-tuple-element.589.refs_0_, bf16[4,4,32,384]{3,2,1,0:T(8,128)(2,1)} %bitcast.110, ...), custom_call_target="tpu_custom_call" | custom-call | tf_op jit(solution)/shard_map/exchange_attention/pallas_call | solution.py:412
  421.9 1.9 add_reduce_fusion
  424.0 79.2 %conditional.11 = (f32[2048,256]{1,0:T(8,128)}, bf16[2048,256]{1,0:T(8,128)(2,1)}, bf16[4,1,64,1600]{3,2,1,0:T(8,128)(2,1)}, f32[128,256]{1,0:T(8,128)S(1)}, f32...) conditional(s32[]{:T(128)} %convert_element_type.51, () %tuple.117, ...), branch_computations={%region_17.18_spmd, %region_18.19_spmd} | conditional | flops 122880 | bytes 5537880 | solution.py:2687
  424.0 74.0 %mixer_backward.1 = (f32[16,72,128]{2,1,0:T(8,128)}, f32[16,32,128]{2,1,0:T(8,128)}, f32[32,16,128]{2,1,0:T(8,128)}, f32[2048,256]{1,0:T(8,128)}, bf16[2048,256]...) custom-call(f32[16,72,128]{2,1,0:T(8,128)} %get-tuple-element.307.first_ref, ...), custom_call_target="tpu_custom_call" | custom-call | tf_op jit(solution)/shard_map/cond/branch_1_fun/mixer_backward/pallas_call | solution.py:692
  498.0 2.4 copy.104
  500.4 1.6 copy.106
  503.2 27.5 %exchange_last.1 = (f32[4,4,72,128]{3,2,1,0:T(8,128)}, f32[4,4,64,128]{3,2,1,0:T(8,128)}, bf16[4,4,32,384]{3,2,1,0:T(8,128)(2,1)S(1)}) custom-call(f32[4,4,72,128]{3,2,1,0:T(8,128)} %bitcast.62.refs_0_, f32[4,4,64,128]{3,2,1,0:T(8,128)} %get-tuple-element.890.refs_1_, bf16[4,4,32,384]{3,2,1,0:T(8,128)(2,1)S(1)} %bitcast.111), custom_call_target="tpu_custom_call" | custom-call | tf_op jit(solution)/shard_map/exchange_last/pallas_call | solution.py:412
  530.7 1.0 iota.21
  531.7 26.4 %conditional.12 = (bf16[4,16,32,512]{3,2,1,0:T(8,128)(2,1)}, f32[4,1,64,384]{3,2,1,0:T(8,128)S(1)}, f32[1600,1]{1,0:T(8,128)}, bf16[2,16,64,1600]{3,2,1,0:T(8,128)(2,1)}) conditional(s32[]{:T(128)} %convert_element_type.51, () %tuple.116, (f32[4,4,72,128]{3,2,1,0:T(8,128)}, f32[4,4,64,128]{3,2,1,0:T(8,128)}, s32[3,1]{0,1:T(1,128)S(1)}, ...), branch_computations={%region_19.20_spmd, %region_20.22_spmd} | conditional | flops 20480 | bytes 12755072 | solution.py:2687
  532.2 1.4 copy.107
  533.6 1.8 sub.27.later_ref
  536.1 20.5 %mixer_inputs.2 = (bf16[2,16,64,1600]{3,2,1,0:T(8,128)(2,1)}, bf16[4,16,32,512]{3,2,1,0:T(8,128)(2,1)}, f32[384,256]{1,0:T(8,128)S(1)}, f32[1600,1]{1,0:T(8,128)}) custom-call(f32[16,72,128]{2,1,0:T(8,128)} %bitcast.168, f32[16,64,128]{2,1,0:T(8,128)} %bitcast.169, f32[384,256]{1,0:T(8,128)} %get-tuple-element.335.channel_ref, ...), custom_call_target="tpu_custom_call" | custom-call | tf_op jit(solution)/shard_map/cond/branch_1_fun/mixer_inputs/pallas_call | solution.py:1717
  556.6 1.4 channel_grads.2
  558.9 1.5 copy.118
  561.6 1.9 reshape.352
  563.6 1.3 pad.15
  565.3 49.9 %exchange_end.1 = (f32[2,64,1600]{2,1,0:T(8,128)S(1)}, f32[128,1600]{1,0:T(8,128)}, f32[32,3264]{1,0:T(8,128)S(1)}, f32[32,768]{1,0:T(8,128)S(1)}, bf16[2,4,4,32...) custom-call(bf16[2,4,4,64,1600]{4,3,2,1,0:T(8,128)(2,1)} %bitcast.14, ...), custom_call_target="tpu_custom_call" | custom-call | tf_op jit(solution)/shard_map/exchange_end/pallas_call | solution.py:412
  615.2 5.9 finish.1
  621.1 1.2 copy.121
  (150 shorter events, 31.0 us)
Async XLA Ops:
  7.2 4.5 copy-start.6
  7.2 273.5 %all-gather.2.cloned.1.call-start = ((), (), s32[]{:S(2)}) async-start(), calls=%async_computation | async-start | bytes 3620864 | tf_op jit(solution)/shard_map/all_gather | solution.py:2759
  8.6 130.6 %copy-start.41 = (bf16[1,128,1600]{2,1,0:T(8,128)(2,1)}, bf16[1,128,1600]{2,1,0:T(8,128)(2,1)S(1)}, u32[]{:S(2)}) copy-start(bf16[1,128,1600]{2,1,0:T(8,128)(2,1)S(1)} %copy.108) | copy-start | bytes 1228804
  11.7 1.1 copy-start.10
  12.8 1.1 copy-start.11
  13.9 1.0 copy-start.15
  14.9 0.9 copy-start.20
  15.8 0.9 copy-start.21
  16.8 0.9 copy-start.23
  17.6 0.8 copy-start.24
  18.5 0.7 copy-start.27
  19.2 0.7 copy-start.28
  19.8 0.7 copy-start.29
  20.5 0.7 copy-start.30
  21.2 0.7 copy-start.31
  21.8 0.7 copy-start.32
  22.5 0.7 copy-start.33
  23.1 0.7 copy-start.34
  23.8 0.7 copy-start.35
  24.4 71.4 %copy-start.50 = (s32[1,3]{1,0:T(1,128)S(1)}, s32[1,3]{1,0:T(1,128)}, u32[]{:S(2)}) copy-start(s32[1,3]{1,0:T(1,128)} %param.37) | copy-start | bytes 40
  27.4 0.8 copy-start.12
  28.2 0.7 copy-start.16
  29.0 0.7 copy-start.18
  29.6 0.7 copy-start.19
  31.6 64.7 %copy-start.3 = (bf16[2,16,32,384]{3,2,1,0:T(8,128)(2,1)}, bf16[2,16,32,384]{3,2,1,0:T(8,128)(2,1)S(1)}, u32[]{:S(2)}) copy-start(bf16[2,16,32,384]{3,2,1,0:T(8,128)(2,1)S(1)} %get-tuple-element.529) | copy-start | bytes 2359300
  93.0 1.2 copy-start.9
  144.1 6.5 %copy-start.36 = (f32[2048,256]{1,0:T(8,128)S(1)}, f32[2048,256]{1,0:T(8,128)}, u32[]{:S(2)}) copy-start(f32[2048,256]{1,0:T(8,128)} %get-tuple-element.279.gate_ref) | copy-start | bytes 6291460 | tf_op jit(solution)/shard_map/cond
  149.2 1.5 copy-start.37
  195.4 1.0 copy-start.14
  195.4 1.1 copy-start.17
  245.4 1.7 copy-start.2
  247.1 1.0 copy-start.8
  306.1 2.0 copy-start
  308.1 45.7 %copy-start.42 = (bf16[1,128,1600]{2,1,0:T(8,128)(2,1)S(1)}, bf16[1,128,1600]{2,1,0:T(8,128)(2,1)}, u32[]{:S(2)}) copy-start(bf16[1,128,1600]{2,1,0:T(8,128)(2,1)} %copy-done.41) | copy-start | bytes 1228804
  353.6 1.9 copy-start.1
  353.6 2.2 copy-start.7
  407.5 0.8 copy-start.4
  409.7 14.3 %copy-start.47 = (f32[256,16]{1,0:T(8,128)S(1)}, f32[256,16]{1,0:T(8,128)}, u32[]{:S(2)}) copy-start(f32[256,16]{1,0:T(8,128)} %get-tuple-element.658) | copy-start | bytes 49156
  424.0 79.2 %copy-start.5 = (bf16[16,32,384]{2,1,0:T(8,128)(2,1)S(1)}, bf16[16,32,384]{2,1,0:T(8,128)(2,1)}, u32[]{:S(2)}) copy-start(bf16[16,32,384]{2,1,0:T(8,128)(2,1)} %copy-done.4) | copy-start | bytes 1179652
  498.0 4.0 copy-start.46
  531.7 28.7 %copy-start.49 = (f32[1,1600]{1,0:T(1,128)S(1)}, f32[1,1600]{1,0:T(1,128)}, u32[]{:S(2)}) copy-start(f32[1,1600]{1,0:T(1,128)} %get-tuple-element.607) | copy-start | bytes 19204
  533.6 2.2 copy-start.38
  533.6 2.5 copy-start.44
  536.1 20.5 %copy-start.48 = (f32[256,16]{1,0:T(8,128)S(1)}, f32[256,16]{1,0:T(8,128)}, u32[]{:S(2)}) copy-start(f32[256,16]{1,0:T(8,128)} %get-tuple-element.349.rate_ref) | copy-start | bytes 49156 | tf_op jit(solution)/shard_map/cond
  558.2 0.7 copy-start.45
  558.9 6.0 copy-start.13
  558.9 6.0 copy-start.22
  563.5 1.7 copy-start.39
  (2 other events, 1.2 us)
Sparse Core Ops, SparseCore 0:
  140.0 47.7 all-gather.1

commit v3 on v2

--- a/solution.py
+++ b/solution.py
@@ -22,7 +22,7 @@
 VMEM = pl.BlockSpec(memory_space=pltpu.VMEM)
 SEMS = 128
 HOPS = (1, 3, 2)
-X, Y, Z = range(3)
+X, Y, Z, FIRST, SECOND = range(5)
 
 
 class Net:
@@ -34,9 +34,15 @@
         self.recv = recv
         self.begun = []
 
-    def device(self, axis=None, hop=0, other_core=False):
+    def device(self, axis=None, hop=0, other_core=False, partner=False):
         place = dict(self.at)
-        if axis is not None:
+        if partner:
+            place[Y], place[Z] = SIDE - 1 - place[Y], SIDE - 1 - place[Z]
+        if axis in (FIRST, SECOND):
+            along_z = self.core == (0 if axis == FIRST else 1)
+            place[Y] = jnp.where(along_z, place[Y], (place[Y] + hop) % SIDE)
+            place[Z] = jnp.where(along_z, (place[Z] + hop) % SIDE, place[Z])
+        elif axis is not None:
             place[axis] = (place[axis] + hop) % SIDE
         core = 1 - self.core if other_core else self.core
         return (core, place[Y] * SIDE + place[Z], place[X])
@@ -227,40 +233,40 @@
     )
 
 
-def reduce_ring(net, name, source, pad, out, order):
+def reduce_ring(net, name, source, pad, out):
     at = net.at
     rows = source.shape[2]
     half = rows // 2
     halves = {1: pl.ds(0, half), 3: pl.ds(half, half)}
     stages = (
-        (order[0], pad.one, pad.via_one, pad.mix_one),
-        (order[1], pad.two, pad.via_two, pad.mix_two),
+        (FIRST, pad.one, pad.via_one, pad.mix_one),
+        (SECOND, pad.two, pad.via_two, pad.mix_two),
     )
 
     def lines(stage, place, part):
-        if stage == 1:
-            return pad.mid.at[place, part]
-        if order[0] == Z:
-            return source.at[:, place, part]
-        return source.at[place, :, part]
+        return pad.mid.at[place, part] if stage else source.at[place, :, part]
 
     whole = pl.ds(0, rows)
-    own = net.local((name, -4), lines(0, at[order[0]], whole), pad.own)
     for stage, (axis, recv, via, mix) in enumerate(stages):
 
         def spot(hop, axis=axis):
             return (at[axis] + hop) % SIDE
 
         arrivals, fetched, passing = [], [], []
+        if stage == 0:
+            yield
         for i, hop in enumerate(NEAR):
-            device = net.device(axis, hop)
             across = lines(stage, spot(2), halves[hop])
-            passing.append(net.start((name, stage, 0, hop), across, via.at[i], device))
+            passing.append(
+                net.start((name, stage, 0, hop), across, via.at[i], net.device(axis, hop))
+            )
+        for i, hop in enumerate(NEAR):
+            if stage == 0:
+                yield
+            other = halves[4 - hop]
             fetched.append(
                 net.local((name, stage, 3, hop), lines(stage, spot(hop), halves[hop]), mix.at[i])
             )
-        for i, hop in enumerate(NEAR):
-            other = halves[4 - hop]
             target = recv.at[i, other] if stage else recv.at[i, :, other]
             arrivals.append(
                 net.start(
@@ -270,6 +276,9 @@
                     net.device(axis, hop),
                 )
             )
+        if stage == 0:
+            yield
+            own = net.local((name, -4), lines(0, spot(0), whole), pad.own)
         yield
         for i, hop in enumerate(NEAR):
             fetched[i].wait()
@@ -305,7 +314,7 @@
                 [lambda lead, part, k=k: pad.one[k, lead, part, :] for k in range(2)],
                 put_mid,
             )
-    mine = at[order[1]]
+    mine = at[SECOND]
 
     def put_out(lead, part, value):
         out[part, :] = value.astype(out.dtype)
@@ -375,7 +384,18 @@
     )
 
 
-def exchange(name, number, program, inputs, outputs, scratch=None, vmem=None, cores=(0, 1)):
+def exchange(
+    name,
+    number,
+    program,
+    inputs,
+    outputs,
+    scratch=None,
+    vmem=None,
+    cores=(0, 1),
+    shared=False,
+    partners=(),
+):
     scratch = scratch or {}
     parts = (inputs, outputs, scratch)
     counts = [len(flat(part)) for part in parts]
@@ -391,21 +411,28 @@
         seq = lax.axis_index("seq")
         coords = {X: lax.axis_index("fsdp"), Y: seq // SIDE, Z: seq % SIDE}
         names = {}
-        for one_core in cores:
-
-            @pl.when(core == one_core)
-            def _():
-                net = Net(one_core, coords, names, send, recv)
-                barrier = pltpu.get_barrier_semaphore()
-                peers = [net.device(axis, hop) for axis in (X, Y, Z) for hop in HOPS]
-                if len(cores) == 2:
-                    peers.append(net.device(other_core=True))
-                for peer in peers:
-                    pl.semaphore_signal(barrier, inc=1, device_id=peer, device_id_type=MESH)
-                pl.semaphore_wait(barrier, len(peers))
-                run_jobs(program(net, held))
-                for copy in net.begun:
-                    copy.wait_send()
+
+        def run(own_core):
+            net = Net(own_core, coords, names, send, recv)
+            barrier = pltpu.get_barrier_semaphore()
+            peers = [net.device(axis, hop) for axis in (X, Y, Z) for hop in HOPS]
+            if len(cores) == 2:
+                peers.append(net.device(other_core=True))
+            peers += [net.device(other_core=other, partner=True) for other in partners]
+            for peer in peers:
+                pl.semaphore_signal(barrier, inc=1, device_id=peer, device_id_type=MESH)
+            pl.semaphore_wait(barrier, len(peers))
+            run_jobs(program(net, held))
+            for copy in net.begun:
+                copy.wait_send()
+
+        if shared:
+            coords[FIRST] = jnp.where(core == 0, coords[Z], coords[Y])
+            coords[SECOND] = jnp.where(core == 0, coords[Y], coords[Z])
+            run(core)
+        else:
+            for one_core in cores:
+                pl.when(core == one_core)(functools.partial(run, one_core))
 
         assert len(names) <= SEMS
 
@@ -501,6 +528,10 @@
     used, decay_ref, drive_ref, cols_ref, rate_ref, out_ref, start_ref, decay_t, drive_t, out_t
 ):
     states = rate_ref.shape[1]
+
+    def col(l, s):
+        return cols_ref[l, pl.ds(FIRST_COL + s, 1), :]
+
     to_lanes(decay_ref, decay_t)
     to_lanes(drive_ref, drive_t)
     out_t[...] = jnp.zeros_like(out_t)
@@ -511,9 +542,9 @@
         drives = [drive_t[l, lines, :] for l in range(STEPS)]
         rates = rate_lines(rate_ref, lines, states)
         for s in range(states):
-            state = drives[0] * cols_ref[s, 0:1, :]
+            state = drives[0] * col(0, s)
             for l in range(1, STEPS):
-                state = jnp.exp2(decays[l] * rates[s]) * state + drives[l] * cols_ref[s, l : l + 1, :]
+                state = jnp.exp2(decays[l] * rates[s]) * state + drives[l] * col(l, s)
             start_ref[s, lines, :] = state
         return carry
 
@@ -529,8 +560,8 @@
         for s in range(states):
             state = start_ref[s, lines, :]
             for l in range(STEPS):
-                state = jnp.exp2(decays[l] * rates[s]) * state + drives[l] * cols_ref[s, l : l + 1, :]
-                outs[l] = outs[l] + state * cols_ref[states + s, l : l + 1, :]
+                state = jnp.exp2(decays[l] * rates[s]) * state + drives[l] * col(l, s)
+                outs[l] = outs[l] + state * col(l, states + s)
         for l in range(STEPS):
             out_t[l, lines, :] = outs[l]
         return carry
@@ -558,6 +589,10 @@
     ends_t,
 ):
     states = rate_ref.shape[1]
+
+    def col(l, s):
+        return cols_ref[l, pl.ds(FIRST_COL + s, 1), :]
+
     blank = jnp.zeros((LINES, CHUNKS), jnp.float32)
     to_lanes(grad_ref, grad_t)
     g_decay_t[...] = jnp.zeros_like(g_decay_t)
@@ -575,7 +610,7 @@
             back = blank
             for l in reversed(range(STEPS)):
                 back = jnp.exp2(decays[l] * rates[s]) * (
-                    grads[l] * cols_ref[states + s, l : l + 1, :] + back
+                    grads[l] * col(l, states + s) + back
                 )
             ends_t[s, lines, :] = back
         return carry
@@ -596,15 +631,15 @@
                 factor = jnp.exp2(decay_t[l, lines, :] * rate)
                 befores.append(state)
                 factors.append(factor)
-                state = factor * state + drive_t[l, lines, :] * cols_ref[s, pl.ds(l, 1), :]
+                state = factor * state + drive_t[l, lines, :] * col(l, s)
             back = ends_t[s, lines, :]
             total_rate = blank
             for l in reversed(range(STEPS)):
                 grad = grad_t[l, lines, :]
-                total = grad * cols_ref[states + s, pl.ds(l, 1), :] + back
+                total = grad * col(l, states + s) + back
                 sums_t[s, l] += total * drive_t[l, lines, :]
                 sums_t[states + s, l] += grad * state
-                g_drive_t[l, lines, :] += total * cols_ref[s, pl.ds(l, 1), :]
+                g_drive_t[l, lines, :] += total * col(l, s)
                 back = total * factors[l]
                 moved = back * befores[l]
                 g_decay_t[l, lines, :] += moved * rate
@@ -620,11 +655,8 @@
 
     lax.fori_loop(0, used // LINES, channels, 0)
 
-    def collapse(i, carry):
-        g_cols_ref[i] = jnp.sum(sums_t[i], axis=1)
-        return carry
-
-    lax.fori_loop(0, 2 * states, collapse, 0)
+    for i in range(2 * states):
+        g_cols_ref[:, FIRST_COL + i, :] = jnp.sum(sums_t[i], axis=1)
     to_rows(g_decay_t, g_decay_ref)
     to_rows(g_drive_t, g_drive_ref)
 
@@ -688,14 +720,32 @@
     return values * lax.rsqrt(jnp.mean(values * values, axis=-1, keepdims=True) + epsilon)
 
 
-def whole_call(name, body, arrays, results, scratch=(), scalars=0, room=48):
+def whole_call(name, body, arrays, results, scratch=(), scalars=0, room=48, fetch=False):
+    count = len(arrays)
+    scratch_shapes = [pltpu.VMEM(shape, kind) for shape, kind in scratch]
+
+    def fetching(*refs):
+        sources, middle, held = refs[:count], refs[count : -count - 1], refs[-count - 1 : -1]
+        copies = [
+            pltpu.make_async_copy(source, target, refs[-1].at[i])
+            for i, (source, target) in enumerate(zip(sources, held))
+        ]
+        for copy in copies:
+            copy.start()
+        for copy in copies:
+            copy.wait()
+        body(*held, *middle)
+
+    if fetch:
+        scratch_shapes += [pltpu.VMEM(array.shape, array.dtype) for array in arrays]
+        scratch_shapes.append(pltpu.SemaphoreType.DMA((count,)))
     return pl.pallas_call(
-        body,
+        fetching if fetch else body,
         out_shape=[jax.ShapeDtypeStruct(shape, kind) for shape, kind in results],
         in_specs=[pl.BlockSpec(memory_space=pltpu.SMEM)] * scalars
-        + [VMEM] * (len(arrays) - scalars),
+        + [ANY if fetch else VMEM] * (count - scalars),
         out_specs=[VMEM] * len(results),
-        scratch_shapes=[pltpu.VMEM(shape, kind) for shape, kind in scratch],
+        scratch_shapes=scratch_shapes,
         compiler_params=pltpu.CompilerParams(vmem_limit_bytes=room * 2**20),
         name=name,
     )(*arrays)
@@ -768,7 +818,7 @@
     gain = gain + jnp.sum(
         one[:, third:] * second_ref[:, pl.ds(0, rest)].astype(jnp.float32), axis=1, keepdims=True
     )
-    gain_ref[...] = gain
+    gain_ref[...] = gain.T
     two = dot_on(out_wide_ref[...], g_pre_ref[...], 0, 0)
     size = one.shape[1] - cut
     begin = -(-size // LANES) * LANES
@@ -791,11 +841,11 @@
         attention_weights_kernel,
         grid=(places // size,),
         out_shape=[jax.ShapeDtypeStruct((places, cut), jnp.bfloat16) for cut in cuts]
-        + [jax.ShapeDtypeStruct((places, 1), jnp.float32)],
+        + [jax.ShapeDtypeStruct((1, places), jnp.float32)],
         in_specs=[columns, columns]
         + [pl.BlockSpec(part.shape, lambda i: (0, 0)) for part in (g_query, g_pre)]
         + [lines(first.shape[1]), lines(second.shape[1])],
-        out_specs=[lines(cut) for cut in cuts] + [lines(1)],
+        out_specs=[lines(cut) for cut in cuts] + [pl.BlockSpec((1, size), lambda i: (0, i))],
         compiler_params=pltpu.CompilerParams(vmem_limit_bytes=32 * 2**20),
         name="attention_weights",
     )(wide, out_wide, g_query, g_pre, first, second)
@@ -817,6 +867,8 @@
     g_normed_ref,
     part_ref,
     meta_gain_ref,
+    g_wide_ref,
+    g_meta_wide_ref,
 ):
     third = first_ref.shape[1]
     rest = g_query_ref.shape[1] - third
@@ -827,13 +879,13 @@
     half = one_ref.shape[1]
     places = wide_ref.shape[1]
     size = places // 4
-    g_normed, g_meta_normed = [], []
-    for i in range(4):
-        spot = pl.ds(i * size, size)
+
+    def part_of(i, carry):
+        spot = pl.ds(pl.multiple_of(i * size, size), size)
         weight = second_ref[spot, keys]
         weight_f = weight.astype(jnp.float32)
         grad = dot_on(wide_ref[:, spot], keyval, 0, 0)
-        part_ref[spot, :] = jnp.sum(grad * weight_f, axis=1, keepdims=True)
+        part_ref[:, spot] = jnp.sum(grad * weight_f, axis=1, keepdims=True).T
         grad = grad + dot_on(
             meta_wide_ref[:, spot].astype(jnp.float32), g_meta, 0, 0, precision=highest
         )
@@ -843,10 +895,13 @@
         total = total + dot_on(
             g_query_ref[:, pl.ds(third, rest)], second_ref[spot, pl.ds(0, rest)], 1, 1
         )
-        g_normed.append(total + dot_on(keyval, weight, 1, 1))
-        g_meta_normed.append(dot_on(g_meta, weight_f, 1, 1, precision=highest))
-    g_normed_ref[...] = close_columns(jnp.concatenate(g_normed, axis=1))
-    g_meta_normed = close_columns(jnp.concatenate(g_meta_normed, axis=1))
+        g_wide_ref[:, spot] = total + dot_on(keyval, weight, 1, 1)
+        g_meta_wide_ref[:, spot] = dot_on(g_meta, weight_f, 1, 1, precision=highest)
+        return carry
+
+    lax.fori_loop(0, 4, part_of, 0)
+    g_normed_ref[...] = close_columns(g_wide_ref[...])
+    g_meta_normed = close_columns(g_meta_wide_ref[...])
     meta = meta_ref[...]
     scale = lax.rsqrt(jnp.mean(meta * meta, axis=-1, keepdims=True) + epsilon)
     unit = meta * scale
@@ -860,43 +915,48 @@
 
 
 def stack_heads(source, target, scale, in_values):
-    rows = source.shape[0]
+    half = source.shape[0] // 2
     groups = target.shape[0]
-    per = target.shape[1] // rows
-    blank = jnp.zeros((rows, HEAD), target.dtype)
+    per = target.shape[1] // (2 * half)
+    blank = jnp.zeros((half, HEAD), target.dtype)
     for group in range(groups):
         for j in range(per):
             head = source[:, pl.ds((group * per + j) * HEAD, HEAD)].astype(jnp.float32) * scale
             head = head.astype(target.dtype)
-            pair = [blank, head] if in_values else [head, blank]
-            target[group, pl.ds(j * rows, rows), :] = jnp.concatenate(pair, axis=1)
+            for part in range(2):
+                value = head[part * half : (part + 1) * half]
+                pair = [blank, value] if in_values else [value, blank]
+                target[group, pl.ds((part * per + j) * half, half), :] = jnp.concatenate(
+                    pair, axis=1
+                )
 
 
 def lay_keys(source, target):
-    rows = source.shape[2]
+    places, rows = source.shape[1:3]
 
     def move(place, carry):
         for half in range(2):
             begin = pl.multiple_of((place * 2 + half) * rows, rows)
-            target[pl.ds(begin, rows), :] = source[half, place]
+            target[pl.ds(begin, rows), :] = source[half, (places - 1 - place) if half else place]
         return carry
 
-    lax.fori_loop(0, source.shape[1], move, 0)
-
-
-def key_bias(bounds_ref, begin, per):
-    rows = bounds_ref.shape[0]
+    lax.fori_loop(0, places, move, 0)
+
+
+def key_bias(bounds_ref, part, begin, per):
+    rows = bounds_ref.shape[0] // 2
+    spot = pl.ds(part * rows, rows)
     keys = begin + lax.broadcasted_iota(jnp.int32, (rows, KEY_ROWS), 1)
-    allowed = (keys >= bounds_ref[:, 0:1]) & (keys <= bounds_ref[:, 1:2])
+    allowed = (keys >= bounds_ref[spot, 0:1]) & (keys <= bounds_ref[spot, 1:2])
     bias = jnp.where(allowed, 0.0, negative_fill)
     return jnp.concatenate([bias] * per, axis=0)
 
 
-def key_bias_turned(bounds_ref, begin, per):
-    rows = bounds_ref.shape[1]
-    keys = begin + lax.broadcasted_iota(jnp.int32, (KEY_ROWS, rows), 0)
+def key_bias_turned(bounds_ref, part, begin, per):
+    rows = bounds_ref.shape[1] // 2
+    keys = begin + lax.broadcasted_iota(jnp.int32, (KEY_ROWS, 2 * rows), 0)
     allowed = (keys >= bounds_ref[0:1, :]) & (keys <= bounds_ref[1:2, :])
-    bias = jnp.where(allowed, 0.0, negative_fill)
+    bias = jnp.where(allowed, 0.0, negative_fill)[:, part * rows : (part + 1) * rows]
     return jnp.concatenate([bias] * per, axis=1)
 
 
@@ -915,55 +975,74 @@
     heads,
     keys,
     scores,
+    tops,
+    totals,
+    outs,
 ):
-    rows = query_ref.shape[0]
+    half = query_ref.shape[0] // 2
     groups = heads.shape[0]
-    per = heads.shape[1] // rows
+    per = heads.shape[1] // (2 * half)
+    stack = per * half
     width = 2 * HEAD
     metas = meta_ref.shape[0]
-    meta_part = pl.ds(scores.shape[1] - metas, metas)
+    meta_part = pl.ds(scores.shape[2] - metas, metas)
     stack_heads(query_ref, heads, score_scale, False)
     lay_keys(keyval_ref, keys)
-    count = count_ref[0]
-    lanes = lax.broadcasted_iota(jnp.int32, mass_ref.shape, 1)
-    for group in range(groups):
-        part = pl.ds(group * width, width)
-        query = heads[group]
-
-        def score(b, top):
+    lanes = lax.broadcasted_iota(jnp.int32, (stack, mass_ref.shape[1]), 1)
+    parts = [pl.ds(group * width, width) for group in range(groups)]
+
+    def across(values):
+        return [values[:, i : i + LANES] for i in range(0, values.shape[1], LANES)]
+
+    for side in range(2):
+        stacked = pl.ds(side * stack, stack)
+        count = count_ref[side]
+        for group in range(groups):
+            value = dot_on(heads[group, stacked, :], meta_ref[:, parts[group]], 1, 1)
+            scores[group, :, meta_part] = value
+            tops[group] = value
+
+        def score(b, carry):
             begin = pl.multiple_of(b * KEY_ROWS, KEY_ROWS)
-            value = dot_on(query, keys[pl.ds(begin, KEY_ROWS), part], 1, 1)
-            value = value + key_bias(bounds_ref, begin, per)
-            scores[:, pl.ds(begin, KEY_ROWS)] = value
-            return jnp.maximum(top, jnp.max(value, axis=1, keepdims=True))
-
-        value = dot_on(query, meta_ref[:, part], 1, 1)
-        scores[:, meta_part] = value
-        top = lax.fori_loop(0, count, score, jnp.max(value, axis=1, keepdims=True))
+            bias = key_bias(bounds_ref, side, begin, per)
+            for group in range(groups):
+                block = keys[pl.ds(begin, KEY_ROWS), parts[group]]
+                value = dot_on(heads[group, stacked, :], block, 1, 1) + bias
+                scores[group, :, pl.ds(begin, KEY_ROWS)] = value
+                tops[group] = functools.reduce(jnp.maximum, across(value), tops[group])
+            return carry
+
+        lax.fori_loop(0, count, score, 0)
+        for group in range(groups):
+            top = jnp.max(tops[group], axis=1, keepdims=True)
+            tops[group] = jnp.broadcast_to(top, tops.shape[1:])
+            value = jnp.exp(scores[group, :, meta_part] - tops[group])
+            totals[group] = value
+            outs[group] = dot_on(value.astype(jnp.bfloat16), meta_ref[:, parts[group]], 1, 0)
 
         def weigh(b, carry):
-            total, out = carry
             begin = pl.multiple_of(b * KEY_ROWS, KEY_ROWS)
-            value = jnp.exp(scores[:, pl.ds(begin, KEY_ROWS)] - top)
-            out = out + dot_on(
-                value.astype(jnp.bfloat16), keys[pl.ds(begin, KEY_ROWS), part], 1, 0
-            )
-            return (total + jnp.sum(value, axis=1, keepdims=True), out)
-
-        value = jnp.exp(scores[:, meta_part] - top)
-        carry = (
-            jnp.sum(value, axis=1, keepdims=True),
-            dot_on(value.astype(jnp.bfloat16), meta_ref[:, part], 1, 0),
-        )
-        total, out = lax.fori_loop(0, count, weigh, carry)
-        out = out * (1.0 / total)
-        for j in range(per):
-            out_ref[:, pl.ds((group * per + j) * HEAD, HEAD)] = out[
-                j * rows : (j + 1) * rows, HEAD:
-            ]
-        mass = top + jnp.log(total)
-        before = mass_ref[...] if group else jnp.zeros_like(mass_ref)
-        mass_ref[...] = jnp.where(lanes == group, mass, before)
+            for group in range(groups):
+                top = tops[group]
+                value = [
+                    jnp.exp(piece - top) for piece in across(scores[group, :, pl.ds(begin, KEY_ROWS)])
+                ]
+                totals[group] += sum(value)
+                value = jnp.concatenate(value, axis=1).astype(jnp.bfloat16)
+                outs[group] += dot_on(value, keys[pl.ds(begin, KEY_ROWS), parts[group]], 1, 0)
+            return carry
+
+        lax.fori_loop(0, count, weigh, 0)
+        mass = jnp.zeros(lanes.shape, jnp.float32)
+        for group in range(groups):
+            total = jnp.sum(totals[group], axis=1, keepdims=True)
+            out = outs[group] * (1.0 / total)
+            for j in range(per):
+                out_ref[pl.ds(side * half, half), pl.ds((group * per + j) * HEAD, HEAD)] = out[
+                    j * half : (j + 1) * half, HEAD:
+                ]
+            mass = jnp.where(lanes == group, tops[group] + jnp.log(total), mass)
+        mass_ref[stacked, :] = mass
     wide = spread_columns(out_ref[...].astype(jnp.bfloat16))
     wide_ref[...] = wide
     most = third_ref.shape[1]
@@ -993,9 +1072,11 @@
         (
             ((groups, stacked, 2 * HEAD), low),
             ((key_rows, meta.shape[1]), low),
-            ((stacked, key_rows + meta.shape[0]), full),
+            ((groups, stacked // 2, key_rows + meta.shape[0]), full),
+            *[((groups, stacked // 2, LANES), full)] * 3,
         ),
         scalars=1,
+        room=60,
     )
 
 
@@ -1017,10 +1098,13 @@
     grads,
     keys,
     grad_ref,
+    g_keys,
+    g_queries,
 ):
-    rows = query_ref.shape[0]
+    half = query_ref.shape[0] // 2
     groups = heads.shape[0]
-    per = heads.shape[1] // rows
+    per = heads.shape[1] // (2 * half)
+    stack = per * half
     width = 2 * HEAD
     most = third_ref.shape[1]
     left = g_pre_ref.shape[1] - most
@@ -1035,48 +1119,70 @@
     stack_heads(query_ref, heads, score_scale, False)
     stack_heads(grad_ref, grads, 1.0, True)
     lay_keys(keyval_ref, keys)
-    g_keyval_ref[...] = jnp.zeros_like(g_keyval_ref)
-    count = count_ref[0]
-    lanes = lax.broadcasted_iota(jnp.int32, mass_ref.shape, 1)
-    for group in range(groups):
-        part = pl.ds(group * width, width)
-        query, grad = heads[group], grads[group]
-        mass = jnp.sum(jnp.where(lanes == group, mass_ref[...], 0.0), axis=1, keepdims=True)
-        balance = []
-        for j in range(per):
-            head = pl.ds((group * per + j) * HEAD, HEAD)
-            balance.append(
-                jnp.sum(grad_ref[:, head].astype(jnp.float32) * out_ref[:, head], axis=1, keepdims=True)
+    g_keys[...] = jnp.zeros_like(g_keys)
+    lanes = lax.broadcasted_iota(jnp.int32, (stack, mass_ref.shape[1]), 1)
+    parts = [pl.ds(group * width, width) for group in range(groups)]
+    for side in range(2):
+        stacked = pl.ds(side * stack, stack)
+        rows = pl.ds(side * half, half)
+        mass_rows, balance_rows = [], []
+        for group in range(groups):
+            mass = jnp.sum(
+                jnp.where(lanes == group, mass_ref[stacked, :], 0.0), axis=1, keepdims=True
             )
-        balance = jnp.concatenate(balance, axis=0)
-
-        mass_row, balance_row = mass.T, balance.T
-
-        def pieces(block, bias):
+            balance = []
+            for j in range(per):
+                head = pl.ds((group * per + j) * HEAD, HEAD)
+                product = grad_ref[rows, head].astype(jnp.float32) * out_ref[rows, head]
+                balance.append(jnp.sum(product, axis=1, keepdims=True))
+            mass_rows.append(mass.T)
+            balance_rows.append(jnp.concatenate(balance, axis=0).T)
+
+        def pieces(group, block, bias):
+            query, grad = heads[group, stacked, :], grads[group, stacked, :]
             value = dot_on(block, query, 1, 1)
             if bias is not None:
                 value = value + bias
-            probs = jnp.exp(value - mass_row)
-            g_scores = (probs * (dot_on(block, grad, 1, 1) - balance_row)).astype(jnp.bfloat16)
+            probs = jnp.exp(value - mass_rows[group])
+            g_scores = probs * (dot_on(block, grad, 1, 1) - balance_rows[group])
+            g_scores = g_scores.astype(jnp.bfloat16)
             g_block = dot_on(g_scores, query, 1, 0) + dot_on(probs.astype(jnp.bfloat16), grad, 1, 0)
             return dot_on(g_scores, block, 0, 0), g_block
 
-        g_query, g_meta = pieces(meta_ref[:, part], None)
-        g_meta_ref[:, part] = g_meta
-
-        def step(b, g_query):
+        for group in range(groups):
+            g_queries[group], g_meta = pieces(group, meta_ref[:, parts[group]], None)
+            if side:
+                g_meta = g_meta + g_meta_ref[:, parts[group]]
+            g_meta_ref[:, parts[group]] = g_meta
+
+        def step(b, carry):
             begin = pl.multiple_of(b * KEY_ROWS, KEY_ROWS)
-            more, g_block = pieces(
-                keys[pl.ds(begin, KEY_ROWS), part], key_bias_turned(bounds_ref, begin, per)
-            )
-            g_keyval_ref[pl.ds(begin, KEY_ROWS), part] = g_block.astype(jnp.bfloat16)
-            return g_query + more
-
-        g_query = lax.fori_loop(0, count, step, g_query) * score_scale
-        for j in range(per):
-            g_query_ref[:, pl.ds((group * per + j) * HEAD, HEAD)] = g_query[
-                j * rows : (j + 1) * rows, :HEAD
+            bias = key_bias_turned(bounds_ref, side, begin, per)
+            for group in range(groups):
+                block = keys[pl.ds(begin, KEY_ROWS), parts[group]]
+                more, g_block = pieces(group, block, bias)
+                g_queries[group] += more
+                g_keys[pl.ds(begin, KEY_ROWS), parts[group]] += g_block
+            return carry
+
+        lax.fori_loop(0, count_ref[side], step, 0)
+        for group in range(groups):
+            g_query = g_queries[group] * score_scale
+            for j in range(per):
+                g_query_ref[rows, pl.ds((group * per + j) * HEAD, HEAD)] = g_query[
+                    j * half : (j + 1) * half, :HEAD
+                ].astype(jnp.bfloat16)
+    places = g_keyval_ref.shape[1]
+
+    def spread(place, carry):
+        for side in range(2):
+            begin = pl.multiple_of((place * 2 + side) * half, half)
+            g_keyval_ref[side, (places - 1 - place) if side else place] = g_keys[
+                pl.ds(begin, half), :
             ].astype(jnp.bfloat16)
+        return carry
+
+    lax.fori_loop(0, places, spread, 0)
 
 
 def attend_backward(count, query, keyval, meta, bounds, out, mass, g_pre, second, third):
@@ -1091,7 +1197,7 @@
         (count, query, keyval, meta, bounds, out, mass, g_pre, second, third),
         (
             ((rows, query_width), low),
-            ((key_rows, meta.shape[1]), low),
+            (keyval.shape, low),
             (meta.shape, jnp.float32),
         ),
         (
@@ -1099,6 +1205,8 @@
             ((groups, stacked, 2 * HEAD), low),
             ((key_rows, meta.shape[1]), low),
             ((rows, query_width), low),
+            ((key_rows, meta.shape[1]), jnp.float32),
+            ((groups, stacked // 2, 2 * HEAD), jnp.float32),
         ),
         scalars=1,
         room=56,
@@ -1127,87 +1235,65 @@
         put(n, dot_on(matrix, source(low, high), 0, 0).astype(jnp.bfloat16))
 
 
-def ffn_kernel(
-    feed_ref,
-    cot_ref,
-    gate_ref,
-    down_ref,
-    out_ref,
-    g_feed_ref,
-    g_gate_ref,
-    g_down_ref,
-    gate_w,
-    up_w,
-    active_s,
-    g_gate_s,
-    g_up_s,
-    sums,
-):
-    rows, size = feed_ref.shape[0], 256
-    places = gate_ref.shape[1]
-    for part, target in enumerate((gate_w, up_w)):
-        close_rows(lambda low, high: gate_ref[part, pl.ds(low, high - low), :], target, places)
-
-    def block(i, carry):
-        spot = pl.ds(pl.multiple_of(i * size, size), size)
-        feed = feed_ref[spot, :]
-        gate = dot_on(feed, gate_w[...], 1, 0)
-        up = dot_on(feed, up_w[...], 1, 0)
-        share = jax.nn.sigmoid(gate)
-        silu = gate * share
-        active = (silu * up).astype(jnp.bfloat16)
-        active_s[spot, :] = active
-        out_ref[spot, :] = dot_on(active, down_ref[...], 1, 0).astype(jnp.bfloat16)
-        g_active = dot_on(cot_ref[spot, :], down_ref[...], 1, 1)
-        g_gate = (g_active * up * (share + silu * (1.0 - share))).astype(jnp.bfloat16)
-        g_up = (g_active * silu).astype(jnp.bfloat16)
-        g_gate_s[spot, :] = g_gate
-        g_up_s[spot, :] = g_up
-        g_feed = dot_on(g_gate, gate_w[...], 1, 1) + dot_on(g_up, up_w[...], 1, 1)
-        g_feed_ref[spot, :] = g_feed.astype(jnp.bfloat16)
-        return carry
-
-    lax.fori_loop(0, rows // size, block, 0)
-    for part, grad in enumerate((g_gate_s, g_up_s)):
-        sums[...] = dot_on(feed_ref[...], grad[...], 0, 0).astype(jnp.bfloat16)
-
-        def put(n, value):
-            for x in range(SIDE):
-                g_gate_ref[part, x, n] = value[x * PADDED : (x + 1) * PADDED]
-
-        spread_rows(lambda low, high: sums[pl.ds(low, high - low), :], put)
-    g_down = dot_on(active_s[...], cot_ref[...], 0, 0).astype(jnp.bfloat16)
-    size = g_down_ref.shape[3]
+def feed_forward_open(held):
+    for part, target in enumerate((held.gate_w, held.up_w)):
+        close_rows(
+            lambda low, high: held.gate[part, pl.ds(low, high - low), :], target, held.gate.shape[1]
+        )
+
+
+def feed_forward_line(held, core, line):
+    low = jnp.bfloat16
+    size = held.feed.shape[2]
+
+    def spot(i):
+        return (jnp.where(core == 0, i, line), jnp.where(core == 0, line, i))
+
+    feed = jnp.concatenate([held.feed[spot(i)] for i in range(SIDE)], axis=0)
+    gate = dot_on(feed, held.gate_w[...], 1, 0)
+    up = dot_on(feed, held.up_w[...], 1, 0)
+    share = jax.nn.sigmoid(gate)
+    silu = gate * share
+    active = (silu * up).astype(low)
+    out = dot_on(active, held.down[...], 1, 0).astype(low)
+    cot = jnp.concatenate([held.cot[spot(i)] for i in range(SIDE)], axis=0)
+    g_active = dot_on(cot, held.down[...], 1, 1)
+    g_gate = (g_active * up * (share + silu * (1.0 - share))).astype(low)
+    g_up = (g_active * silu).astype(low)
+    g_feed = dot_on(g_gate, held.gate_w[...], 1, 1) + dot_on(g_up, held.up_w[...], 1, 1)
+    g_feed = g_feed.astype(low)
+    for i in range(SIDE):
+        rows = slice(i * size, (i + 1) * size)
+        held.out[line, i] = out[rows]
+        held.g_feed[line, i] = g_feed[rows]
+        held.active[spot(i)] = active[rows]
+        held.g_parts[(0,) + spot(i)] = g_gate[rows]
+        held.g_parts[(1,) + spot(i)] = g_up[rows]
+
+
+def all_rows(ref):
+    return ref.reshape(16 * ref.shape[2], ref.shape[3])[...]
+
+
+def feed_forward_gate(held, part):
+    held.products[...] = dot_on(all_rows(held.feed), all_rows(held.g_parts.at[part]), 0, 0).astype(
+        jnp.bfloat16
+    )
+
+    def put(n, value):
+        for x in range(SIDE):
+            held.g_gate[part, x, n] = value[x * PADDED : (x + 1) * PADDED]
+
+    spread_rows(lambda low, high: held.products[pl.ds(low, high - low), :], put)
+
+
+def feed_forward_down(held):
+    g_down = dot_on(all_rows(held.active), all_rows(held.cot), 0, 0).astype(jnp.bfloat16)
+    size = held.g_down.shape[3]
     for x in range(SIDE):
         for part in range(2):
             begin = (2 * x + part) * size
-            g_down_ref[part, x, 0] = g_down[begin : begin + size]
-
-
-def feed_forward(feed, cot, gate, down):
-    rows, width = feed.shape
-    units = down.shape[0]
-    low = jnp.bfloat16
-    return whole_call(
-        "feed_forward",
-        ffn_kernel,
-        (feed, cot, gate, down),
-        (
-            ((rows, width), low),
-            ((rows, width), low),
-            ((2, SIDE, 16, PADDED, units), low),
-            ((2, SIDE, 1, units // 8, width), low),
-        ),
-        (
-            ((width, units), low),
-            ((width, units), low),
-            ((rows, units), low),
-            ((rows, units), low),
-            ((rows, units), low),
-            ((width, units), low),
-        ),
-        room=60,
-    )
+            held.g_down[part, x, 0] = g_down[begin : begin + size]
 
 
 STEP_ROWS = 104
@@ -1217,7 +1303,9 @@
 BIAS_ROW = slice(125, 126)
 SKIP_ROW = slice(126, 127)
 FIRST_PROJ = 128
-PROJ_CUT = 72
+PROJ_CUT = 80
+PROJ_ROWS = 144
+FIRST_COL = 20
 
 
 def channel_matrix(size):
@@ -1230,6 +1318,16 @@
 def two_terms(values):
     most = values.astype(jnp.bfloat16)
     return most, (values - most.astype(jnp.float32)).astype(jnp.bfloat16)
+
+
+def row_places(starts_ref, begin, rows, group):
+    row = begin + lax.broadcasted_iota(jnp.int32, (rows, 1), 0)
+    first, after = jnp.zeros_like(row), jnp.full_like(row, group)
+    for i in range(starts_ref.shape[0]):
+        start = starts_ref[i]
+        first = jnp.where(row >= start, jnp.maximum(first, start), first)
+        after = jnp.where(row < start, jnp.minimum(after, start), after)
+    return row - first, after - 1 - row
 
 
 def shifted_rows(before, rows, back):
@@ -1248,11 +1346,11 @@
 
 
 def mixer_project_kernel(
+    starts_ref,
     tokens_ref,
     gain_ref,
     weight_ref,
     channel_ref,
-    dist_ref,
     normed_ref,
     conv_ref,
     gate_ref,
@@ -1282,16 +1380,19 @@
     gate_ref[...] = mixed[:, lanes:]
     rows = conv_in.astype(jnp.float32)
     channel = rows_ref[...]
-    total = conv_sum(tail_ref[...], rows, dist_ref[...], channel)
+    size = rows.shape[0]
+    dist, _ = row_places(starts_ref, pl.program_id(0) * size, size, 0)
+    total = conv_sum(tail_ref[...], rows, dist, channel)
     tail_ref[...] = rows[-8:]
     inputs = (total * jax.nn.sigmoid(total)).astype(low)
     inputs_ref[...] = inputs
-    proj = dot_on(channel[FIRST_PROJ : FIRST_PROJ + 136].astype(low), inputs, 1, 1)
+    proj = dot_on(channel[FIRST_PROJ : FIRST_PROJ + PROJ_ROWS].astype(low), inputs, 1, 1)
+    proj = proj.astype(low)
     first_ref[0] = proj[:PROJ_CUT]
     second_ref[0] = proj[PROJ_CUT:]
 
 
-def mixer_project(tokens, gain, weight, channel, dist):
+def mixer_project(starts, tokens, gain, weight, channel):
     places, rows, width = tokens.shape[1], tokens.shape[2], tokens.shape[3]
     rows, lanes = 2 * rows, weight.shape[1] // 2
     group = places * rows
@@ -1311,17 +1412,17 @@
             jax.ShapeDtypeStruct((group, lanes), low),
             jax.ShapeDtypeStruct((group, lanes), full),
             jax.ShapeDtypeStruct((group, lanes), low),
-            jax.ShapeDtypeStruct((places, PROJ_CUT, rows), full),
-            jax.ShapeDtypeStruct((places, 136 - PROJ_CUT, rows), full),
+            jax.ShapeDtypeStruct((places, PROJ_CUT, rows), low),
+            jax.ShapeDtypeStruct((places, PROJ_ROWS - PROJ_CUT, rows), low),
             jax.ShapeDtypeStruct((width, 2 * lanes), low),
             jax.ShapeDtypeStruct((channel.shape[1], lanes), full),
         ],
         in_specs=[
+            pl.BlockSpec(memory_space=pltpu.SMEM),
             pl.BlockSpec((2, 1, rows // 2, width), lambda i: (0, i, 0, 0)),
             whole(*gain.shape),
             whole(*weight.shape),
             whole(*channel.shape),
-            line(1),
         ],
         out_specs=[
             line(width),
@@ -1329,20 +1430,20 @@
             line(lanes),
             line(lanes),
             pl.BlockSpec((1, PROJ_CUT, rows), lambda i: (i, 0, 0)),
-            pl.BlockSpec((1, 136 - PROJ_CUT, rows), lambda i: (i, 0, 0)),
+            pl.BlockSpec((1, PROJ_ROWS - PROJ_CUT, rows), lambda i: (i, 0, 0)),
             whole(width, 2 * lanes),
             whole(channel.shape[1], lanes),
         ],
         scratch_shapes=[pltpu.VMEM((8, lanes), full)],
         compiler_params=pltpu.CompilerParams(vmem_limit_bytes=40 * 2**20),
         name="mixer_project",
-    )(tokens, gain, weight, channel, dist)
+    )(starts, tokens, gain, weight, channel)
 
 
 def step_sum(first_ref, second_ref, channel_ref, p):
     low = jnp.bfloat16
-    one = first_ref[p].astype(low)
-    two = second_ref[p, pl.ds(0, STEP_ROWS - PROJ_CUT), :].astype(low)
+    one = first_ref[p]
+    two = second_ref[p][: STEP_ROWS - PROJ_CUT]
     total = dot_on(one, channel_ref[pl.ds(0, PROJ_CUT), :].astype(low), 0, 0)
     total = total + dot_on(
         two, channel_ref[pl.ds(PROJ_CUT, STEP_ROWS - PROJ_CUT), :].astype(low), 0, 0
@@ -1365,12 +1466,11 @@
 
 def mixer_forward_kernel(
     used,
+    starts_ref,
     first_ref,
     second_ref,
-    cols_ref,
     channel_ref,
     inputs_ref,
-    reset_ref,
     gate_ref,
     back_ref,
     partial_ref,
@@ -1380,9 +1480,11 @@
     decay_t,
     drive_t,
     rate_ref,
+    cols_t,
     decay_s,
     drive_s,
     out_t,
+    cols_s,
 ):
     places = first_ref.shape[0]
     rows = first_ref.shape[2]
@@ -1395,13 +1497,17 @@
     def prepare(p, carry):
         spot = pl.ds(pl.multiple_of(p * rows, rows), rows)
         steps = softplus(step_sum(first_ref, second_ref, channel_ref, p)[0])
-        put_blocks(decay_s, spot, steps + reset_ref[spot, :])
+        dist, _ = row_places(starts_ref, p * rows, rows, 0)
+        put_blocks(decay_s, spot, jnp.where(dist == 0, far_away, steps))
+        cols = second_ref[p].astype(jnp.float32).T
+        cols_s[0, spot, :] = jnp.concatenate([cols, jnp.zeros_like(cols)], axis=1)
         put_blocks(drive_s, spot, steps * inputs_ref[spot, :].astype(jnp.float32))
         return carry
 
     lax.fori_loop(0, places, prepare, 0)
+    to_lanes(cols_s, cols_t)
     scan_forward_body(
-        used, decay_s, drive_s, cols_ref, rate_ref, out_ref, start_ref, decay_t, drive_t, out_t
+        used, decay_s, drive_s, cols_t, rate_ref, out_ref, start_ref, decay_t, drive_t, out_t
     )
     weight = dot_on(channel_matrix(lanes), back_ref[...], 1, 0).astype(jnp.bfloat16)
 
@@ -1422,17 +1528,17 @@
     lax.fori_loop(0, places, finish, 0)
 
 
-def mixer_forward(used, first, second, cols, channel, inputs, reset, gate, back):
+def mixer_forward(used, starts, first, second, channel, inputs, gate, back):
     group, lanes = inputs.shape
     places, rows = first.shape[0], first.shape[2]
-    states = cols.shape[0] // 2
+    states = LOG_ROWS.stop - LOG_ROWS.start
     low, full = jnp.bfloat16, jnp.float32
     blocks = (lanes // CHUNKS, group, CHUNKS)
     turned = (STEPS, lanes, CHUNKS)
     return whole_call(
         "mixer_forward",
         functools.partial(mixer_forward_kernel, used),
-        (first, second, cols, channel, inputs, reset, gate, back),
+        (starts, first, second, channel, inputs, gate, back),
         (
             ((2, places, rows // 2, back.shape[1]), low),
             ((group, lanes), low),
@@ -1441,8 +1547,10 @@
             (turned, full),
             (turned, full),
             ((lanes, states), full),
-        ),
-        ((blocks, full), (blocks, full), (turned, full)),
+            ((STEPS, CHUNKS, CHUNKS), full),
+        ),
+        ((blocks, full), (blocks, full), (turned, full), ((1, group, CHUNKS), full)),
+        scalars=1,
     )
 
 
@@ -1450,7 +1558,7 @@
     used,
     first_ref,
     second_ref,
-    cols_ref,
+    cols_t,
     channel_ref,
     inputs_ref,
     gate_ref,
@@ -1464,7 +1572,6 @@
     rate_ref,
     g_first_ref,
     g_second_ref,
-    g_cols_ref,
     g_inputs_ref,
     g_gate_ref,
     g_back_ref,
@@ -1479,6 +1586,8 @@
     g_drive_t,
     sums_t,
     ends_t,
+    g_cols_t,
+    g_cols_s,
 ):
     places = first_ref.shape[0]
     rows = first_ref.shape[2]
@@ -1489,9 +1598,12 @@
     g_weight[...] = jnp.zeros_like(g_weight)
     g_rows_ref[...] = jnp.zeros_like(g_rows_ref)
 
-    def prepare(p, carry):
-        spot = pl.ds(pl.multiple_of(p * rows, rows), rows)
-        grad = jnp.concatenate([grad_ref[0, p], grad_ref[1, p]], axis=0)
+    together = 4
+
+    def prepare(q, carry):
+        spot = pl.ds(pl.multiple_of(q * together * rows, together * rows), together * rows)
+        grad = [grad_ref[i % 2, q * together + i // 2] for i in range(2 * together)]
+        grad = jnp.concatenate(grad, axis=0)
         g_weight[...] += dot_on(mixed_ref[spot, :], grad, 0, 0)
         g_mixed = dot_on(grad, weight, 1, 1)
         gate = gate_ref[spot, :]
@@ -1506,18 +1618,19 @@
         g_rows_ref[SKIP_ROW] += jnp.sum(g_out * inputs, axis=0, keepdims=True)
         return carry
 
-    lax.fori_loop(0, places, prepare, 0)
+    lax.fori_loop(0, places // together, prepare, 0)
+    g_cols_t[...] = jnp.zeros_like(g_cols_t)
     scan_backward_body(
         used,
         decay_t,
         drive_t,
-        cols_ref,
+        cols_t,
         rate_ref,
         start_ref,
         g_out_s,
         g_decay_s,
         g_drive_s,
-        g_cols_ref,
+        g_cols_t,
         g_rate_ref,
         grad_t,
         g_decay_t,
@@ -1525,6 +1638,8 @@
         sums_t,
         ends_t,
     )
+
+    to_rows(g_cols_t, g_cols_s)
 
     def finish(p, carry):
         spot = pl.ds(pl.multiple_of(p * rows, rows), rows)
@@ -1540,8 +1655,11 @@
         g_rows_ref[pl.ds(0, PROJ_CUT), :] += dot_on(one, g_total, 1, 0)
         g_rows_ref[pl.ds(PROJ_CUT, STEP_ROWS - PROJ_CUT), :] += dot_on(two, g_total, 1, 0)
         g_low = dot_on(channel_ref[pl.ds(0, STEP_ROWS), :].astype(low), g_total, 1, 1)
-        g_first_ref[p] = g_low[:PROJ_CUT]
-        g_second_ref[p] = g_low[PROJ_CUT:]
+        g_first_ref[p] = g_low[:PROJ_CUT].astype(low)
+        g_cols = g_cols_s[0, spot, :].T[: PROJ_ROWS - PROJ_CUT]
+        blank = jnp.zeros((PROJ_ROWS - STEP_ROWS, rows), full)
+        g_second = g_cols + jnp.concatenate([g_low[PROJ_CUT:], blank], axis=0)
+        g_second_ref[p] = g_second.astype(low)
         return carry
 
     lax.fori_loop(0, places, finish, 0)
@@ -1594,9 +1712,8 @@
             rate,
         ),
         (
-            ((places, PROJ_CUT, rows), full),
-            ((places, STEP_ROWS - PROJ_CUT, rows), full),
-            (cols.shape, full),
+            ((places, PROJ_CUT, rows), low),
+            ((places, PROJ_ROWS - PROJ_CUT, rows), low),
             ((group, lanes), full),
             ((group, lanes), low),
             ((SIDE, 1, lanes // SIDE, width), low),
@@ -1613,12 +1730,15 @@
             turned,
             ((2 * states, STEPS, LINES, CHUNKS), full),
             (starts.shape, full),
+            (cols.shape, full),
+            ((1, group, CHUNKS), full),
         ),
         room=60,
     )
 
 
 def mixer_inputs_kernel(
+    starts_ref,
     first_ref,
     second_ref,
     channel_ref,
@@ -1629,8 +1749,6 @@
     inputs_ref,
     g_inputs_ref,
     g_gate_ref,
-    dist_ref,
-    later_ref,
     g_normed_ref,
     g_weight_ref,
     g_rows_ref,
@@ -1650,16 +1768,17 @@
         g_rows_ref[...] = jnp.zeros_like(g_rows_ref)
 
     channel = channel_ref[...]
-    proj = channel[FIRST_PROJ : FIRST_PROJ + 136].astype(low)
+    proj = channel[FIRST_PROJ : FIRST_PROJ + PROJ_ROWS].astype(low)
     g_proj = [
         jnp.concatenate([first_ref[i], second_ref[i]], axis=0) for i in range(first_ref.shape[0])
     ]
-    g_proj = jnp.concatenate(g_proj, axis=1).astype(low)
+    g_proj = jnp.concatenate(g_proj, axis=1)
     g_inputs = g_inputs_ref[...] + dot_on(g_proj, proj, 0, 0)
-    g_rows_ref[pl.ds(FIRST_PROJ, 136), :] += dot_on(g_proj, inputs_ref[...], 1, 0)
+    g_rows_ref[pl.ds(FIRST_PROJ, PROJ_ROWS), :] += dot_on(g_proj, inputs_ref[...], 1, 0)
     rows = conv_ref[...].astype(full)
     before = jnp.where(step == steps - 1, 0.0, 1.0) * before_ref[...].astype(full)[-8:]
-    dist = dist_ref[...]
+    size = rows.shape[0]
+    dist, later = row_places(starts_ref, (steps - 1 - step) * size, size, steps * size)
     total = conv_sum(before, rows, dist, channel)
     share = jax.nn.sigmoid(total)
     g_total = g_inputs * (share + total * share * (1.0 - share))
@@ -1667,8 +1786,6 @@
     g_conv = taps[CONV - 1 : CONV] * g_total
     g_taps = [jnp.sum(g_total * rows, axis=0, keepdims=True)]
     after = jnp.concatenate([g_total, head_ref[...]], axis=0)
-    size = rows.shape[0]
-    later = later_ref[...]
     for back in range(1, CONV):
         earlier = shifted_rows(before, rows, back) * jnp.where(dist >= back, 1.0, 0.0)
         g_taps.append(jnp.sum(g_total * earlier, axis=0, keepdims=True))
@@ -1688,7 +1805,8 @@
 
     @pl.when(step == steps - 1)
     def _():
-        gain_ref[...] = jnp.sum(sums[...] * weight_ref[...].astype(full), axis=1, keepdims=True)
+        ones = jnp.ones((8, sums.shape[1]), full)
+        gain_ref[...] = dot_on(ones, sums[...] * weight_ref[...].astype(full), 1, 1, precision=highest)
 
         def put(n, value):
             for x in range(SIDE):
@@ -1697,7 +1815,7 @@
         spread_rows(lambda a, b: sums[pl.ds(a, b - a), :].astype(low), put)
 
 
-def mixer_inputs(first, second, channel, weight, normed, conv, inputs, g_inputs, g_gate, dist, later):
+def mixer_inputs(starts, first, second, channel, weight, normed, conv, inputs, g_inputs, g_gate):
     places, rows = first.shape[0], first.shape[2]
     group, lanes = conv.shape
     width = normed.shape[1]
@@ -1721,11 +1839,12 @@
             jax.ShapeDtypeStruct((2, places, rows // 2, width), low),
             jax.ShapeDtypeStruct((SIDE, 16, PADDED, 2 * lanes), low),
             jax.ShapeDtypeStruct(channel.shape, full),
-            jax.ShapeDtypeStruct((width, 1), full),
+            jax.ShapeDtypeStruct((8, width), full),
         ],
         in_specs=[
+            pl.BlockSpec(memory_space=pltpu.SMEM),
             cube(PROJ_CUT),
-            cube(136 - PROJ_CUT),
+            cube(PROJ_ROWS - PROJ_CUT),
             whole(*channel.shape),
             whole(*weight.shape),
             line(width),
@@ -1734,19 +1853,17 @@
             line(lanes),
             line(lanes),
             line(lanes),
-            line(1),
-            line(1),
         ],
         out_specs=[
             pl.BlockSpec((2, count, rows // 2, width), lambda i: (0, last - i, 0, 0)),
             whole(SIDE, 16, PADDED, 2 * lanes),
             whole(*channel.shape),
-            whole(width, 1),
+            whole(8, width),
         ],
         scratch_shapes=[pltpu.VMEM((8, lanes), full), pltpu.VMEM((width, 2 * lanes), full)],
         compiler_params=pltpu.CompilerParams(vmem_limit_bytes=48 * 2**20),
         name="mixer_inputs",
-    )(first, second, channel, weight, normed, conv, conv, inputs, g_inputs, g_gate, dist, later)
+    )(starts, first, second, channel, weight, normed, conv, conv, inputs, g_inputs, g_gate)
 
 
 def channel_grads_kernel(one_ref, two_ref, rate_ref, channel_ref, out_ref):
@@ -1795,7 +1912,12 @@
 def unpack(small, metas, width):
     full = jnp.float32
     return whole_call(
-        "unpack", unpack_kernel, (small,), (((metas, width), full), ((8, width), full))
+        "unpack",
+        unpack_kernel,
+        (small,),
+        (((metas, width), full), ((8, width), full)),
+        room=60,
+        fetch=True,
     )
 
 
@@ -1904,6 +2026,8 @@
             ((PADDED, 2 * LANES), low),
             ((64, 3 * LANES), low),
         ),
+        room=60,
+        fetch=True,
     )
 
 
@@ -1912,7 +2036,6 @@
     gain_ref,
     g_hidden_ref,
     normed_ref,
-    g_attn_ref,
     sums_ref,
     keys_ref,
     mamba_ref,
@@ -1943,7 +2066,7 @@
         rows = tokens_ref[spot, :].astype(jnp.float32)
         scale = lax.rsqrt(jnp.mean(rows * rows, axis=-1, keepdims=True) + epsilon)
         unit = rows * scale
-        grad = (normed_ref[i] + g_attn_ref[spot, :]) * gain_ref[...]
+        grad = normed_ref[i] * gain_ref[...]
         grad = scale * (grad - unit * jnp.mean(grad * unit, axis=-1, keepdims=True))
         input_out[spot, :] = g_hidden_ref[i] + grad
     piece, width = query_out.shape
@@ -1994,7 +2117,7 @@
     tokens = arrays[0]
     rows, width = tokens.shape
     full = jnp.float32
-    keys = arrays[6]
+    keys = arrays[5]
     metas = LANES
     return whole_call(
         "finish",
@@ -2020,6 +2143,19 @@
     )
 
 
+def pack_gains_kernel(norm_ref, attn_ref, mamba_ref, feed_ref, out_ref):
+    width = norm_ref.shape[1]
+    rows = [ref[...] for ref in (norm_ref, attn_ref, mamba_ref, feed_ref)]
+    rows = jnp.concatenate(rows + [jnp.zeros((8 - len(rows), width), jnp.float32)], axis=0)
+    wide = spread_columns(rows.astype(jnp.bfloat16)).astype(jnp.float32).T
+    out_ref[...] = padded_lanes(wide, LANES).astype(jnp.bfloat16)
+
+
+def pack_gains(*rows):
+    places = rows[0].shape[1] // PIECE * PADDED
+    return whole_call("pack_gains", pack_gains_kernel, rows, (((places, LANES), jnp.bfloat16),))[0]
+
+
 def rms_norm(values, gain):
     return values * lax.rsqrt(jnp.mean(values * values, axis=-1, keepdims=True) + epsilon) * gain
 
@@ -2315,7 +2451,18 @@
         gather_halves(net, 0, held.tokens.at[pl.ds(core * rows, rows)], held.tokens_all)
     )
     if core == 0:
-        jobs += gather_weights(net, held)
+
+        def assigned():
+            upper, lower = pl.ds(0, rows), pl.ds(rows, rows)
+            own = net.local((9, -1), held.tokens.at[upper], held.assigned.at[upper])
+            copy = net.start(
+                (9, 0), held.tokens.at[lower], held.assigned.at[lower], net.device(partner=True)
+            )
+            yield
+            copy.wait_recv()
+            own.wait()
+
+        jobs += [assigned()] + gather_weights(net, held)
     return jobs
 
 
@@ -2354,12 +2501,16 @@
     rows = held.attn_pre.shape[0] // 2
 
     def attn():
+        lower = held.attn_pre.at[pl.ds(rows, rows)]
+        device = net.device(other_core=True, partner=True)
         if core == 0:
             own = net.local((1, -1), held.attn_pre.at[pl.ds(0, rows)], held.attn_half)
-        hand(net, (1, 0), 0, held.attn_pre.at[pl.ds(rows, rows)], held.attn_half)
+            net.start((1, 0), lower, held.attn_half, device)
         yield
         if core == 0:
             own.wait()
+        else:
+            net.copy((1, 0), lower, held.attn_half, device).wait_recv()
 
     return [
         attn(),
@@ -2384,10 +2535,28 @@
 
 
 def program_ffn(net, held):
-    return [
-        reduce_ring(net, 0, held.out, held.out_pad, held.out_sum, order_of(net)),
-        reduce_ring(net, 1, held.grad, held.grad_pad, held.grad_sum, order_of(net)),
+    feed_forward_open(held)
+    jobs = [
+        reduce_ring(net, 1, held.g_feed, held.grad_pad, held.grad_sum),
+        reduce_ring(net, 0, held.out, held.out_pad, held.out_sum),
     ]
+    for job in jobs:
+        next(job)
+
+    def line(hop):
+        feed_forward_line(held, net.core, (net.at[FIRST] + hop) % SIDE)
+
+    def weights():
+        for part in range(2):
+            feed_forward_gate(held, part)
+            yield
+        feed_forward_down(held)
+
+    for hop in (2, 1, 3, 0):
+        line(hop)
+        for job in jobs:
+            next(job)
+    return jobs + [weights()]
 
 
 def shrink(net, name, source, pad, out):
@@ -2419,12 +2588,16 @@
     core = net.core
 
     def attn():
+        device = net.device(other_core=True, partner=True)
+        target = held.g_attn_both.at[1]
         if core == 0:
             own = net.local((5, -1), held.g_attn, held.g_attn_both.at[0])
-        hand(net, (5, 0), 1, held.g_attn, held.g_attn_both.at[1])
+        else:
+            net.start((5, 0), held.g_attn, target, device)
         yield
         if core == 0:
             own.wait()
+            net.copy((5, 0), held.g_attn, target, device).wait_recv()
 
     return [
         swap_cores(net, 3, held.mixed, held.mixed_both),
@@ -2441,7 +2614,7 @@
 
 
 def program_attention(net, held):
-    rows = held.keyval.shape[2] // 2
+    rows = held.keyval.shape[3]
     parts = [getattr(held.parts, name) for name in SUMS]
     taken = [
         net.local((20, i), getattr(held.sources, name), getattr(held.inside, name))
@@ -2457,7 +2630,7 @@
         return reduce_two(
             net,
             i,
-            held.keyval.at[:, :, pl.ds(i * rows, rows)],
+            held.keyval.at[i],
             pad,
             held.keyval_sum.at[pl.ds(i * rows, rows)],
             ((Z, Y), (Y, Z))[i],
@@ -2485,6 +2658,8 @@
             held.g_normed,
             held.gain_part,
             held.meta_gain,
+            held.g_wide,
+            held.g_meta_wide,
         )
         places = held.keys.four.shape[0] // SIDE**3
 
@@ -2522,7 +2697,28 @@
     core = net.core
 
     def normed():
+        half = held.normed_sum.shape[0]
+        device = net.device(other_core=True, partner=True)
+        if core == 0:
+            own = net.local((9, -1), held.g_attn.at[pl.ds(0, half)], held.attn_part)
+            net.start((9, 0), held.g_attn.at[pl.ds(half, half)], held.attn_part, device)
         yield from reduce_halves(net, 0, held.partial, held.normed_pad, held.normed_sum)
+        if core == 0:
+            own.wait()
+        else:
+            lower = held.g_attn.at[pl.ds(half, half)]
+            net.copy((9, 0), lower, held.attn_part, device).wait_recv()
+
+        def put(lead, part, value):
+            held.normed_sum[part, :] = value
+
+        scatter_sum(
+            1,
+            half,
+            lambda lead, part: held.normed_sum[part, :],
+            [lambda lead, part: held.attn_part[part, :]],
+            put,
+        )
         yield from swap_cores(net, 1, held.normed_sum, held.normed_both)
 
     def gains():
@@ -2554,17 +2750,11 @@
         channel(7, held.back, held.back_pad, held.back_sum),
         channel(8, held.channel, held.channel_pad, held.channel_sum),
         gains(),
-        keep_and_hand(net, 9, 0, held.g_attn, held.g_attn_both),
         keep_and_hand(net, 10, 0, held.sums_in, held.sums),
         keep_and_hand(net, 12, 0, held.keys, held.keys_sum),
         swap_cores(net, 13, held.gate, held.gate_both),
         swap_cores(net, 14, held.down, held.down_both),
     ]
-
-
-def padded_blocks(rows, count, size, kind=jnp.bfloat16):
-    width = rows.shape[-1]
-    return pad_to(rows.reshape(count, -1, width), 1, size).astype(kind)
 
 
 def shards(
@@ -2607,26 +2797,16 @@
     rank = w_dt.shape[0]
     states = a_log.shape[0]
     proj = rank + 2 * states
-    proj_pad = 136
     metas = meta_tokens.shape[0]
     down_piece = w_down.shape[0]
     units = 96 * SIDE
     row_start = core * half
 
     lengths = seq_lengths[0]
-    end_rows = jnp.cumsum(lengths)
-    start_rows = end_rows - lengths
-    all_rows = jnp.arange(group, dtype=jnp.int32)
-    my_rows = lax.axis_index("seq") * rows + jnp.arange(rows, dtype=jnp.int32)
-
-    def begins(row_ids):
-        started = row_ids[:, None] >= start_rows[None, :]
-        return jnp.max(jnp.where(started, start_rows[None, :], 0), axis=1)
-
-    dist = (all_rows - begins(all_rows))[:, None]
-    left = jnp.where(all_rows[:, None] < end_rows[None, :], end_rows[None, :], group)
-    left = (jnp.min(left, axis=1) - 1 - all_rows)[:, None]
-    reset = jnp.where(dist == 0, far_away, 0.0).astype(jnp.float32)
+    start_rows = (jnp.cumsum(lengths) - lengths).astype(jnp.int32)
+    place = lax.axis_index("seq")
+    counting = jnp.arange(half, dtype=jnp.int32)
+    my_rows = jnp.concatenate([place * rows + counting, (16 - place) * rows - half + counting])
 
     attention_in, mamba_in, back_in, gate_in, down_in, small_in, channel_in = prepare(
         w_query,
@@ -2665,6 +2845,7 @@
         ),
         dict(
             tokens_all=((2, SIDE, SIDE, half, width), low, ANY),
+            assigned=((rows, width), low, ANY),
             small_all=(cube + small_in.shape, low, ANY),
             mamba_all=(cube + mamba_in.shape[2:], low, ANY),
             back_all=((SIDE,) + back_in.shape, low, ANY),
@@ -2674,6 +2855,7 @@
             third=(cube + (32, last_third), low, ANY),
         ),
         dict(mamba_mid=(mamba_in.shape, low)),
+        partners=(False,),
     )
     weight_one, weight_two, weight_three = (
         part.reshape(64 * 32, -1) for part in (begun.first, begun.second, begun.third)
@@ -2690,7 +2872,7 @@
     normed_wide, query_b, keyval_b, meta_wide, meta_kv = on_core(
         0,
         lambda: attention_project(
-            tokens_b, meta_f, gain_row, weight_one, weight_two, query_width, keys_width
+            begun.assigned, meta_f, gain_row, weight_one, weight_two, query_width, keys_width
         ),
     )
     keyval = exchange(
@@ -2711,21 +2893,19 @@
     normed_all, conv_in, gate_z, inputs_b, proj_first, proj_second, weight_mamba, channel = on_core(
         1,
         lambda: mixer_project(
+            start_rows,
             begun.tokens_all.reshape(2, 16, half, width),
             gain_row,
             mamba_wide,
             begun.channel_all.reshape(4 * 64, -1),
-            dist,
         ),
     )
 
     def proj_pads(size):
-        return dict(
-            two_pad(size, rows, jnp.float32), sum=((size, rows), jnp.float32)
-        )
+        return dict(two_pad(size, rows), sum=((size, rows), low))
 
     def spread_projection(name, number, first, second, gate):
-        cuts = (PROJ_CUT, proj_pad - PROJ_CUT)
+        cuts = (PROJ_CUT, PROJ_ROWS - PROJ_CUT)
         results = exchange(
             name,
             number,
@@ -2736,8 +2916,8 @@
                 gate=(gate, ANY),
             ),
             dict(
-                first_all=((SIDE, SIDE, cuts[0], rows), jnp.float32, ANY),
-                second_all=((SIDE, SIDE, cuts[1], rows), jnp.float32, ANY),
+                first_all=((SIDE, SIDE, cuts[0], rows), low, ANY),
+                second_all=((SIDE, SIDE, cuts[1], rows), low, ANY),
                 gate_own=((SIDE, SIDE, 32, units), low, ANY),
             ),
             dict(
@@ -2762,7 +2942,7 @@
         jnp.where(my_rows[:, None] >= start_rows[None, :], start_rows[None, :], 0), axis=1
     )
     bounds = jnp.stack([my_starts, my_rows], axis=1).astype(jnp.int32)
-    key_blocks = (my_rows[-1:] // KEY_ROWS + 1).astype(jnp.int32)
+    key_blocks = (my_rows[half - 1 :: half] // KEY_ROWS + 1).astype(jnp.int32)
 
     attended, mass, attended_wide, attn_pre = on_core(
         0,
@@ -2771,17 +2951,12 @@
         ),
     )
 
-    col_rows = slice(rank - PROJ_CUT, proj - PROJ_CUT)
-
-    def mamba_core():
-        cols = step_second[:, col_rows].transpose(1, 0, 2).reshape(-1, CHUNKS, STEPS)
-        cols = cols.transpose(0, 2, 1)
-        results = mixer_forward(
-            inner, step_first, step_second, cols, channel, inputs_b, reset, gate_z, back_wide
-        )
-        return [cols] + list(results)
-
-    cols, partial, mixed_y, ssm_out, starts, decay_t, drive_t, scan_rate = on_core(1, mamba_core)
+    partial, mixed_y, ssm_out, starts, decay_t, drive_t, scan_rate, cols = on_core(
+        1,
+        lambda: mixer_forward(
+            inner, start_rows, step_first, step_second, channel, inputs_b, gate_z, back_wide
+        ),
+    )
 
     mixers = exchange(
         "exchange_mixers",
@@ -2802,6 +2977,7 @@
         ),
         dict(pad=half_pad(half, width)),
         vmem=32 * 2**20,
+        partners=(True,),
     )
     tokens_part = lax.dynamic_slice_in_dim(tokens_b, row_start, half, 0).astype(full)
     sent = rms_norm(mixers.attn_half, gain_attn).astype(low).astype(jnp.float32)
@@ -2813,27 +2989,37 @@
         program_feed,
         dict(feed=(rms_norm(hidden, gain_feed).astype(low), ANY)),
         dict(feed_all=((SIDE, SIDE, half, width), low, ANY)),
-    ).feed_all.reshape(16 * half, width)
-    out_partial, feed_partial, g_gate, g_down = feed_forward(
-        feed,
-        cotangent_all,
-        mixers.gate_all.reshape(2, 64 * 32, units),
-        mixers.down_all.reshape(units, width),
-    )
+    ).feed_all
+    block = (SIDE, SIDE, half)
     ffn = exchange(
         "exchange_ffn",
         6,
         program_ffn,
         dict(
-            out=(out_partial.reshape(SIDE, SIDE, half, width), ANY),
-            grad=(feed_partial.reshape(SIDE, SIDE, half, width), ANY),
+            feed=(feed, VMEM),
+            cot=(cotangent_all.reshape(block + (width,)), VMEM),
+            gate=(mixers.gate_all.reshape(2, 64 * 32, units), VMEM),
+            down=(mixers.down_all.reshape(units, width), VMEM),
         ),
         dict(
-            out_sum=((half, width), jnp.float32, VMEM),
-            grad_sum=((half, width), jnp.float32, VMEM),
-        ),
-        dict(out_pad=ring_pad(half, width), grad_pad=ring_pad(half, width)),
-        vmem=48 * 2**20,
+            out_sum=((half, width), full, VMEM),
+            grad_sum=((half, width), full, VMEM),
+            g_gate=((2, SIDE, 16, 32, units), low, VMEM),
+            g_down=((2, SIDE, 1, 48, width), low, VMEM),
+        ),
+        dict(
+            out=(block + (width,), low),
+            g_feed=(block + (width,), low),
+            active=(block + (units,), low),
+            g_parts=((2,) + block + (units,), low),
+            gate_w=((width, units), low),
+            up_w=((width, units), low),
+            products=((width, units), low),
+            out_pad=ring_pad(half, width),
+            grad_pad=ring_pad(half, width),
+        ),
+        vmem=60 * 2**20,
+        shared=True,
     )
     mixed_part = (hidden + ffn.out_sum).astype(low)
     cotangent_f = cotangent_part.astype(jnp.float32)
@@ -2855,8 +3041,8 @@
             g_attn=(grad_attn_pre.astype(low), ANY),
             mixed=(mixed_part, ANY),
             g_hidden=(grad_hidden, ANY),
-            g_gate=(g_gate, ANY),
-            g_down=(g_down, ANY),
+            g_gate=(ffn.g_gate, ANY),
+            g_down=(ffn.g_down, ANY),
         ),
         dict(
             g_mamba_all=((2, SIDE, SIDE, half, width), low, ANY),
@@ -2868,6 +3054,7 @@
         ),
         dict(gate_pad=shrink_pad(16, 32, units), down_pad=shrink_pad(1, 48, width)),
         vmem=32 * 2**20,
+        partners=(True,),
     )
     mixed = back.mixed_both.reshape(rows, width)
     g_gate_own = back.g_gate_sum.reshape(SIDE, SIDE, 32, units)
@@ -2916,7 +3103,7 @@
         8,
         program_attention,
         dict(
-            keyval=(grad_keyval.reshape(SIDE, SIDE, rows, keys_width), ANY),
+            keyval=(grad_keyval.reshape(2, SIDE, SIDE, half, keys_width), ANY),
             gate=(g_gate_own, ANY),
             one=(cubed(sum_one), ANY),
             two=(cubed(sum_two), ANY),
@@ -2928,7 +3115,7 @@
             sums=((32, query_most + width), full, VMEM),
             keys_sum=((32, keys_width + metas), full, VMEM),
             g_normed=((rows, width), full, VMEM),
-            gain_part=((64 * 32, 1), full, VMEM),
+            gain_part=((1, 64 * 32), full, VMEM),
             meta_gain=((1, width), full, VMEM),
         ),
         dict(
@@ -2936,6 +3123,8 @@
             lower_pad=two_pad(half, keys_width),
             gate_mid=((SIDE, SIDE, 32, units), low),
             keyval_sum=((rows, keys_width), full),
+            g_wide=((rows, 64 * 32), full),
+            g_meta_wide=((metas, 64 * 32), full),
             inside={name: (array.shape, array.dtype) for name, array in zip(INSIDE, sources)},
             keys=dict(zip(SUMS[3:], (((64 * 32, cut), low) for cut in small_cuts))),
             pads=dict(zip(SUMS, (three_pad(32, cut) for cut in cuts + small_cuts))),
@@ -2947,8 +3136,9 @@
     gain_attention = (gain_query + attention.gain_part).reshape(64, 32)[:, :piece].reshape(width)
     gain_attention = gain_attention / gain_norm + attention.meta_gain[0]
 
-    def mamba_back_one():
-        g_first, g_second, g_cols, *rest = mixer_backward(
+    g_first, g_second, grad_inputs, grad_gate_z, back_out, grad_rows, grad_rate = on_core(
+        1,
+        lambda: mixer_backward(
             inner,
             step_first,
             step_second,
@@ -2964,13 +3154,7 @@
             decay_t,
             drive_t,
             scan_rate,
-        )
-        g_cols = g_cols.transpose(0, 2, 1).reshape(-1, 16, rows).transpose(1, 0, 2)
-        g_second = jnp.concatenate([g_second[:, : rank - PROJ_CUT], g_cols], axis=1)
-        return [g_first, pad_to(g_second, 1, proj_pad - PROJ_CUT)] + list(rest)
-
-    g_first, g_second, grad_inputs, grad_gate_z, back_out, grad_rows, grad_rate = on_core(
-        1, mamba_back_one
+        ),
     )
     g_first, g_second, last_gate = spread_projection(
         "exchange_last", 9, g_first, g_second, g_gate_own
@@ -2978,6 +3162,7 @@
 
     def mamba_back_two():
         g_normed, g_weight, g_rows, gain = mixer_inputs(
+            start_rows,
             g_first,
             g_second,
             channel,
@@ -2987,16 +3172,15 @@
             inputs_b,
             grad_inputs,
             grad_gate_z,
-            dist,
-            left,
         )
         return g_normed, g_weight, channel_grads(grad_rows, g_rows, grad_rate, channel), gain
 
     grad_normed_partial, mamba_out, channel_out, gain_mixer = on_core(1, mamba_back_two)
-    gain_mixer = gain_mixer[:, 0] / gain_norm
+    gain_mixer = gain_mixer[0] / gain_norm
     grad_gain_norm = jnp.where(on_attention, gain_attention, gain_mixer)
-    gains_out = jnp.stack([grad_gain_norm, grad_gain_attn, grad_gain_mamba, grad_gain_feed], axis=1)
-    gains_out = padded_blocks(pad_to(gains_out, 1, 128), 64, 32)
+    gains_out = pack_gains(
+        *(grad[None] for grad in (grad_gain_norm, grad_gain_attn, grad_gain_mamba, grad_gain_feed))
+    )
     ended = exchange(
         "exchange_end",
         1,
@@ -3015,7 +3199,6 @@
         ),
         dict(
             normed_both=((2, half, width), full, ANY),
-            g_attn_both=((rows, width), full, ANY),
             sums=((32, query_most + width), full, ANY),
             keys_sum=((32, keys_width + metas), full, ANY),
             gate_both=((2, SIDE, SIDE, 32, units), low, ANY),
@@ -3028,6 +3211,7 @@
         dict(
             normed_pad=half_pad(half, width),
             normed_sum=((half, width), full),
+            attn_part=((half, width), full),
             gains_pad=three_pad(32, 128),
             gains_sum=((32, 128), full),
             mamba_pad=x_pad(16, 32, 4 * CHUNKS),
@@ -3037,6 +3221,7 @@
             channel_pad=x_pad(1, 64, 3 * LANES, full),
         ),
         vmem=48 * 2**20,
+        partners=(True,),
     )
     (
         input_grad,
@@ -3065,7 +3250,6 @@
         gain_row,
         back.g_hidden_both,
         ended.normed_both,
-        ended.g_attn_both,
         ended.sums,
         ended.keys_sum,
         ended.mamba_sum.reshape(16, 32, -1),

time: 643 us -> 586 us (0.911)
  local copies, waits for them, and re-layouts: 58.3 us -> 18.7 us
  Pallas kernels: 547 us -> 537 us
    pallas_call x7, Pallas kernels: 153 us -> 128 us  [whole_call(): pl.pallas_call(fetching if fetch else body, out_shape=[jax.ShapeDtypeStru...]
    unnamed x95 -> x62, local copies, waits for them, and re-layouts: 35.1 us -> 13.3 us
    pallas_call x10, Pallas kernels: 355 us -> 367 us  [exchange(): pl.pallas_call(kernel, out_shape=[jax.ShapeDtypeStruct(s, d) for s, d, _...]
  transfers between devices with their start and end apart: 1 -> 1, of which waited for: 0 -> 0; matrix products, arithmetic and copies ran while one was open for 1% -> 0% of each run, Pallas kernels for 20% -> 20%
where the time goes in v3:
time: 586 us; the launch traced here: 581 us
  Pallas kernels  537 us (92%)
  local copies, waits for them, and re-layouts  18.7 us (3%)
  between operations  14.9 us (3%)
  other arithmetic  8.96 us (2%)
    pallas_call x10, Pallas kernels, exchange(): pl.pallas_call(kernel, out_shape=[jax.ShapeDtypeStruct(s, d) for s, d, _...  367 us
    pallas_call x7, Pallas kernels, whole_call(): pl.pallas_call(fetching if fetch else body, out_shape=[jax.ShapeDtypeStru...  128 us
    pallas_call x1, Pallas kernels, mixer_inputs(): pl.pallas_call(mixer_inputs_kernel, grid=(places // count,), out_shape=[j...  24 us
    pallas_call x1, Pallas kernels, mixer_project(): pl.pallas_call(mixer_project_kernel, grid=(places,), out_shape=[jax.Shape...  18.3 us
    unnamed x62, local copies, waits for them, and re-layouts  13.3 us
  transfers between devices with their start and end apart: 1, of which 0 were waited for; matrix products, arithmetic and copies ran while one was open for 0% of the time, Pallas kernels for 20%

profile of v3, /device:TPU:1, one launch (start us, length us, event | category | flops | bytes accessed | tf_op | source)
XLA Modules:
  0.0 580.9 jit_solution(12939240858150186891)
XLA Ops:
  7.2 0.8 reduce-window.4
  8.1 0.7 bitcast_subtract_fusion.1
  8.7 2.0 copy.64
  10.7 1.4 copy.65.refs_7_
  12.2 1.5 copy.66.refs_12_
  13.6 6.5 %prepare.1 = (bf16[32,3904]{1,0:T(8,128)(2,1)}, bf16[16,32,512]{2,1,0:T(8,128)(2,1)}, bf16[64,1600]{1,0:T(8,128)(2,1)}, bf16[2,16,32,384]{3,2,1,0:T(8,128)(2,1)}...) custom-call(f32[25,1600]{1,0:T(8,128)} %refs_0_.1, f32[25,640]{1,0:T(8,128)} %refs_1_.1, ...), custom_call_target="tpu_custom_call" | custom-call | tf_op jit(solution)/shard_map/prepare/pallas_call | solution.py:742
  20.1 57.6 %exchange_start.1 = (bf16[2,4,4,64,1600]{4,3,2,1,0:T(8,128)(2,1)}, bf16[128,1600]{1,0:T(8,128)(2,1)}, bf16[4,4,4,32,256]{4,3,2,1,0:T(8,128)(2,1)}, bf16[4,4,4,32...) custom-call(bf16[128,1600]{1,0:T(8,128)(2,1)} %bitcast.85, ...), custom_call_target="tpu_custom_call" | custom-call | tf_op jit(solution)/shard_map/exchange_start/pallas_call | solution.py:439
  77.8 2.8 unpack.1
  80.7 1.2 slice_reduce_fusion
  82.2 18.3 %conditional.7 = ((bf16[2048,1600]{1,0:T(8,128)(2,1)}, bf16[2048,256]{1,0:T(8,128)(2,1)}, f32[2048,256]{1,0:T(8,128)}, bf16[2048,256]{1,0:T(8,128)(2,1)}, bf16[1...) conditional(s32[]{:T(128)} %convert_element_type.44, () %tuple.89, ...), branch_computations={%region_1.2_spmd, %region_2.3_spmd} | conditional | bytes 8 | solution.py:2869
  82.2 18.3 %mixer_project.1 = (bf16[2048,1600]{1,0:T(8,128)(2,1)}, bf16[2048,256]{1,0:T(8,128)(2,1)}, f32[2048,256]{1,0:T(8,128)}, bf16[2048,256]{1,0:T(8,128)(2,1)}, bf16[...) custom-call(s32[3]{0:T(128)S(1)} %get-tuple-element.227.starts_ref, ...), custom_call_target="tpu_custom_call" | custom-call | tf_op jit(solution)/shard_map/cond/branch_1_fun/mixer_project/pallas_call | solution.py:1407
  100.5 27.2 %exchange_project.1 = (bf16[4,4,80,128]{3,2,1,0:T(8,128)(2,1)}, bf16[4,4,64,128]{3,2,1,0:T(8,128)(2,1)}, bf16[4,4,32,384]{3,2,1,0:T(8,128)(2,1)S(1)}) custom-call(bf16[4,4,80,128]{3,2,1,0:T(8,128)(2,1)} %bitcast.138, bf16[4,4,64,128]{3,2,1,0:T(8,128)(2,1)} %bitcast.142, bf16[4,4,32,384]{3,2,1,0:T(8,128)(2,1)S(1)} %bitcast.89), custom_call_target="tpu_custom_call" | custom-call | tf_op jit(solution)/shard_map/exchange_project/pallas_call | solution.py:439
  127.7 0.7 constant_dynamic-slice_fusion
  128.7 43.5 %conditional.8 = ((bf16[2,16,64,1600]{3,2,1,0:T(8,128)(2,1)}, bf16[2048,256]{1,0:T(8,128)(2,1)}, f32[2,2048,128]{2,1,0:T(8,128)}, f32[16,256,128]{2,1,0:T(8,128)...) conditional(s32[]{:T(128)} %convert_element_type.44, () %tuple.92, ...), branch_computations={%region_3.4_spmd, %region_4.5_spmd} | conditional | bytes 8 | solution.py:2869
  128.7 43.4 %mixer_forward.1 = (bf16[2,16,64,1600]{3,2,1,0:T(8,128)(2,1)}, bf16[2048,256]{1,0:T(8,128)(2,1)}, f32[2,2048,128]{2,1,0:T(8,128)}, f32[16,256,128]{2,1,0:T(8,128...) custom-call(s32[3]{0:T(128)S(1)} %get-tuple-element.232.starts_ref, ...), custom_call_target="tpu_custom_call" | custom-call | tf_op jit(solution)/shard_map/cond/branch_1_fun/mixer_forward/pallas_call | solution.py:742
  172.2 0.5 conditional.9
  172.7 2.4 exchange_keyval.1
  175.3 0.9 copy-done.8
  176.4 42.9 %exchange_mixers.1 = (f32[64,1600]{1,0:T(8,128)S(1)}, f32[64,1600]{1,0:T(8,128)S(1)}, bf16[2,4,4,4,32,384]{5,4,3,2,1,0:T(8,128)(2,1)S(1)}, bf16[4,96,1600]{2,1,0:T(8,128)(2,1)S(1)}) custom-call(bf16[2,4,4,64,1600]{4,3,2,1,0:T(8,128)(2,1)} %bitcast.112, f32[128,1600]{1,0:T(8,128)} %get-tuple-element.479.refs_1_, bf16[4,4,32,384]{3,2,1,0:T(8,128)(2,1)S(1)} %copy-done.8, ...), custom_call_target="tpu_custom_call" | custom-call | tf_op jit(solution)/shard_map/exchange_mixers/pallas_call | solution.py:439
  219.3 1.7 copy-done.2
  221.0 1.0 copy-done.6
  222.5 0.8 multiply_convert_fusion.refs_0_
  223.3 30.0 %exchange_feed.1.refs_0_ = bf16[4,4,64,1600]{3,2,1,0:T(8,128)(2,1)} custom-call(bf16[64,1600]{1,0:T(8,128)(2,1)} %multiply_convert_fusion.refs_0_), custom_call_target="tpu_custom_call" | custom-call | tf_op jit(solution)/shard_map/exchange_feed/pallas_call | solution.py:439
  253.4 54.0 %exchange_ffn.1 = (f32[64,1600]{1,0:T(8,128)}, f32[64,1600]{1,0:T(8,128)}, bf16[2,4,16,32,384]{4,3,2,1,0:T(8,128)(2,1)}, bf16[2,4,1,48,1600]{4,3,2,1,0:T(8,128)(2,1)}) custom-call(bf16[4,4,64,1600]{3,2,1,0:T(8,128)(2,1)} %exchange_feed.1.refs_0_, bf16[4,4,64,1600]{3,2,1,0:T(8,128)(2,1)} %bitcast.121, bf16[2,2048,384]{2,1,0:T(8,128)(2,1)} %bitcast.87, ...), custom_call_target="tpu_custom_call" | custom-call | tf_op jit(solution)/shard_map/exchange_ffn/pallas_call | solution.py:439
  307.4 1.9 multiply_reduce_fusion
  309.3 2.2 multiply_reduce_fusion.1
  311.7 53.3 %exchange_back.1 = (bf16[2,4,4,64,1600]{4,3,2,1,0:T(8,128)(2,1)}, bf16[2,64,1600]{2,1,0:T(8,128)(2,1)}, bf16[2,64,1600]{2,1,0:T(8,128)(2,1)S(1)}, f32[2,64,1600]...) custom-call(bf16[64,1600]{1,0:T(8,128)(2,1)S(1)} %get-tuple-element.740.refs_0_, ...), custom_call_target="tpu_custom_call" | custom-call | tf_op jit(solution)/shard_map/exchange_back/pallas_call | solution.py:439
  365.0 0.8 copy-done.3
  365.7 0.9 copy.69
  366.8 3.5 exchange_attention.1
  370.3 0.7 add_reduce_fusion
  371.3 0.7 reshape.270.attn_ref
  372.0 0.7 reshape.271.mamba_ref
  372.7 0.7 reshape.272.feed_ref
  373.4 69.0 %conditional.11 = ((bf16[16,80,128]{2,1,0:T(8,128)(2,1)S(1)}, bf16[16,64,128]{2,1,0:T(8,128)(2,1)}, f32[2048,256]{1,0:T(8,128)}, bf16[2048,256]{1,0:T(8,128)(2,1...) conditional(s32[]{:T(128)} %convert_element_type.44, () %tuple.99, ...), branch_computations={%region_16.17_spmd, %region_17.18_spmd} | conditional | bytes 8 | solution.py:2869
  373.6 68.8 %mixer_backward.1 = (bf16[16,80,128]{2,1,0:T(8,128)(2,1)S(1)}, bf16[16,64,128]{2,1,0:T(8,128)(2,1)}, f32[2048,256]{1,0:T(8,128)}, bf16[2048,256]{1,0:T(8,128)(2,...) custom-call(bf16[16,80,128]{2,1,0:T(8,128)(2,1)} %get-tuple-element.251.first_ref, ...), custom_call_target="tpu_custom_call" | custom-call | tf_op jit(solution)/shard_map/cond/branch_1_fun/mixer_backward/pallas_call | solution.py:742
  442.4 24.1 %exchange_last.1 = (bf16[4,4,80,128]{3,2,1,0:T(8,128)(2,1)S(1)}, bf16[4,4,64,128]{3,2,1,0:T(8,128)(2,1)S(1)}, bf16[4,4,32,384]{3,2,1,0:T(8,128)(2,1)S(1)}) custom-call(bf16[4,4,80,128]{3,2,1,0:T(8,128)(2,1)S(1)} %bitcast.139, bf16[4,4,64,128]{3,2,1,0:T(8,128)(2,1)} %bitcast.143, bf16[4,4,32,384]{3,2,1,0:T(8,128)(2,1)S(1)} %bitcast.91), custom_call_target="tpu_custom_call" | custom-call | tf_op jit(solution)/shard_map/exchange_last/pallas_call | solution.py:439
  466.5 25.5 %conditional.12 = (bf16[4,16,32,512]{3,2,1,0:T(8,128)(2,1)}, f32[4,1,64,384]{3,2,1,0:T(8,128)}, bf16[2,16,64,1600]{3,2,1,0:T(8,128)(2,1)}, f32[8,1600]{1,0:T(8,128)}) conditional(s32[]{:T(128)} %convert_element_type.44, () %tuple.98, (bf16[4,4,80,128]{3,2,1,0:T(8,128)(2,1)S(1)}, bf16[4,4,64,128]{3,2,1,0:T(8,128)(2,1)S(1)}, s32[3]{0:T(128)S(1)}, ...), branch_computations={%region_18.19_spmd, %region_19.20_spmd} | conditional | bytes 2162804 | solution.py:2869
  466.9 24.0 %mixer_inputs.1 = (bf16[2,16,64,1600]{3,2,1,0:T(8,128)(2,1)}, bf16[4,16,32,512]{3,2,1,0:T(8,128)(2,1)}, f32[384,256]{1,0:T(8,128)S(1)}, f32[8,1600]{1,0:T(8,128)}) custom-call(s32[3]{0:T(128)S(1)} %get-tuple-element.269.starts_ref, bf16[16,80,128]{2,1,0:T(8,128)(2,1)S(1)} %bitcast.140, bf16[16,64,128]{2,1,0:T(8,128)(2,1)S(1)} %bitcast.141, ...), custom_call_target="tpu_custom_call" | custom-call | tf_op jit(solution)/shard_map/cond/branch_1_fun/mixer_inputs/pallas_call | solution.py:1835
  490.9 1.1 channel_grads.1
  492.1 0.9 broadcast_select_fusion.1.norm_ref
  493.4 72.2 %exchange_end.1 = (f32[2,64,1600]{2,1,0:T(8,128)S(1)}, f32[32,3264]{1,0:T(8,128)S(1)}, f32[32,768]{1,0:T(8,128)S(1)}, bf16[2,4,4,32,384]{4,3,2,1,0:T(8,128)(2,1)...) custom-call(bf16[2,4,4,64,1600]{4,3,2,1,0:T(8,128)(2,1)} %bitcast.11, ...), custom_call_target="tpu_custom_call" | custom-call | tf_op jit(solution)/shard_map/exchange_end/pallas_call | solution.py:439
  565.6 4.6 finish.1
  570.2 1.2 copy.70
  571.3 0.5 slice_bitcast_fusion
  571.9 0.7 copy.71
  572.5 0.5 slice_bitcast_fusion.2
  573.1 0.7 copy.72
  (89 shorter events, 2.6 us)
Async XLA Ops:
  7.2 246.2 %all-gather.2.cloned.1.call-start = ((), (), s32[]{:S(2)}) async-start(), calls=%async_computation | async-start | bytes 3620864 | tf_op jit(solution)/shard_map/all_gather | solution.py:2939
  8.1 69.7 %copy-start.30 = (s32[3,1]{0,1:T(1,128)}, s32[3,1]{0,1:T(1,128)S(1)}, u32[]{:S(2)}) copy-start(s32[3,1]{0,1:T(1,128)S(1)} %reduce-window.4) | copy-start | bytes 40
  8.7 119.9 %copy-start.27 = (s32[3]{0:T(128)}, s32[3]{0:T(128)S(1)}, u32[]{:S(2)}) copy-start(s32[3]{0:T(128)S(1)} %bitcast_subtract_fusion.1) | copy-start | bytes 40
  20.1 61.7 %copy-start.16 = (bf16[2,16,32,384]{3,2,1,0:T(8,128)(2,1)S(1)}, bf16[2,16,32,384]{3,2,1,0:T(8,128)(2,1)}, u32[]{:S(2)}) copy-start(bf16[2,16,32,384]{3,2,1,0:T(8,128)(2,1)} %get-tuple-element.460) | copy-start | bytes 2359300
  20.1 61.8 %copy-start.21 = (bf16[1,128,1600]{1,2,0:T(8,128)(2,1)S(1)}, bf16[1,128,1600]{1,2,0:T(8,128)(2,1)}, u32[]{:S(2)}) copy-start(bf16[1,128,1600]{1,2,0:T(8,128)(2,1)} %param.57) | copy-start | bytes 1228804
  77.8 50.9 %copy-start.13 = (bf16[4,64,1600]{2,1,0:T(8,128)(2,1)}, bf16[4,64,1600]{2,1,0:T(8,128)(2,1)S(1)}, u32[]{:S(2)}) copy-start(bf16[4,64,1600]{2,1,0:T(8,128)(2,1)S(1)} %get-tuple-element.468) | copy-start | bytes 2457604
  80.6 91.5 %copy-start.14 = (f32[128,1600]{1,0:T(8,128)}, f32[128,1600]{1,0:T(8,128)S(1)}, u32[]{:S(2)}) copy-start(f32[128,1600]{1,0:T(8,128)S(1)} %get-tuple-element.471.refs_11_) | copy-start | bytes 2457604
  81.8 140.3 %copy-start.24 = (f32[1600]{0:T(1024)}, f32[1600]{0:T(1024)S(1)}, u32[]{:S(2)}) copy-start(f32[1600]{0:T(1024)S(1)} %get-tuple-element.734) | copy-start | bytes 19204
  82.2 45.5 %copy-start.17 = (bf16[1,128,1600]{2,1,0:T(8,128)(2,1)}, bf16[1,128,1600]{2,1,0:T(8,128)(2,1)S(1)}, u32[]{:S(2)}) copy-start(bf16[1,128,1600]{2,1,0:T(8,128)(2,1)S(1)} %copy.63) | copy-start | bytes 1228804
  100.5 272.9 %copy-start.11 = (f32[384,256]{1,0:T(8,128)}, f32[384,256]{1,0:T(8,128)S(1)}, u32[]{:S(2)}) copy-start(f32[384,256]{1,0:T(8,128)S(1)} %get-tuple-element.701) | copy-start | bytes 1179652
  128.4 43.7 %copy-start.20 = (bf16[128,1600]{1,0:T(8,128)(2,1)S(1)}, bf16[128,1600]{1,0:T(8,128)(2,1)}, u32[]{:S(2)}) copy-start(bf16[128,1600]{1,0:T(8,128)(2,1)} %get-tuple-element.470) | copy-start | bytes 1228804
  172.2 3.0 copy-start.29
  172.2 3.0 copy-start.31
  175.3 1.0 copy-start.8
  175.3 1.1 copy-start.9
  176.4 45.8 %copy-start = (bf16[1,128,1600]{2,1,0:T(8,128)(2,1)S(1)}, bf16[1,128,1600]{2,1,0:T(8,128)(2,1)}, u32[]{:S(2)}) copy-start(bf16[1,128,1600]{2,1,0:T(8,128)(2,1)} %copy.64) | copy-start | bytes 1228804
  219.3 1.7 copy-start.2
  220.9 1.0 copy-start.6
  222.5 30.8 %copy-start.25 = (f32[1600]{0:T(1024)S(1)}, f32[1600]{0:T(1024)}, u32[]{:S(2)}) copy-start(f32[1600]{0:T(1024)} %copy-done.24) | copy-start | bytes 19204
  253.4 55.9 %copy-start.18 = (bf16[1,128,1600]{2,1,0:T(8,128)(2,1)S(1)}, bf16[1,128,1600]{2,1,0:T(8,128)(2,1)}, u32[]{:S(2)}) copy-start(bf16[1,128,1600]{2,1,0:T(8,128)(2,1)} %copy-done.17) | copy-start | bytes 1228804
  307.4 4.3 copy-start.1
  307.4 4.3 copy-start.5
  365.0 0.8 copy-start.3
  373.4 69.0 %copy-start.4 = (bf16[16,32,384]{2,1,0:T(8,128)(2,1)S(1)}, bf16[16,32,384]{2,1,0:T(8,128)(2,1)}, u32[]{:S(2)}) copy-start(bf16[16,32,384]{2,1,0:T(8,128)(2,1)} %copy-done.3) | copy-start | bytes 1179652
  373.4 93.1 %copy-start.28 = (s32[3]{0:T(128)S(1)}, s32[3]{0:T(128)}, u32[]{:S(2)}) copy-start(s32[3]{0:T(128)} %copy-done.27) | copy-start | bytes 40
  466.5 25.5 %copy-start.26 = (f32[1,1600]{1,0:T(1,128)S(1)}, f32[1,1600]{1,0:T(1,128)}, u32[]{:S(2)}) copy-start(f32[1,1600]{1,0:T(1,128)} %get-tuple-element.537) | copy-start | bytes 19204
  466.5 26.8 %copy-start.7 = (f32[32,3264]{1,0:T(8,128)S(1)}, f32[32,3264]{1,0:T(8,128)}, u32[]{:S(2)}) copy-start(f32[32,3264]{1,0:T(8,128)} %get-tuple-element.527.refs_2_) | copy-start | bytes 1253380
  466.5 26.8 %copy-start.10 = (f32[32,768]{1,0:T(8,128)S(1)}, f32[32,768]{1,0:T(8,128)}, u32[]{:S(2)}) copy-start(f32[32,768]{1,0:T(8,128)} %get-tuple-element.528.refs_3_) | copy-start | bytes 294916
  466.8 24.0 %copy-start.12 = (f32[384,256]{1,0:T(8,128)S(1)}, f32[384,256]{1,0:T(8,128)}, u32[]{:S(2)}) copy-start(f32[384,256]{1,0:T(8,128)} %get-tuple-element.272.channel_ref) | copy-start | bytes 1179652 | tf_op jit(solution)/shard_map/cond
  466.8 24.0 %copy-start.22 = (f32[128,256]{1,0:T(8,128)S(1)}, f32[128,256]{1,0:T(8,128)}, u32[]{:S(2)}) copy-start(f32[128,256]{1,0:T(8,128)} %get-tuple-element.280.one_ref) | copy-start | bytes 393220 | tf_op jit(solution)/shard_map/cond
  466.8 24.0 %copy-start.23 = (f32[256,16]{1,0:T(8,128)S(1)}, f32[256,16]{1,0:T(8,128)}, u32[]{:S(2)}) copy-start(f32[256,16]{1,0:T(8,128)} %get-tuple-element.282.rate_ref) | copy-start | bytes 49156 | tf_op jit(solution)/shard_map/cond
Sparse Core Ops, SparseCore 0:
  128.6 48.4 all-gather.1

commit v4 on v3

--- a/solution.py
+++ b/solution.py
@@ -1371,7 +1371,9 @@
         rows_ref[...] = dot_on(channel_ref[...], channel_matrix(lanes), 0, 1)
         tail_ref[...] = jnp.zeros_like(tail_ref)
 
-    tokens = jnp.concatenate([tokens_ref[0, 0], tokens_ref[1, 0]], axis=0).astype(jnp.float32)
+    count = tokens_ref.shape[1]
+    tokens = [tokens_ref[part, i] for i in range(count) for part in range(2)]
+    tokens = jnp.concatenate(tokens, axis=0).astype(jnp.float32)
     normed = (unit_rows(tokens) * gain_ref[...]).astype(low)
     normed_ref[...] = normed
     mixed = dot_on(normed, compact_ref[...], 1, 0)
@@ -1388,8 +1390,10 @@
     inputs_ref[...] = inputs
     proj = dot_on(channel[FIRST_PROJ : FIRST_PROJ + PROJ_ROWS].astype(low), inputs, 1, 1)
     proj = proj.astype(low)
-    first_ref[0] = proj[:PROJ_CUT]
-    second_ref[0] = proj[PROJ_CUT:]
+    size = size // count
+    for i in range(count):
+        first_ref[i] = proj[:PROJ_CUT, i * size : (i + 1) * size]
+        second_ref[i] = proj[PROJ_CUT:, i * size : (i + 1) * size]
 
 
 def mixer_project(starts, tokens, gain, weight, channel):
@@ -1398,15 +1402,17 @@
     group = places * rows
     low, full = jnp.bfloat16, jnp.float32
 
+    count = 2
+
     def line(size):
-        return pl.BlockSpec((rows, size), lambda i: (i, 0))
+        return pl.BlockSpec((count * rows, size), lambda i: (i, 0))
 
     def whole(*shape):
         return pl.BlockSpec(shape, lambda i: (0,) * len(shape))
 
     return pl.pallas_call(
         mixer_project_kernel,
-        grid=(places,),
+        grid=(places // count,),
         out_shape=[
             jax.ShapeDtypeStruct((group, width), low),
             jax.ShapeDtypeStruct((group, lanes), low),
@@ -1419,7 +1425,7 @@
         ],
         in_specs=[
             pl.BlockSpec(memory_space=pltpu.SMEM),
-            pl.BlockSpec((2, 1, rows // 2, width), lambda i: (0, i, 0, 0)),
+            pl.BlockSpec((2, count, rows // 2, width), lambda i: (0, i, 0, 0)),
             whole(*gain.shape),
             whole(*weight.shape),
             whole(*channel.shape),
@@ -1429,8 +1435,8 @@
             line(lanes),
             line(lanes),
             line(lanes),
-            pl.BlockSpec((1, PROJ_CUT, rows), lambda i: (i, 0, 0)),
-            pl.BlockSpec((1, PROJ_ROWS - PROJ_CUT, rows), lambda i: (i, 0, 0)),
+            pl.BlockSpec((count, PROJ_CUT, rows), lambda i: (i, 0, 0)),
+            pl.BlockSpec((count, PROJ_ROWS - PROJ_CUT, rows), lambda i: (i, 0, 0)),
             whole(width, 2 * lanes),
             whole(channel.shape[1], lanes),
         ],
@@ -1511,8 +1517,10 @@
     )
     weight = dot_on(channel_matrix(lanes), back_ref[...], 1, 0).astype(jnp.bfloat16)
 
-    def finish(p, carry):
-        spot = pl.ds(pl.multiple_of(p * rows, rows), rows)
+    together = 4
+
+    def finish(q, carry):
+        spot = pl.ds(pl.multiple_of(q * together * rows, together * rows), together * rows)
         gate = gate_ref[spot, :]
         inputs = inputs_ref[spot, :].astype(jnp.float32)
         mixed = (get_blocks(out_ref, spot) + channel_ref[SKIP_ROW] * inputs) * (
@@ -1521,11 +1529,11 @@
         mixed = mixed.astype(jnp.bfloat16)
         mixed_ref[spot, :] = mixed
         value = dot_on(mixed, weight, 1, 0).astype(jnp.bfloat16)
-        partial_ref[0, p] = value[:half]
-        partial_ref[1, p] = value[half:]
+        for i in range(2 * together):
+            partial_ref[i % 2, q * together + i // 2] = value[i * half : (i + 1) * half]
         return carry
 
-    lax.fori_loop(0, places, finish, 0)
+    lax.fori_loop(0, places // together, finish, 0)
 
 
 def mixer_forward(used, starts, first, second, channel, inputs, gate, back):
@@ -1820,7 +1828,7 @@
     group, lanes = conv.shape
     width = normed.shape[1]
     low, full = jnp.bfloat16, jnp.float32
-    count = 2
+    count = 4
     last = places // count - 1
 
     def line(size):
@@ -2156,6 +2164,54 @@
     return whole_call("pack_gains", pack_gains_kernel, rows, (((places, LANES), jnp.bfloat16),))[0]
 
 
+def norm_back(values, gain, grad):
+    scale = lax.rsqrt(jnp.mean(values * values, axis=-1, keepdims=True) + epsilon)
+    unit = values * scale
+    g_unit = grad * gain
+    g_values = scale * (g_unit - unit * jnp.mean(g_unit * unit, axis=-1, keepdims=True))
+    return g_values, jnp.sum(grad * unit, axis=0, keepdims=True)
+
+
+def turn_kernel(
+    gains_ref,
+    hidden_ref,
+    out_ref,
+    grad_ref,
+    cot_ref,
+    attn_ref,
+    mamba_ref,
+    mixed_out,
+    g_hidden_out,
+    g_attn_out,
+    g_mamba_out,
+    attn_gain_out,
+    mamba_gain_out,
+    feed_gain_out,
+):
+    low = jnp.bfloat16
+    hidden = hidden_ref[...]
+    mixed_out[...] = (hidden + out_ref[...]).astype(low)
+    g_norm, feed_gain_out[...] = norm_back(hidden, gains_ref[3:4, :], grad_ref[...])
+    g_hidden = cot_ref[...].astype(jnp.float32) + g_norm
+    g_hidden_out[...] = g_hidden
+    g_sent = 0.5 * g_hidden
+    g_attn, attn_gain_out[...] = norm_back(attn_ref[...], gains_ref[1:2, :], g_sent)
+    g_mamba, mamba_gain_out[...] = norm_back(mamba_ref[...], gains_ref[2:3, :], g_sent)
+    g_attn_out[...] = g_attn.astype(low)
+    g_mamba_out[...] = g_mamba.astype(low)
+
+
+def turn(gains, hidden, *arrays):
+    shape, low, full = hidden.shape, jnp.bfloat16, jnp.float32
+    row = ((1, shape[1]), full)
+    return whole_call(
+        "turn",
+        turn_kernel,
+        (gains, hidden) + arrays,
+        ((shape, low), (shape, full), (shape, low), (shape, low), row, row, row),
+    )
+
+
 def rms_norm(values, gain):
     return values * lax.rsqrt(jnp.mean(values * values, axis=-1, keepdims=True) + epsilon) * gain
 
@@ -2621,9 +2677,15 @@
         for i, name in enumerate(INSIDE)
     ]
 
-    def weight(i, source, hold=0):
+    def weight(i, source):
         pad = getattr(held.pads, SUMS[i])
-        return reduce_three(net, 10 + i, source, pad, parts[i], ORDERS[i], hold)
+        return reduce_three(net, 10 + i, source, pad, parts[i], ORDERS[i])
+
+    def large(i):
+        yield
+        yield from reduce_three(
+            net, 10 + i, getattr(held, SUMS[i]), getattr(held.pads, SUMS[i]), parts[i], ORDERS[i], 1
+        )
 
     def keyval(i):
         pad = (held.upper_pad, held.lower_pad)[i]
@@ -2688,7 +2750,7 @@
         keyval(1),
         swap_two(net, 3, held.gate, held.gate_mid, held.gate_own),
         follow(),
-        *(weight(i, getattr(held, SUMS[i]), 2) for i in range(3)),
+        *(large(i) for i in range(3)),
         last(),
     ]
 
@@ -2861,8 +2923,7 @@
         part.reshape(64 * 32, -1) for part in (begun.first, begun.second, begun.third)
     )
     meta_f, gains = unpack(begun.small_all.reshape(64 * 32, -1), metas, width)
-    gain_norm, gain_attn, gain_mamba, gain_feed = (gains[i] for i in range(4))
-    gain_row = gains[:1]
+    gain_row, gain_attn, gain_mamba, gain_feed = (gains[i : i + 1] for i in range(4))
 
     def on_core(which, work):
         shapes = jax.eval_shape(work)
@@ -3021,24 +3082,30 @@
         vmem=60 * 2**20,
         shared=True,
     )
-    mixed_part = (hidden + ffn.out_sum).astype(low)
-    cotangent_f = cotangent_part.astype(jnp.float32)
-    _, pull_feed = jax.vjp(rms_norm, hidden, gain_feed)
-    grad_hidden_norm, grad_gain_feed = pull_feed(ffn.grad_sum)
-    grad_hidden = cotangent_f + grad_hidden_norm
-    grad_sent = 0.5 * grad_hidden
-    _, pull_attn = jax.vjp(rms_norm, mixers.attn_half, gain_attn)
-    grad_attn_pre, grad_gain_attn = pull_attn(grad_sent)
-    _, pull_mamba = jax.vjp(rms_norm, mixers.mamba_pre, gain_mamba)
-    grad_mamba_pre, grad_gain_mamba = pull_mamba(grad_sent)
-
+    (
+        mixed_part,
+        grad_hidden,
+        grad_attn_pre,
+        grad_mamba_pre,
+        grad_gain_attn,
+        grad_gain_mamba,
+        grad_gain_feed,
+    ) = turn(
+        gains,
+        hidden,
+        ffn.out_sum,
+        ffn.grad_sum,
+        cotangent_part,
+        mixers.attn_half,
+        mixers.mamba_pre,
+    )
     back = exchange(
         "exchange_back",
         7,
         program_back,
         dict(
-            g_mamba=(grad_mamba_pre.astype(low), ANY),
-            g_attn=(grad_attn_pre.astype(low), ANY),
+            g_mamba=(grad_mamba_pre, ANY),
+            g_attn=(grad_attn_pre, ANY),
             mixed=(mixed_part, ANY),
             g_hidden=(grad_hidden, ANY),
             g_gate=(ffn.g_gate, ANY),
@@ -3133,8 +3200,8 @@
         vmem=62 * 2**20,
         cores=(0,),
     )
-    gain_attention = (gain_query + attention.gain_part).reshape(64, 32)[:, :piece].reshape(width)
-    gain_attention = gain_attention / gain_norm + attention.meta_gain[0]
+    gain_attention = (gain_query + attention.gain_part).reshape(64, 32)[:, :piece].reshape(1, width)
+    gain_attention = gain_attention / gain_row + attention.meta_gain
 
     g_first, g_second, grad_inputs, grad_gate_z, back_out, grad_rows, grad_rate = on_core(
         1,
@@ -3176,11 +3243,9 @@
         return g_normed, g_weight, channel_grads(grad_rows, g_rows, grad_rate, channel), gain
 
     grad_normed_partial, mamba_out, channel_out, gain_mixer = on_core(1, mamba_back_two)
-    gain_mixer = gain_mixer[0] / gain_norm
+    gain_mixer = gain_mixer[:1] / gain_row
     grad_gain_norm = jnp.where(on_attention, gain_attention, gain_mixer)
-    gains_out = pack_gains(
-        *(grad[None] for grad in (grad_gain_norm, grad_gain_attn, grad_gain_mamba, grad_gain_feed))
-    )
+    gains_out = pack_gains(grad_gain_norm, grad_gain_attn, grad_gain_mamba, grad_gain_feed)
     ended = exchange(
         "exchange_end",
         1,

time: 586 us -> 578 us (0.986)
  Pallas kernels: 537 us -> 527 us
  other arithmetic: 8.96 us -> 2.55 us
    unnamed x62 -> x52, local copies, waits for them, and re-layouts: 13.3 us -> 18.2 us
    pallas_call x7 -> x8, Pallas kernels: 128 us -> 127 us  [whole_call(): pl.pallas_call(fetching if fetch else body, out_shape=[jax.ShapeDtypeStru...]
  transfers between devices with their start and end apart: 1 -> 1, of which waited for: 0 -> 0; matrix products, arithmetic and copies ran while one was open for 0% -> 0% of each run, Pallas kernels for 20% -> 21%
where the time goes in v4:
time: 578 us; the launch traced here: 568 us
  Pallas kernels  527 us (91%)
  local copies, waits for them, and re-layouts  21.5 us (4%)
  between operations  14.9 us (3%)
    pallas_call x10, Pallas kernels, exchange(): pl.pallas_call(kernel, out_shape=[jax.ShapeDtypeStruct(s, d) for s, d, _...  362 us
    pallas_call x8, Pallas kernels, whole_call(): pl.pallas_call(fetching if fetch else body, out_shape=[jax.ShapeDtypeStru...  127 us
    pallas_call x1, Pallas kernels, mixer_inputs(): pl.pallas_call(mixer_inputs_kernel, grid=(places // count,), out_shape=[j...  23 us
    unnamed x52, local copies, waits for them, and re-layouts  18.2 us
    pallas_call x1, Pallas kernels, mixer_project(): pl.pallas_call(mixer_project_kernel, grid=(places // count,), out_shape=[...  15 us
  transfers between devices with their start and end apart: 1, of which 0 were waited for; matrix products, arithmetic and copies ran while one was open for 0% of the time, Pallas kernels for 21%

profile of v4, /device:TPU:1, one launch (start us, length us, event | category | flops | bytes accessed | tf_op | source)
XLA Modules:
  0.0 568.1 jit_solution(136938818470900623)
XLA Ops:
  7.2 2.0 copy.63
  9.2 1.4 copy.64.refs_7_
  10.7 1.5 copy.65.refs_12_
  12.1 6.5 %prepare.1 = (bf16[32,3904]{1,0:T(8,128)(2,1)}, bf16[16,32,512]{2,1,0:T(8,128)(2,1)}, bf16[64,1600]{1,0:T(8,128)(2,1)}, bf16[2,16,32,384]{3,2,1,0:T(8,128)(2,1)}...) custom-call(f32[25,1600]{1,0:T(8,128)} %refs_0_.1, f32[25,640]{1,0:T(8,128)} %refs_1_.1, ...), custom_call_target="tpu_custom_call" | custom-call | tf_op jit(solution)/shard_map/prepare/pallas_call | solution.py:742
  18.6 58.5 %exchange_start.1 = (bf16[2,4,4,64,1600]{4,3,2,1,0:T(8,128)(2,1)}, bf16[128,1600]{1,0:T(8,128)(2,1)S(1)}, bf16[4,4,4,32,256]{4,3,2,1,0:T(8,128)(2,1)}, bf16[4,4,...) custom-call(bf16[128,1600]{1,0:T(8,128)(2,1)} %bitcast.85, ...), custom_call_target="tpu_custom_call" | custom-call | tf_op jit(solution)/shard_map/exchange_start/pallas_call | solution.py:439
  77.2 2.8 unpack.1
  80.1 1.2 slice_reduce_fusion
  81.3 0.2 reduce-window.4
  81.5 1.2 copy.67
  82.7 15.0 %conditional.7 = ((bf16[2048,1600]{1,0:T(8,128)(2,1)}, bf16[2048,256]{1,0:T(8,128)(2,1)}, f32[2048,256]{1,0:T(8,128)}, bf16[2048,256]{1,0:T(8,128)(2,1)}, bf16[1...) conditional(s32[]{:T(128)} %convert_element_type.34, () %tuple.90, ...), branch_computations={%region_1.2_spmd, %region_2.3_spmd} | conditional | bytes 8 | solution.py:2930
  82.8 15.0 %mixer_project.1 = (bf16[2048,1600]{1,0:T(8,128)(2,1)}, bf16[2048,256]{1,0:T(8,128)(2,1)}, f32[2048,256]{1,0:T(8,128)}, bf16[2048,256]{1,0:T(8,128)(2,1)}, bf16[...) custom-call(s32[3]{0:T(128)S(1)} %get-tuple-element.227.starts_ref, ...), custom_call_target="tpu_custom_call" | custom-call | tf_op jit(solution)/shard_map/cond/branch_1_fun/mixer_project/pallas_call | solution.py:1413
  97.7 28.7 %exchange_project.1 = (bf16[4,4,80,128]{3,2,1,0:T(8,128)(2,1)}, bf16[4,4,64,128]{3,2,1,0:T(8,128)(2,1)}, bf16[4,4,32,384]{3,2,1,0:T(8,128)(2,1)S(1)}) custom-call(bf16[4,4,80,128]{3,2,1,0:T(8,128)(2,1)} %bitcast.133, bf16[4,4,64,128]{3,2,1,0:T(8,128)(2,1)} %bitcast.137, bf16[4,4,32,384]{3,2,1,0:T(8,128)(2,1)S(1)} %bitcast.89), custom_call_target="tpu_custom_call" | custom-call | tf_op jit(solution)/shard_map/exchange_project/pallas_call | solution.py:439
  126.4 0.7 constant_dynamic-slice_fusion.cot_ref
  127.4 41.0 %conditional.8 = ((bf16[2,16,64,1600]{3,2,1,0:T(8,128)(2,1)}, bf16[2048,256]{1,0:T(8,128)(2,1)}, f32[2,2048,128]{2,1,0:T(8,128)}, f32[16,256,128]{2,1,0:T(8,128)...) conditional(s32[]{:T(128)} %convert_element_type.34, () %tuple.89, ...), branch_computations={%region_3.4_spmd, %region_4.5_spmd} | conditional | bytes 8 | solution.py:2930
  127.4 41.0 %mixer_forward.1 = (bf16[2,16,64,1600]{3,2,1,0:T(8,128)(2,1)}, bf16[2048,256]{1,0:T(8,128)(2,1)}, f32[2,2048,128]{2,1,0:T(8,128)}, f32[16,256,128]{2,1,0:T(8,128...) custom-call(s32[3]{0:T(128)S(1)} %get-tuple-element.232.starts_ref, ...), custom_call_target="tpu_custom_call" | custom-call | tf_op jit(solution)/shard_map/cond/branch_1_fun/mixer_forward/pallas_call | solution.py:742
  168.4 0.5 conditional.9
  168.9 2.4 exchange_keyval.1
  171.5 1.0 copy-done.11
  172.6 44.9 %exchange_mixers.1 = (f32[64,1600]{1,0:T(8,128)S(1)}, f32[64,1600]{1,0:T(8,128)S(1)}, bf16[2,4,4,4,32,384]{5,4,3,2,1,0:T(8,128)(2,1)S(1)}, bf16[4,96,1600]{2,1,0:T(8,128)(2,1)S(1)}) custom-call(bf16[2,4,4,64,1600]{4,3,2,1,0:T(8,128)(2,1)} %bitcast.112, f32[128,1600]{1,0:T(8,128)S(1)} %get-tuple-element.485.refs_1_, bf16[4,4,32,384]{3,2,1,0:T(8,128)(2,1)S(1)} %copy-done.11, ...), custom_call_target="tpu_custom_call" | custom-call | tf_op jit(solution)/shard_map/exchange_mixers/pallas_call | solution.py:439
  217.5 1.7 copy-done.1
  219.2 1.0 copy-done.7
  220.4 0.3 multiply_reduce_fusion
  220.7 0.8 multiply_convert_fusion.refs_0_
  221.5 29.9 %exchange_feed.1.refs_0_ = bf16[4,4,64,1600]{3,2,1,0:T(8,128)(2,1)} custom-call(bf16[64,1600]{1,0:T(8,128)(2,1)} %multiply_convert_fusion.refs_0_), custom_call_target="tpu_custom_call" | custom-call | tf_op jit(solution)/shard_map/exchange_feed/pallas_call | solution.py:439
  251.5 54.9 %exchange_ffn.1 = (f32[64,1600]{1,0:T(8,128)}, f32[64,1600]{1,0:T(8,128)}, bf16[2,4,16,32,384]{4,3,2,1,0:T(8,128)(2,1)}, bf16[2,4,1,48,1600]{4,3,2,1,0:T(8,128)(2,1)}) custom-call(bf16[4,4,64,1600]{3,2,1,0:T(8,128)(2,1)} %exchange_feed.1.refs_0_, bf16[4,4,64,1600]{3,2,1,0:T(8,128)(2,1)} %bitcast.121, bf16[2,2048,384]{2,1,0:T(8,128)(2,1)} %bitcast.87, ...), custom_call_target="tpu_custom_call" | custom-call | tf_op jit(solution)/shard_map/exchange_ffn/pallas_call | solution.py:439
  306.5 1.1 copy-done.8
  307.6 1.0 copy-done.9
  308.6 0.7 turn.1
  309.4 1.9 copy-done.2
  311.2 52.6 %exchange_back.1 = (bf16[2,4,4,64,1600]{4,3,2,1,0:T(8,128)(2,1)}, bf16[2,64,1600]{2,1,0:T(8,128)(2,1)S(1)}, bf16[2,64,1600]{2,1,0:T(8,128)(2,1)S(1)}, f32[2,64,1...) custom-call(bf16[64,1600]{1,0:T(8,128)(2,1)S(1)} %get-tuple-element.496.refs_0_, ...), custom_call_target="tpu_custom_call" | custom-call | tf_op jit(solution)/shard_map/exchange_back/pallas_call | solution.py:439
  363.8 0.8 copy-done.4
  364.6 0.9 copy.69
  365.7 3.5 exchange_attention.1
  369.2 0.7 add_reduce_fusion
  370.1 69.7 %conditional.11 = ((bf16[16,80,128]{2,1,0:T(8,128)(2,1)S(1)}, bf16[16,64,128]{2,1,0:T(8,128)(2,1)}, f32[2048,256]{1,0:T(8,128)}, bf16[2048,256]{1,0:T(8,128)(2,1...) conditional(s32[]{:T(128)} %convert_element_type.34, () %tuple.99, ...), branch_computations={%region_13.14_spmd, %region_14.15_spmd} | conditional | bytes 8 | solution.py:2930
  371.0 68.7 %mixer_backward.1 = (bf16[16,80,128]{2,1,0:T(8,128)(2,1)S(1)}, bf16[16,64,128]{2,1,0:T(8,128)(2,1)}, f32[2048,256]{1,0:T(8,128)}, bf16[2048,256]{1,0:T(8,128)(2,...) custom-call(bf16[16,80,128]{2,1,0:T(8,128)(2,1)} %get-tuple-element.251.first_ref, ...), custom_call_target="tpu_custom_call" | custom-call | tf_op jit(solution)/shard_map/cond/branch_1_fun/mixer_backward/pallas_call | solution.py:742
  439.8 35.5 %exchange_last.1 = (bf16[4,4,80,128]{3,2,1,0:T(8,128)(2,1)}, bf16[4,4,64,128]{3,2,1,0:T(8,128)(2,1)S(1)}, bf16[4,4,32,384]{3,2,1,0:T(8,128)(2,1)S(1)}) custom-call(bf16[4,4,80,128]{3,2,1,0:T(8,128)(2,1)S(1)} %bitcast.134, bf16[4,4,64,128]{3,2,1,0:T(8,128)(2,1)} %bitcast.138, bf16[4,4,32,384]{3,2,1,0:T(8,128)(2,1)S(1)} %bitcast.91), custom_call_target="tpu_custom_call" | custom-call | tf_op jit(solution)/shard_map/exchange_last/pallas_call | solution.py:439
  475.4 25.5 %conditional.12 = (bf16[4,16,32,512]{3,2,1,0:T(8,128)(2,1)}, f32[4,1,64,384]{3,2,1,0:T(8,128)}, bf16[2,16,64,1600]{3,2,1,0:T(8,128)(2,1)}, f32[8,1600]{1,0:T(8,128)S(1)}) conditional(s32[]{:T(128)} %convert_element_type.34, () %tuple.98, (bf16[4,4,80,128]{3,2,1,0:T(8,128)(2,1)}, bf16[4,4,64,128]{3,2,1,0:T(8,128)(2,1)S(1)}, s32[3]{0:T(128)S(1)}, ...), branch_computations={%region_15.16_spmd, %region_16.17_spmd} | conditional | bytes 589912 | solution.py:2930
  475.7 23.0 %mixer_inputs.1 = (bf16[2,16,64,1600]{3,2,1,0:T(8,128)(2,1)}, bf16[4,16,32,512]{3,2,1,0:T(8,128)(2,1)}, f32[384,256]{1,0:T(8,128)S(1)}, f32[8,1600]{1,0:T(8,128)S(1)}) custom-call(s32[3]{0:T(128)S(1)} %get-tuple-element.269.starts_ref, bf16[16,80,128]{2,1,0:T(8,128)(2,1)} %bitcast.135, bf16[16,64,128]{2,1,0:T(8,128)(2,1)S(1)} %bitcast.136, ...), custom_call_target="tpu_custom_call" | custom-call | tf_op jit(solution)/shard_map/cond/branch_1_fun/mixer_inputs/pallas_call | solution.py:1843
  498.7 2.1 channel_grads.1
  500.9 0.4 pack_gains.1
  501.3 51.2 %exchange_end.1 = (f32[2,64,1600]{2,1,0:T(8,128)S(1)}, f32[32,3264]{1,0:T(8,128)S(1)}, f32[32,768]{1,0:T(8,128)S(1)}, bf16[2,4,4,32,384]{4,3,2,1,0:T(8,128)(2,1)...) custom-call(bf16[2,4,4,64,1600]{4,3,2,1,0:T(8,128)(2,1)} %bitcast.11, ...), custom_call_target="tpu_custom_call" | custom-call | tf_op jit(solution)/shard_map/exchange_end/pallas_call | solution.py:439
  552.6 4.6 finish.1
  557.2 1.2 copy.70
  558.4 0.5 slice_bitcast_fusion
  558.9 0.7 copy.71
  559.6 0.5 slice_bitcast_fusion.2
  560.1 0.7 copy.72
  (68 shorter events, 1.3 us)
Async XLA Ops:
  7.2 244.3 %all-gather.2.cloned.1.call-start = ((), (), s32[]{:S(2)}) async-start(), calls=%async_computation | async-start | bytes 3620864 | tf_op jit(solution)/shard_map/all_gather | solution.py:3000
  12.1 69.1 %copy-start.23 = (s32[1,3]{1,0:T(1,128)S(1)}, s32[1,3]{1,0:T(1,128)}, u32[]{:S(2)}) copy-start(s32[1,3]{1,0:T(1,128)} %param.37) | copy-start | bytes 40
  18.6 62.8 %copy-start.18 = (bf16[2,16,32,384]{3,2,1,0:T(8,128)(2,1)S(1)}, bf16[2,16,32,384]{3,2,1,0:T(8,128)(2,1)}, u32[]{:S(2)}) copy-start(bf16[2,16,32,384]{3,2,1,0:T(8,128)(2,1)} %get-tuple-element.467) | copy-start | bytes 2359300
  77.2 50.2 %copy-start.15 = (bf16[4,64,1600]{2,1,0:T(8,128)(2,1)}, bf16[4,64,1600]{2,1,0:T(8,128)(2,1)S(1)}, u32[]{:S(2)}) copy-start(bf16[4,64,1600]{2,1,0:T(8,128)(2,1)S(1)} %get-tuple-element.474) | copy-start | bytes 2457604
  80.0 88.4 %copy-start.16 = (f32[128,1600]{1,0:T(8,128)}, f32[128,1600]{1,0:T(8,128)S(1)}, u32[]{:S(2)}) copy-start(f32[128,1600]{1,0:T(8,128)S(1)} %get-tuple-element.477.refs_11_) | copy-start | bytes 2457604
  171.5 1.0 copy-start.11
  171.5 1.1 copy-start.12
  172.6 47.8 %copy-start = (bf16[1,128,1600]{2,1,0:T(8,128)(2,1)S(1)}, bf16[1,128,1600]{2,1,0:T(8,128)(2,1)}, u32[]{:S(2)}) copy-start(bf16[1,128,1600]{2,1,0:T(8,128)(2,1)} %copy.63) | copy-start | bytes 1228804
  217.5 1.7 copy-start.1
  219.2 1.0 copy-start.7
  251.5 55.0 %copy-start.3 = (bf16[64,1600]{1,0:T(8,128)(2,1)S(1)}, bf16[64,1600]{1,0:T(8,128)(2,1)}, u32[]{:S(2)}) copy-start(bf16[64,1600]{1,0:T(8,128)(2,1)} %constant_dynamic-slice_fusion.cot_ref) | copy-start | bytes 614404
  251.5 55.0 %copy-start.13 = (f32[8,1600]{1,0:T(8,128)S(1)}, f32[8,1600]{1,0:T(8,128)}, u32[]{:S(2)}) copy-start(f32[8,1600]{1,0:T(8,128)} %get-tuple-element.461.gains_ref) | copy-start | bytes 153604
  306.4 2.9 copy-start.6
  306.5 1.1 copy-start.8
  307.6 1.0 copy-start.9
  309.3 1.9 copy-start.2
  311.2 54.3 %copy-start.17 = (bf16[128,2048]{1,0:T(8,128)(2,1)S(1)}, bf16[128,2048]{1,0:T(8,128)(2,1)}, u32[]{:S(2)}) copy-start(bf16[128,2048]{1,0:T(8,128)(2,1)} %get-tuple-element.528.refs_6_) | copy-start | bytes 1572868
  363.8 0.8 copy-start.4
  365.7 4.4 copy-start.19
  370.1 69.7 %copy-start.5 = (bf16[16,32,384]{2,1,0:T(8,128)(2,1)S(1)}, bf16[16,32,384]{2,1,0:T(8,128)(2,1)}, u32[]{:S(2)}) copy-start(bf16[16,32,384]{2,1,0:T(8,128)(2,1)} %copy-done.4) | copy-start | bytes 1179652
  475.3 25.5 %copy-start.22 = (f32[1,1600]{1,0:T(1,128)S(1)}, f32[1,1600]{1,0:T(1,128)}, u32[]{:S(2)}) copy-start(f32[1,1600]{1,0:T(1,128)} %get-tuple-element.548) | copy-start | bytes 19204
  475.3 26.0 %copy-start.10 = (f32[32,3264]{1,0:T(8,128)S(1)}, f32[32,3264]{1,0:T(8,128)}, u32[]{:S(2)}) copy-start(f32[32,3264]{1,0:T(8,128)} %get-tuple-element.538.refs_2_) | copy-start | bytes 1253380
  475.4 26.0 %copy-start.14 = (f32[32,768]{1,0:T(8,128)S(1)}, f32[32,768]{1,0:T(8,128)}, u32[]{:S(2)}) copy-start(f32[32,768]{1,0:T(8,128)} %get-tuple-element.539.refs_3_) | copy-start | bytes 294916
  475.6 23.0 %copy-start.20 = (f32[128,256]{1,0:T(8,128)S(1)}, f32[128,256]{1,0:T(8,128)}, u32[]{:S(2)}) copy-start(f32[128,256]{1,0:T(8,128)} %get-tuple-element.280.one_ref) | copy-start | bytes 393220 | tf_op jit(solution)/shard_map/cond
  475.7 23.0 %copy-start.21 = (f32[256,16]{1,0:T(8,128)S(1)}, f32[256,16]{1,0:T(8,128)}, u32[]{:S(2)}) copy-start(f32[256,16]{1,0:T(8,128)} %get-tuple-element.282.rate_ref) | copy-start | bytes 49156 | tf_op jit(solution)/shard_map/cond
Sparse Core Ops, SparseCore 0:
  127.3 48.7 all-gather.1
